TPU v7x, 32 devices: a whole 2x2x4 slice. The times are simulated.
32 devices in a mesh: seq: 8 (over z, x), head: 4 (over y, core).
Axes of the slice: x: 2, y: 2, z: 4, core: 2. Of those that a mesh axis runs over, the one named last changes fastest.
Arguments:
- queries: bfloat16 [2048, 512], P('seq', 'head'), may hold values from -16 to 16
- keys: bfloat16 [2048, 512], P('seq', 'head'), may hold values from -16 to 16
- values: bfloat16 [2048, 512], P('seq', 'head'), may hold values from -16 to 16
- out_weight: bfloat16 [512, 512], replicated, may hold values from -0.5 to 0.5
Outputs:
- mixed: bfloat16 [2048, 512], P(('seq', 'head'))
All inputs are finite; a program needn't handle non-finite values.
Results may differ from a plain program's by a relative error of at most 0.00185.
The roundings to bfloat16 on the way count: a program that leaves them out, or rounds other values in their place, can miss the bound.
Values may be sent and summed in bfloat16 or wider, within the bound.
No kernel may reach another device: no remote copies, remote signals or barrier semaphores. Data moves between devices by JAX's collectives and lax.ppermute only.
A program may use at most 128 MiB of HBM per device.

v0:
```python
import math

import jax
import jax.numpy as jnp
from jax import lax
from jax.sharding import PartitionSpec as P

HD = 64
LEAF = 128


def extended_2(cells, sides, width):
    for axis, dim in sides:
        count = lax.axis_size(axis)
        ends = count - 1
        head = lax.slice_in_dim(cells, 0, width, axis=dim)
        tail = lax.slice_in_dim(cells, cells.shape[dim] - width, cells.shape[dim], axis=dim)
        cells = jnp.concatenate(
            [
                lax.ppermute(tail, axis, [(i, (i + 1) % count) for i in range(ends)]),
                cells,
                lax.ppermute(head, axis, [((i + 1) % count, i) for i in range(ends)]),
            ],
            axis=dim,
        )
    return cells


def as_sent(x):

    def short(part):
        return part.astype(jnp.bfloat16) if part.dtype == jnp.float32 else part

    return jax.tree.map(short, x)


def average_pairs(stacked):
    widened = stacked.astype(jnp.float32).reshape(2, stacked.shape[1] // 2, 2, stacked.shape[2])
    return (0.5 * (widened[:, :, 0] + widened[:, :, 1])).astype(jnp.bfloat16)


def near_set(leaf, extended, seq_index, blocks_dev, seq_size):
    positions = jnp.arange(LEAF, dtype=jnp.int32)
    upper_half = positions >= LEAF // 2
    global_leaf = seq_index * blocks_dev + leaf
    all_blocks = seq_size * blocks_dev
    key_parts = [lax.dynamic_slice_in_dim(extended[0], leaf * LEAF, 3 * LEAF, 1)]
    neighbour = global_leaf - 1 + jnp.arange(3 * LEAF, dtype=jnp.int32) // LEAF
    valid_parts = [(neighbour >= 0) & (neighbour < all_blocks)]
    local_block = leaf >> 1
    global_block = global_leaf >> 1
    parity = global_leaf >> 0 & 1
    level_blocks = all_blocks >> 1
    key_parts.append(lax.dynamic_slice_in_dim(extended[1], local_block * LEAF, LEAF, 1))
    key_parts.append(lax.dynamic_slice_in_dim(extended[1], (local_block + 2) * LEAF, LEAF, 1))
    valid_parts.append((global_block >= 1) & jnp.logical_not(upper_half & (parity == 0)))
    valid_parts.append(
        (global_block + 1 < level_blocks)
        & jnp.logical_not(jnp.logical_not(upper_half) & (parity == 1))
    )
    return (jnp.concatenate(key_parts, axis=1), jnp.concatenate(valid_parts, axis=0))


def shards(queries, keys, values, out_weight):
    tok_count = queries.shape[0]
    width = queries.shape[1]
    seq_size = lax.axis_size("seq")
    seq_index = lax.axis_index("seq")
    blocks_dev = tok_count // LEAF
    near_count = blocks_dev.bit_length() - 1
    far_count = max(0, seq_size.bit_length() - 2)
    scale = 1.0 / math.sqrt(HD)
    positions = jnp.arange(LEAF, dtype=jnp.int32)
    upper_half = positions >= LEAF // 2
    local = [jnp.stack([keys, values], axis=0)]
    local.append(average_pairs(local[-1]))
    extended = [extended_2(stacked, (("seq", 1),), LEAF) for stacked in local]
    own_block = local[near_count]
    far_pairs = []
    far_valid = []
    everything = lax.all_gather(own_block, "seq", axis=1, tiled=True)
    for level_far in range(1, far_count + 1):
        everything = average_pairs(everything)
        group = seq_index >> level_far
        padded = jnp.pad(everything, ((0, 0), (LEAF, LEAF), (0, 0)))
        lower = lax.dynamic_slice_in_dim(padded, group * LEAF, LEAF, 1)
        upper = lax.dynamic_slice_in_dim(padded, (group + 2) * LEAF, LEAF, 1)
        far_pairs.append(jnp.concatenate([lower, upper], axis=1))
    for level_far in range(1, far_count + 1):
        group = seq_index >> level_far
        parity = seq_index >> level_far - 1 & 1
        far_valid.append((group >= 1) & jnp.logical_not(upper_half & (parity == 0)))
        far_valid.append(
            (group + 1 < seq_size >> level_far)
            & jnp.logical_not(jnp.logical_not(upper_half) & (parity == 1))
        )
    far_keys = jnp.concatenate(far_pairs, axis=1)
    far_mask = jnp.concatenate(far_valid, axis=0)
    leaves_step = min(blocks_dev, max(1, 512 // LEAF))
    step_count = blocks_dev // leaves_step

    def attend(step):
        leaves = step * leaves_step + jnp.arange(leaves_step, dtype=jnp.int32)
        near_keys, near_mask = jax.vmap(
            lambda leaf: near_set(leaf, extended, seq_index, blocks_dev, seq_size)
        )(leaves)
        query_block = queries.reshape(leaves_step, LEAF, width)
        head_outputs = []
        for head_number in range(width // HD):
            low_col = head_number * HD
            high_col = low_col + HD
            near_scores = (
                jnp.einsum(
                    "nhs,nos->nho",
                    query_block[:, :, low_col:high_col],
                    near_keys[:, 0, :, low_col:high_col],
                    preferred_element_type=jnp.float32,
                )
                * scale
            )
            near_scores = jnp.where(near_mask[:, None, :], near_scores, -jnp.inf)
            peak = jnp.max(near_scores, axis=-1, keepdims=True)
            far_scores = (
                jnp.einsum(
                    "qs,os->qo",
                    queries[:, low_col:high_col],
                    far_keys[0, :, low_col:high_col],
                    preferred_element_type=jnp.float32,
                )
                * scale
            )
            far_scores = far_scores.reshape(leaves_step, LEAF, far_scores.shape[-1])
            far_scores = jnp.where(far_mask[None, None, :], far_scores, -jnp.inf)
            peak = jnp.maximum(peak, jnp.max(far_scores, axis=-1, keepdims=True))
            near_weights = jnp.exp(near_scores - peak)
            total = jnp.sum(near_weights, axis=-1)
            numer = jnp.einsum(
                "fkm,fmp->fkp",
                near_weights.astype(jnp.bfloat16),
                near_keys[:, 1, :, low_col:high_col],
                preferred_element_type=jnp.float32,
            )
            far_weights = jnp.exp(far_scores - peak)
            total = total + jnp.sum(far_weights, axis=-1)
            far_rounded = far_weights.astype(jnp.bfloat16).reshape(
                leaves_step * LEAF, far_weights.shape[-1]
            )
            far_numer = jnp.dot(
                far_rounded, far_keys[1, :, low_col:high_col], preferred_element_type=jnp.float32
            )
            numer = numer + far_numer.reshape(leaves_step, LEAF, HD)
            head_outputs.append((numer / total[..., None]).astype(jnp.bfloat16))
        return jnp.concatenate(head_outputs, axis=-1).reshape(leaves_step * LEAF, width)

    attended = lax.map(attend, jnp.arange(step_count, dtype=jnp.int32)).reshape(tok_count, width)
    gathered_rows = lax.all_to_all(
        as_sent(attended), "head", split_axis=0, concat_axis=1, tiled=True
    ).astype(attended.dtype)
    return jnp.dot(gathered_rows, out_weight, preferred_element_type=jnp.float32).astype(
        jnp.bfloat16
    )


def solution(mesh):
    in_specs = (P("seq", "head"), P("seq", "head"), P("seq", "head"), P())
    out_specs = P(("seq", "head"), None)
    return jax.shard_map(shards, mesh=mesh, in_specs=in_specs, out_specs=out_specs, check_vma=False)
```

profile of v0, /device:TPU:0, one launch (start us, length us, event | category | flops | bytes accessed | tf_op | source)
XLA Modules:
  0.0 73.5 jit_solution(4320842074816344829)
XLA Ops:
  0.0 1.0 %copy.31 = bf16[1,128,2,128]{3,0,1,2:T(2,128)(2,1)S(1)} copy(bf16[1,128,2,128]{3,2,1,0:T(2,128)(2,1)} %bitcast.94) | data formatting | bytes 131072 | tf_op jit(solution)/shard_map/stack | solution.py:75
  1.0 0.0 copy-start.2
  1.0 1.0 %copy.32 = bf16[1,128,2,128]{3,0,1,2:T(2,128)(2,1)S(1)} copy(bf16[1,128,2,128]{3,2,1,0:T(2,128)(2,1)} %bitcast.96) | data formatting | bytes 131072 | tf_op jit(solution)/shard_map/stack | solution.py:75
  2.0 0.3 maximum_convert_fusion
  2.4 0.1 fusion.59
  2.5 4.8 %collective-permute-start.2 = (bf16[2,128,128]{2,0,1:T(2,128)(2,1)S(1)}, bf16[2,128,128]{2,0,1:T(2,128)(2,1)S(1)}, u32[]{:S(2)}, u32[]{:S(2)}) collective-permute-start(bf16[2,128,128]{2,0,1:T(2,128)(2,1)S(1)} %fusion.59), channel_id=1, source_target_pairs={{0,4},{4,8},{8,12},{12,16},{16,20},{20,24},{24,28},{1,5},{5,9},{9,... | collective-permute-start | bytes 196616 | tf_op jit(solution)/shard_map/ppermute | solution.py:20
  7.3 1.3 %collective-permute-start.3 = (bf16[2,128,128]{2,0,1:T(2,128)(2,1)S(1)}, bf16[2,128,128]{2,0,1:T(2,128)(2,1)}, u32[]{:S(2)}, u32[]{:S(2)}) collective-permute-start(bf16[2,128,128]{2,0,1:T(2,128)(2,1)S(1)} %fusion.59), channel_id=1, source_target_pairs={{4,0},{8,4},{12,8},{16,12},{20,16},{24,20},{28,24},{5,1},{9,5},{13... | collective-permute-start | bytes 196616 | tf_op jit(solution)/shard_map/ppermute | solution.py:22
  8.6 0.1 copy.29
  8.7 0.1 copy.30
  8.8 0.3 fusion.25
  9.1 4.6 %collective-permute-start = (bf16[2,128,128]{2,0,1:T(2,128)(2,1)S(1)}, bf16[2,128,128]{2,0,1:T(2,128)(2,1)S(1)}, u32[]{:S(2)}, u32[]{:S(2)}) collective-permute-start(bf16[2,128,128]{2,0,1:T(2,128)(2,1)S(1)} %get-tuple-element.37), channel_id=1, source_target_pairs={{0,4},{4,8},{8,12},{12,16},{16,20},{20,24},{24,28},{1,5},{5,9},{9,... | collective-permute-start | bytes 196616 | tf_op jit(solution)/shard_map/ppermute | solution.py:20
  13.7 1.3 %collective-permute-start.1 = (bf16[2,128,128]{2,0,1:T(2,128)(2,1)S(1)}, bf16[2,128,128]{2,0,1:T(2,128)(2,1)S(1)}, u32[]{:S(2)}, u32[]{:S(2)}) collective-permute-start(bf16[2,128,128]{2,0,1:T(2,128)(2,1)S(1)} %get-tuple-element.38), channel_id=1, source_target_pairs={{4,0},{8,4},{12,8},{16,12},{20,16},{24,20},{28,24},{5,1},{9,5},{13... | collective-permute-start | bytes 196616 | tf_op jit(solution)/shard_map/ppermute | solution.py:22
  15.0 0.1 fusion.60
  15.1 0.5 fusion.42
  15.6 0.6 broadcast_compare_fusion
  16.2 0.6 add_compare_fusion
  16.8 0.5 fusion.49
  17.3 0.5 iota_compare_fusion
  17.9 0.5 fusion.47
  18.4 34.7 %all-gather = bf16[2,1024,1,128]{3,0,2,1:T(2,128)(2,1)S(1)} all-gather(bf16[2,128,1,128]{3,0,2,1:T(2,128)(2,1)S(1)} %fusion.60), channel_id=2, replica_groups=mesh['seq'=8,'head'=4] {'seq'}, dimensions={1}, use_global_device_ids=true | all-gather | bytes 589824 | tf_op jit(solution)/shard_map/all_gather | solution.py:81
  53.1 0.1 copy.38
  53.2 0.7 fusion.51
  53.9 0.3 copy.52
  54.3 0.3 copy.53
  54.6 0.1 multiply_convert_fusion
  54.8 0.1 copy.41
  54.9 0.4 fusion.50
  55.3 0.1 copy.54
  55.5 0.1 copy.55
  55.6 0.0 copy-start.3
  55.7 0.1 pad_dynamic-slice_fusion.1
  55.9 0.6 copy-done.3
  56.5 0.0 copy-start.5
  56.5 0.3 fusion.54
  56.8 0.4 fusion.52
  57.2 0.1 compare_and_fusion
  57.3 0.1 not_and_fusion.4
  57.4 0.1 not_and_fusion.5
  57.5 0.0 collective-permute-done.2
  57.5 0.0 collective-permute-done.3
  57.5 1.1 %pad_maximum_fusion.3 = bf16[2,384,128]{2,0,1:T(2,128)(2,1)S(1)} fusion(bf16[2,128,128]{2,0,1:T(2,128)(2,1)} %collective-permute-done.3, bf16[2,128,128]{2,0,1:T(2,128)(2,1)S(1)} %fusion.59, bf16[2,128,128]{2,0,1:T(2,128)(2,1)S(1)} %collective-permute-done.2), kind=kLoop, calls=%fused_computation.43 | loop fusion | flops 196608 | bytes 393216 | tf_op jit(solution)/shard_map/concatenate | solution.py:18
  58.6 0.8 %gather_fusion.1 = bf16[2,2,128,128]{3,1,2,0:T(2,128)(2,1)S(1)} fusion(bf16[2,384,128]{2,0,1:T(2,128)(2,1)S(1)} %pad_maximum_fusion.3, s32[2]{0:T(128)S(1)} %copy-done.4), kind=kCustom, calls=%fused_computation.1 | custom fusion | bytes 262168 | tf_op jit(solution)/shard_map/while/body/eval_jaxpr/vmap()/gather | solution.py:54
  59.4 0.1 copy.34
  59.6 0.8 %gather_fusion.2 = bf16[2,2,128,128]{3,1,2,0:T(2,128)(2,1)S(1)} fusion(bf16[2,384,128]{2,0,1:T(2,128)(2,1)S(1)} %pad_maximum_fusion.3, s32[2]{0:T(128)S(1)} %get-tuple-element.52), kind=kCustom, calls=%fused_computation.2 | custom fusion | bytes 262168 | tf_op jit(solution)/shard_map/while/body/eval_jaxpr/vmap()/gather | solution.py:55
  60.4 0.1 copy.35
  60.5 0.0 collective-permute-done
  60.5 0.0 collective-permute-done.1
  60.5 0.4 pad_maximum_fusion.1
  61.0 1.3 %gather_fusion = bf16[2,2,384,128]{3,1,2,0:T(2,128)(2,1)S(1)} fusion(bf16[2,512,128]{2,0,1:T(2,128)(2,1)S(1)} %pad_maximum_fusion.1, s32[2]{0:T(128)S(1)} %fusion.39), kind=kCustom, calls=%fused_computation | custom fusion | bytes 786456 | tf_op jit(solution)/shard_map/while/body/eval_jaxpr/vmap()/gather | solution.py:47
  62.3 0.4 copy.33
  62.8 0.1 pad_maximum_fusion
  62.8 0.6 fusion.55
  63.5 0.7 fusion.53
  64.2 0.2 fusion.14
  64.4 0.2 fusion.30
  64.6 0.2 fusion.16
  64.9 0.2 fusion.28
  65.1 0.1 fusion.10
  65.2 0.2 fusion.8
  65.4 0.1 fusion.12
  65.6 0.2 fusion.9
  65.8 0.1 copy.47
  65.9 6.7 %all_to_all.19 = bf16[4,64,128]{2,1,0:T(8,128)(2,1)S(1)} all-to-all(bf16[4,64,128]{2,1,0:T(8,128)(2,1)S(1)} %bitcast.100), channel_id=1, replica_groups=mesh['seq'=8,'head'=4] {'head'}, dimensions={0} | all-to-all | bytes 131072 | tf_op jit(solution)/shard_map/all_to_all | solution.py:156
  72.7 0.8 %convolution_convert_fusion = bf16[64,512]{1,0:T(8,128)(2,1)} fusion(bf16[512,512]{1,0:T(8,128)(2,1)S(1)} %copy-done, bf16[4,64,128]{2,1,0:T(8,128)(2,1)S(1)} %all_to_all.19), kind=kOutput, calls=%fused_computation.13 | convolution fusion | flops 33587200 | bytes 655360 | tf_op jit(solution)/shard_map/dot_general | solution.py:159
  (35 shorter events, 0.2 us)
Async XLA Ops:
  0.0 72.7 %copy-start = (bf16[512,512]{1,0:T(8,128)(2,1)S(1)}, bf16[512,512]{1,0:T(8,128)(2,1)}, u32[]{:S(2)}) copy-start(bf16[512,512]{1,0:T(8,128)(2,1)} %param.7) | copy-start | bytes 1572868
  0.0 8.6 %copy-start.1 = (bf16[256,128]{1,0:T(8,128)(2,1)S(1)}, bf16[256,128]{1,0:T(8,128)(2,1)}, u32[]{:S(2)}) copy-start(bf16[256,128]{1,0:T(8,128)(2,1)} %param.5) | copy-start | bytes 196612
  1.0 7.7 %copy-start.2 = (bf16[256,128]{1,0:T(8,128)(2,1)S(1)}, bf16[256,128]{1,0:T(8,128)(2,1)}, u32[]{:S(2)}) copy-start(bf16[256,128]{1,0:T(8,128)(2,1)} %param.6) | copy-start | bytes 196612
  2.5 55.0 %collective-permute-start.2 = (bf16[2,128,128]{2,0,1:T(2,128)(2,1)S(1)}, bf16[2,128,128]{2,0,1:T(2,128)(2,1)S(1)}, u32[]{:S(2)}, u32[]{:S(2)}) collective-permute-start(bf16[2,128,128]{2,0,1:T(2,128)(2,1)S(1)} %fusion.59), channel_id=1, source_target_pairs={{0,4},{4,8},{8,12},{12,16},{16,20},{20,24},{24,28},{1,5},{5,9},{9,... | collective-permute-start | bytes 196616 | tf_op jit(solution)/shard_map/ppermute | solution.py:20
  7.3 50.2 %collective-permute-start.3 = (bf16[2,128,128]{2,0,1:T(2,128)(2,1)S(1)}, bf16[2,128,128]{2,0,1:T(2,128)(2,1)}, u32[]{:S(2)}, u32[]{:S(2)}) collective-permute-start(bf16[2,128,128]{2,0,1:T(2,128)(2,1)S(1)} %fusion.59), channel_id=1, source_target_pairs={{4,0},{8,4},{12,8},{16,12},{20,16},{24,20},{28,24},{5,1},{9,5},{13... | collective-permute-start | bytes 196616 | tf_op jit(solution)/shard_map/ppermute | solution.py:22
  9.1 51.4 %collective-permute-start = (bf16[2,128,128]{2,0,1:T(2,128)(2,1)S(1)}, bf16[2,128,128]{2,0,1:T(2,128)(2,1)S(1)}, u32[]{:S(2)}, u32[]{:S(2)}) collective-permute-start(bf16[2,128,128]{2,0,1:T(2,128)(2,1)S(1)} %get-tuple-element.37), channel_id=1, source_target_pairs={{0,4},{4,8},{8,12},{12,16},{16,20},{20,24},{24,28},{1,5},{5,9},{9,... | collective-permute-start | bytes 196616 | tf_op jit(solution)/shard_map/ppermute | solution.py:20
  13.7 46.8 %collective-permute-start.1 = (bf16[2,128,128]{2,0,1:T(2,128)(2,1)S(1)}, bf16[2,128,128]{2,0,1:T(2,128)(2,1)S(1)}, u32[]{:S(2)}, u32[]{:S(2)}) collective-permute-start(bf16[2,128,128]{2,0,1:T(2,128)(2,1)S(1)} %get-tuple-element.38), channel_id=1, source_target_pairs={{4,0},{8,4},{12,8},{16,12},{20,16},{24,20},{28,24},{5,1},{9,5},{13... | collective-permute-start | bytes 196616 | tf_op jit(solution)/shard_map/ppermute | solution.py:22
  55.6 0.8 %copy-start.3 = (bf16[256,128]{1,0:T(8,128)(2,1)S(1)}, bf16[256,128]{1,0:T(8,128)(2,1)}, u32[]{:S(2)}) copy-start(bf16[256,128]{1,0:T(8,128)(2,1)} %param.4) | copy-start | bytes 196612
  56.5 0.7 copy-start.11
  56.5 0.8 %copy-start.8 = (pred[2]{0:T(512)(128)(4,1)S(1)}, pred[2]{0:T(512)(128)(4,1)}, u32[]{:S(2)}) copy-start(pred[2]{0:T(512)(128)(4,1)} %get-tuple-element.54) | copy-start | bytes 10
  56.5 0.8 %copy-start.9 = (pred[2]{0:T(512)(128)(4,1)S(1)}, pred[2]{0:T(512)(128)(4,1)}, u32[]{:S(2)}) copy-start(pred[2]{0:T(512)(128)(4,1)} %get-tuple-element.61) | copy-start | bytes 10
  56.5 0.8 %copy-start.10 = (pred[128]{0:T(512)(128)(4,1)S(1)}, pred[128]{0:T(512)(128)(4,1)}, u32[]{:S(2)}) copy-start(pred[128]{0:T(512)(128)(4,1)} %fusion.49) | copy-start | bytes 388
  56.5 0.9 %copy-start.5 = (pred[2]{0:T(512)(128)(4,1)S(1)}, pred[2]{0:T(512)(128)(4,1)}, u32[]{:S(2)}) copy-start(pred[2]{0:T(512)(128)(4,1)} %get-tuple-element.53) | copy-start | bytes 10
  56.5 0.8 %copy-start.6 = (pred[2]{0:T(512)(128)(4,1)S(1)}, pred[2]{0:T(512)(128)(4,1)}, u32[]{:S(2)}) copy-start(pred[2]{0:T(512)(128)(4,1)} %get-tuple-element.62) | copy-start | bytes 10
  56.5 0.8 %copy-start.7 = (pred[128]{0:T(512)(128)(4,1)S(1)}, pred[128]{0:T(512)(128)(4,1)}, u32[]{:S(2)}) copy-start(pred[128]{0:T(512)(128)(4,1)} %iota_compare_fusion) | copy-start | bytes 388
  56.8 1.8 %copy-start.4 = (s32[2]{0:T(128)S(1)}, s32[2]{0:T(128)}, u32[]{:S(2)}) copy-start(s32[2]{0:T(128)} %get-tuple-element.51) | copy-start | bytes 28
where the time goes:
time: 73.9 us; the launch traced here: 73.5 us
  blocking collectives  41.4 us (56%)
  starting transfers between devices  12 us (16%)
  local copies, waits for them, and re-layouts  9.05 us (12%)
  other arithmetic  6.8 us (9%)
  matrix products  3.67 us (5%)
    all_gather x1, blocking collectives, shards(): everything = lax.all_gather(own_block, 'seq', axis=1, tiled=True)  34.7 us
    ppermute x2, starting transfers between devices, extended_2(): lax.ppermute(tail, axis, [(i, (i + 1) % count) for i in range(ends)])  9.4 us
    all_to_all x1, blocking collectives, shards(): lax.all_to_all(as_sent(attended), 'head', split_axis=0, concat_axis=1, ti...  6.71 us
    ppermute x2, starting transfers between devices, extended_2(): lax.ppermute(head, axis, [((i + 1) % count, i) for i in range(ends)])  2.58 us
    another operation x4, local copies, waits for them, and re-layouts, shards(): local = [jnp.stack([keys, values], axis=0)]  2.22 us
    gather x2, local copies, waits for them, and re-layouts, near_set(): lax.dynamic_slice_in_dim(extended[0], leaf * LEAF, 3 * LEAF, 1)  1.78 us
    unnamed x28, local copies, waits for them, and re-layouts  1.64 us
    concatenate x2, other arithmetic, extended_2(): jnp.concatenate([lax.ppermute(tail, axis, [(i, (i + 1) % count) for i in...  1.52 us
  transfers between devices with their start and end apart: 4, of which 0 were waited for; matrix products, arithmetic and copies ran while one was open for 14% of the time, Pallas kernels for 0%

commit v1 on v0

v1 whole, which is shorter than its diff:
```python
import functools
import math

import jax
import jax.numpy as jnp
from jax import lax
from jax.experimental import pallas as pl
from jax.experimental.pallas import tpu as pltpu
from jax.sharding import PartitionSpec as P

HD = 64
LEAF = 128
HALF = LEAF // 2
NEG = -math.inf


def average_pairs(rows, wide):
    count = rows.shape[0]
    halves = []
    for low in range(0, rows.shape[1], LEAF):
        wide[:count] = rows[:, low : low + LEAF].astype(jnp.float32)
        even = wide[pl.ds(0, count // 2, stride=2), :]
        odd = wide[pl.ds(1, count // 2, stride=2), :]
        halves.append((0.5 * (even + odd)).astype(jnp.bfloat16))
    return jnp.concatenate(halves, axis=1)


def pack_kernel(keys, values, pair, quarter, wide):
    width = keys.shape[1]
    pair[:, :width] = keys[...]
    pair[:, width:] = values[...]
    level_two = average_pairs(average_pairs(pair[...], wide), wide)
    for peer in range(quarter.shape[0]):
        quarter[peer] = level_two


def segments(seq_size):
    far_count = seq_size.bit_length() - 2
    rows = []
    for far in range(1, far_count + 1):
        if seq_size >> far == 2:
            rows.append(LEAF)
        elif far == 1:
            rows.append(3 * HALF)
        else:
            rows.append(2 * LEAF)
    return rows


def attend_kernel(seq_size, queries, own, before, after, far_rows, attended, key_set, wide):
    me = lax.axis_index("seq")
    width = queries.shape[1]
    zero, neg = jnp.float32(0.0), jnp.float32(NEG)

    def bias_of(valid):
        return jnp.where(valid, zero, neg)

    coarse_before = average_pairs(before[...], wide)
    coarse_after = average_pairs(after[...], wide)
    has_before, has_after = bias_of(me >= 1), bias_of(me + 1 < seq_size)

    far_pieces = []
    for far, _ in enumerate(segments(seq_size), 1):
        span = 1 << far
        group = me >> far
        parity = (me >> (far - 1)) & 1
        blocks = seq_size >> far

        def block(number, span=span, far=far):
            found = far_rows[pl.ds(number * span, span)].reshape(span * HALF, 2 * width)
            for _ in range(far - 1):
                found = average_pairs(found, wide)
            return found

        if blocks == 2:
            rows = block(1 - group)
            first = bias_of((group == 1) | (parity == 0))
            second = bias_of((group == 0) | (parity == 1))
            far_pieces += [(rows[:HALF], first), (rows[HALF:], second)]
        elif far == 1:
            third = jnp.where(parity == 0, me + 3, me - 3)
            for peer in (me - 2, me + 2, third):
                ok = (peer >= 0) & (peer < seq_size)
                far_pieces.append((far_rows[jnp.clip(peer, 0, seq_size - 1)], bias_of(ok)))
        else:
            lower = block(jnp.maximum(group - 1, 0))
            upper = block(jnp.minimum(group + 1, blocks - 1))
            has_lower, has_upper = group >= 1, group + 1 < blocks
            far_pieces += [
                (lower[:HALF], bias_of(has_lower)),
                (lower[HALF:], bias_of(has_lower & (parity == 1))),
                (upper[:HALF], bias_of(has_upper & (parity == 0))),
                (upper[HALF:], bias_of(has_upper)),
            ]

    lane = lax.broadcasted_iota(jnp.int32, (1, width), 1)
    first_head = lane < HD
    exponent = math.log2(math.e) / math.sqrt(HD)
    for leaf in range(2):
        if leaf == 0:
            near = [
                (before[LEAF:], has_before),
                (own[...], None),
                (coarse_before[:HALF], has_before),
                (coarse_after, has_after),
            ]
        else:
            near = [
                (own[...], None),
                (after[:LEAF], has_after),
                (coarse_before, has_before),
                (coarse_after[HALF:], has_after),
            ]
        at = 0
        total_rows = key_set.shape[0]
        position = lax.broadcasted_iota(jnp.int32, (1, total_rows), 1)
        bias = jnp.zeros((1, total_rows), jnp.float32)
        for rows, value in near + far_pieces:
            count = rows.shape[0]
            key_set[at : at + count] = rows
            if value is not None:
                bias = jnp.where((position >= at) & (position < at + count), value, bias)
            at += count
        block_queries = queries[leaf * LEAF : (leaf + 1) * LEAF]
        none = jnp.zeros_like(block_queries)
        both = jnp.concatenate(
            [jnp.where(first_head, block_queries, none), jnp.where(first_head, none, block_queries)], axis=0
        )
        scores = lax.dot_general(
            both, key_set[:, :width], (((1,), (1,)), ((), ())), preferred_element_type=jnp.float32
        )
        scores = scores + bias
        peak = jnp.max(scores, axis=1, keepdims=True)
        weights = jnp.exp2((scores - peak) * exponent)
        total = jnp.sum(weights, axis=1, keepdims=True)
        numer = jnp.dot(
            weights.astype(jnp.bfloat16), key_set[:, width:], preferred_element_type=jnp.float32
        )
        shares = numer / total
        attended[leaf * LEAF : (leaf + 1) * LEAF] = jnp.where(
            first_head, shares[:LEAF], shares[LEAF:]
        ).astype(jnp.bfloat16)


def project_kernel(rows, weight, mixed):
    width = rows.shape[2]
    total = jnp.zeros(mixed.shape, jnp.float32)
    for part in range(rows.shape[0]):
        total += jnp.dot(
            rows[part], weight[part * width : (part + 1) * width], preferred_element_type=jnp.float32
        )
    mixed[...] = total.astype(mixed.dtype)


VMEM = pl.BlockSpec(memory_space=pltpu.VMEM)


def shards(queries, keys, values, out_weight):
    tokens, width = queries.shape
    seq_size = lax.axis_size("seq")
    head_size = lax.axis_size("head")
    bf16 = jnp.bfloat16
    wide_rows = max(2 * LEAF, seq_size // 2 * HALF)
    wide = pltpu.VMEM((wide_rows, width), jnp.float32)
    pair, quarter = pl.pallas_call(
        pack_kernel,
        out_shape=(
            jax.ShapeDtypeStruct((tokens, 2 * width), bf16),
            jax.ShapeDtypeStruct((seq_size, HALF, 2 * width), bf16),
        ),
        in_specs=[VMEM] * 2,
        out_specs=(VMEM, VMEM),
        scratch_shapes=[wide],
        name="pack",
    )(keys, values)
    ends = seq_size - 1
    before = lax.ppermute(pair, "seq", [(i, i + 1) for i in range(ends)])
    after = lax.ppermute(pair, "seq", [(i + 1, i) for i in range(ends)])
    far_rows = lax.all_to_all(quarter, "seq", split_axis=0, concat_axis=0)
    set_rows = 3 * LEAF + 3 * HALF + sum(segments(seq_size))
    attended = pl.pallas_call(
        functools.partial(attend_kernel, seq_size),
        out_shape=jax.ShapeDtypeStruct((tokens, width), bf16),
        in_specs=[VMEM] * 5,
        out_specs=VMEM,
        scratch_shapes=[pltpu.VMEM((set_rows, 2 * width), bf16), wide],
        compiler_params=pltpu.CompilerParams(vmem_limit_bytes=40 << 20),
        name="attend",
    )(queries, pair, before, after, far_rows)
    share = tokens // head_size
    gathered = lax.all_to_all(
        attended.reshape(head_size, share, width), "head", split_axis=0, concat_axis=0
    )
    return pl.pallas_call(
        project_kernel,
        out_shape=jax.ShapeDtypeStruct((share, out_weight.shape[1]), bf16),
        in_specs=[VMEM] * 2,
        out_specs=VMEM,
        name="project",
    )(gathered, out_weight)


def solution(mesh):
    in_specs = (P("seq", "head"), P("seq", "head"), P("seq", "head"), P())
    out_specs = P(("seq", "head"), None)
    return jax.shard_map(shards, mesh=mesh, in_specs=in_specs, out_specs=out_specs, check_vma=False)
```

time: 73.9 us -> 30.9 us (0.42)
  blocking collectives: 41.4 us -> 7.16 us
  local copies, waits for them, and re-layouts: 9.05 us -> 0.01 us
  other arithmetic: 6.8 us -> 0 us
  waiting for transfers between devices: 0.01 us -> 5.31 us
  Pallas kernels: 0 us -> 4.78 us
  matrix products: 3.67 us -> 0 us
  starting transfers between devices: 12 us -> 13.2 us
    all_gather x1 -> x0, blocking collectives: 34.7 us -> none  [shards(): everything = lax.all_gather(own_block, 'seq', axis=1, tiled=True)]
    all_to_all x0 -> x1, starting transfers between devices: none -> 7.38 us  [shards(): far_rows = lax.all_to_all(quarter, 'seq', split_axis=0, concat_axis=0)]
    ppermute x4 -> x2, starting transfers between devices: 12 us -> 5.85 us  [the longest x1 4.55 us: shards(): before = lax.ppermute(pair, 'seq', [(i, i + 1) for i in range(ends)])]
    ppermute x4 -> x2, waiting for transfers between devices: 0.01 us -> 5.31 us  [the longest x1 2.66 us: shards(): before = lax.ppermute(pair, 'seq', [(i, i + 1) for i in range(ends)])]
    pallas_call x0 -> x3, Pallas kernels: none -> 4.78 us  [the longest x1 1.93 us: shards(): pl.pallas_call(project_kernel, out_shape=jax.ShapeDtypeStruct((share, out...]
    dot_general x9 -> x0, matrix products: 3.67 us -> none  [the longest x2 1.31 us: attend(): jnp.einsum('nhs,nos->nho', query_block[:, :, low_col:high_col], near_keys...]
    gather x6 -> x0, local copies, waits for them, and re-layouts: 3.66 us -> none  [the longest x2 1.78 us: near_set(): lax.dynamic_slice_in_dim(extended[0], leaf * LEAF, 3 * LEAF, 1)]
    another operation x4 -> x0, local copies, waits for them, and re-layouts: 2.22 us -> none  [shards(): local = [jnp.stack([keys, values], axis=0)]]
  transfers between devices with their start and end apart: 4 -> 3, of which waited for: 0 -> 2; matrix products, arithmetic and copies ran while one was open for 14% -> 0% of each run, Pallas kernels for 0% -> 0%
where the time goes in v1:
time: 30.9 us; the launch traced here: 30.5 us
  starting transfers between devices  13.2 us (43%)
  blocking collectives  7.16 us (23%)
  waiting for transfers between devices  5.31 us (17%)
  Pallas kernels  4.78 us (15%)
    all_to_all x1, starting transfers between devices, shards(): far_rows = lax.all_to_all(quarter, 'seq', split_axis=0, concat_axis=0)  7.38 us
    all_to_all x1, blocking collectives, shards(): lax.all_to_all(attended.reshape(head_size, share, width), 'head', split_a...  7.16 us
    ppermute x1, starting transfers between devices, shards(): before = lax.ppermute(pair, 'seq', [(i, i + 1) for i in range(ends)])  4.55 us
    ppermute x1, waiting for transfers between devices, shards(): before = lax.ppermute(pair, 'seq', [(i, i + 1) for i in range(ends)])  2.66 us
    ppermute x1, waiting for transfers between devices, shards(): after = lax.ppermute(pair, 'seq', [(i + 1, i) for i in range(ends)])  2.65 us
    pallas_call x1, Pallas kernels, shards(): pl.pallas_call(project_kernel, out_shape=jax.ShapeDtypeStruct((share, out...  1.93 us
    pallas_call x1, Pallas kernels, shards(): pl.pallas_call(pack_kernel, out_shape=(jax.ShapeDtypeStruct((tokens, 2 *...  1.66 us
    ppermute x1, starting transfers between devices, shards(): after = lax.ppermute(pair, 'seq', [(i + 1, i) for i in range(ends)])  1.29 us
  transfers between devices with their start and end apart: 3, of which 2 were waited for; matrix products, arithmetic and copies ran while one was open for 0% of the time, Pallas kernels for 0%

profile of v1, /device:TPU:0, one launch (start us, length us, event | category | flops | bytes accessed | tf_op | source)
XLA Modules:
  0.0 30.5 jit_solution(4238487894659085601)
XLA Ops:
  0.0 1.7 %pack.1 = (bf16[256,256]{1,0:T(8,128)(2,1)}, bf16[8,64,256]{2,1,0:T(8,128)(2,1)}) custom-call(bf16[256,128]{1,0:T(8,128)(2,1)} %keys.1, bf16[256,128]{1,0:T(8,128)(2,1)} %values.1), custom_call_target="tpu_custom_call" | custom-call | tf_op jit(solution)/shard_map/pack/pallas_call | solution.py:165
  1.7 0.0 copy-start
  1.7 0.0 copy-start.1
  1.7 7.4 %all-to-all-start = ((bf16[8,64,256]{2,1,0:T(8,128)(2,1)}), bf16[8,64,256]{2,1,0:T(8,128)(2,1)S(1)}, u32[]{:S(2)}, u32[]{:S(2)}) async-start(bf16[8,64,256]{2,1,0:T(8,128)(2,1)} %get-tuple-element.8), calls=%async_computation | async-start | bytes 524288 | tf_op jit(solution)/shard_map/all_to_all | solution.py:179
  9.0 0.0 copy-done
  9.1 1.3 %collective-permute-start.1 = (bf16[256,256]{1,0:T(8,128)(2,1)S(1)}, bf16[256,256]{1,0:T(8,128)(2,1)S(1)}, u32[]{:S(2)}, u32[]{:S(2)}) collective-permute-start(bf16[256,256]{1,0:T(8,128)(2,1)S(1)} %copy-done), channel_id=1, source_target_pairs={{4,0},{8,4},{12,8},{16,12},{20,16},{24,20},{28,24},{5,1},{9,5},{13... | collective-permute-start | bytes 393224 | tf_op jit(solution)/shard_map/ppermute | solution.py:178
  10.4 4.6 %collective-permute-start = (bf16[256,256]{1,0:T(8,128)(2,1)S(1)}, bf16[256,256]{1,0:T(8,128)(2,1)S(1)}, u32[]{:S(2)}, u32[]{:S(2)}) collective-permute-start(bf16[256,256]{1,0:T(8,128)(2,1)S(1)} %copy-done), channel_id=1, source_target_pairs={{0,4},{4,8},{8,12},{12,16},{16,20},{20,24},{24,28},{1,5},{5,9},{9,... | collective-permute-start | bytes 393224 | tf_op jit(solution)/shard_map/ppermute | solution.py:177
  14.9 2.7 %collective-permute-done.1.after = bf16[256,256]{1,0:T(8,128)(2,1)S(1)} collective-permute-done((bf16[256,256]{1,0:T(8,128)(2,1)S(1)}, bf16[256,256]{1,0:T(8,128)(2,1)S(1)}, u32[]{:S(2)}, u32[]{:S(2)}) %collective-permute-start.1) | collective-permute-done | bytes 131104 | tf_op jit(solution)/shard_map/ppermute | solution.py:178
  17.6 2.7 %collective-permute-done.before = bf16[256,256]{1,0:T(8,128)(2,1)S(1)} collective-permute-done((bf16[256,256]{1,0:T(8,128)(2,1)S(1)}, bf16[256,256]{1,0:T(8,128)(2,1)S(1)}, u32[]{:S(2)}, u32[]{:S(2)}) %collective-permute-start) | collective-permute-done | bytes 131104 | tf_op jit(solution)/shard_map/ppermute | solution.py:177
  20.2 0.0 all-to-all-done.far_rows
  20.2 0.0 copy-done.1
  20.2 1.2 %attend.1 = bf16[256,128]{1,0:T(8,128)(2,1)S(1)} custom-call(bf16[256,128]{1,0:T(8,128)(2,1)S(1)} %copy-done.1, bf16[256,256]{1,0:T(8,128)(2,1)S(1)} %copy-done, bf16[256,256]{1,0:T(8,128)(2,1)S(1)} %collective-permute-done.before, bf16[256,256]{1,0:T(8,128)(2,1)S(1)} %collective-permute-done.1.after, bf16[8,64,256]{2,1,0:T(8,128)(2,1)S(1)} %all-to-all-done.far_rows), custom_call_target="tpu_custom_call" | custom-call | tf_op jit(solution)/shard_map/attend/pallas_call | solution.py:181
  21.4 7.2 %all_to_all.10.rows = bf16[4,64,128]{2,1,0:T(8,128)(2,1)} all-to-all(bf16[4,64,128]{2,1,0:T(8,128)(2,1)S(1)} %bitcast.1), channel_id=1, replica_groups=mesh['seq'=8,'head'=4] {'head'}, dimensions={0} | all-to-all | bytes 131072 | tf_op jit(solution)/shard_map/all_to_all | solution.py:191
  28.6 1.9 %project.1 = bf16[64,512]{1,0:T(8,128)(2,1)} custom-call(bf16[4,64,128]{2,1,0:T(8,128)(2,1)} %all_to_all.10.rows, bf16[512,512]{1,0:T(8,128)(2,1)} %weight.1), custom_call_target="tpu_custom_call" | custom-call | tf_op jit(solution)/shard_map/project/pallas_call | solution.py:194
Async XLA Ops:
  1.7 7.4 %copy-start = (bf16[256,256]{1,0:T(8,128)(2,1)S(1)}, bf16[256,256]{1,0:T(8,128)(2,1)}, u32[]{:S(2)}) copy-start(bf16[256,256]{1,0:T(8,128)(2,1)} %get-tuple-element.7.own) | copy-start | bytes 393220
  1.7 18.6 %copy-start.1 = (bf16[256,128]{1,0:T(8,128)(2,1)S(1)}, bf16[256,128]{1,0:T(8,128)(2,1)}, u32[]{:S(2)}) copy-start(bf16[256,128]{1,0:T(8,128)(2,1)} %queries.1) | copy-start | bytes 196612
  1.7 18.6 %all-to-all-start = ((bf16[8,64,256]{2,1,0:T(8,128)(2,1)}), bf16[8,64,256]{2,1,0:T(8,128)(2,1)S(1)}, u32[]{:S(2)}, u32[]{:S(2)}) async-start(bf16[8,64,256]{2,1,0:T(8,128)(2,1)} %get-tuple-element.8), calls=%async_computation | async-start | bytes 524288 | tf_op jit(solution)/shard_map/all_to_all | solution.py:179
  9.1 8.5 %collective-permute-start.1 = (bf16[256,256]{1,0:T(8,128)(2,1)S(1)}, bf16[256,256]{1,0:T(8,128)(2,1)S(1)}, u32[]{:S(2)}, u32[]{:S(2)}) collective-permute-start(bf16[256,256]{1,0:T(8,128)(2,1)S(1)} %copy-done), channel_id=1, source_target_pairs={{4,0},{8,4},{12,8},{16,12},{20,16},{24,20},{28,24},{5,1},{9,5},{13... | collective-permute-start | bytes 393224 | tf_op jit(solution)/shard_map/ppermute | solution.py:178
  10.4 9.9 %collective-permute-start = (bf16[256,256]{1,0:T(8,128)(2,1)S(1)}, bf16[256,256]{1,0:T(8,128)(2,1)S(1)}, u32[]{:S(2)}, u32[]{:S(2)}) collective-permute-start(bf16[256,256]{1,0:T(8,128)(2,1)S(1)} %copy-done), channel_id=1, source_target_pairs={{0,4},{4,8},{8,12},{12,16},{16,20},{20,24},{24,28},{1,5},{5,9},{9,... | collective-permute-start | bytes 393224 | tf_op jit(solution)/shard_map/ppermute | solution.py:177

commit v2 on v1

--- a/solution.py
+++ b/solution.py
@@ -25,13 +25,18 @@
     return jnp.concatenate(halves, axis=1)
 
 
-def pack_kernel(keys, values, pair, quarter, wide):
-    width = keys.shape[1]
-    pair[:, :width] = keys[...]
-    pair[:, width:] = values[...]
-    level_two = average_pairs(average_pairs(pair[...], wide), wide)
-    for peer in range(quarter.shape[0]):
-        quarter[peer] = level_two
+def pack_kernel(keys, values, inner, outer, shares, wide):
+    me = lax.axis_index("seq")
+    odd = me & 1
+    rows = jnp.concatenate([keys[...], values[...]], axis=1)
+    low, high = rows[:LEAF], rows[LEAF:]
+    inner[...] = jnp.where(odd == 1, low, high)
+    outer[...] = jnp.where(odd == 1, high, low)
+    level_one = average_pairs(rows, wide)
+    level_two = average_pairs(level_one, wide)
+    for peer in range(shares.shape[0]):
+        share = jnp.where(me == peer - 1, level_one[:HALF], level_two)
+        shares[peer] = jnp.where(me == peer + 1, level_one[HALF:], share)
 
 
 def segments(seq_size):
@@ -47,7 +52,7 @@
     return rows
 
 
-def attend_kernel(seq_size, queries, own, before, after, far_rows, attended, key_set, wide):
+def attend_kernel(seq_size, queries, keys, values, inner, outer, far_rows, attended, key_set, wide):
     me = lax.axis_index("seq")
     width = queries.shape[1]
     zero, neg = jnp.float32(0.0), jnp.float32(NEG)
@@ -55,8 +60,14 @@
     def bias_of(valid):
         return jnp.where(valid, zero, neg)
 
-    coarse_before = average_pairs(before[...], wide)
-    coarse_after = average_pairs(after[...], wide)
+    odd = me & 1
+    before = jnp.where(odd == 1, inner[...], outer[...])
+    after = jnp.where(odd == 1, outer[...], inner[...])
+    far_half_before = far_rows[jnp.maximum(me - 1, 0)]
+    far_half_after = far_rows[jnp.minimum(me + 1, seq_size - 1)]
+    near_half_before = average_pairs(before, wide)
+    near_half_after = average_pairs(after, wide)
+    own = jnp.concatenate([keys[...], values[...]], axis=1)
     has_before, has_after = bias_of(me >= 1), bias_of(me + 1 < seq_size)
 
     far_pieces = []
@@ -99,17 +110,19 @@
     for leaf in range(2):
         if leaf == 0:
             near = [
-                (before[LEAF:], has_before),
-                (own[...], None),
-                (coarse_before[:HALF], has_before),
-                (coarse_after, has_after),
+                (before, has_before),
+                (own, None),
+                (far_half_before, has_before),
+                (near_half_after, has_after),
+                (far_half_after, has_after),
             ]
         else:
             near = [
-                (own[...], None),
-                (after[:LEAF], has_after),
-                (coarse_before, has_before),
-                (coarse_after[HALF:], has_after),
+                (own, None),
+                (after, has_after),
+                (far_half_before, has_before),
+                (near_half_before, has_before),
+                (far_half_after, has_after),
             ]
         at = 0
         total_rows = key_set.shape[0]
@@ -162,31 +175,34 @@
     bf16 = jnp.bfloat16
     wide_rows = max(2 * LEAF, seq_size // 2 * HALF)
     wide = pltpu.VMEM((wide_rows, width), jnp.float32)
-    pair, quarter = pl.pallas_call(
+    inner, outer, far_shares = pl.pallas_call(
         pack_kernel,
         out_shape=(
-            jax.ShapeDtypeStruct((tokens, 2 * width), bf16),
+            jax.ShapeDtypeStruct((LEAF, 2 * width), bf16),
+            jax.ShapeDtypeStruct((LEAF, 2 * width), bf16),
             jax.ShapeDtypeStruct((seq_size, HALF, 2 * width), bf16),
         ),
         in_specs=[VMEM] * 2,
-        out_specs=(VMEM, VMEM),
+        out_specs=(VMEM, VMEM, VMEM),
         scratch_shapes=[wide],
+        compiler_params=pltpu.CompilerParams(vmem_limit_bytes=16 << 20),
         name="pack",
     )(keys, values)
-    ends = seq_size - 1
-    before = lax.ppermute(pair, "seq", [(i, i + 1) for i in range(ends)])
-    after = lax.ppermute(pair, "seq", [(i + 1, i) for i in range(ends)])
-    far_rows = lax.all_to_all(quarter, "seq", split_axis=0, concat_axis=0)
+    pairs = [(i, i ^ 1) for i in range(seq_size)]
+    others = [(i, i + 1 if i & 1 else i - 1) for i in range(1, seq_size - 1)]
+    far_rows = lax.all_to_all(far_shares, "seq", split_axis=0, concat_axis=0)
+    inner = lax.ppermute(inner, "seq", pairs)
+    outer = lax.ppermute(outer, "seq", others)
     set_rows = 3 * LEAF + 3 * HALF + sum(segments(seq_size))
     attended = pl.pallas_call(
         functools.partial(attend_kernel, seq_size),
         out_shape=jax.ShapeDtypeStruct((tokens, width), bf16),
-        in_specs=[VMEM] * 5,
+        in_specs=[VMEM] * 6,
         out_specs=VMEM,
         scratch_shapes=[pltpu.VMEM((set_rows, 2 * width), bf16), wide],
-        compiler_params=pltpu.CompilerParams(vmem_limit_bytes=40 << 20),
+        compiler_params=pltpu.CompilerParams(vmem_limit_bytes=24 << 20),
         name="attend",
-    )(queries, pair, before, after, far_rows)
+    )(queries, keys, values, inner, outer, far_rows)
     share = tokens // head_size
     gathered = lax.all_to_all(
         attended.reshape(head_size, share, width), "head", split_axis=0, concat_axis=0
@@ -196,6 +212,7 @@
         out_shape=jax.ShapeDtypeStruct((share, out_weight.shape[1]), bf16),
         in_specs=[VMEM] * 2,
         out_specs=VMEM,
+        compiler_params=pltpu.CompilerParams(vmem_limit_bytes=8 << 20),
         name="project",
     )(gathered, out_weight)
 

time: 30.9 us -> 28.7 us (0.929)
  starting transfers between devices: 13.2 us -> 10.1 us
  Pallas kernels: 4.78 us -> 2.85 us
  local copies, waits for them, and re-layouts: 0.01 us -> 1.69 us
  waiting for transfers between devices: 5.31 us -> 6.93 us
  blocking collectives: 7.16 us -> 6.71 us
    all_to_all x1, waiting for transfers between devices: 0.01 us -> 3.83 us  [shards(): far_rows = lax.all_to_all(far_shares, 'seq', split_axis=0, concat_axis=0)]
    ppermute x2, starting transfers between devices: 5.85 us -> 2.67 us  [the longest x1 2.02 us: shards(): inner = lax.ppermute(inner, 'seq', pairs)]
    ppermute x2, waiting for transfers between devices: 5.31 us -> 3.1 us  [the longest x1 3.1 us: shards(): inner = lax.ppermute(inner, 'seq', pairs)]
    unnamed x4 -> x12, local copies, waits for them, and re-layouts: 0.01 us -> 1.69 us
    pallas_call x1, Pallas kernels: 1.93 us -> 0.85 us  [shards(): pl.pallas_call(project_kernel, out_shape=jax.ShapeDtypeStruct((share, out...]
    pallas_call x1, Pallas kernels: 1.66 us -> 0.8 us  [shards(): pl.pallas_call(pack_kernel, out_shape=(jax.ShapeDtypeStruct((LEAF, 2 * wi...]
    all_to_all x1, blocking collectives: 7.16 us -> 6.71 us  [shards(): lax.all_to_all(attended.reshape(head_size, share, width), 'head', split_a...]
where the time goes in v2:
time: 28.7 us; the launch traced here: 28.3 us
  starting transfers between devices  10.1 us (35%)
  waiting for transfers between devices  6.93 us (24%)
  blocking collectives  6.71 us (23%)
  Pallas kernels  2.85 us (10%)
  local copies, waits for them, and re-layouts  1.69 us (6%)
    all_to_all x1, starting transfers between devices, shards(): far_rows = lax.all_to_all(far_shares, 'seq', split_axis=0, concat_axis=0)  7.38 us
    all_to_all x1, blocking collectives, shards(): lax.all_to_all(attended.reshape(head_size, share, width), 'head', split_a...  6.71 us
    all_to_all x1, waiting for transfers between devices, shards(): far_rows = lax.all_to_all(far_shares, 'seq', split_axis=0, concat_axis=0)  3.83 us
    ppermute x1, waiting for transfers between devices, shards(): inner = lax.ppermute(inner, 'seq', pairs)  3.1 us
    ppermute x1, starting transfers between devices, shards(): inner = lax.ppermute(inner, 'seq', pairs)  2.02 us
    unnamed x12, local copies, waits for them, and re-layouts  1.69 us
    pallas_call x1, Pallas kernels, shards(): pl.pallas_call(functools.partial(attend_kernel, seq_size), out_shape=jax....  1.2 us
    pallas_call x1, Pallas kernels, shards(): pl.pallas_call(project_kernel, out_shape=jax.ShapeDtypeStruct((share, out...  0.85 us
  transfers between devices with their start and end apart: 3, of which 2 were waited for; matrix products, arithmetic and copies ran while one was open for 0% of the time, Pallas kernels for 0%

profile of v2, /device:TPU:0, one launch (start us, length us, event | category | flops | bytes accessed | tf_op | source)
XLA Modules:
  0.0 28.3 jit_solution(14572102501340459556)
XLA Ops:
  0.0 0.0 copy-start.1
  0.0 0.8 %copy-done.1 = bf16[256,128]{1,0:T(8,128)(2,1)S(1)} copy-done((bf16[256,128]{1,0:T(8,128)(2,1)S(1)}, bf16[256,128]{1,0:T(8,128)(2,1)}, u32[]{:S(2)}) %copy-start.1) | copy-done | bytes 65560
  0.8 0.0 copy-start.3
  0.8 0.8 %copy-done.3 = bf16[256,128]{1,0:T(8,128)(2,1)S(1)} copy-done((bf16[256,128]{1,0:T(8,128)(2,1)S(1)}, bf16[256,128]{1,0:T(8,128)(2,1)}, u32[]{:S(2)}) %copy-start.3) | copy-done | bytes 65560
  1.7 0.8 %pack.1 = (bf16[128,256]{1,0:T(8,128)(2,1)S(1)}, bf16[128,256]{1,0:T(8,128)(2,1)S(1)}, bf16[8,64,256]{2,1,0:T(8,128)(2,1)}) custom-call(bf16[256,128]{1,0:T(8,128)(2,1)S(1)} %copy-done.1, bf16[256,128]{1,0:T(8,128)(2,1)S(1)} %copy-done.3), custom_call_target="tpu_custom_call" | custom-call | tf_op jit(solution)/shard_map/pack/pallas_call | solution.py:178
  2.5 0.0 copy-start.2
  2.5 0.0 copy-start.4
  2.5 0.0 copy-start.5
  2.5 7.4 %all-to-all-start = ((bf16[8,64,256]{2,1,0:T(8,128)(2,1)}), bf16[8,64,256]{2,1,0:T(8,128)(2,1)S(1)}, u32[]{:S(2)}, u32[]{:S(2)}) async-start(bf16[8,64,256]{2,1,0:T(8,128)(2,1)} %get-tuple-element.10), calls=%async_computation | async-start | bytes 524288 | tf_op jit(solution)/shard_map/all_to_all | solution.py:193
  9.9 0.0 copy-start
  9.9 2.0 %collective-permute-start = (bf16[128,256]{1,0:T(8,128)(2,1)S(1)}, bf16[128,256]{1,0:T(8,128)(2,1)S(1)}, u32[]{:S(2)}, u32[]{:S(2)}) collective-permute-start(bf16[128,256]{1,0:T(8,128)(2,1)S(1)} %get-tuple-element.8), channel_id=1, source_target_pairs={{0,4},{4,0},{8,12},{12,8},{16,20},{20,16},{24,28},{28,24},{1,5},{5... | collective-permute-start | bytes 196616 | tf_op jit(solution)/shard_map/ppermute | solution.py:194
  11.9 0.7 %collective-permute-start.1 = (bf16[128,256]{1,0:T(8,128)(2,1)S(1)}, bf16[128,256]{1,0:T(8,128)(2,1)S(1)}, u32[]{:S(2)}, u32[]{:S(2)}) collective-permute-start(bf16[128,256]{1,0:T(8,128)(2,1)S(1)} %get-tuple-element.9), channel_id=1, source_target_pairs={{4,8},{8,4},{12,16},{16,12},{20,24},{24,20},{5,9},{9,5},{13,17},{1... | collective-permute-start | bytes 196616 | tf_op jit(solution)/shard_map/ppermute | solution.py:195
  12.6 3.1 %collective-permute-done.inner = bf16[128,256]{1,0:T(8,128)(2,1)S(1)} collective-permute-done((bf16[128,256]{1,0:T(8,128)(2,1)S(1)}, bf16[128,256]{1,0:T(8,128)(2,1)S(1)}, u32[]{:S(2)}, u32[]{:S(2)}) %collective-permute-start) | collective-permute-done | bytes 65568 | tf_op jit(solution)/shard_map/ppermute | solution.py:194
  15.7 0.0 collective-permute-done.1.outer
  15.7 3.8 %all-to-all-done.far_rows = bf16[8,64,256]{2,1,0:T(8,128)(2,1)S(1)} async-done(((bf16[8,64,256]{2,1,0:T(8,128)(2,1)}), bf16[8,64,256]{2,1,0:T(8,128)(2,1)S(1)}, u32[]{:S(2)}, u32[]{:S(2)}) %all-to-all-start) | async-done | bytes 262176 | tf_op jit(solution)/shard_map/all_to_all | solution.py:193
  19.5 0.0 copy-done.2
  19.5 0.0 copy-done.4
  19.5 0.0 copy-done.5
  19.5 1.2 %attend.1 = bf16[256,128]{1,0:T(8,128)(2,1)S(1)} custom-call(bf16[256,128]{1,0:T(8,128)(2,1)S(1)} %copy-done.5, bf16[256,128]{1,0:T(8,128)(2,1)S(1)} %copy-done.2, bf16[256,128]{1,0:T(8,128)(2,1)S(1)} %copy-done.4, bf16[128,256]{1,0:T(8,128)(2,1)S(1)} %collective-permute-done.inner, bf16[128,256]{1,0:T(8,128)(2,1)S(1)} %collective-permute-done.1.outer, ...), custom_call_target="tpu_custom_call" | custom-call | tf_op jit(solution)/shard_map/attend/pallas_call | solution.py:197
  20.7 6.7 %all_to_all.10.rows = bf16[4,64,128]{2,1,0:T(8,128)(2,1)S(1)} all-to-all(bf16[4,64,128]{2,1,0:T(8,128)(2,1)S(1)} %bitcast.1), channel_id=1, replica_groups=mesh['seq'=8,'head'=4] {'head'}, dimensions={0} | all-to-all | bytes 131072 | tf_op jit(solution)/shard_map/all_to_all | solution.py:207
  27.4 0.0 copy-done
  27.4 0.8 %project.1 = bf16[64,512]{1,0:T(8,128)(2,1)} custom-call(bf16[4,64,128]{2,1,0:T(8,128)(2,1)S(1)} %all_to_all.10.rows, bf16[512,512]{1,0:T(8,128)(2,1)S(1)} %copy-done), custom_call_target="tpu_custom_call" | custom-call | tf_op jit(solution)/shard_map/project/pallas_call | solution.py:210
Async XLA Ops:
  0.0 0.8 %copy-start.1 = (bf16[256,128]{1,0:T(8,128)(2,1)S(1)}, bf16[256,128]{1,0:T(8,128)(2,1)}, u32[]{:S(2)}) copy-start(bf16[256,128]{1,0:T(8,128)(2,1)} %keys.3) | copy-start | bytes 196612
  0.8 0.8 %copy-start.3 = (bf16[256,128]{1,0:T(8,128)(2,1)S(1)}, bf16[256,128]{1,0:T(8,128)(2,1)}, u32[]{:S(2)}) copy-start(bf16[256,128]{1,0:T(8,128)(2,1)} %values.3) | copy-start | bytes 196612
  2.5 17.0 %copy-start.2 = (bf16[256,128]{1,0:T(8,128)(2,1)S(1)}, bf16[256,128]{1,0:T(8,128)(2,1)}, u32[]{:S(2)}) copy-start(bf16[256,128]{1,0:T(8,128)(2,1)} %keys.3) | copy-start | bytes 196612
  2.5 17.0 %copy-start.4 = (bf16[256,128]{1,0:T(8,128)(2,1)S(1)}, bf16[256,128]{1,0:T(8,128)(2,1)}, u32[]{:S(2)}) copy-start(bf16[256,128]{1,0:T(8,128)(2,1)} %values.3) | copy-start | bytes 196612
  2.5 17.0 %copy-start.5 = (bf16[256,128]{1,0:T(8,128)(2,1)S(1)}, bf16[256,128]{1,0:T(8,128)(2,1)}, u32[]{:S(2)}) copy-start(bf16[256,128]{1,0:T(8,128)(2,1)} %queries.1) | copy-start | bytes 196612
  2.5 17.0 %all-to-all-start = ((bf16[8,64,256]{2,1,0:T(8,128)(2,1)}), bf16[8,64,256]{2,1,0:T(8,128)(2,1)S(1)}, u32[]{:S(2)}, u32[]{:S(2)}) async-start(bf16[8,64,256]{2,1,0:T(8,128)(2,1)} %get-tuple-element.10), calls=%async_computation | async-start | bytes 524288 | tf_op jit(solution)/shard_map/all_to_all | solution.py:193
  9.9 17.6 %copy-start = (bf16[512,512]{1,0:T(8,128)(2,1)S(1)}, bf16[512,512]{1,0:T(8,128)(2,1)}, u32[]{:S(2)}) copy-start(bf16[512,512]{1,0:T(8,128)(2,1)} %weight.1) | copy-start | bytes 1572868
  9.9 5.8 %collective-permute-start = (bf16[128,256]{1,0:T(8,128)(2,1)S(1)}, bf16[128,256]{1,0:T(8,128)(2,1)S(1)}, u32[]{:S(2)}, u32[]{:S(2)}) collective-permute-start(bf16[128,256]{1,0:T(8,128)(2,1)S(1)} %get-tuple-element.8), channel_id=1, source_target_pairs={{0,4},{4,0},{8,12},{12,8},{16,20},{20,16},{24,28},{28,24},{1,5},{5... | collective-permute-start | bytes 196616 | tf_op jit(solution)/shard_map/ppermute | solution.py:194
  11.9 3.8 %collective-permute-start.1 = (bf16[128,256]{1,0:T(8,128)(2,1)S(1)}, bf16[128,256]{1,0:T(8,128)(2,1)S(1)}, u32[]{:S(2)}, u32[]{:S(2)}) collective-permute-start(bf16[128,256]{1,0:T(8,128)(2,1)S(1)} %get-tuple-element.9), channel_id=1, source_target_pairs={{4,8},{8,4},{12,16},{16,12},{20,24},{24,20},{5,9},{9,5},{13,17},{1... | collective-permute-start | bytes 196616 | tf_op jit(solution)/shard_map/ppermute | solution.py:195

commit v3 on v2

v3 whole, which is shorter than its diff:
```python
import functools
import math

import jax
import jax.numpy as jnp
from jax import lax
from jax.experimental import pallas as pl
from jax.experimental.pallas import tpu as pltpu
from jax.sharding import PartitionSpec as P

HD = 64
LEAF = 128
HALF = LEAF // 2
NEG = -math.inf


def average_pairs(rows, wide):
    count = rows.shape[0]
    halves = []
    for low in range(0, rows.shape[1], LEAF):
        wide[:count] = rows[:, low : low + LEAF].astype(jnp.float32)
        even = wide[pl.ds(0, count // 2, stride=2), :]
        odd = wide[pl.ds(1, count // 2, stride=2), :]
        halves.append((0.5 * (even + odd)).astype(jnp.bfloat16))
    return jnp.concatenate(halves, axis=1)


def pack_kernel(far_shares, keys, values, own, inner, outer, quarter, wide, arrived):
    width = keys.shape[1]
    copies = [
        pltpu.make_async_copy(keys, own.at[:, :width], arrived.at[0]),
        pltpu.make_async_copy(values, own.at[:, width:], arrived.at[1]),
    ]
    for copy in copies:
        copy.start()
    me = lax.axis_index("seq")
    odd = me & 1
    for copy in copies:
        copy.wait()
    rows = own[...]
    low, high = rows[:LEAF], rows[LEAF:]
    level_one = average_pairs(rows, wide)
    level_two = average_pairs(level_one, wide)
    first, second = level_one[:HALF], level_one[HALF:]
    inner[:LEAF] = jnp.where(odd == 1, low, high)
    inner[LEAF : LEAF + HALF] = jnp.where(odd == 1, second, first)
    outer[:LEAF] = jnp.where(odd == 1, high, low)
    outer[LEAF:] = jnp.where(odd == 1, first, second)
    if far_shares:
        for peer in range(quarter.shape[0]):
            quarter[peer] = level_two
    else:
        inner[LEAF + HALF :] = level_two
        quarter[...] = level_two


def join_kernel(inner, quarter, block, eighth, wide):
    odd = lax.axis_index("seq") & 1
    theirs = inner[LEAF + HALF :]
    block[:HALF] = jnp.where(odd == 1, theirs, quarter[...])
    block[HALF:] = jnp.where(odd == 1, quarter[...], theirs)
    eighth[...] = average_pairs(block[...], wide)


def set_rows(seq_size):
    rows = 3 * LEAF + 3 * HALF
    for far in range(1, seq_size.bit_length() - 1):
        if seq_size >> far == 2:
            rows += LEAF
        elif far == 1:
            rows += 3 * HALF
        else:
            rows += 2 * LEAF
    return rows


def bias_of(valid):
    return jnp.where(valid, jnp.float32(0.0), jnp.float32(NEG))


def gathered_pieces(seq_size, far_rows, wide):
    me = lax.axis_index("seq")
    pieces = []
    for far in range(1, seq_size.bit_length() - 1):
        span = 1 << far
        group = me >> far
        parity = (me >> (far - 1)) & 1
        blocks = seq_size >> far

        def block(number, span=span, far=far):
            found = far_rows[pl.ds(number * span, span)].reshape(span * HALF, far_rows.shape[2])
            for _ in range(far - 1):
                found = average_pairs(found, wide)
            return found

        if blocks == 2:
            rows = block(1 - group)
            first = bias_of((group == 1) | (parity == 0))
            second = bias_of((group == 0) | (parity == 1))
            pieces += [(rows[:HALF], first), (rows[HALF:], second)]
        elif far == 1:
            third = jnp.where(parity == 0, me + 3, me - 3)
            for peer in (me - 2, me + 2, third):
                ok = (peer >= 0) & (peer < seq_size)
                pieces.append((far_rows[jnp.clip(peer, 0, seq_size - 1)], bias_of(ok)))
        else:
            lower = block(jnp.maximum(group - 1, 0))
            upper = block(jnp.minimum(group + 1, blocks - 1))
            has_lower, has_upper = group >= 1, group + 1 < blocks
            pieces += [
                (lower[:HALF], bias_of(has_lower)),
                (lower[HALF:], bias_of(has_lower & (parity == 1))),
                (upper[:HALF], bias_of(has_upper & (parity == 0))),
                (upper[HALF:], bias_of(has_upper)),
            ]
    return pieces


def paired_pieces(block_2, block_6, eighth_4, wide):
    me = lax.axis_index("seq")
    odd = me & 1
    pair = me >> 1
    middle = (pair == 1) | (pair == 2)
    upper_near = (pair & 1) == 0
    lower = jnp.where(upper_near, block_6[...], block_2[...])
    upper = jnp.where(upper_near, block_2[...], block_6[...])
    has_lower, has_upper = pair >= 1, pair <= 2
    third = jnp.where(odd == 1, lower[HALF:], upper[:HALF])
    has_third = ((odd == 1) & has_lower) | ((odd == 0) & has_upper)
    ends = average_pairs(block_6[...], wide)
    return [
        (lower[:HALF], bias_of(has_lower)),
        (upper[HALF:], bias_of(has_upper)),
        (third, bias_of(has_third)),
        (eighth_4[...], bias_of(pair >= 0)),
        (ends, bias_of(jnp.logical_not(middle))),
    ]


def attend_kernel(seq_size, queries, own, inner, outer, *rest):
    *far, attended, key_set, wide = rest
    me = lax.axis_index("seq")
    width = queries.shape[1]
    odd = me & 1
    from_inner, from_outer = inner[: LEAF + HALF], outer[...]
    before = jnp.where(odd == 1, from_inner, from_outer)
    after = jnp.where(odd == 1, from_outer, from_inner)
    edge_before, edge_after = before[:LEAF], after[:LEAF]
    far_half_before, far_half_after = before[LEAF:], after[LEAF:]
    near_half_before = average_pairs(edge_before, wide)
    near_half_after = average_pairs(edge_after, wide)
    has_before, has_after = bias_of(me >= 1), bias_of(me + 1 < seq_size)
    if len(far) == 1:
        far_pieces = gathered_pieces(seq_size, far[0], wide)
    else:
        far_pieces = paired_pieces(*far, wide)

    lane = lax.broadcasted_iota(jnp.int32, (1, width), 1)
    first_head = lane < HD
    exponent = math.log2(math.e) / math.sqrt(HD)
    for leaf in range(2):
        if leaf == 0:
            near = [
                (edge_before, has_before),
                (own[...], None),
                (far_half_before, has_before),
                (near_half_after, has_after),
                (far_half_after, has_after),
            ]
        else:
            near = [
                (own[...], None),
                (edge_after, has_after),
                (far_half_before, has_before),
                (near_half_before, has_before),
                (far_half_after, has_after),
            ]
        at = 0
        total_rows = key_set.shape[0]
        position = lax.broadcasted_iota(jnp.int32, (1, total_rows), 1)
        bias = jnp.zeros((1, total_rows), jnp.float32)
        for rows, value in near + far_pieces:
            count = rows.shape[0]
            key_set[at : at + count] = rows
            if value is not None:
                bias = jnp.where((position >= at) & (position < at + count), value, bias)
            at += count
        block_queries = queries[leaf * LEAF : (leaf + 1) * LEAF]
        none = jnp.zeros_like(block_queries)
        both = jnp.concatenate(
            [jnp.where(first_head, block_queries, none), jnp.where(first_head, none, block_queries)], axis=0
        )
        scores = lax.dot_general(
            both, key_set[:, :width], (((1,), (1,)), ((), ())), preferred_element_type=jnp.float32
        )
        scores = scores + bias
        peak = jnp.max(scores, axis=1, keepdims=True)
        weights = jnp.exp2((scores - peak) * exponent)
        total = jnp.sum(weights, axis=1, keepdims=True)
        numer = jnp.dot(
            weights.astype(jnp.bfloat16), key_set[:, width:], preferred_element_type=jnp.float32
        )
        shares = numer / total
        attended[leaf * LEAF : (leaf + 1) * LEAF] = jnp.where(
            first_head, shares[:LEAF], shares[LEAF:]
        ).astype(jnp.bfloat16)


def project_kernel(rows, weight, mixed):
    width = rows.shape[2]
    total = jnp.zeros(mixed.shape, jnp.float32)
    for part in range(rows.shape[0]):
        total += jnp.dot(
            rows[part], weight[part * width : (part + 1) * width], preferred_element_type=jnp.float32
        )
    mixed[...] = total.astype(mixed.dtype)


VMEM = pl.BlockSpec(memory_space=pltpu.VMEM)
HBM = pl.BlockSpec(memory_space=pltpu.HBM)


def kernel_call(body, name, megabytes, ins, outs, scratch):
    shapes = tuple(jax.ShapeDtypeStruct(shape, jnp.bfloat16) for shape in outs)
    return pl.pallas_call(
        body,
        out_shape=shapes,
        in_specs=ins,
        out_specs=(VMEM,) * len(outs),
        scratch_shapes=scratch,
        compiler_params=pltpu.CompilerParams(vmem_limit_bytes=megabytes << 20),
        name=name,
    )


def shards(queries, keys, values, out_weight):
    tokens, width = queries.shape
    seq_size = lax.axis_size("seq")
    head_size = lax.axis_size("head")
    pair_width = 2 * width
    paired = seq_size == 8
    wide_rows = 2 * LEAF if paired else max(2 * LEAF, seq_size // 2 * HALF)
    wide = pltpu.VMEM((wide_rows, width), jnp.float32)

    def swap(array, bit):
        return lax.ppermute(array, "seq", [(i, i ^ bit) for i in range(seq_size)])

    own, inner, outer, quarter = kernel_call(
        functools.partial(pack_kernel, not paired),
        "pack",
        16,
        [HBM] * 2,
        [
            (tokens, pair_width),
            (LEAF + HALF + (HALF if paired else 0), pair_width),
            (LEAF + HALF, pair_width),
            (HALF, pair_width) if paired else (seq_size, HALF, pair_width),
        ],
        [wide, pltpu.SemaphoreType.DMA((2,))],
    )(keys, values)
    inner = swap(inner, 1)
    others = [(i, i + 1 if i & 1 else i - 1) for i in range(1, seq_size - 1)]
    outer = lax.ppermute(outer, "seq", others)
    if paired:
        block, eighth = kernel_call(
            join_kernel,
            "join",
            8,
            [VMEM] * 2,
            [(LEAF, pair_width), (HALF, pair_width)],
            [wide],
        )(inner, quarter)
        far = (swap(block, 2), swap(block, 6), swap(eighth, 4))
    else:
        far = (lax.all_to_all(quarter, "seq", split_axis=0, concat_axis=0),)
    (attended,) = kernel_call(
        functools.partial(attend_kernel, seq_size),
        "attend",
        24,
        [VMEM] * (4 + len(far)),
        [(tokens, width)],
        [pltpu.VMEM((set_rows(seq_size), pair_width), jnp.bfloat16), wide],
    )(queries, own, inner, outer, *far)
    share = tokens // head_size
    gathered = lax.all_to_all(
        attended.reshape(head_size, share, width), "head", split_axis=0, concat_axis=0
    )
    (mixed,) = kernel_call(
        project_kernel, "project", 8, [VMEM] * 2, [(share, out_weight.shape[1])], []
    )(gathered, out_weight)
    return mixed


def solution(mesh):
    in_specs = (P("seq", "head"), P("seq", "head"), P("seq", "head"), P())
    out_specs = P(("seq", "head"), None)
    return jax.shard_map(shards, mesh=mesh, in_specs=in_specs, out_specs=out_specs, check_vma=False)
```

time: 28.7 us -> 27 us (0.941)
  starting transfers between devices: 10.1 us -> 8.22 us
  local copies, waits for them, and re-layouts: 1.69 us -> 2.52 us
  Pallas kernels: 2.85 us -> 2.18 us
    all_to_all x1 -> x0, starting transfers between devices: 7.38 us -> none  [shards(): far_rows = lax.all_to_all(far_shares, 'seq', split_axis=0, concat_axis=0)]
    ppermute x1 -> x4, starting transfers between devices: 2.02 us -> 7.56 us  [swap(): return lax.ppermute(array, 'seq', [(i, i ^ bit) for i in range(seq_size)])]
    ppermute x1 -> x4, waiting for transfers between devices: 3.1 us -> 7.01 us  [swap(): return lax.ppermute(array, 'seq', [(i, i ^ bit) for i in range(seq_size)])]
    all_to_all x1 -> x0, waiting for transfers between devices: 3.83 us -> none  [shards(): far_rows = lax.all_to_all(far_shares, 'seq', split_axis=0, concat_axis=0)]
    unnamed x12 -> x8, local copies, waits for them, and re-layouts: 1.69 us -> 2.52 us
    pallas_call x3 -> x4, Pallas kernels: 2.85 us -> 2.18 us  [the longest x1 1.19 us: shards(): kernel_call(functools.partial(attend_kernel, seq_size), 'attend', 24, [VM...]
  transfers between devices with their start and end apart: 3 -> 5, of which waited for: 2 -> 2; matrix products, arithmetic and copies ran while one was open for 0% -> 0% of each run, Pallas kernels for 0% -> 0%
where the time goes in v3:
time: 27 us; the launch traced here: 26.7 us
  starting transfers between devices  8.22 us (30%)
  waiting for transfers between devices  7.01 us (26%)
  blocking collectives  6.71 us (25%)
  local copies, waits for them, and re-layouts  2.52 us (9%)
  Pallas kernels  2.18 us (8%)
    ppermute x4, starting transfers between devices, swap(): return lax.ppermute(array, 'seq', [(i, i ^ bit) for i in range(seq_size)])  7.56 us
    ppermute x4, waiting for transfers between devices, swap(): return lax.ppermute(array, 'seq', [(i, i ^ bit) for i in range(seq_size)])  7.01 us
    all_to_all x1, blocking collectives, shards(): lax.all_to_all(attended.reshape(head_size, share, width), 'head', split_a...  6.71 us
    unnamed x8, local copies, waits for them, and re-layouts  2.52 us
    pallas_call x1, Pallas kernels, shards(): kernel_call(functools.partial(attend_kernel, seq_size), 'attend', 24, [VM...  1.19 us
    pallas_call x1, Pallas kernels, shards(): kernel_call(project_kernel, 'project', 8, [VMEM] * 2, [(share, out_weight...  0.85 us
    ppermute x1, starting transfers between devices, shards(): outer = lax.ppermute(outer, 'seq', others)  0.65 us
  transfers between devices with their start and end apart: 5, of which 2 were waited for; matrix products, arithmetic and copies ran while one was open for 0% of the time, Pallas kernels for 0%

profile of v3, /device:TPU:0, one launch (start us, length us, event | category | flops | bytes accessed | tf_op | source)
XLA Modules:
  0.0 26.7 jit_solution(13394723450014148396)
XLA Ops:
  0.0 0.0 copy-start.2
  0.0 0.8 %copy-done.2 = bf16[256,128]{1,0:T(8,128)(2,1)S(1)} copy-done((bf16[256,128]{1,0:T(8,128)(2,1)S(1)}, bf16[256,128]{1,0:T(8,128)(2,1)}, u32[]{:S(2)}) %copy-start.2) | copy-done | bytes 65560
  0.8 0.0 copy-start.3
  0.8 0.8 %copy-done.3 = bf16[256,128]{1,0:T(8,128)(2,1)S(1)} copy-done((bf16[256,128]{1,0:T(8,128)(2,1)S(1)}, bf16[256,128]{1,0:T(8,128)(2,1)}, u32[]{:S(2)}) %copy-start.3) | copy-done | bytes 65560
  1.7 0.0 copy-start
  1.7 0.1 pack.1
  1.8 3.0 %collective-permute-start = (bf16[256,256]{1,0:T(8,128)(2,1)S(1)}, bf16[256,256]{1,0:T(8,128)(2,1)S(1)}, u32[]{:S(2)}, u32[]{:S(2)}) collective-permute-start(bf16[256,256]{1,0:T(8,128)(2,1)S(1)} %get-tuple-element.12), channel_id=1, source_target_pairs={{0,4},{4,0},{8,12},{12,8},{16,20},{20,16},{24,28},{28,24},{1,5},{5... | collective-permute-start | bytes 393224 | tf_op jit(solution)/shard_map/ppermute | solution.py:246
  4.8 0.7 %collective-permute-start.1 = (bf16[192,256]{1,0:T(8,128)(2,1)S(1)}, bf16[192,256]{1,0:T(8,128)(2,1)S(1)}, u32[]{:S(2)}, u32[]{:S(2)}) collective-permute-start(bf16[192,256]{1,0:T(8,128)(2,1)S(1)} %get-tuple-element.13), channel_id=1, source_target_pairs={{4,8},{8,4},{12,16},{16,12},{20,24},{24,20},{5,9},{9,5},{13,17},{1... | collective-permute-start | bytes 294920 | tf_op jit(solution)/shard_map/ppermute | solution.py:263
  5.5 2.8 %collective-permute-done.inner = bf16[256,256]{1,0:T(8,128)(2,1)S(1)} collective-permute-done((bf16[256,256]{1,0:T(8,128)(2,1)S(1)}, bf16[256,256]{1,0:T(8,128)(2,1)S(1)}, u32[]{:S(2)}, u32[]{:S(2)}) %collective-permute-start) | collective-permute-done | bytes 131104 | tf_op jit(solution)/shard_map/ppermute | solution.py:246
  8.3 3.9 %collective-permute-start.3 = (bf16[128,256]{1,0:T(8,128)(2,1)S(1)}, bf16[128,256]{1,0:T(8,128)(2,1)S(1)}, u32[]{:S(2)}, u32[]{:S(2)}) collective-permute-start(bf16[128,256]{1,0:T(8,128)(2,1)S(1)} %get-tuple-element.15), channel_id=1, source_target_pairs={{0,24},{4,28},{8,16},{12,20},{16,8},{20,12},{24,0},{28,4},{1,25},{... | collective-permute-start | bytes 196616 | tf_op jit(solution)/shard_map/ppermute | solution.py:246
  12.3 0.0 collective-permute-start.2
  12.3 0.6 %collective-permute-start.4 = (bf16[64,256]{1,0:T(8,128)(2,1)S(1)}, bf16[64,256]{1,0:T(8,128)(2,1)S(1)}, u32[]{:S(2)}, u32[]{:S(2)}) collective-permute-start(bf16[64,256]{1,0:T(8,128)(2,1)S(1)} %get-tuple-element.16), channel_id=1, source_target_pairs={{0,16},{4,20},{8,24},{12,28},{16,0},{20,4},{24,8},{28,12},{1,17},{... | collective-permute-start | bytes 98312 | tf_op jit(solution)/shard_map/ppermute | solution.py:246
  12.9 0.0 collective-permute-done.1.outer
  12.9 4.2 %collective-permute-done.4.rest_2_ = bf16[64,256]{1,0:T(8,128)(2,1)S(1)} collective-permute-done((bf16[64,256]{1,0:T(8,128)(2,1)S(1)}, bf16[64,256]{1,0:T(8,128)(2,1)S(1)}, u32[]{:S(2)}, u32[]{:S(2)}) %collective-permute-start.4) | collective-permute-done | bytes 32800 | tf_op jit(solution)/shard_map/ppermute | solution.py:246
  17.1 0.0 collective-permute-done.3.rest_1_
  17.1 0.0 collective-permute-done.2.rest_0_
  17.1 0.0 copy-start.1
  17.1 0.8 %copy-done.1 = bf16[256,128]{1,0:T(8,128)(2,1)S(1)} copy-done((bf16[256,128]{1,0:T(8,128)(2,1)S(1)}, bf16[256,128]{1,0:T(8,128)(2,1)}, u32[]{:S(2)}) %copy-start.1) | copy-done | bytes 65560
  17.9 1.2 %attend.1 = bf16[256,128]{1,0:T(8,128)(2,1)S(1)} custom-call(bf16[256,128]{1,0:T(8,128)(2,1)S(1)} %copy-done.1, bf16[256,256]{1,0:T(8,128)(2,1)S(1)} %get-tuple-element.11.own, bf16[256,256]{1,0:T(8,128)(2,1)S(1)} %collective-permute-done.inner, bf16[192,256]{1,0:T(8,128)(2,1)S(1)} %collective-permute-done.1.outer, ...), custom_call_target="tpu_custom_call" | custom-call | tf_op jit(solution)/shard_map/attend/pallas_call | solution.py:276
  19.1 6.7 %all_to_all.5.rows = bf16[4,64,128]{2,1,0:T(8,128)(2,1)S(1)} all-to-all(bf16[4,64,128]{2,1,0:T(8,128)(2,1)S(1)} %bitcast.1), channel_id=1, replica_groups=mesh['seq'=8,'head'=4] {'head'}, dimensions={0} | all-to-all | bytes 131072 | tf_op jit(solution)/shard_map/all_to_all | solution.py:285
  25.8 0.0 copy-done
  25.8 0.8 %project.1 = bf16[64,512]{1,0:T(8,128)(2,1)} custom-call(bf16[4,64,128]{2,1,0:T(8,128)(2,1)S(1)} %all_to_all.5.rows, bf16[512,512]{1,0:T(8,128)(2,1)S(1)} %copy-done), custom_call_target="tpu_custom_call" | custom-call | tf_op jit(solution)/shard_map/project/pallas_call | solution.py:288
  (1 shorter events, 0.0 us)
Async XLA Ops:
  0.0 0.8 %copy-start.2 = (bf16[256,128]{1,0:T(8,128)(2,1)S(1)}, bf16[256,128]{1,0:T(8,128)(2,1)}, u32[]{:S(2)}) copy-start(bf16[256,128]{1,0:T(8,128)(2,1)} %keys.1) | copy-start | bytes 196612
  0.8 0.8 %copy-start.3 = (bf16[256,128]{1,0:T(8,128)(2,1)S(1)}, bf16[256,128]{1,0:T(8,128)(2,1)}, u32[]{:S(2)}) copy-start(bf16[256,128]{1,0:T(8,128)(2,1)} %values.1) | copy-start | bytes 196612
  1.7 24.1 %copy-start = (bf16[512,512]{1,0:T(8,128)(2,1)S(1)}, bf16[512,512]{1,0:T(8,128)(2,1)}, u32[]{:S(2)}) copy-start(bf16[512,512]{1,0:T(8,128)(2,1)} %weight.1) | copy-start | bytes 1572868
  1.8 6.5 %collective-permute-start = (bf16[256,256]{1,0:T(8,128)(2,1)S(1)}, bf16[256,256]{1,0:T(8,128)(2,1)S(1)}, u32[]{:S(2)}, u32[]{:S(2)}) collective-permute-start(bf16[256,256]{1,0:T(8,128)(2,1)S(1)} %get-tuple-element.12), channel_id=1, source_target_pairs={{0,4},{4,0},{8,12},{12,8},{16,20},{20,16},{24,28},{28,24},{1,5},{5... | collective-permute-start | bytes 393224 | tf_op jit(solution)/shard_map/ppermute | solution.py:246
  4.8 8.1 %collective-permute-start.1 = (bf16[192,256]{1,0:T(8,128)(2,1)S(1)}, bf16[192,256]{1,0:T(8,128)(2,1)S(1)}, u32[]{:S(2)}, u32[]{:S(2)}) collective-permute-start(bf16[192,256]{1,0:T(8,128)(2,1)S(1)} %get-tuple-element.13), channel_id=1, source_target_pairs={{4,8},{8,4},{12,16},{16,12},{20,24},{24,20},{5,9},{9,5},{13,17},{1... | collective-permute-start | bytes 294920 | tf_op jit(solution)/shard_map/ppermute | solution.py:263
  8.3 8.7 %collective-permute-start.3 = (bf16[128,256]{1,0:T(8,128)(2,1)S(1)}, bf16[128,256]{1,0:T(8,128)(2,1)S(1)}, u32[]{:S(2)}, u32[]{:S(2)}) collective-permute-start(bf16[128,256]{1,0:T(8,128)(2,1)S(1)} %get-tuple-element.15), channel_id=1, source_target_pairs={{0,24},{4,28},{8,16},{12,20},{16,8},{20,12},{24,0},{28,4},{1,25},{... | collective-permute-start | bytes 196616 | tf_op jit(solution)/shard_map/ppermute | solution.py:246
  12.3 4.8 %collective-permute-start.2 = (bf16[128,256]{1,0:T(8,128)(2,1)S(1)}, bf16[128,256]{1,0:T(8,128)(2,1)S(1)}, u32[]{:S(2)}, u32[]{:S(2)}) collective-permute-start(bf16[128,256]{1,0:T(8,128)(2,1)S(1)} %get-tuple-element.15), channel_id=1, source_target_pairs={{0,8},{4,12},{8,0},{12,4},{16,24},{20,28},{24,16},{28,20},{1,9},{5... | collective-permute-start | bytes 196616 | tf_op jit(solution)/shard_map/ppermute | solution.py:246
  12.3 4.8 %collective-permute-start.4 = (bf16[64,256]{1,0:T(8,128)(2,1)S(1)}, bf16[64,256]{1,0:T(8,128)(2,1)S(1)}, u32[]{:S(2)}, u32[]{:S(2)}) collective-permute-start(bf16[64,256]{1,0:T(8,128)(2,1)S(1)} %get-tuple-element.16), channel_id=1, source_target_pairs={{0,16},{4,20},{8,24},{12,28},{16,0},{20,4},{24,8},{28,12},{1,17},{... | collective-permute-start | bytes 98312 | tf_op jit(solution)/shard_map/ppermute | solution.py:246
  17.1 0.8 %copy-start.1 = (bf16[256,128]{1,0:T(8,128)(2,1)S(1)}, bf16[256,128]{1,0:T(8,128)(2,1)}, u32[]{:S(2)}) copy-start(bf16[256,128]{1,0:T(8,128)(2,1)} %queries.1) | copy-start | bytes 196612

commit v4 on v3

--- a/solution.py
+++ b/solution.py
@@ -25,11 +25,12 @@
     return jnp.concatenate(halves, axis=1)
 
 
-def pack_kernel(far_shares, keys, values, own, inner, outer, quarter, wide, arrived):
+def pack_kernel(far_shares, queries, keys, values, own_queries, own, inner, outer, quarter, wide, arrived):
     width = keys.shape[1]
     copies = [
         pltpu.make_async_copy(keys, own.at[:, :width], arrived.at[0]),
         pltpu.make_async_copy(values, own.at[:, width:], arrived.at[1]),
+        pltpu.make_async_copy(queries, own_queries, arrived.at[2]),
     ]
     for copy in copies:
         copy.start()
@@ -137,8 +138,9 @@
     ]
 
 
-def attend_kernel(seq_size, queries, own, inner, outer, *rest):
-    *far, attended, key_set, wide = rest
+def attend_kernel(seq_size, far_count, queries, own, inner, outer, *rest):
+    far, shares, scratch = rest[:far_count], rest[far_count:-3], rest[-3:]
+    attended, key_set, wide = scratch
     me = lax.axis_index("seq")
     width = queries.shape[1]
     odd = me & 1
@@ -200,19 +202,24 @@
         numer = jnp.dot(
             weights.astype(jnp.bfloat16), key_set[:, width:], preferred_element_type=jnp.float32
         )
-        shares = numer / total
+        mean = numer / total
         attended[leaf * LEAF : (leaf + 1) * LEAF] = jnp.where(
-            first_head, shares[:LEAF], shares[LEAF:]
+            first_head, mean[:LEAF], mean[LEAF:]
         ).astype(jnp.bfloat16)
-
-
-def project_kernel(rows, weight, mixed):
-    width = rows.shape[2]
+    mine = lax.axis_index("head")
+    for step, share in enumerate(shares):
+        count = share.shape[0]
+        share[...] = attended[pl.ds(pl.multiple_of((mine ^ step) * count, count), count)]
+
+
+def project_kernel(*refs):
+    *parts, weight, mixed = refs
+    mine = lax.axis_index("head")
     total = jnp.zeros(mixed.shape, jnp.float32)
-    for part in range(rows.shape[0]):
-        total += jnp.dot(
-            rows[part], weight[part * width : (part + 1) * width], preferred_element_type=jnp.float32
-        )
+    for step, part in enumerate(parts):
+        width = part.shape[1]
+        columns = pl.ds(pl.multiple_of((mine ^ step) * width, width), width)
+        total += jnp.dot(part[...], weight[columns], preferred_element_type=jnp.float32)
     mixed[...] = total.astype(mixed.dtype)
 
 
@@ -242,22 +249,23 @@
     wide_rows = 2 * LEAF if paired else max(2 * LEAF, seq_size // 2 * HALF)
     wide = pltpu.VMEM((wide_rows, width), jnp.float32)
 
-    def swap(array, bit):
-        return lax.ppermute(array, "seq", [(i, i ^ bit) for i in range(seq_size)])
-
-    own, inner, outer, quarter = kernel_call(
+    def swap(array, bit, axis="seq"):
+        return lax.ppermute(array, axis, [(i, i ^ bit) for i in range(lax.axis_size(axis))])
+
+    own_queries, own, inner, outer, quarter = kernel_call(
         functools.partial(pack_kernel, not paired),
         "pack",
         16,
-        [HBM] * 2,
+        [HBM] * 3,
         [
+            (tokens, width),
             (tokens, pair_width),
             (LEAF + HALF + (HALF if paired else 0), pair_width),
             (LEAF + HALF, pair_width),
             (HALF, pair_width) if paired else (seq_size, HALF, pair_width),
         ],
-        [wide, pltpu.SemaphoreType.DMA((2,))],
-    )(keys, values)
+        [wide, pltpu.SemaphoreType.DMA((3,))],
+    )(*(pltpu.with_memory_space_constraint(array, pltpu.HBM) for array in (queries, keys, values)))
     inner = swap(inner, 1)
     others = [(i, i + 1 if i & 1 else i - 1) for i in range(1, seq_size - 1)]
     outer = lax.ppermute(outer, "seq", others)
@@ -273,21 +281,23 @@
         far = (swap(block, 2), swap(block, 6), swap(eighth, 4))
     else:
         far = (lax.all_to_all(quarter, "seq", split_axis=0, concat_axis=0),)
-    (attended,) = kernel_call(
-        functools.partial(attend_kernel, seq_size),
+    share = tokens // head_size
+    shares = kernel_call(
+        functools.partial(attend_kernel, seq_size, len(far)),
         "attend",
         24,
         [VMEM] * (4 + len(far)),
-        [(tokens, width)],
-        [pltpu.VMEM((set_rows(seq_size), pair_width), jnp.bfloat16), wide],
-    )(queries, own, inner, outer, *far)
-    share = tokens // head_size
-    gathered = lax.all_to_all(
-        attended.reshape(head_size, share, width), "head", split_axis=0, concat_axis=0
-    )
+        [(share, width)] * head_size,
+        [
+            pltpu.VMEM((tokens, width), jnp.bfloat16),
+            pltpu.VMEM((set_rows(seq_size), pair_width), jnp.bfloat16),
+            wide,
+        ],
+    )(own_queries, own, inner, outer, *far)
+    parts = [swap(part, step, "head") if step else part for step, part in enumerate(shares)]
     (mixed,) = kernel_call(
-        project_kernel, "project", 8, [VMEM] * 2, [(share, out_weight.shape[1])], []
-    )(gathered, out_weight)
+        project_kernel, "project", 8, [VMEM] * (head_size + 1), [(share, out_weight.shape[1])], []
+    )(*parts, out_weight)
     return mixed
 
 

time: 27 us -> 23.4 us (0.87)
  blocking collectives: 6.71 us -> 0 us
  waiting for transfers between devices: 7.01 us -> 9.9 us
  local copies, waits for them, and re-layouts: 2.52 us -> 0.01 us
  starting transfers between devices: 8.22 us -> 10.1 us
  Pallas kernels: 2.18 us -> 3.13 us
    all_to_all x1 -> x0, blocking collectives: 6.71 us -> none  [shards(): lax.all_to_all(attended.reshape(head_size, share, width), 'head', split_a...]
    ppermute x4 -> x7, waiting for transfers between devices: 7.01 us -> 9.89 us  [swap(): lax.ppermute(array, axis, [(i, i ^ bit) for i in range(lax.axis_size(axis...]
    unnamed x8 -> x2, local copies, waits for them, and re-layouts: 2.52 us -> 0.01 us
    ppermute x4 -> x7, starting transfers between devices: 7.56 us -> 9.49 us  [swap(): lax.ppermute(array, axis, [(i, i ^ bit) for i in range(lax.axis_size(axis...]
    pallas_call x1, Pallas kernels: 0.12 us -> 1.06 us  [shards(): kernel_call(functools.partial(pack_kernel, not paired), 'pack', 16, [HBM]...]
  transfers between devices with their start and end apart: 5 -> 8, of which waited for: 2 -> 4; matrix products, arithmetic and copies ran while one was open for 0% -> 0% of each run, Pallas kernels for 0% -> 0%
where the time goes in v4:
time: 23.4 us; the launch traced here: 23.2 us
  starting transfers between devices  10.1 us (43%)
  waiting for transfers between devices  9.9 us (42%)
  Pallas kernels  3.13 us (13%)
    ppermute x7, waiting for transfers between devices, swap(): lax.ppermute(array, axis, [(i, i ^ bit) for i in range(lax.axis_size(axis...  9.89 us
    ppermute x7, starting transfers between devices, swap(): lax.ppermute(array, axis, [(i, i ^ bit) for i in range(lax.axis_size(axis...  9.49 us
    pallas_call x1, Pallas kernels, shards(): kernel_call(functools.partial(attend_kernel, seq_size, len(far)), 'attend...  1.2 us
    pallas_call x1, Pallas kernels, shards(): kernel_call(functools.partial(pack_kernel, not paired), 'pack', 16, [HBM]...  1.06 us
    pallas_call x1, Pallas kernels, shards(): kernel_call(project_kernel, 'project', 8, [VMEM] * (head_size + 1), [(sha...  0.85 us
    ppermute x1, starting transfers between devices, shards(): outer = lax.ppermute(outer, 'seq', others)  0.65 us
  transfers between devices with their start and end apart: 8, of which 4 were waited for; matrix products, arithmetic and copies ran while one was open for 0% of the time, Pallas kernels for 0%

profile of v4, /device:TPU:0, one launch (start us, length us, event | category | flops | bytes accessed | tf_op | source)
XLA Modules:
  0.0 23.2 jit_solution(8400189839571905145)
XLA Ops:
  0.0 0.0 copy-start
  0.0 1.1 %pack.1 = (bf16[256,128]{1,0:T(8,128)(2,1)S(1)}, bf16[256,256]{1,0:T(8,128)(2,1)S(1)}, bf16[256,256]{1,0:T(8,128)(2,1)S(1)}, bf16[192,256]{1,0:T(8,128)(2,1)S(1)}, bf16[64,256]{1,0:T(8,128)(2,1)S(1)}) custom-call(bf16[256,128]{1,0:T(8,128)(2,1)} %queries.1, bf16[256,128]{1,0:T(8,128)(2,1)} %keys.1, bf16[256,128]{1,0:T(8,128)(2,1)} %values.1), custom_call_target="tpu_custom_call" | custom-call | tf_op jit(solution)/shard_map/pack/pallas_call | solution.py:255
  1.1 3.0 %collective-permute-start = (bf16[256,256]{1,0:T(8,128)(2,1)S(1)}, bf16[256,256]{1,0:T(8,128)(2,1)S(1)}, u32[]{:S(2)}, u32[]{:S(2)}) collective-permute-start(bf16[256,256]{1,0:T(8,128)(2,1)S(1)} %get-tuple-element.18), channel_id=1, source_target_pairs={{0,4},{4,0},{8,12},{12,8},{16,20},{20,16},{24,28},{28,24},{1,5},{5... | collective-permute-start | bytes 393224 | tf_op jit(solution)/shard_map/ppermute | solution.py:253
  4.1 0.7 %collective-permute-start.1 = (bf16[192,256]{1,0:T(8,128)(2,1)S(1)}, bf16[192,256]{1,0:T(8,128)(2,1)S(1)}, u32[]{:S(2)}, u32[]{:S(2)}) collective-permute-start(bf16[192,256]{1,0:T(8,128)(2,1)S(1)} %get-tuple-element.19), channel_id=1, source_target_pairs={{4,8},{8,4},{12,16},{16,12},{20,24},{24,20},{5,9},{9,5},{13,17},{1... | collective-permute-start | bytes 294920 | tf_op jit(solution)/shard_map/ppermute | solution.py:271
  4.7 2.8 %collective-permute-done.inner = bf16[256,256]{1,0:T(8,128)(2,1)S(1)} collective-permute-done((bf16[256,256]{1,0:T(8,128)(2,1)S(1)}, bf16[256,256]{1,0:T(8,128)(2,1)S(1)}, u32[]{:S(2)}, u32[]{:S(2)}) %collective-permute-start) | collective-permute-done | bytes 131104 | tf_op jit(solution)/shard_map/ppermute | solution.py:253
  7.6 3.9 %collective-permute-start.3 = (bf16[128,256]{1,0:T(8,128)(2,1)S(1)}, bf16[128,256]{1,0:T(8,128)(2,1)S(1)}, u32[]{:S(2)}, u32[]{:S(2)}) collective-permute-start(bf16[128,256]{1,0:T(8,128)(2,1)S(1)} %get-tuple-element.21), channel_id=1, source_target_pairs={{0,24},{4,28},{8,16},{12,20},{16,8},{20,12},{24,0},{28,4},{1,25},{... | collective-permute-start | bytes 196616 | tf_op jit(solution)/shard_map/ppermute | solution.py:253
  11.5 0.0 collective-permute-start.2
  11.5 0.6 %collective-permute-start.4 = (bf16[64,256]{1,0:T(8,128)(2,1)S(1)}, bf16[64,256]{1,0:T(8,128)(2,1)S(1)}, u32[]{:S(2)}, u32[]{:S(2)}) collective-permute-start(bf16[64,256]{1,0:T(8,128)(2,1)S(1)} %get-tuple-element.22), channel_id=1, source_target_pairs={{0,16},{4,20},{8,24},{12,28},{16,0},{20,4},{24,8},{28,12},{1,17},{... | collective-permute-start | bytes 98312 | tf_op jit(solution)/shard_map/ppermute | solution.py:253
  12.2 0.0 collective-permute-done.1.outer
  12.2 4.2 %collective-permute-done.4.rest_2_ = bf16[64,256]{1,0:T(8,128)(2,1)S(1)} collective-permute-done((bf16[64,256]{1,0:T(8,128)(2,1)S(1)}, bf16[64,256]{1,0:T(8,128)(2,1)S(1)}, u32[]{:S(2)}, u32[]{:S(2)}) %collective-permute-start.4) | collective-permute-done | bytes 32800 | tf_op jit(solution)/shard_map/ppermute | solution.py:253
  16.3 0.0 collective-permute-done.3.rest_1_
  16.3 0.0 collective-permute-done.2.rest_0_
  16.3 1.2 %attend.1 = (bf16[64,128]{1,0:T(8,128)(2,1)S(1)}, bf16[64,128]{1,0:T(8,128)(2,1)S(1)}, bf16[64,128]{1,0:T(8,128)(2,1)S(1)}, bf16[64,128]{1,0:T(8,128)(2,1)S(1)}) custom-call(bf16[256,128]{1,0:T(8,128)(2,1)S(1)} %get-tuple-element.16.queries, bf16[256,256]{1,0:T(8,128)(2,1)S(1)} %get-tuple-element.17.own, bf16[256,256]{1,0:T(8,128)(2,1)S(1)} %collective-permute-done.inner, ...), custom_call_target="tpu_custom_call" | custom-call | tf_op jit(solution)/shard_map/attend/pallas_call | solution.py:285
  17.5 0.1 collective-permute-start.5
  17.6 1.6 %collective-permute-start.6 = (bf16[64,128]{1,0:T(8,128)(2,1)S(1)}, bf16[64,128]{1,0:T(8,128)(2,1)S(1)}, u32[]{:S(2)}, u32[]{:S(2)}) collective-permute-start(bf16[64,128]{1,0:T(8,128)(2,1)S(1)} %get-tuple-element.25), channel_id=1, source_target_pairs={{0,2},{1,3},{2,0},{3,1},{4,6},{5,7},{6,4},{7,5},{8,10},{9,11},{10,... | collective-permute-start | bytes 49160 | tf_op jit(solution)/shard_map/ppermute | solution.py:253
  19.2 0.3 %collective-permute-start.7 = (bf16[64,128]{1,0:T(8,128)(2,1)S(1)}, bf16[64,128]{1,0:T(8,128)(2,1)S(1)}, u32[]{:S(2)}, u32[]{:S(2)}) collective-permute-start(bf16[64,128]{1,0:T(8,128)(2,1)S(1)} %get-tuple-element.26), channel_id=1, source_target_pairs={{0,3},{1,2},{2,1},{3,0},{4,7},{5,6},{6,5},{7,4},{8,11},{9,10},{10,... | collective-permute-start | bytes 49160 | tf_op jit(solution)/shard_map/ppermute | solution.py:253
  19.5 0.0 collective-permute-done.5.refs_1_
  19.5 1.9 %collective-permute-done.6.refs_2_ = bf16[64,128]{1,0:T(8,128)(2,1)S(1)} collective-permute-done((bf16[64,128]{1,0:T(8,128)(2,1)S(1)}, bf16[64,128]{1,0:T(8,128)(2,1)S(1)}, u32[]{:S(2)}, u32[]{:S(2)}) %collective-permute-start.6) | collective-permute-done | bytes 16416 | tf_op jit(solution)/shard_map/ppermute | solution.py:253
  21.4 0.9 %collective-permute-done.7.refs_3_ = bf16[64,128]{1,0:T(8,128)(2,1)S(1)} collective-permute-done((bf16[64,128]{1,0:T(8,128)(2,1)S(1)}, bf16[64,128]{1,0:T(8,128)(2,1)S(1)}, u32[]{:S(2)}, u32[]{:S(2)}) %collective-permute-start.7) | collective-permute-done | bytes 16416 | tf_op jit(solution)/shard_map/ppermute | solution.py:253
  22.4 0.0 copy-done
  22.4 0.8 %project.1 = bf16[64,512]{1,0:T(8,128)(2,1)} custom-call(bf16[64,128]{1,0:T(8,128)(2,1)S(1)} %get-tuple-element.23.refs_0_, bf16[64,128]{1,0:T(8,128)(2,1)S(1)} %collective-permute-done.5.refs_1_, bf16[64,128]{1,0:T(8,128)(2,1)S(1)} %collective-permute-done.6.refs_2_, bf16[64,128]{1,0:T(8,128)(2,1)S(1)} %collective-permute-done.7.refs_3_, ...), custom_call_target="tpu_custom_call" | custom-call | tf_op jit(solution)/shard_map/project/pallas_call | solution.py:298
  (1 shorter events, 0.0 us)
Async XLA Ops:
  0.0 22.4 %copy-start = (bf16[512,512]{1,0:T(8,128)(2,1)S(1)}, bf16[512,512]{1,0:T(8,128)(2,1)}, u32[]{:S(2)}) copy-start(bf16[512,512]{1,0:T(8,128)(2,1)} %refs_4_.1) | copy-start | bytes 1572868
  1.1 6.5 %collective-permute-start = (bf16[256,256]{1,0:T(8,128)(2,1)S(1)}, bf16[256,256]{1,0:T(8,128)(2,1)S(1)}, u32[]{:S(2)}, u32[]{:S(2)}) collective-permute-start(bf16[256,256]{1,0:T(8,128)(2,1)S(1)} %get-tuple-element.18), channel_id=1, source_target_pairs={{0,4},{4,0},{8,12},{12,8},{16,20},{20,16},{24,28},{28,24},{1,5},{5... | collective-permute-start | bytes 393224 | tf_op jit(solution)/shard_map/ppermute | solution.py:253
  4.1 8.1 %collective-permute-start.1 = (bf16[192,256]{1,0:T(8,128)(2,1)S(1)}, bf16[192,256]{1,0:T(8,128)(2,1)S(1)}, u32[]{:S(2)}, u32[]{:S(2)}) collective-permute-start(bf16[192,256]{1,0:T(8,128)(2,1)S(1)} %get-tuple-element.19), channel_id=1, source_target_pairs={{4,8},{8,4},{12,16},{16,12},{20,24},{24,20},{5,9},{9,5},{13,17},{1... | collective-permute-start | bytes 294920 | tf_op jit(solution)/shard_map/ppermute | solution.py:271
  7.6 8.7 %collective-permute-start.3 = (bf16[128,256]{1,0:T(8,128)(2,1)S(1)}, bf16[128,256]{1,0:T(8,128)(2,1)S(1)}, u32[]{:S(2)}, u32[]{:S(2)}) collective-permute-start(bf16[128,256]{1,0:T(8,128)(2,1)S(1)} %get-tuple-element.21), channel_id=1, source_target_pairs={{0,24},{4,28},{8,16},{12,20},{16,8},{20,12},{24,0},{28,4},{1,25},{... | collective-permute-start | bytes 196616 | tf_op jit(solution)/shard_map/ppermute | solution.py:253
  11.5 4.8 %collective-permute-start.2 = (bf16[128,256]{1,0:T(8,128)(2,1)S(1)}, bf16[128,256]{1,0:T(8,128)(2,1)S(1)}, u32[]{:S(2)}, u32[]{:S(2)}) collective-permute-start(bf16[128,256]{1,0:T(8,128)(2,1)S(1)} %get-tuple-element.21), channel_id=1, source_target_pairs={{0,8},{4,12},{8,0},{12,4},{16,24},{20,28},{24,16},{28,20},{1,9},{5... | collective-permute-start | bytes 196616 | tf_op jit(solution)/shard_map/ppermute | solution.py:253
  11.5 4.8 %collective-permute-start.4 = (bf16[64,256]{1,0:T(8,128)(2,1)S(1)}, bf16[64,256]{1,0:T(8,128)(2,1)S(1)}, u32[]{:S(2)}, u32[]{:S(2)}) collective-permute-start(bf16[64,256]{1,0:T(8,128)(2,1)S(1)} %get-tuple-element.22), channel_id=1, source_target_pairs={{0,16},{4,20},{8,24},{12,28},{16,0},{20,4},{24,8},{28,12},{1,17},{... | collective-permute-start | bytes 98312 | tf_op jit(solution)/shard_map/ppermute | solution.py:253
  17.5 1.9 %collective-permute-start.5 = (bf16[64,128]{1,0:T(8,128)(2,1)S(1)}, bf16[64,128]{1,0:T(8,128)(2,1)S(1)}, u32[]{:S(2)}, u32[]{:S(2)}) collective-permute-start(bf16[64,128]{1,0:T(8,128)(2,1)S(1)} %get-tuple-element.24), channel_id=1, source_target_pairs={{0,1},{1,0},{2,3},{3,2},{4,5},{5,4},{6,7},{7,6},{8,9},{9,8},{10,11... | collective-permute-start | bytes 49160 | tf_op jit(solution)/shard_map/ppermute | solution.py:253
  17.6 3.8 %collective-permute-start.6 = (bf16[64,128]{1,0:T(8,128)(2,1)S(1)}, bf16[64,128]{1,0:T(8,128)(2,1)S(1)}, u32[]{:S(2)}, u32[]{:S(2)}) collective-permute-start(bf16[64,128]{1,0:T(8,128)(2,1)S(1)} %get-tuple-element.25), channel_id=1, source_target_pairs={{0,2},{1,3},{2,0},{3,1},{4,6},{5,7},{6,4},{7,5},{8,10},{9,11},{10,... | collective-permute-start | bytes 49160 | tf_op jit(solution)/shard_map/ppermute | solution.py:253
  19.2 3.2 %collective-permute-start.7 = (bf16[64,128]{1,0:T(8,128)(2,1)S(1)}, bf16[64,128]{1,0:T(8,128)(2,1)S(1)}, u32[]{:S(2)}, u32[]{:S(2)}) collective-permute-start(bf16[64,128]{1,0:T(8,128)(2,1)S(1)} %get-tuple-element.26), channel_id=1, source_target_pairs={{0,3},{1,2},{2,1},{3,0},{4,7},{5,6},{6,5},{7,4},{8,11},{9,10},{10,... | collective-permute-start | bytes 49160 | tf_op jit(solution)/shard_map/ppermute | solution.py:253

commit v5 on v4

--- a/solution.py
+++ b/solution.py
@@ -44,20 +44,24 @@
     level_two = average_pairs(level_one, wide)
     first, second = level_one[:HALF], level_one[HALF:]
     inner[:LEAF] = jnp.where(odd == 1, low, high)
-    inner[LEAF : LEAF + HALF] = jnp.where(odd == 1, second, first)
+    inner[LEAF:] = jnp.where(odd == 1, second, first)
     outer[:LEAF] = jnp.where(odd == 1, high, low)
     outer[LEAF:] = jnp.where(odd == 1, first, second)
     if far_shares:
         for peer in range(quarter.shape[0]):
             quarter[peer] = level_two
     else:
-        inner[LEAF + HALF :] = level_two
         quarter[...] = level_two
 
 
 def join_kernel(inner, quarter, block, eighth, wide):
     odd = lax.axis_index("seq") & 1
-    theirs = inner[LEAF + HALF :]
+    edge_half = average_pairs(inner[:LEAF], wide)
+    other_half = inner[LEAF:]
+    theirs = jnp.concatenate(
+        [jnp.where(odd == 1, other_half, edge_half), jnp.where(odd == 1, edge_half, other_half)], axis=0
+    )
+    theirs = average_pairs(theirs, wide)
     block[:HALF] = jnp.where(odd == 1, theirs, quarter[...])
     block[HALF:] = jnp.where(odd == 1, quarter[...], theirs)
     eighth[...] = average_pairs(block[...], wide)
@@ -144,7 +148,7 @@
     me = lax.axis_index("seq")
     width = queries.shape[1]
     odd = me & 1
-    from_inner, from_outer = inner[: LEAF + HALF], outer[...]
+    from_inner, from_outer = inner[...], outer[...]
     before = jnp.where(odd == 1, from_inner, from_outer)
     after = jnp.where(odd == 1, from_outer, from_inner)
     edge_before, edge_after = before[:LEAF], after[:LEAF]
@@ -260,7 +264,7 @@
         [
             (tokens, width),
             (tokens, pair_width),
-            (LEAF + HALF + (HALF if paired else 0), pair_width),
+            (LEAF + HALF, pair_width),
             (LEAF + HALF, pair_width),
             (HALF, pair_width) if paired else (seq_size, HALF, pair_width),
         ],
@@ -278,7 +282,8 @@
             [(LEAF, pair_width), (HALF, pair_width)],
             [wide],
         )(inner, quarter)
-        far = (swap(block, 2), swap(block, 6), swap(eighth, 4))
+        block_6 = swap(block, 6)
+        far = (swap(block, 2), block_6, swap(eighth, 4))
     else:
         far = (lax.all_to_all(quarter, "seq", split_axis=0, concat_axis=0),)
     share = tokens // head_size

time: 23.4 us -> 23.6 us (level)
  no operation moved by 1% of the time
where the time goes in v5:
time: 23.6 us; the launch traced here: 23.4 us
  starting transfers between devices  10.2 us (43%)
  waiting for transfers between devices  10.1 us (43%)
  Pallas kernels  3.16 us (13%)
    ppermute x7, waiting for transfers between devices, swap(): lax.ppermute(array, axis, [(i, i ^ bit) for i in range(lax.axis_size(axis...  10.1 us
    ppermute x7, starting transfers between devices, swap(): lax.ppermute(array, axis, [(i, i ^ bit) for i in range(lax.axis_size(axis...  9.5 us
    pallas_call x1, Pallas kernels, shards(): kernel_call(functools.partial(attend_kernel, seq_size, len(far)), 'attend...  1.19 us
    pallas_call x1, Pallas kernels, shards(): kernel_call(functools.partial(pack_kernel, not paired), 'pack', 16, [HBM]...  1.05 us
    pallas_call x1, Pallas kernels, shards(): kernel_call(project_kernel, 'project', 8, [VMEM] * (head_size + 1), [(sha...  0.85 us
    ppermute x1, starting transfers between devices, shards(): outer = lax.ppermute(outer, 'seq', others)  0.65 us
  transfers between devices with their start and end apart: 8, of which 4 were waited for; matrix products, arithmetic and copies ran while one was open for 0% of the time, Pallas kernels for 0%

profile of v5, /device:TPU:0, one launch (start us, length us, event | category | flops | bytes accessed | tf_op | source)
XLA Modules:
  0.0 23.4 jit_solution(9719646758562615583)
XLA Ops:
  0.0 0.0 copy-start
  0.0 1.1 %pack.1 = (bf16[256,128]{1,0:T(8,128)(2,1)S(1)}, bf16[256,256]{1,0:T(8,128)(2,1)S(1)}, bf16[192,256]{1,0:T(8,128)(2,1)S(1)}, bf16[192,256]{1,0:T(8,128)(2,1)S(1)}, bf16[64,256]{1,0:T(8,128)(2,1)S(1)}) custom-call(bf16[256,128]{1,0:T(8,128)(2,1)} %queries.1, bf16[256,128]{1,0:T(8,128)(2,1)} %keys.1, bf16[256,128]{1,0:T(8,128)(2,1)} %values.1), custom_call_target="tpu_custom_call" | custom-call | tf_op jit(solution)/shard_map/pack/pallas_call | solution.py:259
  1.1 3.0 %collective-permute-start = (bf16[192,256]{1,0:T(8,128)(2,1)S(1)}, bf16[192,256]{1,0:T(8,128)(2,1)S(1)}, u32[]{:S(2)}, u32[]{:S(2)}) collective-permute-start(bf16[192,256]{1,0:T(8,128)(2,1)S(1)} %get-tuple-element.18), channel_id=1, source_target_pairs={{0,4},{4,0},{8,12},{12,8},{16,20},{20,16},{24,28},{28,24},{1,5},{5... | collective-permute-start | bytes 294920 | tf_op jit(solution)/shard_map/ppermute | solution.py:257
  4.1 0.7 %collective-permute-start.1 = (bf16[192,256]{1,0:T(8,128)(2,1)S(1)}, bf16[192,256]{1,0:T(8,128)(2,1)S(1)}, u32[]{:S(2)}, u32[]{:S(2)}) collective-permute-start(bf16[192,256]{1,0:T(8,128)(2,1)S(1)} %get-tuple-element.19), channel_id=1, source_target_pairs={{4,8},{8,4},{12,16},{16,12},{20,24},{24,20},{5,9},{9,5},{13,17},{1... | collective-permute-start | bytes 294920 | tf_op jit(solution)/shard_map/ppermute | solution.py:275
  4.7 2.1 %collective-permute-done.inner = bf16[192,256]{1,0:T(8,128)(2,1)S(1)} collective-permute-done((bf16[192,256]{1,0:T(8,128)(2,1)S(1)}, bf16[192,256]{1,0:T(8,128)(2,1)S(1)}, u32[]{:S(2)}, u32[]{:S(2)}) %collective-permute-start) | collective-permute-done | bytes 98336 | tf_op jit(solution)/shard_map/ppermute | solution.py:257
  6.9 0.1 join.1
  6.9 2.0 %collective-permute-start.2 = (bf16[128,256]{1,0:T(8,128)(2,1)S(1)}, bf16[128,256]{1,0:T(8,128)(2,1)S(1)}, u32[]{:S(2)}, u32[]{:S(2)}) collective-permute-start(bf16[128,256]{1,0:T(8,128)(2,1)S(1)} %get-tuple-element.21), channel_id=1, source_target_pairs={{0,8},{4,12},{8,0},{12,4},{16,24},{20,28},{24,16},{28,20},{1,9},{5... | collective-permute-start | bytes 196616 | tf_op jit(solution)/shard_map/ppermute | solution.py:257
  8.9 2.5 %collective-permute-start.3 = (bf16[128,256]{1,0:T(8,128)(2,1)S(1)}, bf16[128,256]{1,0:T(8,128)(2,1)S(1)}, u32[]{:S(2)}, u32[]{:S(2)}) collective-permute-start(bf16[128,256]{1,0:T(8,128)(2,1)S(1)} %get-tuple-element.21), channel_id=1, source_target_pairs={{0,24},{4,28},{8,16},{12,20},{16,8},{20,12},{24,0},{28,4},{1,25},{... | collective-permute-start | bytes 196616 | tf_op jit(solution)/shard_map/ppermute | solution.py:257
  11.4 0.1 collective-permute-start.4
  11.5 0.0 collective-permute-done.1.outer
  11.5 5.0 %collective-permute-done.4.rest_2_ = bf16[64,256]{1,0:T(8,128)(2,1)S(1)} collective-permute-done((bf16[64,256]{1,0:T(8,128)(2,1)S(1)}, bf16[64,256]{1,0:T(8,128)(2,1)S(1)}, u32[]{:S(2)}, u32[]{:S(2)}) %collective-permute-start.4) | collective-permute-done | bytes 32800 | tf_op jit(solution)/shard_map/ppermute | solution.py:257
  16.5 0.0 collective-permute-done.2.rest_0_
  16.6 0.0 collective-permute-done.3.rest_1_
  16.6 1.2 %attend.1 = (bf16[64,128]{1,0:T(8,128)(2,1)S(1)}, bf16[64,128]{1,0:T(8,128)(2,1)S(1)}, bf16[64,128]{1,0:T(8,128)(2,1)S(1)}, bf16[64,128]{1,0:T(8,128)(2,1)S(1)}) custom-call(bf16[256,128]{1,0:T(8,128)(2,1)S(1)} %get-tuple-element.16.queries, bf16[256,256]{1,0:T(8,128)(2,1)S(1)} %get-tuple-element.17.own, bf16[192,256]{1,0:T(8,128)(2,1)S(1)} %collective-permute-done.inner, ...), custom_call_target="tpu_custom_call" | custom-call | tf_op jit(solution)/shard_map/attend/pallas_call | solution.py:290
  17.7 0.1 collective-permute-start.5
  17.8 1.6 %collective-permute-start.6 = (bf16[64,128]{1,0:T(8,128)(2,1)S(1)}, bf16[64,128]{1,0:T(8,128)(2,1)S(1)}, u32[]{:S(2)}, u32[]{:S(2)}) collective-permute-start(bf16[64,128]{1,0:T(8,128)(2,1)S(1)} %get-tuple-element.25), channel_id=1, source_target_pairs={{0,2},{1,3},{2,0},{3,1},{4,6},{5,7},{6,4},{7,5},{8,10},{9,11},{10,... | collective-permute-start | bytes 49160 | tf_op jit(solution)/shard_map/ppermute | solution.py:257
  19.4 0.3 %collective-permute-start.7 = (bf16[64,128]{1,0:T(8,128)(2,1)S(1)}, bf16[64,128]{1,0:T(8,128)(2,1)S(1)}, u32[]{:S(2)}, u32[]{:S(2)}) collective-permute-start(bf16[64,128]{1,0:T(8,128)(2,1)S(1)} %get-tuple-element.26), channel_id=1, source_target_pairs={{0,3},{1,2},{2,1},{3,0},{4,7},{5,6},{6,5},{7,4},{8,11},{9,10},{10,... | collective-permute-start | bytes 49160 | tf_op jit(solution)/shard_map/ppermute | solution.py:257
  19.7 0.0 collective-permute-done.5.refs_1_
  19.7 1.9 %collective-permute-done.6.refs_2_ = bf16[64,128]{1,0:T(8,128)(2,1)S(1)} collective-permute-done((bf16[64,128]{1,0:T(8,128)(2,1)S(1)}, bf16[64,128]{1,0:T(8,128)(2,1)S(1)}, u32[]{:S(2)}, u32[]{:S(2)}) %collective-permute-start.6) | collective-permute-done | bytes 16416 | tf_op jit(solution)/shard_map/ppermute | solution.py:257
  21.6 1.0 %collective-permute-done.7.refs_3_ = bf16[64,128]{1,0:T(8,128)(2,1)S(1)} collective-permute-done((bf16[64,128]{1,0:T(8,128)(2,1)S(1)}, bf16[64,128]{1,0:T(8,128)(2,1)S(1)}, u32[]{:S(2)}, u32[]{:S(2)}) %collective-permute-start.7) | collective-permute-done | bytes 16416 | tf_op jit(solution)/shard_map/ppermute | solution.py:257
  22.6 0.0 copy-done
  22.6 0.8 %project.1 = bf16[64,512]{1,0:T(8,128)(2,1)} custom-call(bf16[64,128]{1,0:T(8,128)(2,1)S(1)} %get-tuple-element.23.refs_0_, bf16[64,128]{1,0:T(8,128)(2,1)S(1)} %collective-permute-done.5.refs_1_, bf16[64,128]{1,0:T(8,128)(2,1)S(1)} %collective-permute-done.6.refs_2_, bf16[64,128]{1,0:T(8,128)(2,1)S(1)} %collective-permute-done.7.refs_3_, ...), custom_call_target="tpu_custom_call" | custom-call | tf_op jit(solution)/shard_map/project/pallas_call | solution.py:303
Async XLA Ops:
  0.0 22.6 %copy-start = (bf16[512,512]{1,0:T(8,128)(2,1)S(1)}, bf16[512,512]{1,0:T(8,128)(2,1)}, u32[]{:S(2)}) copy-start(bf16[512,512]{1,0:T(8,128)(2,1)} %refs_4_.1) | copy-start | bytes 1572868
  1.1 5.8 %collective-permute-start = (bf16[192,256]{1,0:T(8,128)(2,1)S(1)}, bf16[192,256]{1,0:T(8,128)(2,1)S(1)}, u32[]{:S(2)}, u32[]{:S(2)}) collective-permute-start(bf16[192,256]{1,0:T(8,128)(2,1)S(1)} %get-tuple-element.18), channel_id=1, source_target_pairs={{0,4},{4,0},{8,12},{12,8},{16,20},{20,16},{24,28},{28,24},{1,5},{5... | collective-permute-start | bytes 294920 | tf_op jit(solution)/shard_map/ppermute | solution.py:257
  4.1 7.4 %collective-permute-start.1 = (bf16[192,256]{1,0:T(8,128)(2,1)S(1)}, bf16[192,256]{1,0:T(8,128)(2,1)S(1)}, u32[]{:S(2)}, u32[]{:S(2)}) collective-permute-start(bf16[192,256]{1,0:T(8,128)(2,1)S(1)} %get-tuple-element.19), channel_id=1, source_target_pairs={{4,8},{8,4},{12,16},{16,12},{20,24},{24,20},{5,9},{9,5},{13,17},{1... | collective-permute-start | bytes 294920 | tf_op jit(solution)/shard_map/ppermute | solution.py:275
  6.9 9.6 %collective-permute-start.2 = (bf16[128,256]{1,0:T(8,128)(2,1)S(1)}, bf16[128,256]{1,0:T(8,128)(2,1)S(1)}, u32[]{:S(2)}, u32[]{:S(2)}) collective-permute-start(bf16[128,256]{1,0:T(8,128)(2,1)S(1)} %get-tuple-element.21), channel_id=1, source_target_pairs={{0,8},{4,12},{8,0},{12,4},{16,24},{20,28},{24,16},{28,20},{1,9},{5... | collective-permute-start | bytes 196616 | tf_op jit(solution)/shard_map/ppermute | solution.py:257
  8.9 7.6 %collective-permute-start.3 = (bf16[128,256]{1,0:T(8,128)(2,1)S(1)}, bf16[128,256]{1,0:T(8,128)(2,1)S(1)}, u32[]{:S(2)}, u32[]{:S(2)}) collective-permute-start(bf16[128,256]{1,0:T(8,128)(2,1)S(1)} %get-tuple-element.21), channel_id=1, source_target_pairs={{0,24},{4,28},{8,16},{12,20},{16,8},{20,12},{24,0},{28,4},{1,25},{... | collective-permute-start | bytes 196616 | tf_op jit(solution)/shard_map/ppermute | solution.py:257
  11.4 5.2 %collective-permute-start.4 = (bf16[64,256]{1,0:T(8,128)(2,1)S(1)}, bf16[64,256]{1,0:T(8,128)(2,1)S(1)}, u32[]{:S(2)}, u32[]{:S(2)}) collective-permute-start(bf16[64,256]{1,0:T(8,128)(2,1)S(1)} %get-tuple-element.22), channel_id=1, source_target_pairs={{0,16},{4,20},{8,24},{12,28},{16,0},{20,4},{24,8},{28,12},{1,17},{... | collective-permute-start | bytes 98312 | tf_op jit(solution)/shard_map/ppermute | solution.py:257
  17.7 1.9 %collective-permute-start.5 = (bf16[64,128]{1,0:T(8,128)(2,1)S(1)}, bf16[64,128]{1,0:T(8,128)(2,1)S(1)}, u32[]{:S(2)}, u32[]{:S(2)}) collective-permute-start(bf16[64,128]{1,0:T(8,128)(2,1)S(1)} %get-tuple-element.24), channel_id=1, source_target_pairs={{0,1},{1,0},{2,3},{3,2},{4,5},{5,4},{6,7},{7,6},{8,9},{9,8},{10,11... | collective-permute-start | bytes 49160 | tf_op jit(solution)/shard_map/ppermute | solution.py:257
  17.8 3.8 %collective-permute-start.6 = (bf16[64,128]{1,0:T(8,128)(2,1)S(1)}, bf16[64,128]{1,0:T(8,128)(2,1)S(1)}, u32[]{:S(2)}, u32[]{:S(2)}) collective-permute-start(bf16[64,128]{1,0:T(8,128)(2,1)S(1)} %get-tuple-element.25), channel_id=1, source_target_pairs={{0,2},{1,3},{2,0},{3,1},{4,6},{5,7},{6,4},{7,5},{8,10},{9,11},{10,... | collective-permute-start | bytes 49160 | tf_op jit(solution)/shard_map/ppermute | solution.py:257
  19.4 3.2 %collective-permute-start.7 = (bf16[64,128]{1,0:T(8,128)(2,1)S(1)}, bf16[64,128]{1,0:T(8,128)(2,1)S(1)}, u32[]{:S(2)}, u32[]{:S(2)}) collective-permute-start(bf16[64,128]{1,0:T(8,128)(2,1)S(1)} %get-tuple-element.26), channel_id=1, source_target_pairs={{0,3},{1,2},{2,1},{3,0},{4,7},{5,6},{6,5},{7,4},{8,11},{9,10},{10,... | collective-permute-start | bytes 49160 | tf_op jit(solution)/shard_map/ppermute | solution.py:257

commit v6 on v5

--- a/solution.py
+++ b/solution.py
@@ -121,7 +121,7 @@
     return pieces
 
 
-def paired_pieces(block_2, block_6, eighth_4, wide):
+def paired_pieces(block_6, block_2, eighth_4, wide):
     me = lax.axis_index("seq")
     odd = me & 1
     pair = me >> 1
@@ -220,7 +220,7 @@
     *parts, weight, mixed = refs
     mine = lax.axis_index("head")
     total = jnp.zeros(mixed.shape, jnp.float32)
-    for step, part in enumerate(parts):
+    for step, part in enumerate(reversed(parts)):
         width = part.shape[1]
         columns = pl.ds(pl.multiple_of((mine ^ step) * width, width), width)
         total += jnp.dot(part[...], weight[columns], preferred_element_type=jnp.float32)
@@ -282,8 +282,7 @@
             [(LEAF, pair_width), (HALF, pair_width)],
             [wide],
         )(inner, quarter)
-        block_6 = swap(block, 6)
-        far = (swap(block, 2), block_6, swap(eighth, 4))
+        far = (swap(block, 6), swap(block, 2), swap(eighth, 4))
     else:
         far = (lax.all_to_all(quarter, "seq", split_axis=0, concat_axis=0),)
     share = tokens // head_size
@@ -299,10 +298,10 @@
             wide,
         ],
     )(own_queries, own, inner, outer, *far)
-    parts = [swap(part, step, "head") if step else part for step, part in enumerate(shares)]
+    parts = [swap(shares[step], step, "head") for step in range(head_size - 1, 0, -1)]
     (mixed,) = kernel_call(
         project_kernel, "project", 8, [VMEM] * (head_size + 1), [(share, out_weight.shape[1])], []
-    )(*parts, out_weight)
+    )(*parts, shares[0], out_weight)
     return mixed
 
 

time: 23.6 us -> 21.9 us (0.928)
  waiting for transfers between devices: 10.1 us -> 8.27 us
    ppermute x7, waiting for transfers between devices: 10.1 us -> 8.26 us  [swap(): lax.ppermute(array, axis, [(i, i ^ bit) for i in range(lax.axis_size(axis...]
where the time goes in v6:
time: 21.9 us; the launch traced here: 21.7 us
  starting transfers between devices  10.2 us (47%)
  waiting for transfers between devices  8.27 us (38%)
  Pallas kernels  3.17 us (14%)
    ppermute x7, starting transfers between devices, swap(): lax.ppermute(array, axis, [(i, i ^ bit) for i in range(lax.axis_size(axis...  9.56 us
    ppermute x7, waiting for transfers between devices, swap(): lax.ppermute(array, axis, [(i, i ^ bit) for i in range(lax.axis_size(axis...  8.26 us
    pallas_call x1, Pallas kernels, shards(): kernel_call(functools.partial(attend_kernel, seq_size, len(far)), 'attend...  1.2 us
    pallas_call x1, Pallas kernels, shards(): kernel_call(functools.partial(pack_kernel, not paired), 'pack', 16, [HBM]...  1.05 us
    pallas_call x1, Pallas kernels, shards(): kernel_call(project_kernel, 'project', 8, [VMEM] * (head_size + 1), [(sha...  0.85 us
    ppermute x1, starting transfers between devices, shards(): outer = lax.ppermute(outer, 'seq', others)  0.65 us
  transfers between devices with their start and end apart: 8, of which 4 were waited for; matrix products, arithmetic and copies ran while one was open for 0% of the time, Pallas kernels for 0%

profile of v6, /device:TPU:0, one launch (start us, length us, event | category | flops | bytes accessed | tf_op | source)
XLA Modules:
  0.0 21.7 jit_solution(233875649233465900)
XLA Ops:
  0.0 0.0 copy-start
  0.0 1.1 %pack.1 = (bf16[256,128]{1,0:T(8,128)(2,1)S(1)}, bf16[256,256]{1,0:T(8,128)(2,1)S(1)}, bf16[192,256]{1,0:T(8,128)(2,1)S(1)}, bf16[192,256]{1,0:T(8,128)(2,1)S(1)}, bf16[64,256]{1,0:T(8,128)(2,1)S(1)}) custom-call(bf16[256,128]{1,0:T(8,128)(2,1)} %queries.1, bf16[256,128]{1,0:T(8,128)(2,1)} %keys.1, bf16[256,128]{1,0:T(8,128)(2,1)} %values.1), custom_call_target="tpu_custom_call" | custom-call | tf_op jit(solution)/shard_map/pack/pallas_call | solution.py:259
  1.1 3.0 %collective-permute-start = (bf16[192,256]{1,0:T(8,128)(2,1)S(1)}, bf16[192,256]{1,0:T(8,128)(2,1)S(1)}, u32[]{:S(2)}, u32[]{:S(2)}) collective-permute-start(bf16[192,256]{1,0:T(8,128)(2,1)S(1)} %get-tuple-element.18), channel_id=1, source_target_pairs={{0,4},{4,0},{8,12},{12,8},{16,20},{20,16},{24,28},{28,24},{1,5},{5... | collective-permute-start | bytes 294920 | tf_op jit(solution)/shard_map/ppermute | solution.py:257
  4.1 0.7 %collective-permute-start.1 = (bf16[192,256]{1,0:T(8,128)(2,1)S(1)}, bf16[192,256]{1,0:T(8,128)(2,1)S(1)}, u32[]{:S(2)}, u32[]{:S(2)}) collective-permute-start(bf16[192,256]{1,0:T(8,128)(2,1)S(1)} %get-tuple-element.19), channel_id=1, source_target_pairs={{4,8},{8,4},{12,16},{16,12},{20,24},{24,20},{5,9},{9,5},{13,17},{1... | collective-permute-start | bytes 294920 | tf_op jit(solution)/shard_map/ppermute | solution.py:275
  4.7 2.1 %collective-permute-done.inner = bf16[192,256]{1,0:T(8,128)(2,1)S(1)} collective-permute-done((bf16[192,256]{1,0:T(8,128)(2,1)S(1)}, bf16[192,256]{1,0:T(8,128)(2,1)S(1)}, u32[]{:S(2)}, u32[]{:S(2)}) %collective-permute-start) | collective-permute-done | bytes 98336 | tf_op jit(solution)/shard_map/ppermute | solution.py:257
  6.9 0.1 join.1
  6.9 4.0 %collective-permute-start.2 = (bf16[128,256]{1,0:T(8,128)(2,1)S(1)}, bf16[128,256]{1,0:T(8,128)(2,1)S(1)}, u32[]{:S(2)}, u32[]{:S(2)}) collective-permute-start(bf16[128,256]{1,0:T(8,128)(2,1)S(1)} %get-tuple-element.21), channel_id=1, source_target_pairs={{0,24},{4,28},{8,16},{12,20},{16,8},{20,12},{24,0},{28,4},{1,25},{... | collective-permute-start | bytes 196616 | tf_op jit(solution)/shard_map/ppermute | solution.py:257
  10.9 0.0 collective-permute-start.3
  10.9 0.6 %collective-permute-start.4 = (bf16[64,256]{1,0:T(8,128)(2,1)S(1)}, bf16[64,256]{1,0:T(8,128)(2,1)S(1)}, u32[]{:S(2)}, u32[]{:S(2)}) collective-permute-start(bf16[64,256]{1,0:T(8,128)(2,1)S(1)} %get-tuple-element.22), channel_id=1, source_target_pairs={{0,16},{4,20},{8,24},{12,28},{16,0},{20,4},{24,8},{28,12},{1,17},{... | collective-permute-start | bytes 98312 | tf_op jit(solution)/shard_map/ppermute | solution.py:257
  11.6 0.0 collective-permute-done.1.outer
  11.6 4.2 %collective-permute-done.4.rest_2_ = bf16[64,256]{1,0:T(8,128)(2,1)S(1)} collective-permute-done((bf16[64,256]{1,0:T(8,128)(2,1)S(1)}, bf16[64,256]{1,0:T(8,128)(2,1)S(1)}, u32[]{:S(2)}, u32[]{:S(2)}) %collective-permute-start.4) | collective-permute-done | bytes 32800 | tf_op jit(solution)/shard_map/ppermute | solution.py:257
  15.7 0.0 collective-permute-done.2.rest_0_
  15.8 0.0 collective-permute-done.3.rest_1_
  15.8 1.2 %attend.1 = (bf16[64,128]{1,0:T(8,128)(2,1)S(1)}, bf16[64,128]{1,0:T(8,128)(2,1)S(1)}, bf16[64,128]{1,0:T(8,128)(2,1)S(1)}, bf16[64,128]{1,0:T(8,128)(2,1)S(1)}) custom-call(bf16[256,128]{1,0:T(8,128)(2,1)S(1)} %get-tuple-element.16.queries, bf16[256,256]{1,0:T(8,128)(2,1)S(1)} %get-tuple-element.17.own, bf16[192,256]{1,0:T(8,128)(2,1)S(1)} %collective-permute-done.inner, ...), custom_call_target="tpu_custom_call" | custom-call | tf_op jit(solution)/shard_map/attend/pallas_call | solution.py:289
  17.0 0.1 collective-permute-start.5
  17.0 1.6 %collective-permute-start.6 = (bf16[64,128]{1,0:T(8,128)(2,1)S(1)}, bf16[64,128]{1,0:T(8,128)(2,1)S(1)}, u32[]{:S(2)}, u32[]{:S(2)}) collective-permute-start(bf16[64,128]{1,0:T(8,128)(2,1)S(1)} %get-tuple-element.24), channel_id=1, source_target_pairs={{0,2},{1,3},{2,0},{3,1},{4,6},{5,7},{6,4},{7,5},{8,10},{9,11},{10,... | collective-permute-start | bytes 49160 | tf_op jit(solution)/shard_map/ppermute | solution.py:257
  18.6 0.3 %collective-permute-start.7 = (bf16[64,128]{1,0:T(8,128)(2,1)S(1)}, bf16[64,128]{1,0:T(8,128)(2,1)S(1)}, u32[]{:S(2)}, u32[]{:S(2)}) collective-permute-start(bf16[64,128]{1,0:T(8,128)(2,1)S(1)} %get-tuple-element.25), channel_id=1, source_target_pairs={{0,1},{1,0},{2,3},{3,2},{4,5},{5,4},{6,7},{7,6},{8,9},{9,8},{10,11... | collective-permute-start | bytes 49160 | tf_op jit(solution)/shard_map/ppermute | solution.py:257
  18.9 1.4 %collective-permute-done.5.refs_0_ = bf16[64,128]{1,0:T(8,128)(2,1)S(1)} collective-permute-done((bf16[64,128]{1,0:T(8,128)(2,1)S(1)}, bf16[64,128]{1,0:T(8,128)(2,1)S(1)}, u32[]{:S(2)}, u32[]{:S(2)}) %collective-permute-start.5) | collective-permute-done | bytes 16416 | tf_op jit(solution)/shard_map/ppermute | solution.py:257
  20.3 0.5 %collective-permute-done.6.refs_1_ = bf16[64,128]{1,0:T(8,128)(2,1)S(1)} collective-permute-done((bf16[64,128]{1,0:T(8,128)(2,1)S(1)}, bf16[64,128]{1,0:T(8,128)(2,1)S(1)}, u32[]{:S(2)}, u32[]{:S(2)}) %collective-permute-start.6) | collective-permute-done | bytes 16416 | tf_op jit(solution)/shard_map/ppermute | solution.py:257
  20.8 0.0 collective-permute-done.7.refs_2_
  20.8 0.0 copy-done
  20.9 0.9 %project.1 = bf16[64,512]{1,0:T(8,128)(2,1)} custom-call(bf16[64,128]{1,0:T(8,128)(2,1)S(1)} %collective-permute-done.5.refs_0_, bf16[64,128]{1,0:T(8,128)(2,1)S(1)} %collective-permute-done.6.refs_1_, bf16[64,128]{1,0:T(8,128)(2,1)S(1)} %collective-permute-done.7.refs_2_, bf16[64,128]{1,0:T(8,128)(2,1)S(1)} %get-tuple-element.26.refs_3_, ...), custom_call_target="tpu_custom_call" | custom-call | tf_op jit(solution)/shard_map/project/pallas_call | solution.py:302
Async XLA Ops:
  0.0 20.8 %copy-start = (bf16[512,512]{1,0:T(8,128)(2,1)S(1)}, bf16[512,512]{1,0:T(8,128)(2,1)}, u32[]{:S(2)}) copy-start(bf16[512,512]{1,0:T(8,128)(2,1)} %refs_4_.1) | copy-start | bytes 1572868
  1.1 5.8 %collective-permute-start = (bf16[192,256]{1,0:T(8,128)(2,1)S(1)}, bf16[192,256]{1,0:T(8,128)(2,1)S(1)}, u32[]{:S(2)}, u32[]{:S(2)}) collective-permute-start(bf16[192,256]{1,0:T(8,128)(2,1)S(1)} %get-tuple-element.18), channel_id=1, source_target_pairs={{0,4},{4,0},{8,12},{12,8},{16,20},{20,16},{24,28},{28,24},{1,5},{5... | collective-permute-start | bytes 294920 | tf_op jit(solution)/shard_map/ppermute | solution.py:257
  4.1 7.5 %collective-permute-start.1 = (bf16[192,256]{1,0:T(8,128)(2,1)S(1)}, bf16[192,256]{1,0:T(8,128)(2,1)S(1)}, u32[]{:S(2)}, u32[]{:S(2)}) collective-permute-start(bf16[192,256]{1,0:T(8,128)(2,1)S(1)} %get-tuple-element.19), channel_id=1, source_target_pairs={{4,8},{8,4},{12,16},{16,12},{20,24},{24,20},{5,9},{9,5},{13,17},{1... | collective-permute-start | bytes 294920 | tf_op jit(solution)/shard_map/ppermute | solution.py:275
  6.9 8.8 %collective-permute-start.2 = (bf16[128,256]{1,0:T(8,128)(2,1)S(1)}, bf16[128,256]{1,0:T(8,128)(2,1)S(1)}, u32[]{:S(2)}, u32[]{:S(2)}) collective-permute-start(bf16[128,256]{1,0:T(8,128)(2,1)S(1)} %get-tuple-element.21), channel_id=1, source_target_pairs={{0,24},{4,28},{8,16},{12,20},{16,8},{20,12},{24,0},{28,4},{1,25},{... | collective-permute-start | bytes 196616 | tf_op jit(solution)/shard_map/ppermute | solution.py:257
  10.9 4.8 %collective-permute-start.3 = (bf16[128,256]{1,0:T(8,128)(2,1)S(1)}, bf16[128,256]{1,0:T(8,128)(2,1)S(1)}, u32[]{:S(2)}, u32[]{:S(2)}) collective-permute-start(bf16[128,256]{1,0:T(8,128)(2,1)S(1)} %get-tuple-element.21), channel_id=1, source_target_pairs={{0,8},{4,12},{8,0},{12,4},{16,24},{20,28},{24,16},{28,20},{1,9},{5... | collective-permute-start | bytes 196616 | tf_op jit(solution)/shard_map/ppermute | solution.py:257
  10.9 4.8 %collective-permute-start.4 = (bf16[64,256]{1,0:T(8,128)(2,1)S(1)}, bf16[64,256]{1,0:T(8,128)(2,1)S(1)}, u32[]{:S(2)}, u32[]{:S(2)}) collective-permute-start(bf16[64,256]{1,0:T(8,128)(2,1)S(1)} %get-tuple-element.22), channel_id=1, source_target_pairs={{0,16},{4,20},{8,24},{12,28},{16,0},{20,4},{24,8},{28,12},{1,17},{... | collective-permute-start | bytes 98312 | tf_op jit(solution)/shard_map/ppermute | solution.py:257
  17.0 3.3 %collective-permute-start.5 = (bf16[64,128]{1,0:T(8,128)(2,1)S(1)}, bf16[64,128]{1,0:T(8,128)(2,1)S(1)}, u32[]{:S(2)}, u32[]{:S(2)}) collective-permute-start(bf16[64,128]{1,0:T(8,128)(2,1)S(1)} %get-tuple-element.23), channel_id=1, source_target_pairs={{0,3},{1,2},{2,1},{3,0},{4,7},{5,6},{6,5},{7,4},{8,11},{9,10},{10,... | collective-permute-start | bytes 49160 | tf_op jit(solution)/shard_map/ppermute | solution.py:257
  17.0 3.8 %collective-permute-start.6 = (bf16[64,128]{1,0:T(8,128)(2,1)S(1)}, bf16[64,128]{1,0:T(8,128)(2,1)S(1)}, u32[]{:S(2)}, u32[]{:S(2)}) collective-permute-start(bf16[64,128]{1,0:T(8,128)(2,1)S(1)} %get-tuple-element.24), channel_id=1, source_target_pairs={{0,2},{1,3},{2,0},{3,1},{4,6},{5,7},{6,4},{7,5},{8,10},{9,11},{10,... | collective-permute-start | bytes 49160 | tf_op jit(solution)/shard_map/ppermute | solution.py:257
  18.6 2.2 %collective-permute-start.7 = (bf16[64,128]{1,0:T(8,128)(2,1)S(1)}, bf16[64,128]{1,0:T(8,128)(2,1)S(1)}, u32[]{:S(2)}, u32[]{:S(2)}) collective-permute-start(bf16[64,128]{1,0:T(8,128)(2,1)S(1)} %get-tuple-element.25), channel_id=1, source_target_pairs={{0,1},{1,0},{2,3},{3,2},{4,5},{5,4},{6,7},{7,6},{8,9},{9,8},{10,11... | collective-permute-start | bytes 49160 | tf_op jit(solution)/shard_map/ppermute | solution.py:257

commit v7 on v6

--- a/solution.py
+++ b/solution.py
@@ -54,8 +54,9 @@
         quarter[...] = level_two
 
 
-def join_kernel(inner, quarter, block, eighth, wide):
-    odd = lax.axis_index("seq") & 1
+def join_kernel(inner, quarter, block, short, eighth, wide):
+    me = lax.axis_index("seq")
+    odd = me & 1
     edge_half = average_pairs(inner[:LEAF], wide)
     other_half = inner[LEAF:]
     theirs = jnp.concatenate(
@@ -64,7 +65,10 @@
     theirs = average_pairs(theirs, wide)
     block[:HALF] = jnp.where(odd == 1, theirs, quarter[...])
     block[HALF:] = jnp.where(odd == 1, quarter[...], theirs)
-    eighth[...] = average_pairs(block[...], wide)
+    level_three = average_pairs(block[...], wide)
+    eighth[...] = level_three
+    round_the_end = (me == 6) | (me == 1)
+    short[...] = jnp.where(round_the_end, level_three, quarter[...])
 
 
 def set_rows(seq_size):
@@ -121,24 +125,15 @@
     return pieces
 
 
-def paired_pieces(block_6, block_2, eighth_4, wide):
-    me = lax.axis_index("seq")
-    odd = me & 1
-    pair = me >> 1
-    middle = (pair == 1) | (pair == 2)
-    upper_near = (pair & 1) == 0
-    lower = jnp.where(upper_near, block_6[...], block_2[...])
-    upper = jnp.where(upper_near, block_2[...], block_6[...])
-    has_lower, has_upper = pair >= 1, pair <= 2
-    third = jnp.where(odd == 1, lower[HALF:], upper[:HALF])
-    has_third = ((odd == 1) & has_lower) | ((odd == 0) & has_upper)
-    ends = average_pairs(block_6[...], wide)
+def paired_pieces(long, short, eighth, wide):
+    me = lax.axis_index("seq")
+    at_end = (me == 6) | (me == 1)
     return [
-        (lower[:HALF], bias_of(has_lower)),
-        (upper[HALF:], bias_of(has_upper)),
-        (third, bias_of(has_third)),
-        (eighth_4[...], bias_of(pair >= 0)),
-        (ends, bias_of(jnp.logical_not(middle))),
+        (long[:HALF], bias_of(jnp.logical_not(at_end))),
+        (long[HALF:], bias_of(jnp.logical_not(at_end))),
+        (average_pairs(long[...], wide), bias_of(at_end)),
+        (short[...], None),
+        (eighth[...], None),
     ]
 
 
@@ -274,15 +269,21 @@
     others = [(i, i + 1 if i & 1 else i - 1) for i in range(1, seq_size - 1)]
     outer = lax.ppermute(outer, "seq", others)
     if paired:
-        block, eighth = kernel_call(
+        block, short, eighth = kernel_call(
             join_kernel,
             "join",
             8,
             [VMEM] * 2,
-            [(LEAF, pair_width), (HALF, pair_width)],
+            [(LEAF, pair_width), (HALF, pair_width), (HALF, pair_width)],
             [wide],
         )(inner, quarter)
-        far = (swap(block, 6), swap(block, 2), swap(eighth, 4))
+        down_up = [(i, (i + 2 if i & 1 else i - 2) % seq_size) for i in range(seq_size)]
+        up_down = [(target, source) for source, target in down_up]
+        far = (
+            lax.ppermute(block, "seq", down_up),
+            lax.ppermute(short, "seq", up_down),
+            swap(eighth, 4),
+        )
     else:
         far = (lax.all_to_all(quarter, "seq", split_axis=0, concat_axis=0),)
     share = tokens // head_size

time: 21.9 us -> 22.7 us (1.037)
  waiting for transfers between devices: 8.27 us -> 8.79 us
  starting transfers between devices: 10.2 us -> 10.6 us
    ppermute x0 -> x2, waiting for transfers between devices: none -> 4.7 us  [the longest x1 4.7 us: shards(): lax.ppermute(short, 'seq', up_down)]
    ppermute x7 -> x5, waiting for transfers between devices: 8.26 us -> 4.09 us  [swap(): lax.ppermute(array, axis, [(i, i ^ bit) for i in range(lax.axis_size(axis...]
    ppermute x0 -> x2, starting transfers between devices: none -> 3.99 us  [the longest x1 3.99 us: shards(): lax.ppermute(block, 'seq', down_up)]
    ppermute x7 -> x5, starting transfers between devices: 9.56 us -> 5.93 us  [swap(): lax.ppermute(array, axis, [(i, i ^ bit) for i in range(lax.axis_size(axis...]
where the time goes in v7:
time: 22.7 us; the launch traced here: 22.6 us
  starting transfers between devices  10.6 us (47%)
  waiting for transfers between devices  8.79 us (39%)
  Pallas kernels  3.17 us (14%)
    ppermute x5, starting transfers between devices, swap(): lax.ppermute(array, axis, [(i, i ^ bit) for i in range(lax.axis_size(axis...  5.93 us
    ppermute x1, waiting for transfers between devices, shards(): lax.ppermute(short, 'seq', up_down)  4.7 us
    ppermute x5, waiting for transfers between devices, swap(): lax.ppermute(array, axis, [(i, i ^ bit) for i in range(lax.axis_size(axis...  4.09 us
    ppermute x1, starting transfers between devices, shards(): lax.ppermute(block, 'seq', down_up)  3.99 us
    pallas_call x1, Pallas kernels, shards(): kernel_call(functools.partial(attend_kernel, seq_size, len(far)), 'attend...  1.2 us
    pallas_call x1, Pallas kernels, shards(): kernel_call(functools.partial(pack_kernel, not paired), 'pack', 16, [HBM]...  1.05 us
    pallas_call x1, Pallas kernels, shards(): kernel_call(project_kernel, 'project', 8, [VMEM] * (head_size + 1), [(sha...  0.85 us
    ppermute x1, starting transfers between devices, shards(): outer = lax.ppermute(outer, 'seq', others)  0.65 us
  transfers between devices with their start and end apart: 8, of which 4 were waited for; matrix products, arithmetic and copies ran while one was open for 0% of the time, Pallas kernels for 0%

profile of v7, /device:TPU:0, one launch (start us, length us, event | category | flops | bytes accessed | tf_op | source)
XLA Modules:
  0.0 22.6 jit_solution(18092355510375603226)
XLA Ops:
  0.0 0.0 copy-start
  0.0 1.1 %pack.1 = (bf16[256,128]{1,0:T(8,128)(2,1)S(1)}, bf16[256,256]{1,0:T(8,128)(2,1)S(1)}, bf16[192,256]{1,0:T(8,128)(2,1)S(1)}, bf16[192,256]{1,0:T(8,128)(2,1)S(1)}, bf16[64,256]{1,0:T(8,128)(2,1)S(1)}) custom-call(bf16[256,128]{1,0:T(8,128)(2,1)} %queries.1, bf16[256,128]{1,0:T(8,128)(2,1)} %keys.1, bf16[256,128]{1,0:T(8,128)(2,1)} %values.1), custom_call_target="tpu_custom_call" | custom-call | tf_op jit(solution)/shard_map/pack/pallas_call | solution.py:254
  1.1 3.0 %collective-permute-start = (bf16[192,256]{1,0:T(8,128)(2,1)S(1)}, bf16[192,256]{1,0:T(8,128)(2,1)S(1)}, u32[]{:S(2)}, u32[]{:S(2)}) collective-permute-start(bf16[192,256]{1,0:T(8,128)(2,1)S(1)} %get-tuple-element.19), channel_id=1, source_target_pairs={{0,4},{4,0},{8,12},{12,8},{16,20},{20,16},{24,28},{28,24},{1,5},{5... | collective-permute-start | bytes 294920 | tf_op jit(solution)/shard_map/ppermute | solution.py:252
  4.1 0.7 %collective-permute-start.1 = (bf16[192,256]{1,0:T(8,128)(2,1)S(1)}, bf16[192,256]{1,0:T(8,128)(2,1)S(1)}, u32[]{:S(2)}, u32[]{:S(2)}) collective-permute-start(bf16[192,256]{1,0:T(8,128)(2,1)S(1)} %get-tuple-element.20), channel_id=1, source_target_pairs={{4,8},{8,4},{12,16},{16,12},{20,24},{24,20},{5,9},{9,5},{13,17},{1... | collective-permute-start | bytes 294920 | tf_op jit(solution)/shard_map/ppermute | solution.py:270
  4.7 2.1 %collective-permute-done.inner = bf16[192,256]{1,0:T(8,128)(2,1)S(1)} collective-permute-done((bf16[192,256]{1,0:T(8,128)(2,1)S(1)}, bf16[192,256]{1,0:T(8,128)(2,1)S(1)}, u32[]{:S(2)}, u32[]{:S(2)}) %collective-permute-start) | collective-permute-done | bytes 98336 | tf_op jit(solution)/shard_map/ppermute | solution.py:252
  6.9 0.1 join.1
  6.9 4.0 %collective-permute-start.2 = (bf16[128,256]{1,0:T(8,128)(2,1)S(1)}, bf16[128,256]{1,0:T(8,128)(2,1)S(1)}, u32[]{:S(2)}, u32[]{:S(2)}) collective-permute-start(bf16[128,256]{1,0:T(8,128)(2,1)S(1)} %get-tuple-element.22), channel_id=1, source_target_pairs={{0,24},{4,12},{8,0},{12,20},{16,8},{20,28},{24,16},{28,4},{1,25},{... | collective-permute-start | bytes 196616 | tf_op jit(solution)/shard_map/ppermute | solution.py:283
  10.9 0.0 collective-permute-start.3
  10.9 1.0 %collective-permute-start.4 = (bf16[64,256]{1,0:T(8,128)(2,1)S(1)}, bf16[64,256]{1,0:T(8,128)(2,1)S(1)}, u32[]{:S(2)}, u32[]{:S(2)}) collective-permute-start(bf16[64,256]{1,0:T(8,128)(2,1)S(1)} %get-tuple-element.24), channel_id=1, source_target_pairs={{0,16},{4,20},{8,24},{12,28},{16,0},{20,4},{24,8},{28,12},{1,17},{... | collective-permute-start | bytes 98312 | tf_op jit(solution)/shard_map/ppermute | solution.py:252
  11.9 0.0 collective-permute-done.1.outer
  11.9 4.7 %collective-permute-done.3.rest_1_ = bf16[64,256]{1,0:T(8,128)(2,1)S(1)} collective-permute-done((bf16[64,256]{1,0:T(8,128)(2,1)S(1)}, bf16[64,256]{1,0:T(8,128)(2,1)S(1)}, u32[]{:S(2)}, u32[]{:S(2)}) %collective-permute-start.3) | collective-permute-done | bytes 32800 | tf_op jit(solution)/shard_map/ppermute | solution.py:284
  16.6 0.0 collective-permute-done.4.rest_2_
  16.6 0.0 collective-permute-done.2.rest_0_
  16.6 1.2 %attend.1 = (bf16[64,128]{1,0:T(8,128)(2,1)S(1)}, bf16[64,128]{1,0:T(8,128)(2,1)S(1)}, bf16[64,128]{1,0:T(8,128)(2,1)S(1)}, bf16[64,128]{1,0:T(8,128)(2,1)S(1)}) custom-call(bf16[256,128]{1,0:T(8,128)(2,1)S(1)} %get-tuple-element.17.queries, bf16[256,256]{1,0:T(8,128)(2,1)S(1)} %get-tuple-element.18.own, bf16[192,256]{1,0:T(8,128)(2,1)S(1)} %collective-permute-done.inner, ...), custom_call_target="tpu_custom_call" | custom-call | tf_op jit(solution)/shard_map/attend/pallas_call | solution.py:290
  17.8 0.1 collective-permute-start.5
  17.9 1.6 %collective-permute-start.6 = (bf16[64,128]{1,0:T(8,128)(2,1)S(1)}, bf16[64,128]{1,0:T(8,128)(2,1)S(1)}, u32[]{:S(2)}, u32[]{:S(2)}) collective-permute-start(bf16[64,128]{1,0:T(8,128)(2,1)S(1)} %get-tuple-element.26), channel_id=1, source_target_pairs={{0,2},{1,3},{2,0},{3,1},{4,6},{5,7},{6,4},{7,5},{8,10},{9,11},{10,... | collective-permute-start | bytes 49160 | tf_op jit(solution)/shard_map/ppermute | solution.py:252
  19.5 0.3 %collective-permute-start.7 = (bf16[64,128]{1,0:T(8,128)(2,1)S(1)}, bf16[64,128]{1,0:T(8,128)(2,1)S(1)}, u32[]{:S(2)}, u32[]{:S(2)}) collective-permute-start(bf16[64,128]{1,0:T(8,128)(2,1)S(1)} %get-tuple-element.27), channel_id=1, source_target_pairs={{0,1},{1,0},{2,3},{3,2},{4,5},{5,4},{6,7},{7,6},{8,9},{9,8},{10,11... | collective-permute-start | bytes 49160 | tf_op jit(solution)/shard_map/ppermute | solution.py:252
  19.8 1.4 %collective-permute-done.5.refs_0_ = bf16[64,128]{1,0:T(8,128)(2,1)S(1)} collective-permute-done((bf16[64,128]{1,0:T(8,128)(2,1)S(1)}, bf16[64,128]{1,0:T(8,128)(2,1)S(1)}, u32[]{:S(2)}, u32[]{:S(2)}) %collective-permute-start.5) | collective-permute-done | bytes 16416 | tf_op jit(solution)/shard_map/ppermute | solution.py:252
  21.2 0.6 %collective-permute-done.6.refs_1_ = bf16[64,128]{1,0:T(8,128)(2,1)S(1)} collective-permute-done((bf16[64,128]{1,0:T(8,128)(2,1)S(1)}, bf16[64,128]{1,0:T(8,128)(2,1)S(1)}, u32[]{:S(2)}, u32[]{:S(2)}) %collective-permute-start.6) | collective-permute-done | bytes 16416 | tf_op jit(solution)/shard_map/ppermute | solution.py:252
  21.7 0.0 collective-permute-done.7.refs_2_
  21.7 0.0 copy-done
  21.7 0.9 %project.1 = bf16[64,512]{1,0:T(8,128)(2,1)} custom-call(bf16[64,128]{1,0:T(8,128)(2,1)S(1)} %collective-permute-done.5.refs_0_, bf16[64,128]{1,0:T(8,128)(2,1)S(1)} %collective-permute-done.6.refs_1_, bf16[64,128]{1,0:T(8,128)(2,1)S(1)} %collective-permute-done.7.refs_2_, bf16[64,128]{1,0:T(8,128)(2,1)S(1)} %get-tuple-element.28.refs_3_, ...), custom_call_target="tpu_custom_call" | custom-call | tf_op jit(solution)/shard_map/project/pallas_call | solution.py:303
Async XLA Ops:
  0.0 21.7 %copy-start = (bf16[512,512]{1,0:T(8,128)(2,1)S(1)}, bf16[512,512]{1,0:T(8,128)(2,1)}, u32[]{:S(2)}) copy-start(bf16[512,512]{1,0:T(8,128)(2,1)} %refs_4_.1) | copy-start | bytes 1572868
  1.1 5.8 %collective-permute-start = (bf16[192,256]{1,0:T(8,128)(2,1)S(1)}, bf16[192,256]{1,0:T(8,128)(2,1)S(1)}, u32[]{:S(2)}, u32[]{:S(2)}) collective-permute-start(bf16[192,256]{1,0:T(8,128)(2,1)S(1)} %get-tuple-element.19), channel_id=1, source_target_pairs={{0,4},{4,0},{8,12},{12,8},{16,20},{20,16},{24,28},{28,24},{1,5},{5... | collective-permute-start | bytes 294920 | tf_op jit(solution)/shard_map/ppermute | solution.py:252
  4.1 7.9 %collective-permute-start.1 = (bf16[192,256]{1,0:T(8,128)(2,1)S(1)}, bf16[192,256]{1,0:T(8,128)(2,1)S(1)}, u32[]{:S(2)}, u32[]{:S(2)}) collective-permute-start(bf16[192,256]{1,0:T(8,128)(2,1)S(1)} %get-tuple-element.20), channel_id=1, source_target_pairs={{4,8},{8,4},{12,16},{16,12},{20,24},{24,20},{5,9},{9,5},{13,17},{1... | collective-permute-start | bytes 294920 | tf_op jit(solution)/shard_map/ppermute | solution.py:270
  6.9 9.7 %collective-permute-start.2 = (bf16[128,256]{1,0:T(8,128)(2,1)S(1)}, bf16[128,256]{1,0:T(8,128)(2,1)S(1)}, u32[]{:S(2)}, u32[]{:S(2)}) collective-permute-start(bf16[128,256]{1,0:T(8,128)(2,1)S(1)} %get-tuple-element.22), channel_id=1, source_target_pairs={{0,24},{4,12},{8,0},{12,20},{16,8},{20,28},{24,16},{28,4},{1,25},{... | collective-permute-start | bytes 196616 | tf_op jit(solution)/shard_map/ppermute | solution.py:283
  10.9 5.7 %collective-permute-start.3 = (bf16[64,256]{1,0:T(8,128)(2,1)S(1)}, bf16[64,256]{1,0:T(8,128)(2,1)S(1)}, u32[]{:S(2)}, u32[]{:S(2)}) collective-permute-start(bf16[64,256]{1,0:T(8,128)(2,1)S(1)} %get-tuple-element.23), channel_id=1, source_target_pairs={{24,0},{12,4},{0,8},{20,12},{8,16},{28,20},{16,24},{4,28},{25,1},{... | collective-permute-start | bytes 98312 | tf_op jit(solution)/shard_map/ppermute | solution.py:284
  10.9 5.7 %collective-permute-start.4 = (bf16[64,256]{1,0:T(8,128)(2,1)S(1)}, bf16[64,256]{1,0:T(8,128)(2,1)S(1)}, u32[]{:S(2)}, u32[]{:S(2)}) collective-permute-start(bf16[64,256]{1,0:T(8,128)(2,1)S(1)} %get-tuple-element.24), channel_id=1, source_target_pairs={{0,16},{4,20},{8,24},{12,28},{16,0},{20,4},{24,8},{28,12},{1,17},{... | collective-permute-start | bytes 98312 | tf_op jit(solution)/shard_map/ppermute | solution.py:252
  17.8 3.3 %collective-permute-start.5 = (bf16[64,128]{1,0:T(8,128)(2,1)S(1)}, bf16[64,128]{1,0:T(8,128)(2,1)S(1)}, u32[]{:S(2)}, u32[]{:S(2)}) collective-permute-start(bf16[64,128]{1,0:T(8,128)(2,1)S(1)} %get-tuple-element.25), channel_id=1, source_target_pairs={{0,3},{1,2},{2,1},{3,0},{4,7},{5,6},{6,5},{7,4},{8,11},{9,10},{10,... | collective-permute-start | bytes 49160 | tf_op jit(solution)/shard_map/ppermute | solution.py:252
  17.9 3.8 %collective-permute-start.6 = (bf16[64,128]{1,0:T(8,128)(2,1)S(1)}, bf16[64,128]{1,0:T(8,128)(2,1)S(1)}, u32[]{:S(2)}, u32[]{:S(2)}) collective-permute-start(bf16[64,128]{1,0:T(8,128)(2,1)S(1)} %get-tuple-element.26), channel_id=1, source_target_pairs={{0,2},{1,3},{2,0},{3,1},{4,6},{5,7},{6,4},{7,5},{8,10},{9,11},{10,... | collective-permute-start | bytes 49160 | tf_op jit(solution)/shard_map/ppermute | solution.py:252
  19.5 2.2 %collective-permute-start.7 = (bf16[64,128]{1,0:T(8,128)(2,1)S(1)}, bf16[64,128]{1,0:T(8,128)(2,1)S(1)}, u32[]{:S(2)}, u32[]{:S(2)}) collective-permute-start(bf16[64,128]{1,0:T(8,128)(2,1)S(1)} %get-tuple-element.27), channel_id=1, source_target_pairs={{0,1},{1,0},{2,3},{3,2},{4,5},{5,4},{6,7},{7,6},{8,9},{9,8},{10,11... | collective-permute-start | bytes 49160 | tf_op jit(solution)/shard_map/ppermute | solution.py:252

commit v8 on v6

--- a/solution.py
+++ b/solution.py
@@ -67,8 +67,11 @@
     eighth[...] = average_pairs(block[...], wide)
 
 
-def set_rows(seq_size):
-    rows = 3 * LEAF + 3 * HALF
+NEAR_ROWS = 3 * LEAF + 3 * HALF
+
+
+def far_row_count(seq_size):
+    rows = 0
     for far in range(1, seq_size.bit_length() - 1):
         if seq_size >> far == 2:
             rows += LEAF
@@ -142,11 +145,38 @@
     ]
 
 
-def attend_kernel(seq_size, far_count, queries, own, inner, outer, *rest):
-    far, shares, scratch = rest[:far_count], rest[far_count:-3], rest[-3:]
-    attended, key_set, wide = scratch
+def place(pieces, values, keys):
+    at = 0
+    width = values.shape[1]
+    total_rows = values.shape[0]
+    position = lax.broadcasted_iota(jnp.int32, (1, total_rows), 1)
+    bias = jnp.zeros((1, total_rows), jnp.float32)
+    for rows, value in pieces:
+        count = rows.shape[0]
+        keys[at : at + count] = rows[:, :width]
+        values[at : at + count] = rows[:, width:]
+        if value is not None:
+            bias = jnp.where((position >= at) & (position < at + count), value, bias)
+        at += count
+    return bias
+
+
+def split_heads(rows):
+    first_head = lax.broadcasted_iota(jnp.int32, (1, rows.shape[1]), 1) < HD
+    none = jnp.zeros_like(rows)
+    return jnp.concatenate(
+        [jnp.where(first_head, rows, none), jnp.where(first_head, none, rows)], axis=0
+    )
+
+
+def scores_of(queries, keys):
+    return lax.dot_general(
+        queries, keys[...], (((1,), (1,)), ((), ())), preferred_element_type=jnp.float32
+    )
+
+
+def near_kernel(seq_size, queries, own, inner, outer, scores, values, keys, wide):
     me = lax.axis_index("seq")
-    width = queries.shape[1]
     odd = me & 1
     from_inner, from_outer = inner[...], outer[...]
     before = jnp.where(odd == 1, from_inner, from_outer)
@@ -156,14 +186,6 @@
     near_half_before = average_pairs(edge_before, wide)
     near_half_after = average_pairs(edge_after, wide)
     has_before, has_after = bias_of(me >= 1), bias_of(me + 1 < seq_size)
-    if len(far) == 1:
-        far_pieces = gathered_pieces(seq_size, far[0], wide)
-    else:
-        far_pieces = paired_pieces(*far, wide)
-
-    lane = lax.broadcasted_iota(jnp.int32, (1, width), 1)
-    first_head = lane < HD
-    exponent = math.log2(math.e) / math.sqrt(HD)
     for leaf in range(2):
         if leaf == 0:
             near = [
@@ -181,30 +203,35 @@
                 (near_half_before, has_before),
                 (far_half_after, has_after),
             ]
-        at = 0
-        total_rows = key_set.shape[0]
-        position = lax.broadcasted_iota(jnp.int32, (1, total_rows), 1)
-        bias = jnp.zeros((1, total_rows), jnp.float32)
-        for rows, value in near + far_pieces:
-            count = rows.shape[0]
-            key_set[at : at + count] = rows
-            if value is not None:
-                bias = jnp.where((position >= at) & (position < at + count), value, bias)
-            at += count
-        block_queries = queries[leaf * LEAF : (leaf + 1) * LEAF]
-        none = jnp.zeros_like(block_queries)
-        both = jnp.concatenate(
-            [jnp.where(first_head, block_queries, none), jnp.where(first_head, none, block_queries)], axis=0
+        bias = place(near, values.at[leaf], keys)
+        rows = split_heads(queries[leaf * LEAF : (leaf + 1) * LEAF])
+        scores[leaf] = scores_of(rows, keys) + bias
+
+
+def attend_kernel(seq_size, far_count, queries, near_scores, near_values, *rest):
+    far, shares, scratch = rest[:far_count], rest[far_count:-4], rest[-4:]
+    attended, keys, values, wide = scratch
+    if far_count == 1:
+        pieces = gathered_pieces(seq_size, far[0], wide)
+    else:
+        pieces = paired_pieces(*far, wide)
+    bias = place(pieces, values, keys)
+    first_head = lax.broadcasted_iota(jnp.int32, (1, values.shape[1]), 1) < HD
+    exponent = math.log2(math.e) / math.sqrt(HD)
+    for leaf in range(2):
+        rows = split_heads(queries[leaf * LEAF : (leaf + 1) * LEAF])
+        near = near_scores[leaf]
+        far_scores = scores_of(rows, keys) + bias
+        peak = jnp.maximum(
+            jnp.max(near, axis=1, keepdims=True), jnp.max(far_scores, axis=1, keepdims=True)
         )
-        scores = lax.dot_general(
-            both, key_set[:, :width], (((1,), (1,)), ((), ())), preferred_element_type=jnp.float32
-        )
-        scores = scores + bias
-        peak = jnp.max(scores, axis=1, keepdims=True)
-        weights = jnp.exp2((scores - peak) * exponent)
-        total = jnp.sum(weights, axis=1, keepdims=True)
+        near = jnp.exp2((near - peak) * exponent)
+        far_weights = jnp.exp2((far_scores - peak) * exponent)
+        total = jnp.sum(near, axis=1, keepdims=True) + jnp.sum(far_weights, axis=1, keepdims=True)
         numer = jnp.dot(
-            weights.astype(jnp.bfloat16), key_set[:, width:], preferred_element_type=jnp.float32
+            near.astype(jnp.bfloat16), near_values[leaf], preferred_element_type=jnp.float32
+        ) + jnp.dot(
+            far_weights.astype(jnp.bfloat16), values[...], preferred_element_type=jnp.float32
         )
         mean = numer / total
         attended[leaf * LEAF : (leaf + 1) * LEAF] = jnp.where(
@@ -231,8 +258,11 @@
 HBM = pl.BlockSpec(memory_space=pltpu.HBM)
 
 
-def kernel_call(body, name, megabytes, ins, outs, scratch):
-    shapes = tuple(jax.ShapeDtypeStruct(shape, jnp.bfloat16) for shape in outs)
+def kernel_call(body, name, megabytes, ins, outs, scratch, flops=0):
+    shapes = tuple(
+        out if isinstance(out, jax.ShapeDtypeStruct) else jax.ShapeDtypeStruct(out, jnp.bfloat16)
+        for out in outs
+    )
     return pl.pallas_call(
         body,
         out_shape=shapes,
@@ -240,6 +270,7 @@
         out_specs=(VMEM,) * len(outs),
         scratch_shapes=scratch,
         compiler_params=pltpu.CompilerParams(vmem_limit_bytes=megabytes << 20),
+        cost_estimate=pl.CostEstimate(flops=flops, bytes_accessed=1 << 20, transcendentals=0),
         name=name,
     )
 
@@ -286,18 +317,33 @@
     else:
         far = (lax.all_to_all(quarter, "seq", split_axis=0, concat_axis=0),)
     share = tokens // head_size
+    near_scores, near_values = kernel_call(
+        functools.partial(near_kernel, seq_size),
+        "near",
+        16,
+        [VMEM] * 4,
+        [
+            jax.ShapeDtypeStruct((2, 2 * LEAF, NEAR_ROWS), jnp.float32),
+            (2, NEAR_ROWS, width),
+        ],
+        [pltpu.VMEM((NEAR_ROWS, width), jnp.bfloat16), wide],
+        flops=8 * LEAF * NEAR_ROWS * width,
+    )(own_queries, own, inner, outer)
+    far_rows = far_row_count(seq_size)
     shares = kernel_call(
         functools.partial(attend_kernel, seq_size, len(far)),
         "attend",
         24,
-        [VMEM] * (4 + len(far)),
+        [VMEM] * (3 + len(far)),
         [(share, width)] * head_size,
         [
             pltpu.VMEM((tokens, width), jnp.bfloat16),
-            pltpu.VMEM((set_rows(seq_size), pair_width), jnp.bfloat16),
+            pltpu.VMEM((far_rows, width), jnp.bfloat16),
+            pltpu.VMEM((far_rows, width), jnp.bfloat16),
             wide,
         ],
-    )(own_queries, own, inner, outer, *far)
+        flops=16 * LEAF * (NEAR_ROWS + far_rows) * width,
+    )(own_queries, near_scores, near_values, *far)
     parts = [swap(shares[step], step, "head") for step in range(head_size - 1, 0, -1)]
     (mixed,) = kernel_call(
         project_kernel, "project", 8, [VMEM] * (head_size + 1), [(share, out_weight.shape[1])], []

time: 21.9 us -> 21.7 us (level)
  waiting for transfers between devices: 8.27 us -> 7.85 us
  Pallas kernels: 3.17 us -> 3.41 us
    ppermute x7, waiting for transfers between devices: 8.26 us -> 7.84 us  [swap(): lax.ppermute(array, axis, [(i, i ^ bit) for i in range(lax.axis_size(axis...]
    pallas_call x0 -> x1, Pallas kernels: none -> 0.42 us  [shards(): kernel_call(functools.partial(near_kernel, seq_size), 'near', 16, [VMEM]...]
  transfers between devices with their start and end apart: 8 -> 8, of which waited for: 4 -> 4; matrix products, arithmetic and copies ran while one was open for 0% -> 0% of each run, Pallas kernels for 0% -> 2%
where the time goes in v8:
time: 21.7 us; the launch traced here: 21.5 us
  starting transfers between devices  10.2 us (47%)
  waiting for transfers between devices  7.85 us (36%)
  Pallas kernels  3.41 us (16%)
    ppermute x7, starting transfers between devices, swap(): lax.ppermute(array, axis, [(i, i ^ bit) for i in range(lax.axis_size(axis...  9.56 us
    ppermute x7, waiting for transfers between devices, swap(): lax.ppermute(array, axis, [(i, i ^ bit) for i in range(lax.axis_size(axis...  7.84 us
    pallas_call x1, Pallas kernels, shards(): kernel_call(functools.partial(pack_kernel, not paired), 'pack', 16, [HBM]...  1.05 us
    pallas_call x1, Pallas kernels, shards(): kernel_call(functools.partial(attend_kernel, seq_size, len(far)), 'attend...  1.02 us
    pallas_call x1, Pallas kernels, shards(): kernel_call(project_kernel, 'project', 8, [VMEM] * (head_size + 1), [(sha...  0.85 us
    ppermute x1, starting transfers between devices, shards(): outer = lax.ppermute(outer, 'seq', others)  0.65 us
  transfers between devices with their start and end apart: 8, of which 4 were waited for; matrix products, arithmetic and copies ran while one was open for 0% of the time, Pallas kernels for 2%

profile of v8, /device:TPU:0, one launch (start us, length us, event | category | flops | bytes accessed | tf_op | source)
XLA Modules:
  0.0 21.5 jit_solution(6355021556530827344)
XLA Ops:
  0.0 0.0 copy-start
  0.0 1.1 %pack.1 = (bf16[256,128]{1,0:T(8,128)(2,1)S(1)}, bf16[256,256]{1,0:T(8,128)(2,1)S(1)}, bf16[192,256]{1,0:T(8,128)(2,1)S(1)}, bf16[192,256]{1,0:T(8,128)(2,1)S(1)}, bf16[64,256]{1,0:T(8,128)(2,1)S(1)}) custom-call(bf16[256,128]{1,0:T(8,128)(2,1)} %queries.1, bf16[256,128]{1,0:T(8,128)(2,1)} %keys.1, bf16[256,128]{1,0:T(8,128)(2,1)} %values.1), custom_call_target="tpu_custom_call" | custom-call | bytes 1048576 | tf_op jit(solution)/shard_map/pack/pallas_call | solution.py:290
  1.1 3.0 %collective-permute-start = (bf16[192,256]{1,0:T(8,128)(2,1)S(1)}, bf16[192,256]{1,0:T(8,128)(2,1)S(1)}, u32[]{:S(2)}, u32[]{:S(2)}) collective-permute-start(bf16[192,256]{1,0:T(8,128)(2,1)S(1)} %get-tuple-element.20), channel_id=1, source_target_pairs={{0,4},{4,0},{8,12},{12,8},{16,20},{20,16},{24,28},{28,24},{1,5},{5... | collective-permute-start | bytes 294920 | tf_op jit(solution)/shard_map/ppermute | solution.py:288
  4.1 0.7 %collective-permute-start.1 = (bf16[192,256]{1,0:T(8,128)(2,1)S(1)}, bf16[192,256]{1,0:T(8,128)(2,1)S(1)}, u32[]{:S(2)}, u32[]{:S(2)}) collective-permute-start(bf16[192,256]{1,0:T(8,128)(2,1)S(1)} %get-tuple-element.21), channel_id=1, source_target_pairs={{4,8},{8,4},{12,16},{16,12},{20,24},{24,20},{5,9},{9,5},{13,17},{1... | collective-permute-start | bytes 294920 | tf_op jit(solution)/shard_map/ppermute | solution.py:306
  4.7 2.1 %collective-permute-done.inner = bf16[192,256]{1,0:T(8,128)(2,1)S(1)} collective-permute-done((bf16[192,256]{1,0:T(8,128)(2,1)S(1)}, bf16[192,256]{1,0:T(8,128)(2,1)S(1)}, u32[]{:S(2)}, u32[]{:S(2)}) %collective-permute-start) | collective-permute-done | bytes 98336 | tf_op jit(solution)/shard_map/ppermute | solution.py:288
  6.9 0.1 join.1
  6.9 4.0 %collective-permute-start.2 = (bf16[128,256]{1,0:T(8,128)(2,1)S(1)}, bf16[128,256]{1,0:T(8,128)(2,1)S(1)}, u32[]{:S(2)}, u32[]{:S(2)}) collective-permute-start(bf16[128,256]{1,0:T(8,128)(2,1)S(1)} %get-tuple-element.25), channel_id=1, source_target_pairs={{0,24},{4,28},{8,16},{12,20},{16,8},{20,12},{24,0},{28,4},{1,25},{... | collective-permute-start | bytes 196616 | tf_op jit(solution)/shard_map/ppermute | solution.py:288
  10.9 0.0 collective-permute-start.3
  10.9 0.6 %collective-permute-start.4 = (bf16[64,256]{1,0:T(8,128)(2,1)S(1)}, bf16[64,256]{1,0:T(8,128)(2,1)S(1)}, u32[]{:S(2)}, u32[]{:S(2)}) collective-permute-start(bf16[64,256]{1,0:T(8,128)(2,1)S(1)} %get-tuple-element.26), channel_id=1, source_target_pairs={{0,16},{4,20},{8,24},{12,28},{16,0},{20,4},{24,8},{28,12},{1,17},{... | collective-permute-start | bytes 98312 | tf_op jit(solution)/shard_map/ppermute | solution.py:288
  11.6 0.0 collective-permute-done.1.outer
  11.6 0.4 %near.1 = (f32[2,256,576]{2,1,0:T(8,128)S(1)}, bf16[2,576,128]{2,1,0:T(8,128)(2,1)S(1)}) custom-call(bf16[256,128]{1,0:T(8,128)(2,1)S(1)} %get-tuple-element.18.queries, bf16[256,256]{1,0:T(8,128)(2,1)S(1)} %get-tuple-element.19.own, bf16[192,256]{1,0:T(8,128)(2,1)S(1)} %collective-permute-done.inner, bf16[192,256]{1,0:T(8,128)(2,1)S(1)} %collective-permute-done.1.outer), custom_call_target="tpu_custom_call" | custom-call | flops 75497472 | bytes 1048576 | tf_op jit(solution)/shard_map/near/pallas_call | solution.py:320
  12.0 3.7 %collective-permute-done.4.rest_2_ = bf16[64,256]{1,0:T(8,128)(2,1)S(1)} collective-permute-done((bf16[64,256]{1,0:T(8,128)(2,1)S(1)}, bf16[64,256]{1,0:T(8,128)(2,1)S(1)}, u32[]{:S(2)}, u32[]{:S(2)}) %collective-permute-start.4) | collective-permute-done | bytes 32800 | tf_op jit(solution)/shard_map/ppermute | solution.py:288
  15.7 0.0 collective-permute-done.2.rest_0_
  15.8 0.0 collective-permute-done.3.rest_1_
  15.8 1.0 %attend.1 = (bf16[64,128]{1,0:T(8,128)(2,1)S(1)}, bf16[64,128]{1,0:T(8,128)(2,1)S(1)}, bf16[64,128]{1,0:T(8,128)(2,1)S(1)}, bf16[64,128]{1,0:T(8,128)(2,1)S(1)}) custom-call(bf16[256,128]{1,0:T(8,128)(2,1)S(1)} %get-tuple-element.18.queries, f32[2,256,576]{2,1,0:T(8,128)S(1)} %get-tuple-element.22.near_scores, ...), custom_call_target="tpu_custom_call" | custom-call | flops 234881024 | bytes 1048576 | tf_op jit(solution)/shard_map/attend/pallas_call | solution.py:333
  16.8 0.1 collective-permute-start.5
  16.9 1.6 %collective-permute-start.6 = (bf16[64,128]{1,0:T(8,128)(2,1)S(1)}, bf16[64,128]{1,0:T(8,128)(2,1)S(1)}, u32[]{:S(2)}, u32[]{:S(2)}) collective-permute-start(bf16[64,128]{1,0:T(8,128)(2,1)S(1)} %get-tuple-element.28), channel_id=1, source_target_pairs={{0,2},{1,3},{2,0},{3,1},{4,6},{5,7},{6,4},{7,5},{8,10},{9,11},{10,... | collective-permute-start | bytes 49160 | tf_op jit(solution)/shard_map/ppermute | solution.py:288
  18.4 0.3 %collective-permute-start.7 = (bf16[64,128]{1,0:T(8,128)(2,1)S(1)}, bf16[64,128]{1,0:T(8,128)(2,1)S(1)}, u32[]{:S(2)}, u32[]{:S(2)}) collective-permute-start(bf16[64,128]{1,0:T(8,128)(2,1)S(1)} %get-tuple-element.29), channel_id=1, source_target_pairs={{0,1},{1,0},{2,3},{3,2},{4,5},{5,4},{6,7},{7,6},{8,9},{9,8},{10,11... | collective-permute-start | bytes 49160 | tf_op jit(solution)/shard_map/ppermute | solution.py:288
  18.7 1.4 %collective-permute-done.5.refs_0_ = bf16[64,128]{1,0:T(8,128)(2,1)S(1)} collective-permute-done((bf16[64,128]{1,0:T(8,128)(2,1)S(1)}, bf16[64,128]{1,0:T(8,128)(2,1)S(1)}, u32[]{:S(2)}, u32[]{:S(2)}) %collective-permute-start.5) | collective-permute-done | bytes 16416 | tf_op jit(solution)/shard_map/ppermute | solution.py:288
  20.1 0.6 %collective-permute-done.6.refs_1_ = bf16[64,128]{1,0:T(8,128)(2,1)S(1)} collective-permute-done((bf16[64,128]{1,0:T(8,128)(2,1)S(1)}, bf16[64,128]{1,0:T(8,128)(2,1)S(1)}, u32[]{:S(2)}, u32[]{:S(2)}) %collective-permute-start.6) | collective-permute-done | bytes 16416 | tf_op jit(solution)/shard_map/ppermute | solution.py:288
  20.7 0.0 collective-permute-done.7.refs_2_
  20.7 0.0 copy-done
  20.7 0.9 %project.1 = bf16[64,512]{1,0:T(8,128)(2,1)} custom-call(bf16[64,128]{1,0:T(8,128)(2,1)S(1)} %collective-permute-done.5.refs_0_, bf16[64,128]{1,0:T(8,128)(2,1)S(1)} %collective-permute-done.6.refs_1_, bf16[64,128]{1,0:T(8,128)(2,1)S(1)} %collective-permute-done.7.refs_2_, bf16[64,128]{1,0:T(8,128)(2,1)S(1)} %get-tuple-element.30.refs_3_, ...), custom_call_target="tpu_custom_call" | custom-call | bytes 1048576 | tf_op jit(solution)/shard_map/project/pallas_call | solution.py:348
Async XLA Ops:
  0.0 20.7 %copy-start = (bf16[512,512]{1,0:T(8,128)(2,1)S(1)}, bf16[512,512]{1,0:T(8,128)(2,1)}, u32[]{:S(2)}) copy-start(bf16[512,512]{1,0:T(8,128)(2,1)} %refs_4_.1) | copy-start | bytes 1572868
  1.1 5.8 %collective-permute-start = (bf16[192,256]{1,0:T(8,128)(2,1)S(1)}, bf16[192,256]{1,0:T(8,128)(2,1)S(1)}, u32[]{:S(2)}, u32[]{:S(2)}) collective-permute-start(bf16[192,256]{1,0:T(8,128)(2,1)S(1)} %get-tuple-element.20), channel_id=1, source_target_pairs={{0,4},{4,0},{8,12},{12,8},{16,20},{20,16},{24,28},{28,24},{1,5},{5... | collective-permute-start | bytes 294920 | tf_op jit(solution)/shard_map/ppermute | solution.py:288
  4.1 7.5 %collective-permute-start.1 = (bf16[192,256]{1,0:T(8,128)(2,1)S(1)}, bf16[192,256]{1,0:T(8,128)(2,1)S(1)}, u32[]{:S(2)}, u32[]{:S(2)}) collective-permute-start(bf16[192,256]{1,0:T(8,128)(2,1)S(1)} %get-tuple-element.21), channel_id=1, source_target_pairs={{4,8},{8,4},{12,16},{16,12},{20,24},{24,20},{5,9},{9,5},{13,17},{1... | collective-permute-start | bytes 294920 | tf_op jit(solution)/shard_map/ppermute | solution.py:306
  6.9 8.8 %collective-permute-start.2 = (bf16[128,256]{1,0:T(8,128)(2,1)S(1)}, bf16[128,256]{1,0:T(8,128)(2,1)S(1)}, u32[]{:S(2)}, u32[]{:S(2)}) collective-permute-start(bf16[128,256]{1,0:T(8,128)(2,1)S(1)} %get-tuple-element.25), channel_id=1, source_target_pairs={{0,24},{4,28},{8,16},{12,20},{16,8},{20,12},{24,0},{28,4},{1,25},{... | collective-permute-start | bytes 196616 | tf_op jit(solution)/shard_map/ppermute | solution.py:288
  10.9 4.8 %collective-permute-start.3 = (bf16[128,256]{1,0:T(8,128)(2,1)S(1)}, bf16[128,256]{1,0:T(8,128)(2,1)S(1)}, u32[]{:S(2)}, u32[]{:S(2)}) collective-permute-start(bf16[128,256]{1,0:T(8,128)(2,1)S(1)} %get-tuple-element.25), channel_id=1, source_target_pairs={{0,8},{4,12},{8,0},{12,4},{16,24},{20,28},{24,16},{28,20},{1,9},{5... | collective-permute-start | bytes 196616 | tf_op jit(solution)/shard_map/ppermute | solution.py:288
  10.9 4.8 %collective-permute-start.4 = (bf16[64,256]{1,0:T(8,128)(2,1)S(1)}, bf16[64,256]{1,0:T(8,128)(2,1)S(1)}, u32[]{:S(2)}, u32[]{:S(2)}) collective-permute-start(bf16[64,256]{1,0:T(8,128)(2,1)S(1)} %get-tuple-element.26), channel_id=1, source_target_pairs={{0,16},{4,20},{8,24},{12,28},{16,0},{20,4},{24,8},{28,12},{1,17},{... | collective-permute-start | bytes 98312 | tf_op jit(solution)/shard_map/ppermute | solution.py:288
  16.8 3.3 %collective-permute-start.5 = (bf16[64,128]{1,0:T(8,128)(2,1)S(1)}, bf16[64,128]{1,0:T(8,128)(2,1)S(1)}, u32[]{:S(2)}, u32[]{:S(2)}) collective-permute-start(bf16[64,128]{1,0:T(8,128)(2,1)S(1)} %get-tuple-element.27), channel_id=1, source_target_pairs={{0,3},{1,2},{2,1},{3,0},{4,7},{5,6},{6,5},{7,4},{8,11},{9,10},{10,... | collective-permute-start | bytes 49160 | tf_op jit(solution)/shard_map/ppermute | solution.py:288
  16.9 3.8 %collective-permute-start.6 = (bf16[64,128]{1,0:T(8,128)(2,1)S(1)}, bf16[64,128]{1,0:T(8,128)(2,1)S(1)}, u32[]{:S(2)}, u32[]{:S(2)}) collective-permute-start(bf16[64,128]{1,0:T(8,128)(2,1)S(1)} %get-tuple-element.28), channel_id=1, source_target_pairs={{0,2},{1,3},{2,0},{3,1},{4,6},{5,7},{6,4},{7,5},{8,10},{9,11},{10,... | collective-permute-start | bytes 49160 | tf_op jit(solution)/shard_map/ppermute | solution.py:288
  18.4 2.2 %collective-permute-start.7 = (bf16[64,128]{1,0:T(8,128)(2,1)S(1)}, bf16[64,128]{1,0:T(8,128)(2,1)S(1)}, u32[]{:S(2)}, u32[]{:S(2)}) collective-permute-start(bf16[64,128]{1,0:T(8,128)(2,1)S(1)} %get-tuple-element.29), channel_id=1, source_target_pairs={{0,1},{1,0},{2,3},{3,2},{4,5},{5,4},{6,7},{7,6},{8,9},{9,8},{10,11... | collective-permute-start | bytes 49160 | tf_op jit(solution)/shard_map/ppermute | solution.py:288

commit v9 on v8

--- a/solution.py
+++ b/solution.py
@@ -67,11 +67,12 @@
     eighth[...] = average_pairs(block[...], wide)
 
 
-NEAR_ROWS = 3 * LEAF + 3 * HALF
+NEAR_ROWS = 4 * LEAF
+PAD = 16
 
 
 def far_row_count(seq_size):
-    rows = 0
+    rows = HALF
     for far in range(1, seq_size.bit_length() - 1):
         if seq_size >> far == 2:
             rows += LEAF
@@ -175,14 +176,15 @@
     )
 
 
-def near_kernel(seq_size, queries, own, inner, outer, scores, values, keys, wide):
+def near_kernel(seq_size, queries, own, inner, outer, scores, values, shared, keys, wide):
     me = lax.axis_index("seq")
     odd = me & 1
     from_inner, from_outer = inner[...], outer[...]
     before = jnp.where(odd == 1, from_inner, from_outer)
     after = jnp.where(odd == 1, from_outer, from_inner)
     edge_before, edge_after = before[:LEAF], after[:LEAF]
-    far_half_before, far_half_after = before[LEAF:], after[LEAF:]
+    far_half_after = after[LEAF:]
+    shared[...] = before[LEAF:]
     near_half_before = average_pairs(edge_before, wide)
     near_half_after = average_pairs(edge_after, wide)
     has_before, has_after = bias_of(me >= 1), bias_of(me + 1 < seq_size)
@@ -191,7 +193,6 @@
             near = [
                 (edge_before, has_before),
                 (own[...], None),
-                (far_half_before, has_before),
                 (near_half_after, has_after),
                 (far_half_after, has_after),
             ]
@@ -199,7 +200,6 @@
             near = [
                 (own[...], None),
                 (edge_after, has_after),
-                (far_half_before, has_before),
                 (near_half_before, has_before),
                 (far_half_after, has_after),
             ]
@@ -208,39 +208,45 @@
         scores[leaf] = scores_of(rows, keys) + bias
 
 
-def attend_kernel(seq_size, far_count, queries, near_scores, near_values, *rest):
-    far, shares, scratch = rest[:far_count], rest[far_count:-4], rest[-4:]
-    attended, keys, values, wide = scratch
-    if far_count == 1:
+def attend_leaf(leaf, queries, near_scores, near_values, keys, values, bias, same, other):
+    first_head = lax.broadcasted_iota(jnp.int32, (1, values.shape[1]), 1) < HD
+    exponent = math.log2(math.e) / math.sqrt(HD)
+    rows = split_heads(queries[pl.ds(pl.multiple_of(leaf * LEAF, LEAF), LEAF)])
+    near = near_scores[leaf]
+    far_scores = scores_of(rows, keys) + bias
+    peak = jnp.maximum(
+        jnp.max(near, axis=1, keepdims=True), jnp.max(far_scores, axis=1, keepdims=True)
+    )
+    near = jnp.exp2((near - peak) * exponent)
+    far_weights = jnp.exp2((far_scores - peak) * exponent)
+    total = jnp.sum(near, axis=1, keepdims=True) + jnp.sum(far_weights, axis=1, keepdims=True)
+    numer = jnp.dot(
+        near.astype(jnp.bfloat16), near_values[leaf], preferred_element_type=jnp.float32
+    ) + jnp.dot(far_weights.astype(jnp.bfloat16), values[...], preferred_element_type=jnp.float32)
+    mean = numer / total
+    attended = jnp.where(first_head, mean[:LEAF], mean[LEAF:]).astype(jnp.bfloat16)
+    second = (lax.axis_index("head") & 1) == 1
+    same[:HALF] = jnp.where(second, attended[HALF:], attended[:HALF])
+    other[:HALF] = jnp.where(second, attended[:HALF], attended[HALF:])
+
+
+def leaves_kernel(seq_size, queries, near_scores, near_values, shared, *rest):
+    *far, same, other, keys, values, bias, wide = rest
+    if len(far) == 1:
         pieces = gathered_pieces(seq_size, far[0], wide)
     else:
         pieces = paired_pieces(*far, wide)
-    bias = place(pieces, values, keys)
-    first_head = lax.broadcasted_iota(jnp.int32, (1, values.shape[1]), 1) < HD
-    exponent = math.log2(math.e) / math.sqrt(HD)
-    for leaf in range(2):
-        rows = split_heads(queries[leaf * LEAF : (leaf + 1) * LEAF])
-        near = near_scores[leaf]
-        far_scores = scores_of(rows, keys) + bias
-        peak = jnp.maximum(
-            jnp.max(near, axis=1, keepdims=True), jnp.max(far_scores, axis=1, keepdims=True)
-        )
-        near = jnp.exp2((near - peak) * exponent)
-        far_weights = jnp.exp2((far_scores - peak) * exponent)
-        total = jnp.sum(near, axis=1, keepdims=True) + jnp.sum(far_weights, axis=1, keepdims=True)
-        numer = jnp.dot(
-            near.astype(jnp.bfloat16), near_values[leaf], preferred_element_type=jnp.float32
-        ) + jnp.dot(
-            far_weights.astype(jnp.bfloat16), values[...], preferred_element_type=jnp.float32
-        )
-        mean = numer / total
-        attended[leaf * LEAF : (leaf + 1) * LEAF] = jnp.where(
-            first_head, mean[:LEAF], mean[LEAF:]
-        ).astype(jnp.bfloat16)
-    mine = lax.axis_index("head")
-    for step, share in enumerate(shares):
-        count = share.shape[0]
-        share[...] = attended[pl.ds(pl.multiple_of((mine ^ step) * count, count), count)]
+    shared_bias = bias_of(lax.axis_index("seq") >= 1)
+    bias[...] = jnp.broadcast_to(place([(shared, shared_bias)] + pieces, values, keys), bias.shape)
+    leaf = (lax.axis_index("head") >> 1) ^ 1
+    attend_leaf(leaf, queries, near_scores, near_values, keys, values, bias[:1], same, other)
+    for share in (same, other):
+        share[HALF:] = jnp.zeros((PAD, share.shape[1]), share.dtype)
+
+
+def stays_kernel(queries, near_scores, near_values, keys, values, bias, same, other):
+    leaf = lax.axis_index("head") >> 1
+    attend_leaf(leaf, queries, near_scores, near_values, keys, values, bias[:1], same, other)
 
 
 def project_kernel(*refs):
@@ -250,7 +256,7 @@
     for step, part in enumerate(reversed(parts)):
         width = part.shape[1]
         columns = pl.ds(pl.multiple_of((mine ^ step) * width, width), width)
-        total += jnp.dot(part[...], weight[columns], preferred_element_type=jnp.float32)
+        total += jnp.dot(part[: mixed.shape[0]], weight[columns], preferred_element_type=jnp.float32)
     mixed[...] = total.astype(mixed.dtype)
 
 
@@ -317,7 +323,7 @@
     else:
         far = (lax.all_to_all(quarter, "seq", split_axis=0, concat_axis=0),)
     share = tokens // head_size
-    near_scores, near_values = kernel_call(
+    near_scores, near_values, shared = kernel_call(
         functools.partial(near_kernel, seq_size),
         "near",
         16,
@@ -325,29 +331,36 @@
         [
             jax.ShapeDtypeStruct((2, 2 * LEAF, NEAR_ROWS), jnp.float32),
             (2, NEAR_ROWS, width),
+            (HALF, pair_width),
         ],
         [pltpu.VMEM((NEAR_ROWS, width), jnp.bfloat16), wide],
         flops=8 * LEAF * NEAR_ROWS * width,
     )(own_queries, own, inner, outer)
     far_rows = far_row_count(seq_size)
-    shares = kernel_call(
-        functools.partial(attend_kernel, seq_size, len(far)),
-        "attend",
+
+    leaf_flops = 8 * LEAF * (NEAR_ROWS + far_rows) * width
+    share_2, share_3, far_keys, far_values, far_bias = kernel_call(
+        functools.partial(leaves_kernel, seq_size),
+        "leaves",
         24,
-        [VMEM] * (3 + len(far)),
-        [(share, width)] * head_size,
+        [VMEM] * (4 + len(far)),
         [
-            pltpu.VMEM((tokens, width), jnp.bfloat16),
-            pltpu.VMEM((far_rows, width), jnp.bfloat16),
-            pltpu.VMEM((far_rows, width), jnp.bfloat16),
-            wide,
+            (share + PAD, width),
+            (share + PAD, width),
+            (far_rows, width),
+            (far_rows, width),
+            jax.ShapeDtypeStruct((8, far_rows), jnp.float32),
         ],
-        flops=16 * LEAF * (NEAR_ROWS + far_rows) * width,
-    )(own_queries, near_scores, near_values, *far)
-    parts = [swap(shares[step], step, "head") for step in range(head_size - 1, 0, -1)]
+        [wide],
+        flops=leaf_flops,
+    )(own_queries, near_scores, near_values, shared, *far)
+    share_0, share_1 = kernel_call(
+        stays_kernel, "stays", 16, [VMEM] * 6, [(share, width)] * 2, [], flops=leaf_flops
+    )(own_queries, near_scores, near_values, far_keys, far_values, far_bias)
+    parts = [swap(share_3, 3, "head"), swap(share_2, 2, "head"), swap(share_1, 1, "head"), share_0]
     (mixed,) = kernel_call(
         project_kernel, "project", 8, [VMEM] * (head_size + 1), [(share, out_weight.shape[1])], []
-    )(*parts, shares[0], out_weight)
+    )(*parts, out_weight)
     return mixed
 
 

time: 21.7 us -> 21.2 us (0.977)
  waiting for transfers between devices: 7.85 us -> 7.28 us
    ppermute x7, waiting for transfers between devices: 7.84 us -> 7.28 us  [swap(): lax.ppermute(array, axis, [(i, i ^ bit) for i in range(lax.axis_size(axis...]
    pallas_call x1 -> x2, Pallas kernels: 1.02 us -> 1.16 us  [the longest x1 0.59 us: shards(): kernel_call(functools.partial(leaves_kernel, seq_size), 'leaves', 24, [VM...]
  transfers between devices with their start and end apart: 8 -> 8, of which waited for: 4 -> 4; matrix products, arithmetic and copies ran while one was open for 0% -> 0% of each run, Pallas kernels for 2% -> 5%
where the time goes in v9:
time: 21.2 us; the launch traced here: 21.1 us
  starting transfers between devices  10.3 us (49%)
  waiting for transfers between devices  7.28 us (34%)
  Pallas kernels  3.46 us (16%)
    ppermute x7, starting transfers between devices, swap(): lax.ppermute(array, axis, [(i, i ^ bit) for i in range(lax.axis_size(axis...  9.62 us
    ppermute x7, waiting for transfers between devices, swap(): lax.ppermute(array, axis, [(i, i ^ bit) for i in range(lax.axis_size(axis...  7.28 us
    pallas_call x1, Pallas kernels, shards(): kernel_call(functools.partial(pack_kernel, not paired), 'pack', 16, [HBM]...  0.99 us
    pallas_call x1, Pallas kernels, shards(): kernel_call(project_kernel, 'project', 8, [VMEM] * (head_size + 1), [(sha...  0.85 us
    ppermute x1, starting transfers between devices, shards(): outer = lax.ppermute(outer, 'seq', others)  0.65 us
    pallas_call x1, Pallas kernels, shards(): kernel_call(functools.partial(leaves_kernel, seq_size), 'leaves', 24, [VM...  0.59 us
    pallas_call x1, Pallas kernels, shards(): kernel_call(stays_kernel, 'stays', 16, [VMEM] * 6, [(share, width)] * 2,...  0.57 us
  transfers between devices with their start and end apart: 8, of which 4 were waited for; matrix products, arithmetic and copies ran while one was open for 0% of the time, Pallas kernels for 5%

profile of v9, /device:TPU:0, one launch (start us, length us, event | category | flops | bytes accessed | tf_op | source)
XLA Modules:
  0.0 21.1 jit_solution(8176463685559203296)
XLA Ops:
  0.0 1.0 %pack.1 = (bf16[256,128]{1,0:T(8,128)(2,1)S(1)}, bf16[256,256]{1,0:T(8,128)(2,1)S(1)}, bf16[192,256]{1,0:T(8,128)(2,1)S(1)}, bf16[192,256]{1,0:T(8,128)(2,1)S(1)}, bf16[64,256]{1,0:T(8,128)(2,1)S(1)}) custom-call(bf16[256,128]{1,0:T(8,128)(2,1)} %queries.1, bf16[256,128]{1,0:T(8,128)(2,1)} %keys.1, bf16[256,128]{1,0:T(8,128)(2,1)} %values.1), custom_call_target="tpu_custom_call" | custom-call | bytes 1048576 | tf_op jit(solution)/shard_map/pack/pallas_call | solution.py:296
  1.0 3.0 %collective-permute-start = (bf16[192,256]{1,0:T(8,128)(2,1)S(1)}, bf16[192,256]{1,0:T(8,128)(2,1)S(1)}, u32[]{:S(2)}, u32[]{:S(2)}) collective-permute-start(bf16[192,256]{1,0:T(8,128)(2,1)S(1)} %get-tuple-element.24), channel_id=1, source_target_pairs={{0,4},{4,0},{8,12},{12,8},{16,20},{20,16},{24,28},{28,24},{1,5},{5... | collective-permute-start | bytes 294920 | tf_op jit(solution)/shard_map/ppermute | solution.py:294
  4.0 0.7 %collective-permute-start.1 = (bf16[192,256]{1,0:T(8,128)(2,1)S(1)}, bf16[192,256]{1,0:T(8,128)(2,1)S(1)}, u32[]{:S(2)}, u32[]{:S(2)}) collective-permute-start(bf16[192,256]{1,0:T(8,128)(2,1)S(1)} %get-tuple-element.25), channel_id=1, source_target_pairs={{4,8},{8,4},{12,16},{16,12},{20,24},{24,20},{5,9},{9,5},{13,17},{1... | collective-permute-start | bytes 294920 | tf_op jit(solution)/shard_map/ppermute | solution.py:312
  4.7 2.1 %collective-permute-done.inner = bf16[192,256]{1,0:T(8,128)(2,1)S(1)} collective-permute-done((bf16[192,256]{1,0:T(8,128)(2,1)S(1)}, bf16[192,256]{1,0:T(8,128)(2,1)S(1)}, u32[]{:S(2)}, u32[]{:S(2)}) %collective-permute-start) | collective-permute-done | bytes 98336 | tf_op jit(solution)/shard_map/ppermute | solution.py:294
  6.8 0.1 join.1
  6.9 4.0 %collective-permute-start.2 = (bf16[128,256]{1,0:T(8,128)(2,1)S(1)}, bf16[128,256]{1,0:T(8,128)(2,1)S(1)}, u32[]{:S(2)}, u32[]{:S(2)}) collective-permute-start(bf16[128,256]{1,0:T(8,128)(2,1)S(1)} %get-tuple-element.30), channel_id=1, source_target_pairs={{0,24},{4,28},{8,16},{12,20},{16,8},{20,12},{24,0},{28,4},{1,25},{... | collective-permute-start | bytes 196616 | tf_op jit(solution)/shard_map/ppermute | solution.py:294
  10.9 0.0 collective-permute-start.3
  10.9 0.6 %collective-permute-start.4 = (bf16[64,256]{1,0:T(8,128)(2,1)S(1)}, bf16[64,256]{1,0:T(8,128)(2,1)S(1)}, u32[]{:S(2)}, u32[]{:S(2)}) collective-permute-start(bf16[64,256]{1,0:T(8,128)(2,1)S(1)} %get-tuple-element.31), channel_id=1, source_target_pairs={{0,16},{4,20},{8,24},{12,28},{16,0},{20,4},{24,8},{28,12},{1,17},{... | collective-permute-start | bytes 98312 | tf_op jit(solution)/shard_map/ppermute | solution.py:294
  11.5 0.0 collective-permute-done.1.outer
  11.5 0.4 %near.1 = (f32[2,256,512]{2,1,0:T(8,128)S(1)}, bf16[2,512,128]{2,1,0:T(8,128)(2,1)S(1)}, bf16[64,256]{1,0:T(8,128)(2,1)S(1)}) custom-call(bf16[256,128]{1,0:T(8,128)(2,1)S(1)} %get-tuple-element.22.queries, bf16[256,256]{1,0:T(8,128)(2,1)S(1)} %get-tuple-element.23.own, bf16[192,256]{1,0:T(8,128)(2,1)S(1)} %collective-permute-done.inner, ...), custom_call_target="tpu_custom_call" | custom-call | flops 67108864 | bytes 1048576 | tf_op jit(solution)/shard_map/near/pallas_call | solution.py:326
  11.9 3.8 %collective-permute-done.4.rest_2_ = bf16[64,256]{1,0:T(8,128)(2,1)S(1)} collective-permute-done((bf16[64,256]{1,0:T(8,128)(2,1)S(1)}, bf16[64,256]{1,0:T(8,128)(2,1)S(1)}, u32[]{:S(2)}, u32[]{:S(2)}) %collective-permute-start.4) | collective-permute-done | bytes 32800 | tf_op jit(solution)/shard_map/ppermute | solution.py:294
  15.7 0.0 collective-permute-done.2.rest_0_
  15.7 0.0 collective-permute-done.3.rest_1_
  15.7 0.6 %leaves.1 = (bf16[80,128]{1,0:T(8,128)(2,1)S(1)}, bf16[80,128]{1,0:T(8,128)(2,1)S(1)}, bf16[384,128]{1,0:T(8,128)(2,1)S(1)}, bf16[384,128]{1,0:T(8,128)(2,1)S(1)}, f32[8,384]{1,0:T(8,128)S(1)}) custom-call(bf16[256,128]{1,0:T(8,128)(2,1)S(1)} %get-tuple-element.22.queries, f32[2,256,512]{2,1,0:T(8,128)S(1)} %get-tuple-element.26.near_scores, ...), custom_call_target="tpu_custom_call" | custom-call | flops 117440512 | bytes 1048576 | tf_op jit(solution)/shard_map/leaves/pallas_call | solution.py:342
  16.3 0.1 collective-permute-start.5
  16.4 1.6 %collective-permute-start.6 = (bf16[80,128]{1,0:T(8,128)(2,1)S(1)}, bf16[80,128]{1,0:T(8,128)(2,1)S(1)}, u32[]{:S(2)}, u32[]{:S(2)}) collective-permute-start(bf16[80,128]{1,0:T(8,128)(2,1)S(1)} %get-tuple-element.33), channel_id=1, source_target_pairs={{0,2},{1,3},{2,0},{3,1},{4,6},{5,7},{6,4},{7,5},{8,10},{9,11},{10,... | collective-permute-start | bytes 61448 | tf_op jit(solution)/shard_map/ppermute | solution.py:294
  18.0 0.0 copy-start
  18.0 0.6 %stays.1 = (bf16[64,128]{1,0:T(8,128)(2,1)S(1)}, bf16[64,128]{1,0:T(8,128)(2,1)S(1)}) custom-call(bf16[256,128]{1,0:T(8,128)(2,1)S(1)} %get-tuple-element.22.queries, f32[2,256,512]{2,1,0:T(8,128)S(1)} %get-tuple-element.26.near_scores, bf16[2,512,128]{2,1,0:T(8,128)(2,1)S(1)} %get-tuple-element.27.near_values, bf16[384,128]{1,0:T(8,128)(2,1)S(1)} %get-tuple-element.34.keys, ...), custom_call_target="tpu_custom_call" | custom-call | flops 117440512 | bytes 1048576 | tf_op jit(solution)/shard_map/stays/pallas_call | solution.py:357
  18.5 0.3 %collective-permute-start.7 = (bf16[64,128]{1,0:T(8,128)(2,1)S(1)}, bf16[64,128]{1,0:T(8,128)(2,1)S(1)}, u32[]{:S(2)}, u32[]{:S(2)}) collective-permute-start(bf16[64,128]{1,0:T(8,128)(2,1)S(1)} %get-tuple-element.37), channel_id=1, source_target_pairs={{0,1},{1,0},{2,3},{3,2},{4,5},{5,4},{6,7},{7,6},{8,9},{9,8},{10,11... | collective-permute-start | bytes 49160 | tf_op jit(solution)/shard_map/ppermute | solution.py:294
  18.9 0.9 %collective-permute-done.7.refs_2_ = bf16[64,128]{1,0:T(8,128)(2,1)S(1)} collective-permute-done((bf16[64,128]{1,0:T(8,128)(2,1)S(1)}, bf16[64,128]{1,0:T(8,128)(2,1)S(1)}, u32[]{:S(2)}, u32[]{:S(2)}) %collective-permute-start.7) | collective-permute-done | bytes 16416 | tf_op jit(solution)/shard_map/ppermute | solution.py:294
  19.8 0.0 collective-permute-done.5.refs_0_
  19.8 0.4 %collective-permute-done.6.refs_1_ = bf16[80,128]{1,0:T(8,128)(2,1)S(1)} collective-permute-done((bf16[80,128]{1,0:T(8,128)(2,1)S(1)}, bf16[80,128]{1,0:T(8,128)(2,1)S(1)}, u32[]{:S(2)}, u32[]{:S(2)}) %collective-permute-start.6) | collective-permute-done | bytes 20512 | tf_op jit(solution)/shard_map/ppermute | solution.py:294
  20.2 0.0 copy-done
  20.2 0.9 %project.1 = bf16[64,512]{1,0:T(8,128)(2,1)} custom-call(bf16[80,128]{1,0:T(8,128)(2,1)S(1)} %collective-permute-done.5.refs_0_, bf16[80,128]{1,0:T(8,128)(2,1)S(1)} %collective-permute-done.6.refs_1_, bf16[64,128]{1,0:T(8,128)(2,1)S(1)} %collective-permute-done.7.refs_2_, bf16[64,128]{1,0:T(8,128)(2,1)S(1)} %get-tuple-element.38.refs_3_, ...), custom_call_target="tpu_custom_call" | custom-call | bytes 1048576 | tf_op jit(solution)/shard_map/project/pallas_call | solution.py:361
Async XLA Ops:
  1.0 5.8 %collective-permute-start = (bf16[192,256]{1,0:T(8,128)(2,1)S(1)}, bf16[192,256]{1,0:T(8,128)(2,1)S(1)}, u32[]{:S(2)}, u32[]{:S(2)}) collective-permute-start(bf16[192,256]{1,0:T(8,128)(2,1)S(1)} %get-tuple-element.24), channel_id=1, source_target_pairs={{0,4},{4,0},{8,12},{12,8},{16,20},{20,16},{24,28},{28,24},{1,5},{5... | collective-permute-start | bytes 294920 | tf_op jit(solution)/shard_map/ppermute | solution.py:294
  4.0 7.5 %collective-permute-start.1 = (bf16[192,256]{1,0:T(8,128)(2,1)S(1)}, bf16[192,256]{1,0:T(8,128)(2,1)S(1)}, u32[]{:S(2)}, u32[]{:S(2)}) collective-permute-start(bf16[192,256]{1,0:T(8,128)(2,1)S(1)} %get-tuple-element.25), channel_id=1, source_target_pairs={{4,8},{8,4},{12,16},{16,12},{20,24},{24,20},{5,9},{9,5},{13,17},{1... | collective-permute-start | bytes 294920 | tf_op jit(solution)/shard_map/ppermute | solution.py:312
  6.9 8.8 %collective-permute-start.2 = (bf16[128,256]{1,0:T(8,128)(2,1)S(1)}, bf16[128,256]{1,0:T(8,128)(2,1)S(1)}, u32[]{:S(2)}, u32[]{:S(2)}) collective-permute-start(bf16[128,256]{1,0:T(8,128)(2,1)S(1)} %get-tuple-element.30), channel_id=1, source_target_pairs={{0,24},{4,28},{8,16},{12,20},{16,8},{20,12},{24,0},{28,4},{1,25},{... | collective-permute-start | bytes 196616 | tf_op jit(solution)/shard_map/ppermute | solution.py:294
  10.9 4.8 %collective-permute-start.3 = (bf16[128,256]{1,0:T(8,128)(2,1)S(1)}, bf16[128,256]{1,0:T(8,128)(2,1)S(1)}, u32[]{:S(2)}, u32[]{:S(2)}) collective-permute-start(bf16[128,256]{1,0:T(8,128)(2,1)S(1)} %get-tuple-element.30), channel_id=1, source_target_pairs={{0,8},{4,12},{8,0},{12,4},{16,24},{20,28},{24,16},{28,20},{1,9},{5... | collective-permute-start | bytes 196616 | tf_op jit(solution)/shard_map/ppermute | solution.py:294
  10.9 4.8 %collective-permute-start.4 = (bf16[64,256]{1,0:T(8,128)(2,1)S(1)}, bf16[64,256]{1,0:T(8,128)(2,1)S(1)}, u32[]{:S(2)}, u32[]{:S(2)}) collective-permute-start(bf16[64,256]{1,0:T(8,128)(2,1)S(1)} %get-tuple-element.31), channel_id=1, source_target_pairs={{0,16},{4,20},{8,24},{12,28},{16,0},{20,4},{24,8},{28,12},{1,17},{... | collective-permute-start | bytes 98312 | tf_op jit(solution)/shard_map/ppermute | solution.py:294
  16.3 3.5 %collective-permute-start.5 = (bf16[80,128]{1,0:T(8,128)(2,1)S(1)}, bf16[80,128]{1,0:T(8,128)(2,1)S(1)}, u32[]{:S(2)}, u32[]{:S(2)}) collective-permute-start(bf16[80,128]{1,0:T(8,128)(2,1)S(1)} %get-tuple-element.32), channel_id=1, source_target_pairs={{0,3},{1,2},{2,1},{3,0},{4,7},{5,6},{6,5},{7,4},{8,11},{9,10},{10,... | collective-permute-start | bytes 61448 | tf_op jit(solution)/shard_map/ppermute | solution.py:294
  16.4 3.8 %collective-permute-start.6 = (bf16[80,128]{1,0:T(8,128)(2,1)S(1)}, bf16[80,128]{1,0:T(8,128)(2,1)S(1)}, u32[]{:S(2)}, u32[]{:S(2)}) collective-permute-start(bf16[80,128]{1,0:T(8,128)(2,1)S(1)} %get-tuple-element.33), channel_id=1, source_target_pairs={{0,2},{1,3},{2,0},{3,1},{4,6},{5,7},{6,4},{7,5},{8,10},{9,11},{10,... | collective-permute-start | bytes 61448 | tf_op jit(solution)/shard_map/ppermute | solution.py:294
  18.0 2.3 %copy-start = (bf16[512,512]{1,0:T(8,128)(2,1)S(1)}, bf16[512,512]{1,0:T(8,128)(2,1)}, u32[]{:S(2)}) copy-start(bf16[512,512]{1,0:T(8,128)(2,1)} %refs_4_.1) | copy-start | bytes 1572868
  18.5 1.2 %collective-permute-start.7 = (bf16[64,128]{1,0:T(8,128)(2,1)S(1)}, bf16[64,128]{1,0:T(8,128)(2,1)S(1)}, u32[]{:S(2)}, u32[]{:S(2)}) collective-permute-start(bf16[64,128]{1,0:T(8,128)(2,1)S(1)} %get-tuple-element.37), channel_id=1, source_target_pairs={{0,1},{1,0},{2,3},{3,2},{4,5},{5,4},{6,7},{7,6},{8,9},{9,8},{10,11... | collective-permute-start | bytes 49160 | tf_op jit(solution)/shard_map/ppermute | solution.py:294

commit v10 on v9

--- a/solution.py
+++ b/solution.py
@@ -212,19 +212,24 @@
     first_head = lax.broadcasted_iota(jnp.int32, (1, values.shape[1]), 1) < HD
     exponent = math.log2(math.e) / math.sqrt(HD)
     rows = split_heads(queries[pl.ds(pl.multiple_of(leaf * LEAF, LEAF), LEAF)])
-    near = near_scores[leaf]
-    far_scores = scores_of(rows, keys) + bias
-    peak = jnp.maximum(
-        jnp.max(near, axis=1, keepdims=True), jnp.max(far_scores, axis=1, keepdims=True)
-    )
-    near = jnp.exp2((near - peak) * exponent)
-    far_weights = jnp.exp2((far_scores - peak) * exponent)
-    total = jnp.sum(near, axis=1, keepdims=True) + jnp.sum(far_weights, axis=1, keepdims=True)
-    numer = jnp.dot(
-        near.astype(jnp.bfloat16), near_values[leaf], preferred_element_type=jnp.float32
-    ) + jnp.dot(far_weights.astype(jnp.bfloat16), values[...], preferred_element_type=jnp.float32)
-    mean = numer / total
-    attended = jnp.where(first_head, mean[:LEAF], mean[LEAF:]).astype(jnp.bfloat16)
+    means = []
+    for head in range(2):
+        span = slice(head * LEAF, (head + 1) * LEAF)
+        near = near_scores[leaf, span]
+        far_scores = scores_of(rows[span], keys) + bias
+        peak = jnp.maximum(
+            jnp.max(near, axis=1, keepdims=True), jnp.max(far_scores, axis=1, keepdims=True)
+        )
+        near = jnp.exp2((near - peak) * exponent)
+        far_weights = jnp.exp2((far_scores - peak) * exponent)
+        total = jnp.sum(near, axis=1, keepdims=True) + jnp.sum(far_weights, axis=1, keepdims=True)
+        numer = jnp.dot(
+            near.astype(jnp.bfloat16), near_values[leaf], preferred_element_type=jnp.float32
+        ) + jnp.dot(
+            far_weights.astype(jnp.bfloat16), values[...], preferred_element_type=jnp.float32
+        )
+        means.append(numer / total)
+    attended = jnp.where(first_head, means[0], means[1]).astype(jnp.bfloat16)
     second = (lax.axis_index("head") & 1) == 1
     same[:HALF] = jnp.where(second, attended[HALF:], attended[:HALF])
     other[:HALF] = jnp.where(second, attended[:HALF], attended[HALF:])

time: 21.2 us -> 21.4 us (level)
  Pallas kernels: 3.46 us -> 3.84 us
  transfers between devices with their start and end apart: 8 -> 8, of which waited for: 4 -> 4; matrix products, arithmetic and copies ran while one was open for 0% -> 0% of each run, Pallas kernels for 5% -> 6%
where the time goes in v10:
time: 21.4 us; the launch traced here: 21.3 us
  starting transfers between devices  10.3 us (48%)
  waiting for transfers between devices  7.09 us (33%)
  Pallas kernels  3.84 us (18%)
    ppermute x7, starting transfers between devices, swap(): lax.ppermute(array, axis, [(i, i ^ bit) for i in range(lax.axis_size(axis...  9.63 us
    ppermute x7, waiting for transfers between devices, swap(): lax.ppermute(array, axis, [(i, i ^ bit) for i in range(lax.axis_size(axis...  7.09 us
    pallas_call x1, Pallas kernels, shards(): kernel_call(functools.partial(pack_kernel, not paired), 'pack', 16, [HBM]...  0.99 us
    pallas_call x1, Pallas kernels, shards(): kernel_call(project_kernel, 'project', 8, [VMEM] * (head_size + 1), [(sha...  0.85 us
    pallas_call x1, Pallas kernels, shards(): kernel_call(functools.partial(leaves_kernel, seq_size), 'leaves', 24, [VM...  0.79 us
    pallas_call x1, Pallas kernels, shards(): kernel_call(stays_kernel, 'stays', 16, [VMEM] * 6, [(share, width)] * 2,...  0.75 us
    ppermute x1, starting transfers between devices, shards(): outer = lax.ppermute(outer, 'seq', others)  0.65 us
  transfers between devices with their start and end apart: 8, of which 4 were waited for; matrix products, arithmetic and copies ran while one was open for 0% of the time, Pallas kernels for 6%

profile of v10, /device:TPU:0, one launch (start us, length us, event | category | flops | bytes accessed | tf_op | source)
XLA Modules:
  0.0 21.3 jit_solution(10103921418167819756)
XLA Ops:
  0.0 1.0 %pack.1 = (bf16[256,128]{1,0:T(8,128)(2,1)S(1)}, bf16[256,256]{1,0:T(8,128)(2,1)S(1)}, bf16[192,256]{1,0:T(8,128)(2,1)S(1)}, bf16[192,256]{1,0:T(8,128)(2,1)S(1)}, bf16[64,256]{1,0:T(8,128)(2,1)S(1)}) custom-call(bf16[256,128]{1,0:T(8,128)(2,1)} %queries.1, bf16[256,128]{1,0:T(8,128)(2,1)} %keys.1, bf16[256,128]{1,0:T(8,128)(2,1)} %values.1), custom_call_target="tpu_custom_call" | custom-call | bytes 1048576 | tf_op jit(solution)/shard_map/pack/pallas_call | solution.py:301
  1.0 3.0 %collective-permute-start = (bf16[192,256]{1,0:T(8,128)(2,1)S(1)}, bf16[192,256]{1,0:T(8,128)(2,1)S(1)}, u32[]{:S(2)}, u32[]{:S(2)}) collective-permute-start(bf16[192,256]{1,0:T(8,128)(2,1)S(1)} %get-tuple-element.24), channel_id=1, source_target_pairs={{0,4},{4,0},{8,12},{12,8},{16,20},{20,16},{24,28},{28,24},{1,5},{5... | collective-permute-start | bytes 294920 | tf_op jit(solution)/shard_map/ppermute | solution.py:299
  4.0 0.7 %collective-permute-start.1 = (bf16[192,256]{1,0:T(8,128)(2,1)S(1)}, bf16[192,256]{1,0:T(8,128)(2,1)S(1)}, u32[]{:S(2)}, u32[]{:S(2)}) collective-permute-start(bf16[192,256]{1,0:T(8,128)(2,1)S(1)} %get-tuple-element.25), channel_id=1, source_target_pairs={{4,8},{8,4},{12,16},{16,12},{20,24},{24,20},{5,9},{9,5},{13,17},{1... | collective-permute-start | bytes 294920 | tf_op jit(solution)/shard_map/ppermute | solution.py:317
  4.7 2.1 %collective-permute-done.inner = bf16[192,256]{1,0:T(8,128)(2,1)S(1)} collective-permute-done((bf16[192,256]{1,0:T(8,128)(2,1)S(1)}, bf16[192,256]{1,0:T(8,128)(2,1)S(1)}, u32[]{:S(2)}, u32[]{:S(2)}) %collective-permute-start) | collective-permute-done | bytes 98336 | tf_op jit(solution)/shard_map/ppermute | solution.py:299
  6.8 0.1 join.1
  6.9 4.0 %collective-permute-start.2 = (bf16[128,256]{1,0:T(8,128)(2,1)S(1)}, bf16[128,256]{1,0:T(8,128)(2,1)S(1)}, u32[]{:S(2)}, u32[]{:S(2)}) collective-permute-start(bf16[128,256]{1,0:T(8,128)(2,1)S(1)} %get-tuple-element.30), channel_id=1, source_target_pairs={{0,24},{4,28},{8,16},{12,20},{16,8},{20,12},{24,0},{28,4},{1,25},{... | collective-permute-start | bytes 196616 | tf_op jit(solution)/shard_map/ppermute | solution.py:299
  10.9 0.0 collective-permute-start.3
  10.9 0.6 %collective-permute-start.4 = (bf16[64,256]{1,0:T(8,128)(2,1)S(1)}, bf16[64,256]{1,0:T(8,128)(2,1)S(1)}, u32[]{:S(2)}, u32[]{:S(2)}) collective-permute-start(bf16[64,256]{1,0:T(8,128)(2,1)S(1)} %get-tuple-element.31), channel_id=1, source_target_pairs={{0,16},{4,20},{8,24},{12,28},{16,0},{20,4},{24,8},{28,12},{1,17},{... | collective-permute-start | bytes 98312 | tf_op jit(solution)/shard_map/ppermute | solution.py:299
  11.5 0.0 collective-permute-done.1.outer
  11.5 0.4 %near.1 = (f32[2,256,512]{2,1,0:T(8,128)S(1)}, bf16[2,512,128]{2,1,0:T(8,128)(2,1)S(1)}, bf16[64,256]{1,0:T(8,128)(2,1)S(1)}) custom-call(bf16[256,128]{1,0:T(8,128)(2,1)S(1)} %get-tuple-element.22.queries, bf16[256,256]{1,0:T(8,128)(2,1)S(1)} %get-tuple-element.23.own, bf16[192,256]{1,0:T(8,128)(2,1)S(1)} %collective-permute-done.inner, ...), custom_call_target="tpu_custom_call" | custom-call | flops 67108864 | bytes 1048576 | tf_op jit(solution)/shard_map/near/pallas_call | solution.py:331
  11.9 3.8 %collective-permute-done.4.rest_2_ = bf16[64,256]{1,0:T(8,128)(2,1)S(1)} collective-permute-done((bf16[64,256]{1,0:T(8,128)(2,1)S(1)}, bf16[64,256]{1,0:T(8,128)(2,1)S(1)}, u32[]{:S(2)}, u32[]{:S(2)}) %collective-permute-start.4) | collective-permute-done | bytes 32800 | tf_op jit(solution)/shard_map/ppermute | solution.py:299
  15.7 0.0 collective-permute-done.2.rest_0_
  15.7 0.0 collective-permute-done.3.rest_1_
  15.7 0.8 %leaves.1 = (bf16[80,128]{1,0:T(8,128)(2,1)S(1)}, bf16[80,128]{1,0:T(8,128)(2,1)S(1)}, bf16[384,128]{1,0:T(8,128)(2,1)S(1)}, bf16[384,128]{1,0:T(8,128)(2,1)S(1)}, f32[8,384]{1,0:T(8,128)S(1)}) custom-call(bf16[256,128]{1,0:T(8,128)(2,1)S(1)} %get-tuple-element.22.queries, f32[2,256,512]{2,1,0:T(8,128)S(1)} %get-tuple-element.26.near_scores, ...), custom_call_target="tpu_custom_call" | custom-call | flops 117440512 | bytes 1048576 | tf_op jit(solution)/shard_map/leaves/pallas_call | solution.py:347
  16.5 0.1 collective-permute-start.5
  16.6 1.6 %collective-permute-start.6 = (bf16[80,128]{1,0:T(8,128)(2,1)S(1)}, bf16[80,128]{1,0:T(8,128)(2,1)S(1)}, u32[]{:S(2)}, u32[]{:S(2)}) collective-permute-start(bf16[80,128]{1,0:T(8,128)(2,1)S(1)} %get-tuple-element.33), channel_id=1, source_target_pairs={{0,2},{1,3},{2,0},{3,1},{4,6},{5,7},{6,4},{7,5},{8,10},{9,11},{10,... | collective-permute-start | bytes 61448 | tf_op jit(solution)/shard_map/ppermute | solution.py:299
  18.2 0.0 copy-start
  18.2 0.8 %stays.1 = (bf16[64,128]{1,0:T(8,128)(2,1)S(1)}, bf16[64,128]{1,0:T(8,128)(2,1)S(1)}) custom-call(bf16[256,128]{1,0:T(8,128)(2,1)S(1)} %get-tuple-element.22.queries, f32[2,256,512]{2,1,0:T(8,128)S(1)} %get-tuple-element.26.near_scores, bf16[2,512,128]{2,1,0:T(8,128)(2,1)S(1)} %get-tuple-element.27.near_values, bf16[384,128]{1,0:T(8,128)(2,1)S(1)} %get-tuple-element.34.keys, ...), custom_call_target="tpu_custom_call" | custom-call | flops 117440512 | bytes 1048576 | tf_op jit(solution)/shard_map/stays/pallas_call | solution.py:362
  18.9 0.3 %collective-permute-start.7 = (bf16[64,128]{1,0:T(8,128)(2,1)S(1)}, bf16[64,128]{1,0:T(8,128)(2,1)S(1)}, u32[]{:S(2)}, u32[]{:S(2)}) collective-permute-start(bf16[64,128]{1,0:T(8,128)(2,1)S(1)} %get-tuple-element.37), channel_id=1, source_target_pairs={{0,1},{1,0},{2,3},{3,2},{4,5},{5,4},{6,7},{7,6},{8,9},{9,8},{10,11... | collective-permute-start | bytes 49160 | tf_op jit(solution)/shard_map/ppermute | solution.py:299
  19.2 0.9 %collective-permute-done.7.refs_2_ = bf16[64,128]{1,0:T(8,128)(2,1)S(1)} collective-permute-done((bf16[64,128]{1,0:T(8,128)(2,1)S(1)}, bf16[64,128]{1,0:T(8,128)(2,1)S(1)}, u32[]{:S(2)}, u32[]{:S(2)}) %collective-permute-start.7) | collective-permute-done | bytes 16416 | tf_op jit(solution)/shard_map/ppermute | solution.py:299
  20.2 0.0 collective-permute-done.5.refs_0_
  20.2 0.2 %collective-permute-done.6.refs_1_ = bf16[80,128]{1,0:T(8,128)(2,1)S(1)} collective-permute-done((bf16[80,128]{1,0:T(8,128)(2,1)S(1)}, bf16[80,128]{1,0:T(8,128)(2,1)S(1)}, u32[]{:S(2)}, u32[]{:S(2)}) %collective-permute-start.6) | collective-permute-done | bytes 20512 | tf_op jit(solution)/shard_map/ppermute | solution.py:299
  20.4 0.0 copy-done
  20.4 0.9 %project.1 = bf16[64,512]{1,0:T(8,128)(2,1)} custom-call(bf16[80,128]{1,0:T(8,128)(2,1)S(1)} %collective-permute-done.5.refs_0_, bf16[80,128]{1,0:T(8,128)(2,1)S(1)} %collective-permute-done.6.refs_1_, bf16[64,128]{1,0:T(8,128)(2,1)S(1)} %collective-permute-done.7.refs_2_, bf16[64,128]{1,0:T(8,128)(2,1)S(1)} %get-tuple-element.38.refs_3_, ...), custom_call_target="tpu_custom_call" | custom-call | bytes 1048576 | tf_op jit(solution)/shard_map/project/pallas_call | solution.py:366
Async XLA Ops:
  1.0 5.8 %collective-permute-start = (bf16[192,256]{1,0:T(8,128)(2,1)S(1)}, bf16[192,256]{1,0:T(8,128)(2,1)S(1)}, u32[]{:S(2)}, u32[]{:S(2)}) collective-permute-start(bf16[192,256]{1,0:T(8,128)(2,1)S(1)} %get-tuple-element.24), channel_id=1, source_target_pairs={{0,4},{4,0},{8,12},{12,8},{16,20},{20,16},{24,28},{28,24},{1,5},{5... | collective-permute-start | bytes 294920 | tf_op jit(solution)/shard_map/ppermute | solution.py:299
  4.0 7.5 %collective-permute-start.1 = (bf16[192,256]{1,0:T(8,128)(2,1)S(1)}, bf16[192,256]{1,0:T(8,128)(2,1)S(1)}, u32[]{:S(2)}, u32[]{:S(2)}) collective-permute-start(bf16[192,256]{1,0:T(8,128)(2,1)S(1)} %get-tuple-element.25), channel_id=1, source_target_pairs={{4,8},{8,4},{12,16},{16,12},{20,24},{24,20},{5,9},{9,5},{13,17},{1... | collective-permute-start | bytes 294920 | tf_op jit(solution)/shard_map/ppermute | solution.py:317
  6.9 8.8 %collective-permute-start.2 = (bf16[128,256]{1,0:T(8,128)(2,1)S(1)}, bf16[128,256]{1,0:T(8,128)(2,1)S(1)}, u32[]{:S(2)}, u32[]{:S(2)}) collective-permute-start(bf16[128,256]{1,0:T(8,128)(2,1)S(1)} %get-tuple-element.30), channel_id=1, source_target_pairs={{0,24},{4,28},{8,16},{12,20},{16,8},{20,12},{24,0},{28,4},{1,25},{... | collective-permute-start | bytes 196616 | tf_op jit(solution)/shard_map/ppermute | solution.py:299
  10.9 4.8 %collective-permute-start.3 = (bf16[128,256]{1,0:T(8,128)(2,1)S(1)}, bf16[128,256]{1,0:T(8,128)(2,1)S(1)}, u32[]{:S(2)}, u32[]{:S(2)}) collective-permute-start(bf16[128,256]{1,0:T(8,128)(2,1)S(1)} %get-tuple-element.30), channel_id=1, source_target_pairs={{0,8},{4,12},{8,0},{12,4},{16,24},{20,28},{24,16},{28,20},{1,9},{5... | collective-permute-start | bytes 196616 | tf_op jit(solution)/shard_map/ppermute | solution.py:299
  10.9 4.8 %collective-permute-start.4 = (bf16[64,256]{1,0:T(8,128)(2,1)S(1)}, bf16[64,256]{1,0:T(8,128)(2,1)S(1)}, u32[]{:S(2)}, u32[]{:S(2)}) collective-permute-start(bf16[64,256]{1,0:T(8,128)(2,1)S(1)} %get-tuple-element.31), channel_id=1, source_target_pairs={{0,16},{4,20},{8,24},{12,28},{16,0},{20,4},{24,8},{28,12},{1,17},{... | collective-permute-start | bytes 98312 | tf_op jit(solution)/shard_map/ppermute | solution.py:299
  16.5 3.7 %collective-permute-start.5 = (bf16[80,128]{1,0:T(8,128)(2,1)S(1)}, bf16[80,128]{1,0:T(8,128)(2,1)S(1)}, u32[]{:S(2)}, u32[]{:S(2)}) collective-permute-start(bf16[80,128]{1,0:T(8,128)(2,1)S(1)} %get-tuple-element.32), channel_id=1, source_target_pairs={{0,3},{1,2},{2,1},{3,0},{4,7},{5,6},{6,5},{7,4},{8,11},{9,10},{10,... | collective-permute-start | bytes 61448 | tf_op jit(solution)/shard_map/ppermute | solution.py:299
  16.6 3.8 %collective-permute-start.6 = (bf16[80,128]{1,0:T(8,128)(2,1)S(1)}, bf16[80,128]{1,0:T(8,128)(2,1)S(1)}, u32[]{:S(2)}, u32[]{:S(2)}) collective-permute-start(bf16[80,128]{1,0:T(8,128)(2,1)S(1)} %get-tuple-element.33), channel_id=1, source_target_pairs={{0,2},{1,3},{2,0},{3,1},{4,6},{5,7},{6,4},{7,5},{8,10},{9,11},{10,... | collective-permute-start | bytes 61448 | tf_op jit(solution)/shard_map/ppermute | solution.py:299
  18.2 2.3 %copy-start = (bf16[512,512]{1,0:T(8,128)(2,1)S(1)}, bf16[512,512]{1,0:T(8,128)(2,1)}, u32[]{:S(2)}) copy-start(bf16[512,512]{1,0:T(8,128)(2,1)} %refs_4_.1) | copy-start | bytes 1572868
  18.9 1.2 %collective-permute-start.7 = (bf16[64,128]{1,0:T(8,128)(2,1)S(1)}, bf16[64,128]{1,0:T(8,128)(2,1)S(1)}, u32[]{:S(2)}, u32[]{:S(2)}) collective-permute-start(bf16[64,128]{1,0:T(8,128)(2,1)S(1)} %get-tuple-element.37), channel_id=1, source_target_pairs={{0,1},{1,0},{2,3},{3,2},{4,5},{5,4},{6,7},{7,6},{8,9},{9,8},{10,11... | collective-permute-start | bytes 49160 | tf_op jit(solution)/shard_map/ppermute | solution.py:299

commit v11 on v9

--- a/solution.py
+++ b/solution.py
@@ -54,8 +54,9 @@
         quarter[...] = level_two
 
 
-def join_kernel(inner, quarter, block, eighth, wide):
-    odd = lax.axis_index("seq") & 1
+def join_kernel(inner, quarter, block, across, eighth, wide):
+    me = lax.axis_index("seq")
+    odd = me & 1
     edge_half = average_pairs(inner[:LEAF], wide)
     other_half = inner[LEAF:]
     theirs = jnp.concatenate(
@@ -64,7 +65,11 @@
     theirs = average_pairs(theirs, wide)
     block[:HALF] = jnp.where(odd == 1, theirs, quarter[...])
     block[HALF:] = jnp.where(odd == 1, quarter[...], theirs)
-    eighth[...] = average_pairs(block[...], wide)
+    level_three = average_pairs(block[...], wide)
+    eighth[...] = level_three
+    middle = (me >= 2) & (me < 6)
+    across[:HALF] = jnp.where(middle, block[:HALF], level_three)
+    across[HALF:] = block[HALF:]
 
 
 NEAR_ROWS = 4 * LEAF
@@ -125,7 +130,7 @@
     return pieces
 
 
-def paired_pieces(block_6, block_2, eighth_4, wide):
+def paired_pieces(block_6, block_2, eighth_4):
     me = lax.axis_index("seq")
     odd = me & 1
     pair = me >> 1
@@ -136,13 +141,12 @@
     has_lower, has_upper = pair >= 1, pair <= 2
     third = jnp.where(odd == 1, lower[HALF:], upper[:HALF])
     has_third = ((odd == 1) & has_lower) | ((odd == 0) & has_upper)
-    ends = average_pairs(block_6[...], wide)
     return [
         (lower[:HALF], bias_of(has_lower)),
         (upper[HALF:], bias_of(has_upper)),
         (third, bias_of(has_third)),
         (eighth_4[...], bias_of(pair >= 0)),
-        (ends, bias_of(jnp.logical_not(middle))),
+        (block_6[:HALF], bias_of(jnp.logical_not(middle))),
     ]
 
 
@@ -235,7 +239,7 @@
     if len(far) == 1:
         pieces = gathered_pieces(seq_size, far[0], wide)
     else:
-        pieces = paired_pieces(*far, wide)
+        pieces = paired_pieces(*far)
     shared_bias = bias_of(lax.axis_index("seq") >= 1)
     bias[...] = jnp.broadcast_to(place([(shared, shared_bias)] + pieces, values, keys), bias.shape)
     leaf = (lax.axis_index("head") >> 1) ^ 1
@@ -249,14 +253,32 @@
     attend_leaf(leaf, queries, near_scores, near_values, keys, values, bias[:1], same, other)
 
 
-def project_kernel(*refs):
-    *parts, weight, mixed = refs
-    mine = lax.axis_index("head")
-    total = jnp.zeros(mixed.shape, jnp.float32)
-    for step, part in enumerate(reversed(parts)):
-        width = part.shape[1]
-        columns = pl.ds(pl.multiple_of((mine ^ step) * width, width), width)
-        total += jnp.dot(part[: mixed.shape[0]], weight[columns], preferred_element_type=jnp.float32)
+def side_by_side(same, other, rows, columns):
+    second = (lax.axis_index("head") & 1) == 1
+    width = same.shape[1]
+    columns[:, :width] = jnp.where(second, other[:rows], same[:rows])
+    columns[:, width:] = jnp.where(second, same[:rows], other[:rows])
+    return columns[...]
+
+
+def chip_rows(weight, chip, count):
+    return weight[pl.ds(pl.multiple_of(chip * count, count), count)]
+
+
+def begin_kernel(same, other, weight, partial, columns):
+    chip = lax.axis_index("head") >> 1
+    shares = side_by_side(same, other, partial.shape[0], columns)
+    partial[...] = jnp.dot(
+        shares, chip_rows(weight, chip, columns.shape[1]), preferred_element_type=jnp.float32
+    )
+
+
+def project_kernel(partial, other, same, weight, mixed, columns):
+    chip = (lax.axis_index("head") >> 1) ^ 1
+    shares = side_by_side(same, other, partial.shape[0], columns)
+    total = partial[...] + jnp.dot(
+        shares, chip_rows(weight, chip, columns.shape[1]), preferred_element_type=jnp.float32
+    )
     mixed[...] = total.astype(mixed.dtype)
 
 
@@ -311,15 +333,15 @@
     others = [(i, i + 1 if i & 1 else i - 1) for i in range(1, seq_size - 1)]
     outer = lax.ppermute(outer, "seq", others)
     if paired:
-        block, eighth = kernel_call(
+        block, across, eighth = kernel_call(
             join_kernel,
             "join",
             8,
             [VMEM] * 2,
-            [(LEAF, pair_width), (HALF, pair_width)],
+            [(LEAF, pair_width), (LEAF, pair_width), (HALF, pair_width)],
             [wide],
         )(inner, quarter)
-        far = (swap(block, 6), swap(block, 2), swap(eighth, 4))
+        far = (swap(across, 6), swap(block, 2), swap(eighth, 4))
     else:
         far = (lax.all_to_all(quarter, "seq", split_axis=0, concat_axis=0),)
     share = tokens // head_size
@@ -357,10 +379,19 @@
     share_0, share_1 = kernel_call(
         stays_kernel, "stays", 16, [VMEM] * 6, [(share, width)] * 2, [], flops=leaf_flops
     )(own_queries, near_scores, near_values, far_keys, far_values, far_bias)
-    parts = [swap(share_3, 3, "head"), swap(share_2, 2, "head"), swap(share_1, 1, "head"), share_0]
+    columns = pltpu.VMEM((share, pair_width), jnp.bfloat16)
+    part_3, part_2 = swap(share_3, 3, "head"), swap(share_2, 2, "head")
+    (partial,) = kernel_call(
+        begin_kernel,
+        "begin",
+        8,
+        [VMEM] * 3,
+        [jax.ShapeDtypeStruct((share, out_weight.shape[1]), jnp.float32)],
+        [columns],
+    )(share_0, swap(share_1, 1, "head"), out_weight)
     (mixed,) = kernel_call(
-        project_kernel, "project", 8, [VMEM] * (head_size + 1), [(share, out_weight.shape[1])], []
-    )(*parts, out_weight)
+        project_kernel, "project", 8, [VMEM] * 4, [(share, out_weight.shape[1])], [columns]
+    )(partial, part_3, part_2, out_weight)
     return mixed
 
 

time: 21.2 us -> 21.2 us (level)
    pallas_call x2 -> x3, Pallas kernels: 0.92 us -> 1.05 us  [the longest x1 0.81 us: shards(): kernel_call(project_kernel, 'project', 8, [VMEM] * 4, [(share, out_weight...]
  transfers between devices with their start and end apart: 8 -> 8, of which waited for: 4 -> 4; matrix products, arithmetic and copies ran while one was open for 0% -> 0% of each run, Pallas kernels for 5% -> 6%
where the time goes in v11:
time: 21.2 us; the launch traced here: 21 us
  starting transfers between devices  10.3 us (49%)
  waiting for transfers between devices  7.1 us (33%)
  Pallas kernels  3.58 us (17%)
    ppermute x7, starting transfers between devices, swap(): lax.ppermute(array, axis, [(i, i ^ bit) for i in range(lax.axis_size(axis...  9.62 us
    ppermute x7, waiting for transfers between devices, swap(): lax.ppermute(array, axis, [(i, i ^ bit) for i in range(lax.axis_size(axis...  7.1 us
    pallas_call x1, Pallas kernels, shards(): kernel_call(functools.partial(pack_kernel, not paired), 'pack', 16, [HBM]...  0.99 us
    pallas_call x1, Pallas kernels, shards(): kernel_call(project_kernel, 'project', 8, [VMEM] * 4, [(share, out_weight...  0.81 us
    ppermute x1, starting transfers between devices, shards(): outer = lax.ppermute(outer, 'seq', others)  0.65 us
    pallas_call x1, Pallas kernels, shards(): kernel_call(functools.partial(leaves_kernel, seq_size), 'leaves', 24, [VM...  0.59 us
    pallas_call x1, Pallas kernels, shards(): kernel_call(stays_kernel, 'stays', 16, [VMEM] * 6, [(share, width)] * 2,...  0.57 us
  transfers between devices with their start and end apart: 8, of which 4 were waited for; matrix products, arithmetic and copies ran while one was open for 0% of the time, Pallas kernels for 6%

profile of v11, /device:TPU:0, one launch (start us, length us, event | category | flops | bytes accessed | tf_op | source)
XLA Modules:
  0.0 21.0 jit_solution(12160173383499155283)
XLA Ops:
  0.0 1.0 %pack.1 = (bf16[256,128]{1,0:T(8,128)(2,1)S(1)}, bf16[256,256]{1,0:T(8,128)(2,1)S(1)}, bf16[192,256]{1,0:T(8,128)(2,1)S(1)}, bf16[192,256]{1,0:T(8,128)(2,1)S(1)}, bf16[64,256]{1,0:T(8,128)(2,1)S(1)}) custom-call(bf16[256,128]{1,0:T(8,128)(2,1)} %queries.1, bf16[256,128]{1,0:T(8,128)(2,1)} %keys.1, bf16[256,128]{1,0:T(8,128)(2,1)} %values.1), custom_call_target="tpu_custom_call" | custom-call | bytes 1048576 | tf_op jit(solution)/shard_map/pack/pallas_call | solution.py:318
  1.0 3.0 %collective-permute-start = (bf16[192,256]{1,0:T(8,128)(2,1)S(1)}, bf16[192,256]{1,0:T(8,128)(2,1)S(1)}, u32[]{:S(2)}, u32[]{:S(2)}) collective-permute-start(bf16[192,256]{1,0:T(8,128)(2,1)S(1)} %get-tuple-element.25), channel_id=1, source_target_pairs={{0,4},{4,0},{8,12},{12,8},{16,20},{20,16},{24,28},{28,24},{1,5},{5... | collective-permute-start | bytes 294920 | tf_op jit(solution)/shard_map/ppermute | solution.py:316
  4.0 0.7 %collective-permute-start.1 = (bf16[192,256]{1,0:T(8,128)(2,1)S(1)}, bf16[192,256]{1,0:T(8,128)(2,1)S(1)}, u32[]{:S(2)}, u32[]{:S(2)}) collective-permute-start(bf16[192,256]{1,0:T(8,128)(2,1)S(1)} %get-tuple-element.26), channel_id=1, source_target_pairs={{4,8},{8,4},{12,16},{16,12},{20,24},{24,20},{5,9},{9,5},{13,17},{1... | collective-permute-start | bytes 294920 | tf_op jit(solution)/shard_map/ppermute | solution.py:334
  4.7 2.1 %collective-permute-done.inner = bf16[192,256]{1,0:T(8,128)(2,1)S(1)} collective-permute-done((bf16[192,256]{1,0:T(8,128)(2,1)S(1)}, bf16[192,256]{1,0:T(8,128)(2,1)S(1)}, u32[]{:S(2)}, u32[]{:S(2)}) %collective-permute-start) | collective-permute-done | bytes 98336 | tf_op jit(solution)/shard_map/ppermute | solution.py:316
  6.8 0.1 join.1
  6.9 4.0 %collective-permute-start.2 = (bf16[128,256]{1,0:T(8,128)(2,1)S(1)}, bf16[128,256]{1,0:T(8,128)(2,1)S(1)}, u32[]{:S(2)}, u32[]{:S(2)}) collective-permute-start(bf16[128,256]{1,0:T(8,128)(2,1)S(1)} %get-tuple-element.31), channel_id=1, source_target_pairs={{0,24},{4,28},{8,16},{12,20},{16,8},{20,12},{24,0},{28,4},{1,25},{... | collective-permute-start | bytes 196616 | tf_op jit(solution)/shard_map/ppermute | solution.py:316
  10.9 0.0 collective-permute-start.3
  10.9 0.6 %collective-permute-start.4 = (bf16[64,256]{1,0:T(8,128)(2,1)S(1)}, bf16[64,256]{1,0:T(8,128)(2,1)S(1)}, u32[]{:S(2)}, u32[]{:S(2)}) collective-permute-start(bf16[64,256]{1,0:T(8,128)(2,1)S(1)} %get-tuple-element.33), channel_id=1, source_target_pairs={{0,16},{4,20},{8,24},{12,28},{16,0},{20,4},{24,8},{28,12},{1,17},{... | collective-permute-start | bytes 98312 | tf_op jit(solution)/shard_map/ppermute | solution.py:316
  11.5 0.0 collective-permute-done.1.outer
  11.5 0.4 %near.1 = (f32[2,256,512]{2,1,0:T(8,128)S(1)}, bf16[2,512,128]{2,1,0:T(8,128)(2,1)S(1)}, bf16[64,256]{1,0:T(8,128)(2,1)S(1)}) custom-call(bf16[256,128]{1,0:T(8,128)(2,1)S(1)} %get-tuple-element.23.queries, bf16[256,256]{1,0:T(8,128)(2,1)S(1)} %get-tuple-element.24.own, bf16[192,256]{1,0:T(8,128)(2,1)S(1)} %collective-permute-done.inner, ...), custom_call_target="tpu_custom_call" | custom-call | flops 67108864 | bytes 1048576 | tf_op jit(solution)/shard_map/near/pallas_call | solution.py:348
  11.9 3.8 %collective-permute-done.4.rest_2_ = bf16[64,256]{1,0:T(8,128)(2,1)S(1)} collective-permute-done((bf16[64,256]{1,0:T(8,128)(2,1)S(1)}, bf16[64,256]{1,0:T(8,128)(2,1)S(1)}, u32[]{:S(2)}, u32[]{:S(2)}) %collective-permute-start.4) | collective-permute-done | bytes 32800 | tf_op jit(solution)/shard_map/ppermute | solution.py:316
  15.7 0.0 collective-permute-done.2.rest_0_
  15.7 0.0 collective-permute-done.3.rest_1_
  15.7 0.6 %leaves.1 = (bf16[80,128]{1,0:T(8,128)(2,1)S(1)}, bf16[80,128]{1,0:T(8,128)(2,1)S(1)}, bf16[384,128]{1,0:T(8,128)(2,1)S(1)}, bf16[384,128]{1,0:T(8,128)(2,1)S(1)}, f32[8,384]{1,0:T(8,128)S(1)}) custom-call(bf16[256,128]{1,0:T(8,128)(2,1)S(1)} %get-tuple-element.23.queries, f32[2,256,512]{2,1,0:T(8,128)S(1)} %get-tuple-element.27.near_scores, ...), custom_call_target="tpu_custom_call" | custom-call | flops 117440512 | bytes 1048576 | tf_op jit(solution)/shard_map/leaves/pallas_call | solution.py:364
  16.3 0.1 collective-permute-start.6
  16.4 1.6 %collective-permute-start.7 = (bf16[80,128]{1,0:T(8,128)(2,1)S(1)}, bf16[80,128]{1,0:T(8,128)(2,1)S(1)}, u32[]{:S(2)}, u32[]{:S(2)}) collective-permute-start(bf16[80,128]{1,0:T(8,128)(2,1)S(1)} %get-tuple-element.40), channel_id=1, source_target_pairs={{0,2},{1,3},{2,0},{3,1},{4,6},{5,7},{6,4},{7,5},{8,10},{9,11},{10,... | collective-permute-start | bytes 61448 | tf_op jit(solution)/shard_map/ppermute | solution.py:316
  18.0 0.0 copy-start
  18.0 0.6 %stays.1 = (bf16[64,128]{1,0:T(8,128)(2,1)S(1)}, bf16[64,128]{1,0:T(8,128)(2,1)S(1)}) custom-call(bf16[256,128]{1,0:T(8,128)(2,1)S(1)} %get-tuple-element.23.queries, f32[2,256,512]{2,1,0:T(8,128)S(1)} %get-tuple-element.27.near_scores, bf16[2,512,128]{2,1,0:T(8,128)(2,1)S(1)} %get-tuple-element.28.near_values, bf16[384,128]{1,0:T(8,128)(2,1)S(1)} %get-tuple-element.34.keys, ...), custom_call_target="tpu_custom_call" | custom-call | flops 117440512 | bytes 1048576 | tf_op jit(solution)/shard_map/stays/pallas_call | solution.py:379
  18.5 0.3 %collective-permute-start.5 = (bf16[64,128]{1,0:T(8,128)(2,1)S(1)}, bf16[64,128]{1,0:T(8,128)(2,1)S(1)}, u32[]{:S(2)}, u32[]{:S(2)}) collective-permute-start(bf16[64,128]{1,0:T(8,128)(2,1)S(1)} %get-tuple-element.38), channel_id=1, source_target_pairs={{0,1},{1,0},{2,3},{3,2},{4,5},{5,4},{6,7},{7,6},{8,9},{9,8},{10,11... | collective-permute-start | bytes 49160 | tf_op jit(solution)/shard_map/ppermute | solution.py:316
  18.9 0.9 %collective-permute-done.5.other = bf16[64,128]{1,0:T(8,128)(2,1)S(1)} collective-permute-done((bf16[64,128]{1,0:T(8,128)(2,1)S(1)}, bf16[64,128]{1,0:T(8,128)(2,1)S(1)}, u32[]{:S(2)}, u32[]{:S(2)}) %collective-permute-start.5) | collective-permute-done | bytes 16416 | tf_op jit(solution)/shard_map/ppermute | solution.py:316
  19.8 0.0 copy-done
  19.8 0.2 begin.1.partial
  20.0 0.0 collective-permute-done.6.other
  20.0 0.3 %collective-permute-done.7.same = bf16[80,128]{1,0:T(8,128)(2,1)S(1)} collective-permute-done((bf16[80,128]{1,0:T(8,128)(2,1)S(1)}, bf16[80,128]{1,0:T(8,128)(2,1)S(1)}, u32[]{:S(2)}, u32[]{:S(2)}) %collective-permute-start.7) | collective-permute-done | bytes 20512 | tf_op jit(solution)/shard_map/ppermute | solution.py:316
  20.2 0.8 %project.1 = bf16[64,512]{1,0:T(8,128)(2,1)} custom-call(f32[64,512]{1,0:T(8,128)S(1)} %begin.1.partial, bf16[80,128]{1,0:T(8,128)(2,1)S(1)} %collective-permute-done.6.other, bf16[80,128]{1,0:T(8,128)(2,1)S(1)} %collective-permute-done.7.same, bf16[512,512]{1,0:T(8,128)(2,1)S(1)} %copy-done), custom_call_target="tpu_custom_call" | custom-call | bytes 1048576 | tf_op jit(solution)/shard_map/project/pallas_call | solution.py:392
Async XLA Ops:
  1.0 5.8 %collective-permute-start = (bf16[192,256]{1,0:T(8,128)(2,1)S(1)}, bf16[192,256]{1,0:T(8,128)(2,1)S(1)}, u32[]{:S(2)}, u32[]{:S(2)}) collective-permute-start(bf16[192,256]{1,0:T(8,128)(2,1)S(1)} %get-tuple-element.25), channel_id=1, source_target_pairs={{0,4},{4,0},{8,12},{12,8},{16,20},{20,16},{24,28},{28,24},{1,5},{5... | collective-permute-start | bytes 294920 | tf_op jit(solution)/shard_map/ppermute | solution.py:316
  4.0 7.5 %collective-permute-start.1 = (bf16[192,256]{1,0:T(8,128)(2,1)S(1)}, bf16[192,256]{1,0:T(8,128)(2,1)S(1)}, u32[]{:S(2)}, u32[]{:S(2)}) collective-permute-start(bf16[192,256]{1,0:T(8,128)(2,1)S(1)} %get-tuple-element.26), channel_id=1, source_target_pairs={{4,8},{8,4},{12,16},{16,12},{20,24},{24,20},{5,9},{9,5},{13,17},{1... | collective-permute-start | bytes 294920 | tf_op jit(solution)/shard_map/ppermute | solution.py:334
  6.9 8.8 %collective-permute-start.2 = (bf16[128,256]{1,0:T(8,128)(2,1)S(1)}, bf16[128,256]{1,0:T(8,128)(2,1)S(1)}, u32[]{:S(2)}, u32[]{:S(2)}) collective-permute-start(bf16[128,256]{1,0:T(8,128)(2,1)S(1)} %get-tuple-element.31), channel_id=1, source_target_pairs={{0,24},{4,28},{8,16},{12,20},{16,8},{20,12},{24,0},{28,4},{1,25},{... | collective-permute-start | bytes 196616 | tf_op jit(solution)/shard_map/ppermute | solution.py:316
  10.9 4.8 %collective-permute-start.3 = (bf16[128,256]{1,0:T(8,128)(2,1)S(1)}, bf16[128,256]{1,0:T(8,128)(2,1)S(1)}, u32[]{:S(2)}, u32[]{:S(2)}) collective-permute-start(bf16[128,256]{1,0:T(8,128)(2,1)S(1)} %get-tuple-element.32), channel_id=1, source_target_pairs={{0,8},{4,12},{8,0},{12,4},{16,24},{20,28},{24,16},{28,20},{1,9},{5... | collective-permute-start | bytes 196616 | tf_op jit(solution)/shard_map/ppermute | solution.py:316
  10.9 4.8 %collective-permute-start.4 = (bf16[64,256]{1,0:T(8,128)(2,1)S(1)}, bf16[64,256]{1,0:T(8,128)(2,1)S(1)}, u32[]{:S(2)}, u32[]{:S(2)}) collective-permute-start(bf16[64,256]{1,0:T(8,128)(2,1)S(1)} %get-tuple-element.33), channel_id=1, source_target_pairs={{0,16},{4,20},{8,24},{12,28},{16,0},{20,4},{24,8},{28,12},{1,17},{... | collective-permute-start | bytes 98312 | tf_op jit(solution)/shard_map/ppermute | solution.py:316
  16.3 3.7 %collective-permute-start.6 = (bf16[80,128]{1,0:T(8,128)(2,1)S(1)}, bf16[80,128]{1,0:T(8,128)(2,1)S(1)}, u32[]{:S(2)}, u32[]{:S(2)}) collective-permute-start(bf16[80,128]{1,0:T(8,128)(2,1)S(1)} %get-tuple-element.39), channel_id=1, source_target_pairs={{0,3},{1,2},{2,1},{3,0},{4,7},{5,6},{6,5},{7,4},{8,11},{9,10},{10,... | collective-permute-start | bytes 61448 | tf_op jit(solution)/shard_map/ppermute | solution.py:316
  16.4 3.8 %collective-permute-start.7 = (bf16[80,128]{1,0:T(8,128)(2,1)S(1)}, bf16[80,128]{1,0:T(8,128)(2,1)S(1)}, u32[]{:S(2)}, u32[]{:S(2)}) collective-permute-start(bf16[80,128]{1,0:T(8,128)(2,1)S(1)} %get-tuple-element.40), channel_id=1, source_target_pairs={{0,2},{1,3},{2,0},{3,1},{4,6},{5,7},{6,4},{7,5},{8,10},{9,11},{10,... | collective-permute-start | bytes 61448 | tf_op jit(solution)/shard_map/ppermute | solution.py:316
  18.0 1.8 %copy-start = (bf16[512,512]{1,0:T(8,128)(2,1)S(1)}, bf16[512,512]{1,0:T(8,128)(2,1)}, u32[]{:S(2)}) copy-start(bf16[512,512]{1,0:T(8,128)(2,1)} %weight.3) | copy-start | bytes 1572868
  18.5 1.2 %collective-permute-start.5 = (bf16[64,128]{1,0:T(8,128)(2,1)S(1)}, bf16[64,128]{1,0:T(8,128)(2,1)S(1)}, u32[]{:S(2)}, u32[]{:S(2)}) collective-permute-start(bf16[64,128]{1,0:T(8,128)(2,1)S(1)} %get-tuple-element.38), channel_id=1, source_target_pairs={{0,1},{1,0},{2,3},{3,2},{4,5},{5,4},{6,7},{7,6},{8,9},{9,8},{10,11... | collective-permute-start | bytes 49160 | tf_op jit(solution)/shard_map/ppermute | solution.py:316

commit v12 on v11

--- a/solution.py
+++ b/solution.py
@@ -54,7 +54,7 @@
         quarter[...] = level_two
 
 
-def join_kernel(inner, quarter, block, across, eighth, wide):
+def join_kernel(inner, quarter, upward, downward, eighth, wide):
     me = lax.axis_index("seq")
     odd = me & 1
     edge_half = average_pairs(inner[:LEAF], wide)
@@ -63,13 +63,14 @@
         [jnp.where(odd == 1, other_half, edge_half), jnp.where(odd == 1, edge_half, other_half)], axis=0
     )
     theirs = average_pairs(theirs, wide)
-    block[:HALF] = jnp.where(odd == 1, theirs, quarter[...])
-    block[HALF:] = jnp.where(odd == 1, quarter[...], theirs)
-    level_three = average_pairs(block[...], wide)
+    first = jnp.where(odd == 1, theirs, quarter[...])
+    second = jnp.where(odd == 1, quarter[...], theirs)
+    level_three = average_pairs(jnp.concatenate([first, second], axis=0), wide)
+    upward[:HALF] = jnp.where(me >= 6, level_three, first)
+    upward[HALF:] = second
+    downward[:HALF] = jnp.where(me < 2, level_three, first)
+    downward[HALF:] = second
     eighth[...] = level_three
-    middle = (me >= 2) & (me < 6)
-    across[:HALF] = jnp.where(middle, block[:HALF], level_three)
-    across[HALF:] = block[HALF:]
 
 
 NEAR_ROWS = 4 * LEAF
@@ -130,23 +131,17 @@
     return pieces
 
 
-def paired_pieces(block_6, block_2, eighth_4):
+def paired_pieces(lower, upper, eighth):
     me = lax.axis_index("seq")
     odd = me & 1
-    pair = me >> 1
-    middle = (pair == 1) | (pair == 2)
-    upper_near = (pair & 1) == 0
-    lower = jnp.where(upper_near, block_6[...], block_2[...])
-    upper = jnp.where(upper_near, block_2[...], block_6[...])
-    has_lower, has_upper = pair >= 1, pair <= 2
-    third = jnp.where(odd == 1, lower[HALF:], upper[:HALF])
+    has_lower, has_upper = me >= 2, me < 6
     has_third = ((odd == 1) & has_lower) | ((odd == 0) & has_upper)
     return [
-        (lower[:HALF], bias_of(has_lower)),
+        (lower[:HALF], None),
         (upper[HALF:], bias_of(has_upper)),
-        (third, bias_of(has_third)),
-        (eighth_4[...], bias_of(pair >= 0)),
-        (block_6[:HALF], bias_of(jnp.logical_not(middle))),
+        (jnp.where(odd == 1, lower[HALF:], upper[:HALF]), bias_of(has_third)),
+        (eighth[...], None),
+        (upper[:HALF], bias_of(jnp.logical_not(has_upper))),
     ]
 
 
@@ -333,7 +328,7 @@
     others = [(i, i + 1 if i & 1 else i - 1) for i in range(1, seq_size - 1)]
     outer = lax.ppermute(outer, "seq", others)
     if paired:
-        block, across, eighth = kernel_call(
+        upward, downward, eighth = kernel_call(
             join_kernel,
             "join",
             8,
@@ -341,7 +336,12 @@
             [(LEAF, pair_width), (LEAF, pair_width), (HALF, pair_width)],
             [wide],
         )(inner, quarter)
-        far = (swap(across, 6), swap(block, 2), swap(eighth, 4))
+        shift = [(i, (i + 2) % seq_size) for i in range(seq_size)]
+        far = (
+            lax.ppermute(upward, "seq", shift),
+            lax.ppermute(downward, "seq", [(target, source) for source, target in shift]),
+            swap(eighth, 4),
+        )
     else:
         far = (lax.all_to_all(quarter, "seq", split_axis=0, concat_axis=0),)
     share = tokens // head_size

time: 21.2 us -> 21.5 us (1.014)
  starting transfers between devices: 10.3 us -> 10.6 us
    ppermute x0 -> x2, starting transfers between devices: none -> 4.05 us  [the longest x1 2.09 us: shards(): lax.ppermute(downward, 'seq', [(target, source) for source, target in shi...]
    ppermute x7 -> x5, starting transfers between devices: 9.62 us -> 5.93 us  [swap(): lax.ppermute(array, axis, [(i, i ^ bit) for i in range(lax.axis_size(axis...]
    ppermute x7 -> x5, waiting for transfers between devices: 7.1 us -> 7.09 us  [swap(): lax.ppermute(array, axis, [(i, i ^ bit) for i in range(lax.axis_size(axis...]
where the time goes in v12:
time: 21.5 us; the launch traced here: 21.4 us
  starting transfers between devices  10.6 us (49%)
  waiting for transfers between devices  7.1 us (33%)
  Pallas kernels  3.57 us (17%)
    ppermute x5, waiting for transfers between devices, swap(): lax.ppermute(array, axis, [(i, i ^ bit) for i in range(lax.axis_size(axis...  7.09 us
    ppermute x5, starting transfers between devices, swap(): lax.ppermute(array, axis, [(i, i ^ bit) for i in range(lax.axis_size(axis...  5.93 us
    ppermute x1, starting transfers between devices, shards(): lax.ppermute(downward, 'seq', [(target, source) for source, target in shi...  2.09 us
    ppermute x1, starting transfers between devices, shards(): lax.ppermute(upward, 'seq', shift)  1.96 us
    pallas_call x1, Pallas kernels, shards(): kernel_call(functools.partial(pack_kernel, not paired), 'pack', 16, [HBM]...  0.99 us
    pallas_call x1, Pallas kernels, shards(): kernel_call(project_kernel, 'project', 8, [VMEM] * 4, [(share, out_weight...  0.81 us
    ppermute x1, starting transfers between devices, shards(): outer = lax.ppermute(outer, 'seq', others)  0.65 us
    pallas_call x1, Pallas kernels, shards(): kernel_call(functools.partial(leaves_kernel, seq_size), 'leaves', 24, [VM...  0.58 us
  transfers between devices with their start and end apart: 8, of which 4 were waited for; matrix products, arithmetic and copies ran while one was open for 0% of the time, Pallas kernels for 6%

profile of v12, /device:TPU:0, one launch (start us, length us, event | category | flops | bytes accessed | tf_op | source)
XLA Modules:
  0.0 21.4 jit_solution(450161923052844307)
XLA Ops:
  0.0 1.0 %pack.1 = (bf16[256,128]{1,0:T(8,128)(2,1)S(1)}, bf16[256,256]{1,0:T(8,128)(2,1)S(1)}, bf16[192,256]{1,0:T(8,128)(2,1)S(1)}, bf16[192,256]{1,0:T(8,128)(2,1)S(1)}, bf16[64,256]{1,0:T(8,128)(2,1)S(1)}) custom-call(bf16[256,128]{1,0:T(8,128)(2,1)} %queries.1, bf16[256,128]{1,0:T(8,128)(2,1)} %keys.1, bf16[256,128]{1,0:T(8,128)(2,1)} %values.1), custom_call_target="tpu_custom_call" | custom-call | bytes 1048576 | tf_op jit(solution)/shard_map/pack/pallas_call | solution.py:313
  1.0 3.0 %collective-permute-start = (bf16[192,256]{1,0:T(8,128)(2,1)S(1)}, bf16[192,256]{1,0:T(8,128)(2,1)S(1)}, u32[]{:S(2)}, u32[]{:S(2)}) collective-permute-start(bf16[192,256]{1,0:T(8,128)(2,1)S(1)} %get-tuple-element.25), channel_id=1, source_target_pairs={{0,4},{4,0},{8,12},{12,8},{16,20},{20,16},{24,28},{28,24},{1,5},{5... | collective-permute-start | bytes 294920 | tf_op jit(solution)/shard_map/ppermute | solution.py:311
  4.0 0.7 %collective-permute-start.1 = (bf16[192,256]{1,0:T(8,128)(2,1)S(1)}, bf16[192,256]{1,0:T(8,128)(2,1)S(1)}, u32[]{:S(2)}, u32[]{:S(2)}) collective-permute-start(bf16[192,256]{1,0:T(8,128)(2,1)S(1)} %get-tuple-element.26), channel_id=1, source_target_pairs={{4,8},{8,4},{12,16},{16,12},{20,24},{24,20},{5,9},{9,5},{13,17},{1... | collective-permute-start | bytes 294920 | tf_op jit(solution)/shard_map/ppermute | solution.py:329
  4.7 2.1 %collective-permute-done.inner = bf16[192,256]{1,0:T(8,128)(2,1)S(1)} collective-permute-done((bf16[192,256]{1,0:T(8,128)(2,1)S(1)}, bf16[192,256]{1,0:T(8,128)(2,1)S(1)}, u32[]{:S(2)}, u32[]{:S(2)}) %collective-permute-start) | collective-permute-done | bytes 98336 | tf_op jit(solution)/shard_map/ppermute | solution.py:311
  6.8 0.1 join.1
  6.9 2.0 %collective-permute-start.2 = (bf16[128,256]{1,0:T(8,128)(2,1)S(1)}, bf16[128,256]{1,0:T(8,128)(2,1)S(1)}, u32[]{:S(2)}, u32[]{:S(2)}) collective-permute-start(bf16[128,256]{1,0:T(8,128)(2,1)S(1)} %get-tuple-element.31), channel_id=1, source_target_pairs={{0,8},{4,12},{8,16},{12,20},{16,24},{20,28},{24,0},{28,4},{1,9},{5... | collective-permute-start | bytes 196616 | tf_op jit(solution)/shard_map/ppermute | solution.py:341
  8.8 2.1 %collective-permute-start.3 = (bf16[128,256]{1,0:T(8,128)(2,1)S(1)}, bf16[128,256]{1,0:T(8,128)(2,1)S(1)}, u32[]{:S(2)}, u32[]{:S(2)}) collective-permute-start(bf16[128,256]{1,0:T(8,128)(2,1)S(1)} %get-tuple-element.32), channel_id=1, source_target_pairs={{8,0},{12,4},{16,8},{20,12},{24,16},{28,20},{0,24},{4,28},{9,1},{1... | collective-permute-start | bytes 196616 | tf_op jit(solution)/shard_map/ppermute | solution.py:342
  10.9 0.9 %collective-permute-start.4 = (bf16[64,256]{1,0:T(8,128)(2,1)S(1)}, bf16[64,256]{1,0:T(8,128)(2,1)S(1)}, u32[]{:S(2)}, u32[]{:S(2)}) collective-permute-start(bf16[64,256]{1,0:T(8,128)(2,1)S(1)} %get-tuple-element.33), channel_id=1, source_target_pairs={{0,16},{4,20},{8,24},{12,28},{16,0},{20,4},{24,8},{28,12},{1,17},{... | collective-permute-start | bytes 98312 | tf_op jit(solution)/shard_map/ppermute | solution.py:311
  11.9 0.0 collective-permute-done.1.outer
  11.9 0.4 %near.1 = (f32[2,256,512]{2,1,0:T(8,128)S(1)}, bf16[2,512,128]{2,1,0:T(8,128)(2,1)S(1)}, bf16[64,256]{1,0:T(8,128)(2,1)S(1)}) custom-call(bf16[256,128]{1,0:T(8,128)(2,1)S(1)} %get-tuple-element.23.queries, bf16[256,256]{1,0:T(8,128)(2,1)S(1)} %get-tuple-element.24.own, bf16[192,256]{1,0:T(8,128)(2,1)S(1)} %collective-permute-done.inner, ...), custom_call_target="tpu_custom_call" | custom-call | flops 67108864 | bytes 1048576 | tf_op jit(solution)/shard_map/near/pallas_call | solution.py:348
  12.3 3.8 %collective-permute-done.4.rest_2_ = bf16[64,256]{1,0:T(8,128)(2,1)S(1)} collective-permute-done((bf16[64,256]{1,0:T(8,128)(2,1)S(1)}, bf16[64,256]{1,0:T(8,128)(2,1)S(1)}, u32[]{:S(2)}, u32[]{:S(2)}) %collective-permute-start.4) | collective-permute-done | bytes 32800 | tf_op jit(solution)/shard_map/ppermute | solution.py:311
  16.0 0.0 collective-permute-done.2.rest_0_
  16.1 0.0 collective-permute-done.3.rest_1_
  16.1 0.6 %leaves.1 = (bf16[80,128]{1,0:T(8,128)(2,1)S(1)}, bf16[80,128]{1,0:T(8,128)(2,1)S(1)}, bf16[384,128]{1,0:T(8,128)(2,1)S(1)}, bf16[384,128]{1,0:T(8,128)(2,1)S(1)}, f32[8,384]{1,0:T(8,128)S(1)}) custom-call(bf16[256,128]{1,0:T(8,128)(2,1)S(1)} %get-tuple-element.23.queries, f32[2,256,512]{2,1,0:T(8,128)S(1)} %get-tuple-element.27.near_scores, ...), custom_call_target="tpu_custom_call" | custom-call | flops 117440512 | bytes 1048576 | tf_op jit(solution)/shard_map/leaves/pallas_call | solution.py:364
  16.6 0.1 collective-permute-start.6
  16.7 1.6 %collective-permute-start.7 = (bf16[80,128]{1,0:T(8,128)(2,1)S(1)}, bf16[80,128]{1,0:T(8,128)(2,1)S(1)}, u32[]{:S(2)}, u32[]{:S(2)}) collective-permute-start(bf16[80,128]{1,0:T(8,128)(2,1)S(1)} %get-tuple-element.40), channel_id=1, source_target_pairs={{0,2},{1,3},{2,0},{3,1},{4,6},{5,7},{6,4},{7,5},{8,10},{9,11},{10,... | collective-permute-start | bytes 61448 | tf_op jit(solution)/shard_map/ppermute | solution.py:311
  18.3 0.0 copy-start
  18.3 0.6 %stays.1 = (bf16[64,128]{1,0:T(8,128)(2,1)S(1)}, bf16[64,128]{1,0:T(8,128)(2,1)S(1)}) custom-call(bf16[256,128]{1,0:T(8,128)(2,1)S(1)} %get-tuple-element.23.queries, f32[2,256,512]{2,1,0:T(8,128)S(1)} %get-tuple-element.27.near_scores, bf16[2,512,128]{2,1,0:T(8,128)(2,1)S(1)} %get-tuple-element.28.near_values, bf16[384,128]{1,0:T(8,128)(2,1)S(1)} %get-tuple-element.34.keys, ...), custom_call_target="tpu_custom_call" | custom-call | flops 117440512 | bytes 1048576 | tf_op jit(solution)/shard_map/stays/pallas_call | solution.py:379
  18.9 0.3 %collective-permute-start.5 = (bf16[64,128]{1,0:T(8,128)(2,1)S(1)}, bf16[64,128]{1,0:T(8,128)(2,1)S(1)}, u32[]{:S(2)}, u32[]{:S(2)}) collective-permute-start(bf16[64,128]{1,0:T(8,128)(2,1)S(1)} %get-tuple-element.38), channel_id=1, source_target_pairs={{0,1},{1,0},{2,3},{3,2},{4,5},{5,4},{6,7},{7,6},{8,9},{9,8},{10,11... | collective-permute-start | bytes 49160 | tf_op jit(solution)/shard_map/ppermute | solution.py:311
  19.2 0.9 %collective-permute-done.5.other = bf16[64,128]{1,0:T(8,128)(2,1)S(1)} collective-permute-done((bf16[64,128]{1,0:T(8,128)(2,1)S(1)}, bf16[64,128]{1,0:T(8,128)(2,1)S(1)}, u32[]{:S(2)}, u32[]{:S(2)}) %collective-permute-start.5) | collective-permute-done | bytes 16416 | tf_op jit(solution)/shard_map/ppermute | solution.py:311
  20.1 0.0 copy-done
  20.1 0.2 begin.1.partial
  20.3 0.0 collective-permute-done.6.other
  20.3 0.3 %collective-permute-done.7.same = bf16[80,128]{1,0:T(8,128)(2,1)S(1)} collective-permute-done((bf16[80,128]{1,0:T(8,128)(2,1)S(1)}, bf16[80,128]{1,0:T(8,128)(2,1)S(1)}, u32[]{:S(2)}, u32[]{:S(2)}) %collective-permute-start.7) | collective-permute-done | bytes 20512 | tf_op jit(solution)/shard_map/ppermute | solution.py:311
  20.6 0.8 %project.1 = bf16[64,512]{1,0:T(8,128)(2,1)} custom-call(f32[64,512]{1,0:T(8,128)S(1)} %begin.1.partial, bf16[80,128]{1,0:T(8,128)(2,1)S(1)} %collective-permute-done.6.other, bf16[80,128]{1,0:T(8,128)(2,1)S(1)} %collective-permute-done.7.same, bf16[512,512]{1,0:T(8,128)(2,1)S(1)} %copy-done), custom_call_target="tpu_custom_call" | custom-call | bytes 1048576 | tf_op jit(solution)/shard_map/project/pallas_call | solution.py:392
Async XLA Ops:
  1.0 5.8 %collective-permute-start = (bf16[192,256]{1,0:T(8,128)(2,1)S(1)}, bf16[192,256]{1,0:T(8,128)(2,1)S(1)}, u32[]{:S(2)}, u32[]{:S(2)}) collective-permute-start(bf16[192,256]{1,0:T(8,128)(2,1)S(1)} %get-tuple-element.25), channel_id=1, source_target_pairs={{0,4},{4,0},{8,12},{12,8},{16,20},{20,16},{24,28},{28,24},{1,5},{5... | collective-permute-start | bytes 294920 | tf_op jit(solution)/shard_map/ppermute | solution.py:311
  4.0 7.9 %collective-permute-start.1 = (bf16[192,256]{1,0:T(8,128)(2,1)S(1)}, bf16[192,256]{1,0:T(8,128)(2,1)S(1)}, u32[]{:S(2)}, u32[]{:S(2)}) collective-permute-start(bf16[192,256]{1,0:T(8,128)(2,1)S(1)} %get-tuple-element.26), channel_id=1, source_target_pairs={{4,8},{8,4},{12,16},{16,12},{20,24},{24,20},{5,9},{9,5},{13,17},{1... | collective-permute-start | bytes 294920 | tf_op jit(solution)/shard_map/ppermute | solution.py:329
  6.9 9.2 %collective-permute-start.2 = (bf16[128,256]{1,0:T(8,128)(2,1)S(1)}, bf16[128,256]{1,0:T(8,128)(2,1)S(1)}, u32[]{:S(2)}, u32[]{:S(2)}) collective-permute-start(bf16[128,256]{1,0:T(8,128)(2,1)S(1)} %get-tuple-element.31), channel_id=1, source_target_pairs={{0,8},{4,12},{8,16},{12,20},{16,24},{20,28},{24,0},{28,4},{1,9},{5... | collective-permute-start | bytes 196616 | tf_op jit(solution)/shard_map/ppermute | solution.py:341
  8.8 7.2 %collective-permute-start.3 = (bf16[128,256]{1,0:T(8,128)(2,1)S(1)}, bf16[128,256]{1,0:T(8,128)(2,1)S(1)}, u32[]{:S(2)}, u32[]{:S(2)}) collective-permute-start(bf16[128,256]{1,0:T(8,128)(2,1)S(1)} %get-tuple-element.32), channel_id=1, source_target_pairs={{8,0},{12,4},{16,8},{20,12},{24,16},{28,20},{0,24},{4,28},{9,1},{1... | collective-permute-start | bytes 196616 | tf_op jit(solution)/shard_map/ppermute | solution.py:342
  10.9 5.1 %collective-permute-start.4 = (bf16[64,256]{1,0:T(8,128)(2,1)S(1)}, bf16[64,256]{1,0:T(8,128)(2,1)S(1)}, u32[]{:S(2)}, u32[]{:S(2)}) collective-permute-start(bf16[64,256]{1,0:T(8,128)(2,1)S(1)} %get-tuple-element.33), channel_id=1, source_target_pairs={{0,16},{4,20},{8,24},{12,28},{16,0},{20,4},{24,8},{28,12},{1,17},{... | collective-permute-start | bytes 98312 | tf_op jit(solution)/shard_map/ppermute | solution.py:311
  16.6 3.7 %collective-permute-start.6 = (bf16[80,128]{1,0:T(8,128)(2,1)S(1)}, bf16[80,128]{1,0:T(8,128)(2,1)S(1)}, u32[]{:S(2)}, u32[]{:S(2)}) collective-permute-start(bf16[80,128]{1,0:T(8,128)(2,1)S(1)} %get-tuple-element.39), channel_id=1, source_target_pairs={{0,3},{1,2},{2,1},{3,0},{4,7},{5,6},{6,5},{7,4},{8,11},{9,10},{10,... | collective-permute-start | bytes 61448 | tf_op jit(solution)/shard_map/ppermute | solution.py:311
  16.7 3.8 %collective-permute-start.7 = (bf16[80,128]{1,0:T(8,128)(2,1)S(1)}, bf16[80,128]{1,0:T(8,128)(2,1)S(1)}, u32[]{:S(2)}, u32[]{:S(2)}) collective-permute-start(bf16[80,128]{1,0:T(8,128)(2,1)S(1)} %get-tuple-element.40), channel_id=1, source_target_pairs={{0,2},{1,3},{2,0},{3,1},{4,6},{5,7},{6,4},{7,5},{8,10},{9,11},{10,... | collective-permute-start | bytes 61448 | tf_op jit(solution)/shard_map/ppermute | solution.py:311
  18.3 1.8 %copy-start = (bf16[512,512]{1,0:T(8,128)(2,1)S(1)}, bf16[512,512]{1,0:T(8,128)(2,1)}, u32[]{:S(2)}) copy-start(bf16[512,512]{1,0:T(8,128)(2,1)} %weight.3) | copy-start | bytes 1572868
  18.9 1.2 %collective-permute-start.5 = (bf16[64,128]{1,0:T(8,128)(2,1)S(1)}, bf16[64,128]{1,0:T(8,128)(2,1)S(1)}, u32[]{:S(2)}, u32[]{:S(2)}) collective-permute-start(bf16[64,128]{1,0:T(8,128)(2,1)S(1)} %get-tuple-element.38), channel_id=1, source_target_pairs={{0,1},{1,0},{2,3},{3,2},{4,5},{5,4},{6,7},{7,6},{8,9},{9,8},{10,11... | collective-permute-start | bytes 49160 | tf_op jit(solution)/shard_map/ppermute | solution.py:311

commit v13 on v12

--- a/solution.py
+++ b/solution.py
@@ -54,7 +54,7 @@
         quarter[...] = level_two
 
 
-def join_kernel(inner, quarter, upward, downward, eighth, wide):
+def join_kernel(inner, quarter, upward, block, eighth, wide):
     me = lax.axis_index("seq")
     odd = me & 1
     edge_half = average_pairs(inner[:LEAF], wide)
@@ -68,8 +68,8 @@
     level_three = average_pairs(jnp.concatenate([first, second], axis=0), wide)
     upward[:HALF] = jnp.where(me >= 6, level_three, first)
     upward[HALF:] = second
-    downward[:HALF] = jnp.where(me < 2, level_three, first)
-    downward[HALF:] = second
+    block[:HALF] = first
+    block[HALF:] = second
     eighth[...] = level_three
 
 
@@ -131,7 +131,7 @@
     return pieces
 
 
-def paired_pieces(lower, upper, eighth):
+def paired_pieces(lower, upper, eighth, first_eighth):
     me = lax.axis_index("seq")
     odd = me & 1
     has_lower, has_upper = me >= 2, me < 6
@@ -141,7 +141,7 @@
         (upper[HALF:], bias_of(has_upper)),
         (jnp.where(odd == 1, lower[HALF:], upper[:HALF]), bias_of(has_third)),
         (eighth[...], None),
-        (upper[:HALF], bias_of(jnp.logical_not(has_upper))),
+        (first_eighth[...], bias_of(jnp.logical_not(has_upper))),
     ]
 
 
@@ -328,7 +328,7 @@
     others = [(i, i + 1 if i & 1 else i - 1) for i in range(1, seq_size - 1)]
     outer = lax.ppermute(outer, "seq", others)
     if paired:
-        upward, downward, eighth = kernel_call(
+        upward, block, eighth = kernel_call(
             join_kernel,
             "join",
             8,
@@ -336,11 +336,11 @@
             [(LEAF, pair_width), (LEAF, pair_width), (HALF, pair_width)],
             [wide],
         )(inner, quarter)
-        shift = [(i, (i + 2) % seq_size) for i in range(seq_size)]
         far = (
-            lax.ppermute(upward, "seq", shift),
-            lax.ppermute(downward, "seq", [(target, source) for source, target in shift]),
+            lax.ppermute(upward, "seq", [(i, (i + 2) % seq_size) for i in range(seq_size)]),
+            lax.ppermute(block, "seq", [(i + 2, i) for i in range(seq_size - 2)]),
             swap(eighth, 4),
+            lax.ppermute(eighth, "seq", [(i, i + 6) for i in range(2)]),
         )
     else:
         far = (lax.all_to_all(quarter, "seq", split_axis=0, concat_axis=0),)

time: 21.5 us -> 24.2 us (1.13)
  starting transfers between devices: 10.6 us -> 15.8 us
  waiting for transfers between devices: 7.1 us -> 4.49 us
    ppermute x5, waiting for transfers between devices: 7.09 us -> 3.31 us  [swap(): lax.ppermute(array, axis, [(i, i ^ bit) for i in range(lax.axis_size(axis...]
    ppermute x5, starting transfers between devices: 5.93 us -> 8.71 us  [swap(): lax.ppermute(array, axis, [(i, i ^ bit) for i in range(lax.axis_size(axis...]
    ppermute x2 -> x3, starting transfers between devices: 4.05 us -> 6.48 us  [the longest x1 3.24 us: shards(): lax.ppermute(eighth, 'seq', [(i, i + 6) for i in range(2)])]
    ppermute x2 -> x3, waiting for transfers between devices: 0.01 us -> 1.17 us  [the longest x1 1.17 us: shards(): lax.ppermute(eighth, 'seq', [(i, i + 6) for i in range(2)])]
  transfers between devices with their start and end apart: 8 -> 9, of which waited for: 4 -> 4; matrix products, arithmetic and copies ran while one was open for 0% -> 0% of each run, Pallas kernels for 6% -> 5%
where the time goes in v13:
time: 24.2 us; the launch traced here: 24 us
  starting transfers between devices  15.8 us (65%)
  waiting for transfers between devices  4.49 us (19%)
  Pallas kernels  3.57 us (15%)
    ppermute x5, starting transfers between devices, swap(): lax.ppermute(array, axis, [(i, i ^ bit) for i in range(lax.axis_size(axis...  8.71 us
    ppermute x5, waiting for transfers between devices, swap(): lax.ppermute(array, axis, [(i, i ^ bit) for i in range(lax.axis_size(axis...  3.31 us
    ppermute x1, starting transfers between devices, shards(): lax.ppermute(eighth, 'seq', [(i, i + 6) for i in range(2)])  3.24 us
    ppermute x1, starting transfers between devices, shards(): lax.ppermute(upward, 'seq', [(i, (i + 2) % seq_size) for i in range(seq_s...  1.96 us
    ppermute x1, starting transfers between devices, shards(): lax.ppermute(block, 'seq', [(i + 2, i) for i in range(seq_size - 2)])  1.28 us
    ppermute x1, waiting for transfers between devices, shards(): lax.ppermute(eighth, 'seq', [(i, i + 6) for i in range(2)])  1.17 us
    pallas_call x1, Pallas kernels, shards(): kernel_call(functools.partial(pack_kernel, not paired), 'pack', 16, [HBM]...  0.99 us
    pallas_call x1, Pallas kernels, shards(): kernel_call(project_kernel, 'project', 8, [VMEM] * 4, [(share, out_weight...  0.81 us
  transfers between devices with their start and end apart: 9, of which 4 were waited for; matrix products, arithmetic and copies ran while one was open for 0% of the time, Pallas kernels for 5%

profile of v13, /device:TPU:0, one launch (start us, length us, event | category | flops | bytes accessed | tf_op | source)
XLA Modules:
  0.0 24.0 jit_solution(2136503656716234831)
XLA Ops:
  0.0 1.0 %pack.1 = (bf16[256,128]{1,0:T(8,128)(2,1)S(1)}, bf16[256,256]{1,0:T(8,128)(2,1)S(1)}, bf16[192,256]{1,0:T(8,128)(2,1)S(1)}, bf16[192,256]{1,0:T(8,128)(2,1)S(1)}, bf16[64,256]{1,0:T(8,128)(2,1)S(1)}) custom-call(bf16[256,128]{1,0:T(8,128)(2,1)} %queries.1, bf16[256,128]{1,0:T(8,128)(2,1)} %keys.1, bf16[256,128]{1,0:T(8,128)(2,1)} %values.1), custom_call_target="tpu_custom_call" | custom-call | bytes 1048576 | tf_op jit(solution)/shard_map/pack/pallas_call | solution.py:313
  1.0 3.0 %collective-permute-start = (bf16[192,256]{1,0:T(8,128)(2,1)S(1)}, bf16[192,256]{1,0:T(8,128)(2,1)S(1)}, u32[]{:S(2)}, u32[]{:S(2)}) collective-permute-start(bf16[192,256]{1,0:T(8,128)(2,1)S(1)} %get-tuple-element.25), channel_id=1, source_target_pairs={{0,4},{4,0},{8,12},{12,8},{16,20},{20,16},{24,28},{28,24},{1,5},{5... | collective-permute-start | bytes 294920 | tf_op jit(solution)/shard_map/ppermute | solution.py:311
  4.0 0.7 %collective-permute-start.1 = (bf16[192,256]{1,0:T(8,128)(2,1)S(1)}, bf16[192,256]{1,0:T(8,128)(2,1)S(1)}, u32[]{:S(2)}, u32[]{:S(2)}) collective-permute-start(bf16[192,256]{1,0:T(8,128)(2,1)S(1)} %get-tuple-element.26), channel_id=1, source_target_pairs={{4,8},{8,4},{12,16},{16,12},{20,24},{24,20},{5,9},{9,5},{13,17},{1... | collective-permute-start | bytes 294920 | tf_op jit(solution)/shard_map/ppermute | solution.py:329
  4.7 2.1 %collective-permute-done.inner = bf16[192,256]{1,0:T(8,128)(2,1)S(1)} collective-permute-done((bf16[192,256]{1,0:T(8,128)(2,1)S(1)}, bf16[192,256]{1,0:T(8,128)(2,1)S(1)}, u32[]{:S(2)}, u32[]{:S(2)}) %collective-permute-start) | collective-permute-done | bytes 98336 | tf_op jit(solution)/shard_map/ppermute | solution.py:311
  6.8 0.1 join.1
  6.9 2.0 %collective-permute-start.2 = (bf16[128,256]{1,0:T(8,128)(2,1)S(1)}, bf16[128,256]{1,0:T(8,128)(2,1)S(1)}, u32[]{:S(2)}, u32[]{:S(2)}) collective-permute-start(bf16[128,256]{1,0:T(8,128)(2,1)S(1)} %get-tuple-element.31), channel_id=1, source_target_pairs={{0,8},{4,12},{8,16},{12,20},{16,24},{20,28},{24,0},{28,4},{1,9},{5... | collective-permute-start | bytes 196616 | tf_op jit(solution)/shard_map/ppermute | solution.py:340
  8.8 1.3 %collective-permute-start.3 = (bf16[128,256]{1,0:T(8,128)(2,1)S(1)}, bf16[128,256]{1,0:T(8,128)(2,1)S(1)}, u32[]{:S(2)}, u32[]{:S(2)}) collective-permute-start(bf16[128,256]{1,0:T(8,128)(2,1)S(1)} %get-tuple-element.32), channel_id=1, source_target_pairs={{8,0},{12,4},{16,8},{20,12},{24,16},{28,20},{9,1},{13,5},{17,9},{2... | collective-permute-start | bytes 196616 | tf_op jit(solution)/shard_map/ppermute | solution.py:341
  10.1 3.7 %collective-permute-start.4 = (bf16[64,256]{1,0:T(8,128)(2,1)S(1)}, bf16[64,256]{1,0:T(8,128)(2,1)S(1)}, u32[]{:S(2)}, u32[]{:S(2)}) collective-permute-start(bf16[64,256]{1,0:T(8,128)(2,1)S(1)} %get-tuple-element.33), channel_id=1, source_target_pairs={{0,16},{4,20},{8,24},{12,28},{16,0},{20,4},{24,8},{28,12},{1,17},{... | collective-permute-start | bytes 98312 | tf_op jit(solution)/shard_map/ppermute | solution.py:311
  13.8 3.2 %collective-permute-start.5 = (bf16[64,256]{1,0:T(8,128)(2,1)S(1)}, bf16[64,256]{1,0:T(8,128)(2,1)S(1)}, u32[]{:S(2)}, u32[]{:S(2)}) collective-permute-start(bf16[64,256]{1,0:T(8,128)(2,1)S(1)} %get-tuple-element.33), channel_id=1, source_target_pairs={{0,24},{4,28},{1,25},{5,29},{2,26},{6,30},{3,27},{7,31}} | collective-permute-start | bytes 98312 | tf_op jit(solution)/shard_map/ppermute | solution.py:343
  17.1 0.0 collective-permute-done.1.outer
  17.1 0.4 %near.1 = (f32[2,256,512]{2,1,0:T(8,128)S(1)}, bf16[2,512,128]{2,1,0:T(8,128)(2,1)S(1)}, bf16[64,256]{1,0:T(8,128)(2,1)S(1)}) custom-call(bf16[256,128]{1,0:T(8,128)(2,1)S(1)} %get-tuple-element.23.queries, bf16[256,256]{1,0:T(8,128)(2,1)S(1)} %get-tuple-element.24.own, bf16[192,256]{1,0:T(8,128)(2,1)S(1)} %collective-permute-done.inner, ...), custom_call_target="tpu_custom_call" | custom-call | flops 67108864 | bytes 1048576 | tf_op jit(solution)/shard_map/near/pallas_call | solution.py:348
  17.5 0.0 collective-permute-done.4.rest_2_
  17.5 1.2 %collective-permute-done.5.rest_3_ = bf16[64,256]{1,0:T(8,128)(2,1)S(1)} collective-permute-done((bf16[64,256]{1,0:T(8,128)(2,1)S(1)}, bf16[64,256]{1,0:T(8,128)(2,1)S(1)}, u32[]{:S(2)}, u32[]{:S(2)}) %collective-permute-start.5) | collective-permute-done | bytes 32800 | tf_op jit(solution)/shard_map/ppermute | solution.py:343
  18.7 0.0 collective-permute-done.2.rest_0_
  18.7 0.0 collective-permute-done.3.rest_1_
  18.7 0.6 %leaves.1 = (bf16[80,128]{1,0:T(8,128)(2,1)S(1)}, bf16[80,128]{1,0:T(8,128)(2,1)S(1)}, bf16[384,128]{1,0:T(8,128)(2,1)S(1)}, bf16[384,128]{1,0:T(8,128)(2,1)S(1)}, f32[8,384]{1,0:T(8,128)S(1)}) custom-call(bf16[256,128]{1,0:T(8,128)(2,1)S(1)} %get-tuple-element.23.queries, f32[2,256,512]{2,1,0:T(8,128)S(1)} %get-tuple-element.27.near_scores, ...), custom_call_target="tpu_custom_call" | custom-call | flops 117440512 | bytes 1048576 | tf_op jit(solution)/shard_map/leaves/pallas_call | solution.py:364
  19.3 0.1 collective-permute-start.7
  19.3 1.6 %collective-permute-start.8 = (bf16[80,128]{1,0:T(8,128)(2,1)S(1)}, bf16[80,128]{1,0:T(8,128)(2,1)S(1)}, u32[]{:S(2)}, u32[]{:S(2)}) collective-permute-start(bf16[80,128]{1,0:T(8,128)(2,1)S(1)} %get-tuple-element.40), channel_id=1, source_target_pairs={{0,2},{1,3},{2,0},{3,1},{4,6},{5,7},{6,4},{7,5},{8,10},{9,11},{10,... | collective-permute-start | bytes 61448 | tf_op jit(solution)/shard_map/ppermute | solution.py:311
  20.9 0.0 copy-start
  20.9 0.6 %stays.1 = (bf16[64,128]{1,0:T(8,128)(2,1)S(1)}, bf16[64,128]{1,0:T(8,128)(2,1)S(1)}) custom-call(bf16[256,128]{1,0:T(8,128)(2,1)S(1)} %get-tuple-element.23.queries, f32[2,256,512]{2,1,0:T(8,128)S(1)} %get-tuple-element.27.near_scores, bf16[2,512,128]{2,1,0:T(8,128)(2,1)S(1)} %get-tuple-element.28.near_values, bf16[384,128]{1,0:T(8,128)(2,1)S(1)} %get-tuple-element.34.keys, ...), custom_call_target="tpu_custom_call" | custom-call | flops 117440512 | bytes 1048576 | tf_op jit(solution)/shard_map/stays/pallas_call | solution.py:379
  21.5 0.3 %collective-permute-start.6 = (bf16[64,128]{1,0:T(8,128)(2,1)S(1)}, bf16[64,128]{1,0:T(8,128)(2,1)S(1)}, u32[]{:S(2)}, u32[]{:S(2)}) collective-permute-start(bf16[64,128]{1,0:T(8,128)(2,1)S(1)} %get-tuple-element.38), channel_id=1, source_target_pairs={{0,1},{1,0},{2,3},{3,2},{4,5},{5,4},{6,7},{7,6},{8,9},{9,8},{10,11... | collective-permute-start | bytes 49160 | tf_op jit(solution)/shard_map/ppermute | solution.py:311
  21.8 0.9 %collective-permute-done.6.other = bf16[64,128]{1,0:T(8,128)(2,1)S(1)} collective-permute-done((bf16[64,128]{1,0:T(8,128)(2,1)S(1)}, bf16[64,128]{1,0:T(8,128)(2,1)S(1)}, u32[]{:S(2)}, u32[]{:S(2)}) %collective-permute-start.6) | collective-permute-done | bytes 16416 | tf_op jit(solution)/shard_map/ppermute | solution.py:311
  22.8 0.0 copy-done
  22.8 0.2 begin.1.partial
  22.9 0.0 collective-permute-done.7.other
  22.9 0.3 %collective-permute-done.8.same = bf16[80,128]{1,0:T(8,128)(2,1)S(1)} collective-permute-done((bf16[80,128]{1,0:T(8,128)(2,1)S(1)}, bf16[80,128]{1,0:T(8,128)(2,1)S(1)}, u32[]{:S(2)}, u32[]{:S(2)}) %collective-permute-start.8) | collective-permute-done | bytes 20512 | tf_op jit(solution)/shard_map/ppermute | solution.py:311
  23.2 0.8 %project.1 = bf16[64,512]{1,0:T(8,128)(2,1)} custom-call(f32[64,512]{1,0:T(8,128)S(1)} %begin.1.partial, bf16[80,128]{1,0:T(8,128)(2,1)S(1)} %collective-permute-done.7.other, bf16[80,128]{1,0:T(8,128)(2,1)S(1)} %collective-permute-done.8.same, bf16[512,512]{1,0:T(8,128)(2,1)S(1)} %copy-done), custom_call_target="tpu_custom_call" | custom-call | bytes 1048576 | tf_op jit(solution)/shard_map/project/pallas_call | solution.py:392
Async XLA Ops:
  1.0 5.8 %collective-permute-start = (bf16[192,256]{1,0:T(8,128)(2,1)S(1)}, bf16[192,256]{1,0:T(8,128)(2,1)S(1)}, u32[]{:S(2)}, u32[]{:S(2)}) collective-permute-start(bf16[192,256]{1,0:T(8,128)(2,1)S(1)} %get-tuple-element.25), channel_id=1, source_target_pairs={{0,4},{4,0},{8,12},{12,8},{16,20},{20,16},{24,28},{28,24},{1,5},{5... | collective-permute-start | bytes 294920 | tf_op jit(solution)/shard_map/ppermute | solution.py:311
  4.0 13.1 %collective-permute-start.1 = (bf16[192,256]{1,0:T(8,128)(2,1)S(1)}, bf16[192,256]{1,0:T(8,128)(2,1)S(1)}, u32[]{:S(2)}, u32[]{:S(2)}) collective-permute-start(bf16[192,256]{1,0:T(8,128)(2,1)S(1)} %get-tuple-element.26), channel_id=1, source_target_pairs={{4,8},{8,4},{12,16},{16,12},{20,24},{24,20},{5,9},{9,5},{13,17},{1... | collective-permute-start | bytes 294920 | tf_op jit(solution)/shard_map/ppermute | solution.py:329
  6.9 11.8 %collective-permute-start.2 = (bf16[128,256]{1,0:T(8,128)(2,1)S(1)}, bf16[128,256]{1,0:T(8,128)(2,1)S(1)}, u32[]{:S(2)}, u32[]{:S(2)}) collective-permute-start(bf16[128,256]{1,0:T(8,128)(2,1)S(1)} %get-tuple-element.31), channel_id=1, source_target_pairs={{0,8},{4,12},{8,16},{12,20},{16,24},{20,28},{24,0},{28,4},{1,9},{5... | collective-permute-start | bytes 196616 | tf_op jit(solution)/shard_map/ppermute | solution.py:340
  8.8 9.8 %collective-permute-start.3 = (bf16[128,256]{1,0:T(8,128)(2,1)S(1)}, bf16[128,256]{1,0:T(8,128)(2,1)S(1)}, u32[]{:S(2)}, u32[]{:S(2)}) collective-permute-start(bf16[128,256]{1,0:T(8,128)(2,1)S(1)} %get-tuple-element.32), channel_id=1, source_target_pairs={{8,0},{12,4},{16,8},{20,12},{24,16},{28,20},{9,1},{13,5},{17,9},{2... | collective-permute-start | bytes 196616 | tf_op jit(solution)/shard_map/ppermute | solution.py:341
  10.1 7.4 %collective-permute-start.4 = (bf16[64,256]{1,0:T(8,128)(2,1)S(1)}, bf16[64,256]{1,0:T(8,128)(2,1)S(1)}, u32[]{:S(2)}, u32[]{:S(2)}) collective-permute-start(bf16[64,256]{1,0:T(8,128)(2,1)S(1)} %get-tuple-element.33), channel_id=1, source_target_pairs={{0,16},{4,20},{8,24},{12,28},{16,0},{20,4},{24,8},{28,12},{1,17},{... | collective-permute-start | bytes 98312 | tf_op jit(solution)/shard_map/ppermute | solution.py:311
  13.8 4.8 %collective-permute-start.5 = (bf16[64,256]{1,0:T(8,128)(2,1)S(1)}, bf16[64,256]{1,0:T(8,128)(2,1)S(1)}, u32[]{:S(2)}, u32[]{:S(2)}) collective-permute-start(bf16[64,256]{1,0:T(8,128)(2,1)S(1)} %get-tuple-element.33), channel_id=1, source_target_pairs={{0,24},{4,28},{1,25},{5,29},{2,26},{6,30},{3,27},{7,31}} | collective-permute-start | bytes 98312 | tf_op jit(solution)/shard_map/ppermute | solution.py:343
  19.3 3.7 %collective-permute-start.7 = (bf16[80,128]{1,0:T(8,128)(2,1)S(1)}, bf16[80,128]{1,0:T(8,128)(2,1)S(1)}, u32[]{:S(2)}, u32[]{:S(2)}) collective-permute-start(bf16[80,128]{1,0:T(8,128)(2,1)S(1)} %get-tuple-element.39), channel_id=1, source_target_pairs={{0,3},{1,2},{2,1},{3,0},{4,7},{5,6},{6,5},{7,4},{8,11},{9,10},{10,... | collective-permute-start | bytes 61448 | tf_op jit(solution)/shard_map/ppermute | solution.py:311
  19.3 3.8 %collective-permute-start.8 = (bf16[80,128]{1,0:T(8,128)(2,1)S(1)}, bf16[80,128]{1,0:T(8,128)(2,1)S(1)}, u32[]{:S(2)}, u32[]{:S(2)}) collective-permute-start(bf16[80,128]{1,0:T(8,128)(2,1)S(1)} %get-tuple-element.40), channel_id=1, source_target_pairs={{0,2},{1,3},{2,0},{3,1},{4,6},{5,7},{6,4},{7,5},{8,10},{9,11},{10,... | collective-permute-start | bytes 61448 | tf_op jit(solution)/shard_map/ppermute | solution.py:311
  20.9 1.8 %copy-start = (bf16[512,512]{1,0:T(8,128)(2,1)S(1)}, bf16[512,512]{1,0:T(8,128)(2,1)}, u32[]{:S(2)}) copy-start(bf16[512,512]{1,0:T(8,128)(2,1)} %weight.3) | copy-start | bytes 1572868
  21.5 1.2 %collective-permute-start.6 = (bf16[64,128]{1,0:T(8,128)(2,1)S(1)}, bf16[64,128]{1,0:T(8,128)(2,1)S(1)}, u32[]{:S(2)}, u32[]{:S(2)}) collective-permute-start(bf16[64,128]{1,0:T(8,128)(2,1)S(1)} %get-tuple-element.38), channel_id=1, source_target_pairs={{0,1},{1,0},{2,3},{3,2},{4,5},{5,4},{6,7},{7,6},{8,9},{9,8},{10,11... | collective-permute-start | bytes 49160 | tf_op jit(solution)/shard_map/ppermute | solution.py:311

commit v14 on v11

--- a/solution.py
+++ b/solution.py
@@ -330,7 +330,8 @@
         [wide, pltpu.SemaphoreType.DMA((3,))],
     )(*(pltpu.with_memory_space_constraint(array, pltpu.HBM) for array in (queries, keys, values)))
     inner = swap(inner, 1)
-    others = [(i, i + 1 if i & 1 else i - 1) for i in range(1, seq_size - 1)]
+    ends = [(i, i) for i in (0, seq_size - 1)]
+    others = ends + [(i, i + 1 if i & 1 else i - 1) for i in range(1, seq_size - 1)]
     outer = lax.ppermute(outer, "seq", others)
     if paired:
         block, across, eighth = kernel_call(

time: 21.2 us -> 21.2 us (level)
  no operation moved by 1% of the time
where the time goes in v14:
time: 21.2 us; the launch traced here: 21 us
  starting transfers between devices  10.3 us (49%)
  waiting for transfers between devices  7.1 us (33%)
  Pallas kernels  3.58 us (17%)
    ppermute x7, starting transfers between devices, swap(): lax.ppermute(array, axis, [(i, i ^ bit) for i in range(lax.axis_size(axis...  9.62 us
    ppermute x7, waiting for transfers between devices, swap(): lax.ppermute(array, axis, [(i, i ^ bit) for i in range(lax.axis_size(axis...  7.1 us
    pallas_call x1, Pallas kernels, shards(): kernel_call(functools.partial(pack_kernel, not paired), 'pack', 16, [HBM]...  0.99 us
    pallas_call x1, Pallas kernels, shards(): kernel_call(project_kernel, 'project', 8, [VMEM] * 4, [(share, out_weight...  0.81 us
    ppermute x1, starting transfers between devices, shards(): outer = lax.ppermute(outer, 'seq', others)  0.65 us
    pallas_call x1, Pallas kernels, shards(): kernel_call(functools.partial(leaves_kernel, seq_size), 'leaves', 24, [VM...  0.59 us
    pallas_call x1, Pallas kernels, shards(): kernel_call(stays_kernel, 'stays', 16, [VMEM] * 6, [(share, width)] * 2,...  0.57 us
  transfers between devices with their start and end apart: 8, of which 4 were waited for; matrix products, arithmetic and copies ran while one was open for 0% of the time, Pallas kernels for 6%

profile of v14, /device:TPU:0, one launch (start us, length us, event | category | flops | bytes accessed | tf_op | source)
XLA Modules:
  0.0 21.0 jit_solution(11294960422036588964)
XLA Ops:
  0.0 1.0 %pack.1 = (bf16[256,128]{1,0:T(8,128)(2,1)S(1)}, bf16[256,256]{1,0:T(8,128)(2,1)S(1)}, bf16[192,256]{1,0:T(8,128)(2,1)S(1)}, bf16[192,256]{1,0:T(8,128)(2,1)S(1)}, bf16[64,256]{1,0:T(8,128)(2,1)S(1)}) custom-call(bf16[256,128]{1,0:T(8,128)(2,1)} %queries.1, bf16[256,128]{1,0:T(8,128)(2,1)} %keys.1, bf16[256,128]{1,0:T(8,128)(2,1)} %values.1), custom_call_target="tpu_custom_call" | custom-call | bytes 1048576 | tf_op jit(solution)/shard_map/pack/pallas_call | solution.py:318
  1.0 3.0 %collective-permute-start = (bf16[192,256]{1,0:T(8,128)(2,1)S(1)}, bf16[192,256]{1,0:T(8,128)(2,1)S(1)}, u32[]{:S(2)}, u32[]{:S(2)}) collective-permute-start(bf16[192,256]{1,0:T(8,128)(2,1)S(1)} %get-tuple-element.25), channel_id=1, source_target_pairs={{0,4},{4,0},{8,12},{12,8},{16,20},{20,16},{24,28},{28,24},{1,5},{5... | collective-permute-start | bytes 294920 | tf_op jit(solution)/shard_map/ppermute | solution.py:316
  4.0 0.7 %collective-permute-start.1 = (bf16[192,256]{1,0:T(8,128)(2,1)S(1)}, bf16[192,256]{1,0:T(8,128)(2,1)S(1)}, u32[]{:S(2)}, u32[]{:S(2)}) collective-permute-start(bf16[192,256]{1,0:T(8,128)(2,1)S(1)} %get-tuple-element.26), channel_id=1, source_target_pairs={{0,0},{28,28},{4,8},{8,4},{12,16},{16,12},{20,24},{24,20},{1,1},{2... | collective-permute-start | bytes 294920 | tf_op jit(solution)/shard_map/ppermute | solution.py:335
  4.7 2.1 %collective-permute-done.inner = bf16[192,256]{1,0:T(8,128)(2,1)S(1)} collective-permute-done((bf16[192,256]{1,0:T(8,128)(2,1)S(1)}, bf16[192,256]{1,0:T(8,128)(2,1)S(1)}, u32[]{:S(2)}, u32[]{:S(2)}) %collective-permute-start) | collective-permute-done | bytes 98336 | tf_op jit(solution)/shard_map/ppermute | solution.py:316
  6.8 0.1 join.1
  6.9 4.0 %collective-permute-start.2 = (bf16[128,256]{1,0:T(8,128)(2,1)S(1)}, bf16[128,256]{1,0:T(8,128)(2,1)S(1)}, u32[]{:S(2)}, u32[]{:S(2)}) collective-permute-start(bf16[128,256]{1,0:T(8,128)(2,1)S(1)} %get-tuple-element.31), channel_id=1, source_target_pairs={{0,24},{4,28},{8,16},{12,20},{16,8},{20,12},{24,0},{28,4},{1,25},{... | collective-permute-start | bytes 196616 | tf_op jit(solution)/shard_map/ppermute | solution.py:316
  10.9 0.0 collective-permute-start.3
  10.9 0.6 %collective-permute-start.4 = (bf16[64,256]{1,0:T(8,128)(2,1)S(1)}, bf16[64,256]{1,0:T(8,128)(2,1)S(1)}, u32[]{:S(2)}, u32[]{:S(2)}) collective-permute-start(bf16[64,256]{1,0:T(8,128)(2,1)S(1)} %get-tuple-element.33), channel_id=1, source_target_pairs={{0,16},{4,20},{8,24},{12,28},{16,0},{20,4},{24,8},{28,12},{1,17},{... | collective-permute-start | bytes 98312 | tf_op jit(solution)/shard_map/ppermute | solution.py:316
  11.5 0.0 collective-permute-done.1.outer
  11.5 0.4 %near.1 = (f32[2,256,512]{2,1,0:T(8,128)S(1)}, bf16[2,512,128]{2,1,0:T(8,128)(2,1)S(1)}, bf16[64,256]{1,0:T(8,128)(2,1)S(1)}) custom-call(bf16[256,128]{1,0:T(8,128)(2,1)S(1)} %get-tuple-element.23.queries, bf16[256,256]{1,0:T(8,128)(2,1)S(1)} %get-tuple-element.24.own, bf16[192,256]{1,0:T(8,128)(2,1)S(1)} %collective-permute-done.inner, ...), custom_call_target="tpu_custom_call" | custom-call | flops 67108864 | bytes 1048576 | tf_op jit(solution)/shard_map/near/pallas_call | solution.py:349
  11.9 3.8 %collective-permute-done.4.rest_2_ = bf16[64,256]{1,0:T(8,128)(2,1)S(1)} collective-permute-done((bf16[64,256]{1,0:T(8,128)(2,1)S(1)}, bf16[64,256]{1,0:T(8,128)(2,1)S(1)}, u32[]{:S(2)}, u32[]{:S(2)}) %collective-permute-start.4) | collective-permute-done | bytes 32800 | tf_op jit(solution)/shard_map/ppermute | solution.py:316
  15.7 0.0 collective-permute-done.2.rest_0_
  15.7 0.0 collective-permute-done.3.rest_1_
  15.7 0.6 %leaves.1 = (bf16[80,128]{1,0:T(8,128)(2,1)S(1)}, bf16[80,128]{1,0:T(8,128)(2,1)S(1)}, bf16[384,128]{1,0:T(8,128)(2,1)S(1)}, bf16[384,128]{1,0:T(8,128)(2,1)S(1)}, f32[8,384]{1,0:T(8,128)S(1)}) custom-call(bf16[256,128]{1,0:T(8,128)(2,1)S(1)} %get-tuple-element.23.queries, f32[2,256,512]{2,1,0:T(8,128)S(1)} %get-tuple-element.27.near_scores, ...), custom_call_target="tpu_custom_call" | custom-call | flops 117440512 | bytes 1048576 | tf_op jit(solution)/shard_map/leaves/pallas_call | solution.py:365
  16.3 0.1 collective-permute-start.6
  16.4 1.6 %collective-permute-start.7 = (bf16[80,128]{1,0:T(8,128)(2,1)S(1)}, bf16[80,128]{1,0:T(8,128)(2,1)S(1)}, u32[]{:S(2)}, u32[]{:S(2)}) collective-permute-start(bf16[80,128]{1,0:T(8,128)(2,1)S(1)} %get-tuple-element.40), channel_id=1, source_target_pairs={{0,2},{1,3},{2,0},{3,1},{4,6},{5,7},{6,4},{7,5},{8,10},{9,11},{10,... | collective-permute-start | bytes 61448 | tf_op jit(solution)/shard_map/ppermute | solution.py:316
  18.0 0.0 copy-start
  18.0 0.6 %stays.1 = (bf16[64,128]{1,0:T(8,128)(2,1)S(1)}, bf16[64,128]{1,0:T(8,128)(2,1)S(1)}) custom-call(bf16[256,128]{1,0:T(8,128)(2,1)S(1)} %get-tuple-element.23.queries, f32[2,256,512]{2,1,0:T(8,128)S(1)} %get-tuple-element.27.near_scores, bf16[2,512,128]{2,1,0:T(8,128)(2,1)S(1)} %get-tuple-element.28.near_values, bf16[384,128]{1,0:T(8,128)(2,1)S(1)} %get-tuple-element.34.keys, ...), custom_call_target="tpu_custom_call" | custom-call | flops 117440512 | bytes 1048576 | tf_op jit(solution)/shard_map/stays/pallas_call | solution.py:380
  18.5 0.3 %collective-permute-start.5 = (bf16[64,128]{1,0:T(8,128)(2,1)S(1)}, bf16[64,128]{1,0:T(8,128)(2,1)S(1)}, u32[]{:S(2)}, u32[]{:S(2)}) collective-permute-start(bf16[64,128]{1,0:T(8,128)(2,1)S(1)} %get-tuple-element.38), channel_id=1, source_target_pairs={{0,1},{1,0},{2,3},{3,2},{4,5},{5,4},{6,7},{7,6},{8,9},{9,8},{10,11... | collective-permute-start | bytes 49160 | tf_op jit(solution)/shard_map/ppermute | solution.py:316
  18.9 0.9 %collective-permute-done.5.other = bf16[64,128]{1,0:T(8,128)(2,1)S(1)} collective-permute-done((bf16[64,128]{1,0:T(8,128)(2,1)S(1)}, bf16[64,128]{1,0:T(8,128)(2,1)S(1)}, u32[]{:S(2)}, u32[]{:S(2)}) %collective-permute-start.5) | collective-permute-done | bytes 16416 | tf_op jit(solution)/shard_map/ppermute | solution.py:316
  19.8 0.0 copy-done
  19.8 0.2 begin.1.partial
  20.0 0.0 collective-permute-done.6.other
  20.0 0.3 %collective-permute-done.7.same = bf16[80,128]{1,0:T(8,128)(2,1)S(1)} collective-permute-done((bf16[80,128]{1,0:T(8,128)(2,1)S(1)}, bf16[80,128]{1,0:T(8,128)(2,1)S(1)}, u32[]{:S(2)}, u32[]{:S(2)}) %collective-permute-start.7) | collective-permute-done | bytes 20512 | tf_op jit(solution)/shard_map/ppermute | solution.py:316
  20.2 0.8 %project.1 = bf16[64,512]{1,0:T(8,128)(2,1)} custom-call(f32[64,512]{1,0:T(8,128)S(1)} %begin.1.partial, bf16[80,128]{1,0:T(8,128)(2,1)S(1)} %collective-permute-done.6.other, bf16[80,128]{1,0:T(8,128)(2,1)S(1)} %collective-permute-done.7.same, bf16[512,512]{1,0:T(8,128)(2,1)S(1)} %copy-done), custom_call_target="tpu_custom_call" | custom-call | bytes 1048576 | tf_op jit(solution)/shard_map/project/pallas_call | solution.py:393
Async XLA Ops:
  1.0 5.8 %collective-permute-start = (bf16[192,256]{1,0:T(8,128)(2,1)S(1)}, bf16[192,256]{1,0:T(8,128)(2,1)S(1)}, u32[]{:S(2)}, u32[]{:S(2)}) collective-permute-start(bf16[192,256]{1,0:T(8,128)(2,1)S(1)} %get-tuple-element.25), channel_id=1, source_target_pairs={{0,4},{4,0},{8,12},{12,8},{16,20},{20,16},{24,28},{28,24},{1,5},{5... | collective-permute-start | bytes 294920 | tf_op jit(solution)/shard_map/ppermute | solution.py:316
  4.0 7.5 %collective-permute-start.1 = (bf16[192,256]{1,0:T(8,128)(2,1)S(1)}, bf16[192,256]{1,0:T(8,128)(2,1)S(1)}, u32[]{:S(2)}, u32[]{:S(2)}) collective-permute-start(bf16[192,256]{1,0:T(8,128)(2,1)S(1)} %get-tuple-element.26), channel_id=1, source_target_pairs={{0,0},{28,28},{4,8},{8,4},{12,16},{16,12},{20,24},{24,20},{1,1},{2... | collective-permute-start | bytes 294920 | tf_op jit(solution)/shard_map/ppermute | solution.py:335
  6.9 8.8 %collective-permute-start.2 = (bf16[128,256]{1,0:T(8,128)(2,1)S(1)}, bf16[128,256]{1,0:T(8,128)(2,1)S(1)}, u32[]{:S(2)}, u32[]{:S(2)}) collective-permute-start(bf16[128,256]{1,0:T(8,128)(2,1)S(1)} %get-tuple-element.31), channel_id=1, source_target_pairs={{0,24},{4,28},{8,16},{12,20},{16,8},{20,12},{24,0},{28,4},{1,25},{... | collective-permute-start | bytes 196616 | tf_op jit(solution)/shard_map/ppermute | solution.py:316
  10.9 4.8 %collective-permute-start.3 = (bf16[128,256]{1,0:T(8,128)(2,1)S(1)}, bf16[128,256]{1,0:T(8,128)(2,1)S(1)}, u32[]{:S(2)}, u32[]{:S(2)}) collective-permute-start(bf16[128,256]{1,0:T(8,128)(2,1)S(1)} %get-tuple-element.32), channel_id=1, source_target_pairs={{0,8},{4,12},{8,0},{12,4},{16,24},{20,28},{24,16},{28,20},{1,9},{5... | collective-permute-start | bytes 196616 | tf_op jit(solution)/shard_map/ppermute | solution.py:316
  10.9 4.8 %collective-permute-start.4 = (bf16[64,256]{1,0:T(8,128)(2,1)S(1)}, bf16[64,256]{1,0:T(8,128)(2,1)S(1)}, u32[]{:S(2)}, u32[]{:S(2)}) collective-permute-start(bf16[64,256]{1,0:T(8,128)(2,1)S(1)} %get-tuple-element.33), channel_id=1, source_target_pairs={{0,16},{4,20},{8,24},{12,28},{16,0},{20,4},{24,8},{28,12},{1,17},{... | collective-permute-start | bytes 98312 | tf_op jit(solution)/shard_map/ppermute | solution.py:316
  16.3 3.7 %collective-permute-start.6 = (bf16[80,128]{1,0:T(8,128)(2,1)S(1)}, bf16[80,128]{1,0:T(8,128)(2,1)S(1)}, u32[]{:S(2)}, u32[]{:S(2)}) collective-permute-start(bf16[80,128]{1,0:T(8,128)(2,1)S(1)} %get-tuple-element.39), channel_id=1, source_target_pairs={{0,3},{1,2},{2,1},{3,0},{4,7},{5,6},{6,5},{7,4},{8,11},{9,10},{10,... | collective-permute-start | bytes 61448 | tf_op jit(solution)/shard_map/ppermute | solution.py:316
  16.4 3.8 %collective-permute-start.7 = (bf16[80,128]{1,0:T(8,128)(2,1)S(1)}, bf16[80,128]{1,0:T(8,128)(2,1)S(1)}, u32[]{:S(2)}, u32[]{:S(2)}) collective-permute-start(bf16[80,128]{1,0:T(8,128)(2,1)S(1)} %get-tuple-element.40), channel_id=1, source_target_pairs={{0,2},{1,3},{2,0},{3,1},{4,6},{5,7},{6,4},{7,5},{8,10},{9,11},{10,... | collective-permute-start | bytes 61448 | tf_op jit(solution)/shard_map/ppermute | solution.py:316
  18.0 1.8 %copy-start = (bf16[512,512]{1,0:T(8,128)(2,1)S(1)}, bf16[512,512]{1,0:T(8,128)(2,1)}, u32[]{:S(2)}) copy-start(bf16[512,512]{1,0:T(8,128)(2,1)} %weight.3) | copy-start | bytes 1572868
  18.5 1.2 %collective-permute-start.5 = (bf16[64,128]{1,0:T(8,128)(2,1)S(1)}, bf16[64,128]{1,0:T(8,128)(2,1)S(1)}, u32[]{:S(2)}, u32[]{:S(2)}) collective-permute-start(bf16[64,128]{1,0:T(8,128)(2,1)S(1)} %get-tuple-element.38), channel_id=1, source_target_pairs={{0,1},{1,0},{2,3},{3,2},{4,5},{5,4},{6,7},{7,6},{8,9},{9,8},{10,11... | collective-permute-start | bytes 49160 | tf_op jit(solution)/shard_map/ppermute | solution.py:316

commit v15 on v13

--- a/solution.py
+++ b/solution.py
@@ -54,7 +54,7 @@
         quarter[...] = level_two
 
 
-def join_kernel(inner, quarter, upward, block, eighth, wide):
+def join_kernel(inner, quarter, short, block, eighth, wide):
     me = lax.axis_index("seq")
     odd = me & 1
     edge_half = average_pairs(inner[:LEAF], wide)
@@ -66,9 +66,8 @@
     first = jnp.where(odd == 1, theirs, quarter[...])
     second = jnp.where(odd == 1, quarter[...], theirs)
     level_three = average_pairs(jnp.concatenate([first, second], axis=0), wide)
-    upward[:HALF] = jnp.where(me >= 6, level_three, first)
-    upward[HALF:] = second
-    block[:HALF] = first
+    short[...] = jnp.where((me == 6) | (me == 1), level_three, quarter[...])
+    block[:HALF] = jnp.where((me == 0) | (me == 7), level_three, first)
     block[HALF:] = second
     eighth[...] = level_three
 
@@ -77,8 +76,10 @@
 PAD = 16
 
 
-def far_row_count(seq_size):
-    rows = HALF
+def last_row_count(seq_size, paired):
+    if paired:
+        return 3 * HALF
+    rows = 0
     for far in range(1, seq_size.bit_length() - 1):
         if seq_size >> far == 2:
             rows += LEAF
@@ -131,18 +132,10 @@
     return pieces
 
 
-def paired_pieces(lower, upper, eighth, first_eighth):
+def paired_pieces(block, eighth):
     me = lax.axis_index("seq")
-    odd = me & 1
-    has_lower, has_upper = me >= 2, me < 6
-    has_third = ((odd == 1) & has_lower) | ((odd == 0) & has_upper)
-    return [
-        (lower[:HALF], None),
-        (upper[HALF:], bias_of(has_upper)),
-        (jnp.where(odd == 1, lower[HALF:], upper[:HALF]), bias_of(has_third)),
-        (eighth[...], None),
-        (first_eighth[...], bias_of(jnp.logical_not(has_upper))),
-    ]
+    inside = jnp.logical_not((me == 6) | (me == 1))
+    return [(block[:HALF], None), (block[HALF:], bias_of(inside)), (eighth[...], None)]
 
 
 def place(pieces, values, keys):
@@ -207,21 +200,35 @@
         scores[leaf] = scores_of(rows, keys) + bias
 
 
-def attend_leaf(leaf, queries, near_scores, near_values, keys, values, bias, same, other):
+def mid_kernel(queries, shared, *rest):
+    *short, scores, values, keys = rest
+    pieces = [(shared, bias_of(lax.axis_index("seq") >= 1))] + [(rows, None) for rows in short]
+    bias = place(pieces, values, keys)
+    for leaf in range(2):
+        rows = split_heads(queries[leaf * LEAF : (leaf + 1) * LEAF])
+        scores[leaf] = scores_of(rows, keys) + bias
+
+
+def attend_leaf(leaf, queries, scored, keys, values, bias, same, other):
     first_head = lax.broadcasted_iota(jnp.int32, (1, values.shape[1]), 1) < HD
     exponent = math.log2(math.e) / math.sqrt(HD)
     rows = split_heads(queries[pl.ds(pl.multiple_of(leaf * LEAF, LEAF), LEAF)])
-    near = near_scores[leaf]
-    far_scores = scores_of(rows, keys) + bias
-    peak = jnp.maximum(
-        jnp.max(near, axis=1, keepdims=True), jnp.max(far_scores, axis=1, keepdims=True)
-    )
-    near = jnp.exp2((near - peak) * exponent)
-    far_weights = jnp.exp2((far_scores - peak) * exponent)
-    total = jnp.sum(near, axis=1, keepdims=True) + jnp.sum(far_weights, axis=1, keepdims=True)
-    numer = jnp.dot(
-        near.astype(jnp.bfloat16), near_values[leaf], preferred_element_type=jnp.float32
-    ) + jnp.dot(far_weights.astype(jnp.bfloat16), values[...], preferred_element_type=jnp.float32)
+    near_scores, near_values, mid_scores, mid_values = scored
+    parts = [
+        (near_scores[leaf], near_values[leaf]),
+        (mid_scores[leaf], mid_values[...]),
+        (scores_of(rows, keys) + bias, values[...]),
+    ]
+    peak = functools.reduce(
+        jnp.maximum, [jnp.max(scores, axis=1, keepdims=True) for scores, _ in parts]
+    )
+    total, numer = 0.0, 0.0
+    for scores, part_values in parts:
+        weights = jnp.exp2((scores - peak) * exponent)
+        total = total + jnp.sum(weights, axis=1, keepdims=True)
+        numer = numer + jnp.dot(
+            weights.astype(jnp.bfloat16), part_values, preferred_element_type=jnp.float32
+        )
     mean = numer / total
     attended = jnp.where(first_head, mean[:LEAF], mean[LEAF:]).astype(jnp.bfloat16)
     second = (lax.axis_index("head") & 1) == 1
@@ -229,23 +236,26 @@
     other[:HALF] = jnp.where(second, attended[:HALF], attended[HALF:])
 
 
-def leaves_kernel(seq_size, queries, near_scores, near_values, shared, *rest):
+def leaves_kernel(seq_size, queries, near_scores, near_values, mid_scores, mid_values, *rest):
     *far, same, other, keys, values, bias, wide = rest
     if len(far) == 1:
         pieces = gathered_pieces(seq_size, far[0], wide)
     else:
         pieces = paired_pieces(*far)
-    shared_bias = bias_of(lax.axis_index("seq") >= 1)
-    bias[...] = jnp.broadcast_to(place([(shared, shared_bias)] + pieces, values, keys), bias.shape)
+    bias[...] = jnp.broadcast_to(place(pieces, values, keys), bias.shape)
     leaf = (lax.axis_index("head") >> 1) ^ 1
-    attend_leaf(leaf, queries, near_scores, near_values, keys, values, bias[:1], same, other)
+    scored = (near_scores, near_values, mid_scores, mid_values)
+    attend_leaf(leaf, queries, scored, keys, values, bias[:1], same, other)
     for share in (same, other):
         share[HALF:] = jnp.zeros((PAD, share.shape[1]), share.dtype)
 
 
-def stays_kernel(queries, near_scores, near_values, keys, values, bias, same, other):
+def stays_kernel(
+    queries, near_scores, near_values, mid_scores, mid_values, keys, values, bias, same, other
+):
     leaf = lax.axis_index("head") >> 1
-    attend_leaf(leaf, queries, near_scores, near_values, keys, values, bias[:1], same, other)
+    scored = (near_scores, near_values, mid_scores, mid_values)
+    attend_leaf(leaf, queries, scored, keys, values, bias[:1], same, other)
 
 
 def side_by_side(same, other, rows, columns):
@@ -328,21 +338,22 @@
     others = [(i, i + 1 if i & 1 else i - 1) for i in range(1, seq_size - 1)]
     outer = lax.ppermute(outer, "seq", others)
     if paired:
-        upward, block, eighth = kernel_call(
+        short, block, eighth = kernel_call(
             join_kernel,
             "join",
             8,
             [VMEM] * 2,
-            [(LEAF, pair_width), (LEAF, pair_width), (HALF, pair_width)],
+            [(HALF, pair_width), (LEAF, pair_width), (HALF, pair_width)],
             [wide],
         )(inner, quarter)
+        shift = [(i, (i - 2 if i & 1 else i + 2) % seq_size) for i in range(seq_size)]
+        early = (lax.ppermute(short, "seq", shift),)
         far = (
-            lax.ppermute(upward, "seq", [(i, (i + 2) % seq_size) for i in range(seq_size)]),
-            lax.ppermute(block, "seq", [(i + 2, i) for i in range(seq_size - 2)]),
+            lax.ppermute(block, "seq", [(target, source) for source, target in shift]),
             swap(eighth, 4),
-            lax.ppermute(eighth, "seq", [(i, i + 6) for i in range(2)]),
         )
     else:
+        early = ()
         far = (lax.all_to_all(quarter, "seq", split_axis=0, concat_axis=0),)
     share = tokens // head_size
     near_scores, near_values, shared = kernel_call(
@@ -358,27 +369,37 @@
         [pltpu.VMEM((NEAR_ROWS, width), jnp.bfloat16), wide],
         flops=8 * LEAF * NEAR_ROWS * width,
     )(own_queries, own, inner, outer)
-    far_rows = far_row_count(seq_size)
-
-    leaf_flops = 8 * LEAF * (NEAR_ROWS + far_rows) * width
+    mid_rows = HALF * (1 + len(early))
+    mid_scores, mid_values = kernel_call(
+        mid_kernel,
+        "mid",
+        8,
+        [VMEM] * (2 + len(early)),
+        [jax.ShapeDtypeStruct((2, 2 * LEAF, mid_rows), jnp.float32), (mid_rows, width)],
+        [pltpu.VMEM((mid_rows, width), jnp.bfloat16)],
+        flops=520 * 10**6,
+    )(own_queries, shared, *early)
+    scored = (near_scores, near_values, mid_scores, mid_values)
+    last_rows = last_row_count(seq_size, paired)
+    leaf_flops = 8 * LEAF * (NEAR_ROWS + mid_rows + last_rows) * width
     share_2, share_3, far_keys, far_values, far_bias = kernel_call(
         functools.partial(leaves_kernel, seq_size),
         "leaves",
         24,
-        [VMEM] * (4 + len(far)),
+        [VMEM] * (5 + len(far)),
         [
             (share + PAD, width),
             (share + PAD, width),
-            (far_rows, width),
-            (far_rows, width),
-            jax.ShapeDtypeStruct((8, far_rows), jnp.float32),
+            (last_rows, width),
+            (last_rows, width),
+            jax.ShapeDtypeStruct((8, last_rows), jnp.float32),
         ],
         [wide],
         flops=leaf_flops,
-    )(own_queries, near_scores, near_values, shared, *far)
+    )(own_queries, *scored, *far)
     share_0, share_1 = kernel_call(
-        stays_kernel, "stays", 16, [VMEM] * 6, [(share, width)] * 2, [], flops=leaf_flops
-    )(own_queries, near_scores, near_values, far_keys, far_values, far_bias)
+        stays_kernel, "stays", 16, [VMEM] * 8, [(share, width)] * 2, [], flops=leaf_flops
+    )(own_queries, *scored, far_keys, far_values, far_bias)
     columns = pltpu.VMEM((share, pair_width), jnp.bfloat16)
     part_3, part_2 = swap(share_3, 3, "head"), swap(share_2, 2, "head")
     (partial,) = kernel_call(

time: 24.2 us -> 21.6 us (0.89)
  starting transfers between devices: 15.8 us -> 10.6 us
  waiting for transfers between devices: 4.49 us -> 6.64 us
  Pallas kernels: 3.57 us -> 3.85 us
    ppermute x5, starting transfers between devices: 8.71 us -> 5.93 us  [swap(): lax.ppermute(array, axis, [(i, i ^ bit) for i in range(lax.axis_size(axis...]
    ppermute x3 -> x2, starting transfers between devices: 6.48 us -> 4.05 us  [the longest x1 2.09 us: shards(): lax.ppermute(block, 'seq', [(target, source) for source, target in shift])]
    ppermute x5, waiting for transfers between devices: 3.31 us -> 4.89 us  [swap(): lax.ppermute(array, axis, [(i, i ^ bit) for i in range(lax.axis_size(axis...]
    ppermute x3 -> x2, waiting for transfers between devices: 1.17 us -> 1.75 us  [the longest x1 1.74 us: shards(): early = (lax.ppermute(short, 'seq', shift),)]
    pallas_call x2 -> x3, Pallas kernels: 0.63 us -> 0.87 us  [the longest x1 0.61 us: shards(): kernel_call(stays_kernel, 'stays', 16, [VMEM] * 8, [(share, width)] * 2,...]
  transfers between devices with their start and end apart: 9 -> 8, of which waited for: 4 -> 5; matrix products, arithmetic and copies ran while one was open for 0% -> 0% of each run, Pallas kernels for 5% -> 7%
where the time goes in v15:
time: 21.6 us; the launch traced here: 21.2 us
  starting transfers between devices  10.6 us (49%)
  waiting for transfers between devices  6.64 us (31%)
  Pallas kernels  3.85 us (18%)
    ppermute x5, starting transfers between devices, swap(): lax.ppermute(array, axis, [(i, i ^ bit) for i in range(lax.axis_size(axis...  5.93 us
    ppermute x5, waiting for transfers between devices, swap(): lax.ppermute(array, axis, [(i, i ^ bit) for i in range(lax.axis_size(axis...  4.89 us
    ppermute x1, starting transfers between devices, shards(): lax.ppermute(block, 'seq', [(target, source) for source, target in shift])  2.09 us
    ppermute x1, starting transfers between devices, shards(): early = (lax.ppermute(short, 'seq', shift),)  1.96 us
    ppermute x1, waiting for transfers between devices, shards(): early = (lax.ppermute(short, 'seq', shift),)  1.74 us
    pallas_call x1, Pallas kernels, shards(): kernel_call(functools.partial(pack_kernel, not paired), 'pack', 16, [HBM]...  0.99 us
    pallas_call x1, Pallas kernels, shards(): kernel_call(project_kernel, 'project', 8, [VMEM] * 4, [(share, out_weight...  0.81 us
    ppermute x1, starting transfers between devices, shards(): outer = lax.ppermute(outer, 'seq', others)  0.65 us
  transfers between devices with their start and end apart: 8, of which 5 were waited for; matrix products, arithmetic and copies ran while one was open for 0% of the time, Pallas kernels for 7%

profile of v15, /device:TPU:0, one launch (start us, length us, event | category | flops | bytes accessed | tf_op | source)
XLA Modules:
  0.0 21.2 jit_solution(10366287347032949908)
XLA Ops:
  0.0 1.0 %pack.1 = (bf16[256,128]{1,0:T(8,128)(2,1)S(1)}, bf16[256,256]{1,0:T(8,128)(2,1)S(1)}, bf16[192,256]{1,0:T(8,128)(2,1)S(1)}, bf16[192,256]{1,0:T(8,128)(2,1)S(1)}, bf16[64,256]{1,0:T(8,128)(2,1)S(1)}) custom-call(bf16[256,128]{1,0:T(8,128)(2,1)} %queries.1, bf16[256,128]{1,0:T(8,128)(2,1)} %keys.1, bf16[256,128]{1,0:T(8,128)(2,1)} %values.1), custom_call_target="tpu_custom_call" | custom-call | bytes 1048576 | tf_op jit(solution)/shard_map/pack/pallas_call | solution.py:323
  1.0 3.0 %collective-permute-start = (bf16[192,256]{1,0:T(8,128)(2,1)S(1)}, bf16[192,256]{1,0:T(8,128)(2,1)S(1)}, u32[]{:S(2)}, u32[]{:S(2)}) collective-permute-start(bf16[192,256]{1,0:T(8,128)(2,1)S(1)} %get-tuple-element.27), channel_id=1, source_target_pairs={{0,4},{4,0},{8,12},{12,8},{16,20},{20,16},{24,28},{28,24},{1,5},{5... | collective-permute-start | bytes 294920 | tf_op jit(solution)/shard_map/ppermute | solution.py:321
  4.0 0.7 %collective-permute-start.1 = (bf16[192,256]{1,0:T(8,128)(2,1)S(1)}, bf16[192,256]{1,0:T(8,128)(2,1)S(1)}, u32[]{:S(2)}, u32[]{:S(2)}) collective-permute-start(bf16[192,256]{1,0:T(8,128)(2,1)S(1)} %get-tuple-element.28), channel_id=1, source_target_pairs={{4,8},{8,4},{12,16},{16,12},{20,24},{24,20},{5,9},{9,5},{13,17},{1... | collective-permute-start | bytes 294920 | tf_op jit(solution)/shard_map/ppermute | solution.py:339
  4.7 2.1 %collective-permute-done.inner = bf16[192,256]{1,0:T(8,128)(2,1)S(1)} collective-permute-done((bf16[192,256]{1,0:T(8,128)(2,1)S(1)}, bf16[192,256]{1,0:T(8,128)(2,1)S(1)}, u32[]{:S(2)}, u32[]{:S(2)}) %collective-permute-start) | collective-permute-done | bytes 98336 | tf_op jit(solution)/shard_map/ppermute | solution.py:321
  6.8 0.1 join.1
  6.9 2.0 %collective-permute-start.2 = (bf16[64,256]{1,0:T(8,128)(2,1)S(1)}, bf16[64,256]{1,0:T(8,128)(2,1)S(1)}, u32[]{:S(2)}, u32[]{:S(2)}) collective-permute-start(bf16[64,256]{1,0:T(8,128)(2,1)S(1)} %get-tuple-element.33), channel_id=1, source_target_pairs={{0,8},{4,28},{8,16},{12,4},{16,24},{20,12},{24,0},{28,20},{1,9},{5... | collective-permute-start | bytes 98312 | tf_op jit(solution)/shard_map/ppermute | solution.py:350
  8.8 2.1 %collective-permute-start.3 = (bf16[128,256]{1,0:T(8,128)(2,1)S(1)}, bf16[128,256]{1,0:T(8,128)(2,1)S(1)}, u32[]{:S(2)}, u32[]{:S(2)}) collective-permute-start(bf16[128,256]{1,0:T(8,128)(2,1)S(1)} %get-tuple-element.36), channel_id=1, source_target_pairs={{8,0},{28,4},{16,8},{4,12},{24,16},{12,20},{0,24},{20,28},{9,1},{2... | collective-permute-start | bytes 196616 | tf_op jit(solution)/shard_map/ppermute | solution.py:352
  10.9 0.9 %collective-permute-start.4 = (bf16[64,256]{1,0:T(8,128)(2,1)S(1)}, bf16[64,256]{1,0:T(8,128)(2,1)S(1)}, u32[]{:S(2)}, u32[]{:S(2)}) collective-permute-start(bf16[64,256]{1,0:T(8,128)(2,1)S(1)} %get-tuple-element.37), channel_id=1, source_target_pairs={{0,16},{4,20},{8,24},{12,28},{16,0},{20,4},{24,8},{28,12},{1,17},{... | collective-permute-start | bytes 98312 | tf_op jit(solution)/shard_map/ppermute | solution.py:321
  11.9 0.0 collective-permute-done.1.outer
  11.9 0.4 %near.1 = (f32[2,256,512]{2,1,0:T(8,128)S(1)}, bf16[2,512,128]{2,1,0:T(8,128)(2,1)S(1)}, bf16[64,256]{1,0:T(8,128)(2,1)S(1)}) custom-call(bf16[256,128]{1,0:T(8,128)(2,1)S(1)} %get-tuple-element.25.queries, bf16[256,256]{1,0:T(8,128)(2,1)S(1)} %get-tuple-element.26.own, bf16[192,256]{1,0:T(8,128)(2,1)S(1)} %collective-permute-done.inner, ...), custom_call_target="tpu_custom_call" | custom-call | flops 67108864 | bytes 1048576 | tf_op jit(solution)/shard_map/near/pallas_call | solution.py:359
  12.3 1.7 %collective-permute-done.2.rest_0_ = bf16[64,256]{1,0:T(8,128)(2,1)S(1)} collective-permute-done((bf16[64,256]{1,0:T(8,128)(2,1)S(1)}, bf16[64,256]{1,0:T(8,128)(2,1)S(1)}, u32[]{:S(2)}, u32[]{:S(2)}) %collective-permute-start.2) | collective-permute-done | bytes 32800 | tf_op jit(solution)/shard_map/ppermute | solution.py:350
  14.0 0.2 mid.1
  14.2 1.6 %collective-permute-done.4.rest_1_ = bf16[64,256]{1,0:T(8,128)(2,1)S(1)} collective-permute-done((bf16[64,256]{1,0:T(8,128)(2,1)S(1)}, bf16[64,256]{1,0:T(8,128)(2,1)S(1)}, u32[]{:S(2)}, u32[]{:S(2)}) %collective-permute-start.4) | collective-permute-done | bytes 32800 | tf_op jit(solution)/shard_map/ppermute | solution.py:321
  15.8 0.0 collective-permute-done.3.rest_0_
  15.8 0.6 %leaves.1 = (bf16[80,128]{1,0:T(8,128)(2,1)S(1)}, bf16[80,128]{1,0:T(8,128)(2,1)S(1)}, bf16[192,128]{1,0:T(8,128)(2,1)S(1)}, bf16[192,128]{1,0:T(8,128)(2,1)S(1)}, f32[8,192]{1,0:T(8,128)S(1)}) custom-call(bf16[256,128]{1,0:T(8,128)(2,1)S(1)} %get-tuple-element.25.queries, f32[2,256,512]{2,1,0:T(8,128)S(1)} %get-tuple-element.29.near_scores, ...), custom_call_target="tpu_custom_call" | custom-call | flops 109051904 | bytes 1048576 | tf_op jit(solution)/shard_map/leaves/pallas_call | solution.py:385
  16.5 0.1 collective-permute-start.6
  16.5 1.7 %collective-permute-start.7 = (bf16[80,128]{1,0:T(8,128)(2,1)S(1)}, bf16[80,128]{1,0:T(8,128)(2,1)S(1)}, u32[]{:S(2)}, u32[]{:S(2)}) collective-permute-start(bf16[80,128]{1,0:T(8,128)(2,1)S(1)} %get-tuple-element.44), channel_id=1, source_target_pairs={{0,2},{1,3},{2,0},{3,1},{4,6},{5,7},{6,4},{7,5},{8,10},{9,11},{10,... | collective-permute-start | bytes 61448 | tf_op jit(solution)/shard_map/ppermute | solution.py:321
  18.2 0.0 copy-start
  18.2 0.6 %stays.1 = (bf16[64,128]{1,0:T(8,128)(2,1)S(1)}, bf16[64,128]{1,0:T(8,128)(2,1)S(1)}) custom-call(bf16[256,128]{1,0:T(8,128)(2,1)S(1)} %get-tuple-element.25.queries, f32[2,256,512]{2,1,0:T(8,128)S(1)} %get-tuple-element.29.near_scores, bf16[2,512,128]{2,1,0:T(8,128)(2,1)S(1)} %get-tuple-element.30.near_values, ...), custom_call_target="tpu_custom_call" | custom-call | flops 109051904 | bytes 1048576 | tf_op jit(solution)/shard_map/stays/pallas_call | solution.py:400
  18.8 0.3 %collective-permute-start.5 = (bf16[64,128]{1,0:T(8,128)(2,1)S(1)}, bf16[64,128]{1,0:T(8,128)(2,1)S(1)}, u32[]{:S(2)}, u32[]{:S(2)}) collective-permute-start(bf16[64,128]{1,0:T(8,128)(2,1)S(1)} %get-tuple-element.42), channel_id=1, source_target_pairs={{0,1},{1,0},{2,3},{3,2},{4,5},{5,4},{6,7},{7,6},{8,9},{9,8},{10,11... | collective-permute-start | bytes 49160 | tf_op jit(solution)/shard_map/ppermute | solution.py:321
  19.1 1.0 %collective-permute-done.5.other = bf16[64,128]{1,0:T(8,128)(2,1)S(1)} collective-permute-done((bf16[64,128]{1,0:T(8,128)(2,1)S(1)}, bf16[64,128]{1,0:T(8,128)(2,1)S(1)}, u32[]{:S(2)}, u32[]{:S(2)}) %collective-permute-start.5) | collective-permute-done | bytes 16416 | tf_op jit(solution)/shard_map/ppermute | solution.py:321
  20.1 0.0 copy-done
  20.1 0.2 begin.1.partial
  20.2 0.0 collective-permute-done.6.other
  20.2 0.1 collective-permute-done.7.same
  20.4 0.8 %project.1 = bf16[64,512]{1,0:T(8,128)(2,1)} custom-call(f32[64,512]{1,0:T(8,128)S(1)} %begin.1.partial, bf16[80,128]{1,0:T(8,128)(2,1)S(1)} %collective-permute-done.6.other, bf16[80,128]{1,0:T(8,128)(2,1)S(1)} %collective-permute-done.7.same, bf16[512,512]{1,0:T(8,128)(2,1)S(1)} %copy-done), custom_call_target="tpu_custom_call" | custom-call | bytes 1048576 | tf_op jit(solution)/shard_map/project/pallas_call | solution.py:413
Async XLA Ops:
  1.0 5.8 %collective-permute-start = (bf16[192,256]{1,0:T(8,128)(2,1)S(1)}, bf16[192,256]{1,0:T(8,128)(2,1)S(1)}, u32[]{:S(2)}, u32[]{:S(2)}) collective-permute-start(bf16[192,256]{1,0:T(8,128)(2,1)S(1)} %get-tuple-element.27), channel_id=1, source_target_pairs={{0,4},{4,0},{8,12},{12,8},{16,20},{20,16},{24,28},{28,24},{1,5},{5... | collective-permute-start | bytes 294920 | tf_op jit(solution)/shard_map/ppermute | solution.py:321
  4.0 7.9 %collective-permute-start.1 = (bf16[192,256]{1,0:T(8,128)(2,1)S(1)}, bf16[192,256]{1,0:T(8,128)(2,1)S(1)}, u32[]{:S(2)}, u32[]{:S(2)}) collective-permute-start(bf16[192,256]{1,0:T(8,128)(2,1)S(1)} %get-tuple-element.28), channel_id=1, source_target_pairs={{4,8},{8,4},{12,16},{16,12},{20,24},{24,20},{5,9},{9,5},{13,17},{1... | collective-permute-start | bytes 294920 | tf_op jit(solution)/shard_map/ppermute | solution.py:339
  6.9 7.1 %collective-permute-start.2 = (bf16[64,256]{1,0:T(8,128)(2,1)S(1)}, bf16[64,256]{1,0:T(8,128)(2,1)S(1)}, u32[]{:S(2)}, u32[]{:S(2)}) collective-permute-start(bf16[64,256]{1,0:T(8,128)(2,1)S(1)} %get-tuple-element.33), channel_id=1, source_target_pairs={{0,8},{4,28},{8,16},{12,4},{16,24},{20,12},{24,0},{28,20},{1,9},{5... | collective-permute-start | bytes 98312 | tf_op jit(solution)/shard_map/ppermute | solution.py:350
  8.8 7.0 %collective-permute-start.3 = (bf16[128,256]{1,0:T(8,128)(2,1)S(1)}, bf16[128,256]{1,0:T(8,128)(2,1)S(1)}, u32[]{:S(2)}, u32[]{:S(2)}) collective-permute-start(bf16[128,256]{1,0:T(8,128)(2,1)S(1)} %get-tuple-element.36), channel_id=1, source_target_pairs={{8,0},{28,4},{16,8},{4,12},{24,16},{12,20},{0,24},{20,28},{9,1},{2... | collective-permute-start | bytes 196616 | tf_op jit(solution)/shard_map/ppermute | solution.py:352
  10.9 4.9 %collective-permute-start.4 = (bf16[64,256]{1,0:T(8,128)(2,1)S(1)}, bf16[64,256]{1,0:T(8,128)(2,1)S(1)}, u32[]{:S(2)}, u32[]{:S(2)}) collective-permute-start(bf16[64,256]{1,0:T(8,128)(2,1)S(1)} %get-tuple-element.37), channel_id=1, source_target_pairs={{0,16},{4,20},{8,24},{12,28},{16,0},{20,4},{24,8},{28,12},{1,17},{... | collective-permute-start | bytes 98312 | tf_op jit(solution)/shard_map/ppermute | solution.py:321
  16.5 3.8 %collective-permute-start.6 = (bf16[80,128]{1,0:T(8,128)(2,1)S(1)}, bf16[80,128]{1,0:T(8,128)(2,1)S(1)}, u32[]{:S(2)}, u32[]{:S(2)}) collective-permute-start(bf16[80,128]{1,0:T(8,128)(2,1)S(1)} %get-tuple-element.43), channel_id=1, source_target_pairs={{0,3},{1,2},{2,1},{3,0},{4,7},{5,6},{6,5},{7,4},{8,11},{9,10},{10,... | collective-permute-start | bytes 61448 | tf_op jit(solution)/shard_map/ppermute | solution.py:321
  16.5 3.8 %collective-permute-start.7 = (bf16[80,128]{1,0:T(8,128)(2,1)S(1)}, bf16[80,128]{1,0:T(8,128)(2,1)S(1)}, u32[]{:S(2)}, u32[]{:S(2)}) collective-permute-start(bf16[80,128]{1,0:T(8,128)(2,1)S(1)} %get-tuple-element.44), channel_id=1, source_target_pairs={{0,2},{1,3},{2,0},{3,1},{4,6},{5,7},{6,4},{7,5},{8,10},{9,11},{10,... | collective-permute-start | bytes 61448 | tf_op jit(solution)/shard_map/ppermute | solution.py:321
  18.2 1.9 %copy-start = (bf16[512,512]{1,0:T(8,128)(2,1)S(1)}, bf16[512,512]{1,0:T(8,128)(2,1)}, u32[]{:S(2)}) copy-start(bf16[512,512]{1,0:T(8,128)(2,1)} %weight.3) | copy-start | bytes 1572868
  18.8 1.2 %collective-permute-start.5 = (bf16[64,128]{1,0:T(8,128)(2,1)S(1)}, bf16[64,128]{1,0:T(8,128)(2,1)S(1)}, u32[]{:S(2)}, u32[]{:S(2)}) collective-permute-start(bf16[64,128]{1,0:T(8,128)(2,1)S(1)} %get-tuple-element.42), channel_id=1, source_target_pairs={{0,1},{1,0},{2,3},{3,2},{4,5},{5,4},{6,7},{7,6},{8,9},{9,8},{10,11... | collective-permute-start | bytes 49160 | tf_op jit(solution)/shard_map/ppermute | solution.py:321

commit v16 on v15

--- a/solution.py
+++ b/solution.py
@@ -54,7 +54,7 @@
         quarter[...] = level_two
 
 
-def join_kernel(inner, quarter, short, block, eighth, wide):
+def join_kernel(inner, quarter, upward, downward, eighth, wide):
     me = lax.axis_index("seq")
     odd = me & 1
     edge_half = average_pairs(inner[:LEAF], wide)
@@ -66,9 +66,10 @@
     first = jnp.where(odd == 1, theirs, quarter[...])
     second = jnp.where(odd == 1, quarter[...], theirs)
     level_three = average_pairs(jnp.concatenate([first, second], axis=0), wide)
-    short[...] = jnp.where((me == 6) | (me == 1), level_three, quarter[...])
-    block[:HALF] = jnp.where((me == 0) | (me == 7), level_three, first)
-    block[HALF:] = second
+    upward[:HALF] = jnp.where(me >= 6, level_three, first)
+    upward[HALF:] = second
+    downward[:HALF] = jnp.where(me < 2, level_three, first)
+    downward[HALF:] = second
     eighth[...] = level_three
 
 
@@ -78,7 +79,7 @@
 
 def last_row_count(seq_size, paired):
     if paired:
-        return 3 * HALF
+        return LEAF
     rows = 0
     for far in range(1, seq_size.bit_length() - 1):
         if seq_size >> far == 2:
@@ -132,10 +133,16 @@
     return pieces
 
 
-def paired_pieces(block, eighth):
-    me = lax.axis_index("seq")
-    inside = jnp.logical_not((me == 6) | (me == 1))
-    return [(block[:HALF], None), (block[HALF:], bias_of(inside)), (eighth[...], None)]
+def early_pieces(lower, eighth):
+    me = lax.axis_index("seq")
+    whole = ((me & 1) == 1) & (me >= 2)
+    return [(lower[:HALF], None), (lower[HALF:], bias_of(whole)), (eighth[...], None)]
+
+
+def late_pieces(upper):
+    me = lax.axis_index("seq")
+    whole = ((me & 1) == 0) | (me >= 6)
+    return [(upper[:HALF], bias_of(whole)), (upper[HALF:], bias_of(me < 6))]
 
 
 def place(pieces, values, keys):
@@ -201,8 +208,10 @@
 
 
 def mid_kernel(queries, shared, *rest):
-    *short, scores, values, keys = rest
-    pieces = [(shared, bias_of(lax.axis_index("seq") >= 1))] + [(rows, None) for rows in short]
+    *early, scores, values, keys = rest
+    pieces = [(shared, bias_of(lax.axis_index("seq") >= 1))]
+    if early:
+        pieces += early_pieces(*early)
     bias = place(pieces, values, keys)
     for leaf in range(2):
         rows = split_heads(queries[leaf * LEAF : (leaf + 1) * LEAF])
@@ -236,12 +245,9 @@
     other[:HALF] = jnp.where(second, attended[:HALF], attended[HALF:])
 
 
-def leaves_kernel(seq_size, queries, near_scores, near_values, mid_scores, mid_values, *rest):
-    *far, same, other, keys, values, bias, wide = rest
-    if len(far) == 1:
-        pieces = gathered_pieces(seq_size, far[0], wide)
-    else:
-        pieces = paired_pieces(*far)
+def leaves_kernel(seq_size, paired, queries, near_scores, near_values, mid_scores, mid_values, *rest):
+    late, same, other, keys, values, bias, wide = rest
+    pieces = late_pieces(late) if paired else gathered_pieces(seq_size, late, wide)
     bias[...] = jnp.broadcast_to(place(pieces, values, keys), bias.shape)
     leaf = (lax.axis_index("head") >> 1) ^ 1
     scored = (near_scores, near_values, mid_scores, mid_values)
@@ -338,23 +344,20 @@
     others = [(i, i + 1 if i & 1 else i - 1) for i in range(1, seq_size - 1)]
     outer = lax.ppermute(outer, "seq", others)
     if paired:
-        short, block, eighth = kernel_call(
+        upward, downward, eighth = kernel_call(
             join_kernel,
             "join",
             8,
             [VMEM] * 2,
-            [(HALF, pair_width), (LEAF, pair_width), (HALF, pair_width)],
+            [(LEAF, pair_width), (LEAF, pair_width), (HALF, pair_width)],
             [wide],
         )(inner, quarter)
-        shift = [(i, (i - 2 if i & 1 else i + 2) % seq_size) for i in range(seq_size)]
-        early = (lax.ppermute(short, "seq", shift),)
-        far = (
-            lax.ppermute(block, "seq", [(target, source) for source, target in shift]),
-            swap(eighth, 4),
-        )
+        shift = [(i, (i + 2) % seq_size) for i in range(seq_size)]
+        early = (lax.ppermute(upward, "seq", shift), swap(eighth, 4))
+        late = lax.ppermute(downward, "seq", [(target, source) for source, target in shift])
     else:
         early = ()
-        far = (lax.all_to_all(quarter, "seq", split_axis=0, concat_axis=0),)
+        late = lax.all_to_all(quarter, "seq", split_axis=0, concat_axis=0)
     share = tokens // head_size
     near_scores, near_values, shared = kernel_call(
         functools.partial(near_kernel, seq_size),
@@ -369,7 +372,7 @@
         [pltpu.VMEM((NEAR_ROWS, width), jnp.bfloat16), wide],
         flops=8 * LEAF * NEAR_ROWS * width,
     )(own_queries, own, inner, outer)
-    mid_rows = HALF * (1 + len(early))
+    mid_rows = 4 * HALF if paired else HALF
     mid_scores, mid_values = kernel_call(
         mid_kernel,
         "mid",
@@ -377,16 +380,16 @@
         [VMEM] * (2 + len(early)),
         [jax.ShapeDtypeStruct((2, 2 * LEAF, mid_rows), jnp.float32), (mid_rows, width)],
         [pltpu.VMEM((mid_rows, width), jnp.bfloat16)],
-        flops=520 * 10**6,
+        flops=10**9,
     )(own_queries, shared, *early)
     scored = (near_scores, near_values, mid_scores, mid_values)
     last_rows = last_row_count(seq_size, paired)
     leaf_flops = 8 * LEAF * (NEAR_ROWS + mid_rows + last_rows) * width
     share_2, share_3, far_keys, far_values, far_bias = kernel_call(
-        functools.partial(leaves_kernel, seq_size),
+        functools.partial(leaves_kernel, seq_size, paired),
         "leaves",
         24,
-        [VMEM] * (5 + len(far)),
+        [VMEM] * 6,
         [
             (share + PAD, width),
             (share + PAD, width),
@@ -396,7 +399,7 @@
         ],
         [wide],
         flops=leaf_flops,
-    )(own_queries, *scored, *far)
+    )(own_queries, *scored, late)
     share_0, share_1 = kernel_call(
         stays_kernel, "stays", 16, [VMEM] * 8, [(share, width)] * 2, [], flops=leaf_flops
     )(own_queries, *scored, far_keys, far_values, far_bias)

time: 21.6 us -> 21.2 us (0.981)
  waiting for transfers between devices: 6.64 us -> 5.6 us
  starting transfers between devices: 10.6 us -> 11.5 us
    ppermute x5, starting transfers between devices: 5.93 us -> 7.58 us  [swap(): lax.ppermute(array, axis, [(i, i ^ bit) for i in range(lax.axis_size(axis...]
    ppermute x2, starting transfers between devices: 4.05 us -> 3.31 us  [the longest x1 1.96 us: shards(): early = (lax.ppermute(upward, 'seq', shift), swap(eighth, 4))]
    ppermute x2, waiting for transfers between devices: 1.75 us -> 1.21 us  [the longest x1 0.79 us: shards(): lax.ppermute(downward, 'seq', [(target, source) for source, target in shi...]
    ppermute x5, waiting for transfers between devices: 4.89 us -> 4.39 us  [swap(): lax.ppermute(array, axis, [(i, i ^ bit) for i in range(lax.axis_size(axis...]
  transfers between devices with their start and end apart: 8 -> 8, of which waited for: 5 -> 6; matrix products, arithmetic and copies ran while one was open for 0% -> 0% of each run, Pallas kernels for 7% -> 7%
where the time goes in v16:
time: 21.2 us; the launch traced here: 21 us
  starting transfers between devices  11.5 us (54%)
  waiting for transfers between devices  5.6 us (26%)
  Pallas kernels  3.78 us (18%)
    ppermute x5, starting transfers between devices, swap(): lax.ppermute(array, axis, [(i, i ^ bit) for i in range(lax.axis_size(axis...  7.58 us
    ppermute x5, waiting for transfers between devices, swap(): lax.ppermute(array, axis, [(i, i ^ bit) for i in range(lax.axis_size(axis...  4.39 us
    ppermute x1, starting transfers between devices, shards(): early = (lax.ppermute(upward, 'seq', shift), swap(eighth, 4))  1.96 us
    ppermute x1, starting transfers between devices, shards(): lax.ppermute(downward, 'seq', [(target, source) for source, target in shi...  1.35 us
    pallas_call x1, Pallas kernels, shards(): kernel_call(functools.partial(pack_kernel, not paired), 'pack', 16, [HBM]...  0.99 us
    pallas_call x1, Pallas kernels, shards(): kernel_call(project_kernel, 'project', 8, [VMEM] * 4, [(share, out_weight...  0.81 us
    ppermute x1, waiting for transfers between devices, shards(): lax.ppermute(downward, 'seq', [(target, source) for source, target in shi...  0.79 us
    ppermute x1, starting transfers between devices, shards(): outer = lax.ppermute(outer, 'seq', others)  0.65 us
  transfers between devices with their start and end apart: 8, of which 6 were waited for; matrix products, arithmetic and copies ran while one was open for 0% of the time, Pallas kernels for 7%

profile of v16, /device:TPU:0, one launch (start us, length us, event | category | flops | bytes accessed | tf_op | source)
XLA Modules:
  0.0 21.0 jit_solution(12371737584684210665)
XLA Ops:
  0.0 1.0 %pack.1 = (bf16[256,128]{1,0:T(8,128)(2,1)S(1)}, bf16[256,256]{1,0:T(8,128)(2,1)S(1)}, bf16[192,256]{1,0:T(8,128)(2,1)S(1)}, bf16[192,256]{1,0:T(8,128)(2,1)S(1)}, bf16[64,256]{1,0:T(8,128)(2,1)S(1)}) custom-call(bf16[256,128]{1,0:T(8,128)(2,1)} %queries.1, bf16[256,128]{1,0:T(8,128)(2,1)} %keys.1, bf16[256,128]{1,0:T(8,128)(2,1)} %values.1), custom_call_target="tpu_custom_call" | custom-call | bytes 1048576 | tf_op jit(solution)/shard_map/pack/pallas_call | solution.py:329
  1.0 3.0 %collective-permute-start = (bf16[192,256]{1,0:T(8,128)(2,1)S(1)}, bf16[192,256]{1,0:T(8,128)(2,1)S(1)}, u32[]{:S(2)}, u32[]{:S(2)}) collective-permute-start(bf16[192,256]{1,0:T(8,128)(2,1)S(1)} %get-tuple-element.27), channel_id=1, source_target_pairs={{0,4},{4,0},{8,12},{12,8},{16,20},{20,16},{24,28},{28,24},{1,5},{5... | collective-permute-start | bytes 294920 | tf_op jit(solution)/shard_map/ppermute | solution.py:327
  4.0 0.7 %collective-permute-start.1 = (bf16[192,256]{1,0:T(8,128)(2,1)S(1)}, bf16[192,256]{1,0:T(8,128)(2,1)S(1)}, u32[]{:S(2)}, u32[]{:S(2)}) collective-permute-start(bf16[192,256]{1,0:T(8,128)(2,1)S(1)} %get-tuple-element.28), channel_id=1, source_target_pairs={{4,8},{8,4},{12,16},{16,12},{20,24},{24,20},{5,9},{9,5},{13,17},{1... | collective-permute-start | bytes 294920 | tf_op jit(solution)/shard_map/ppermute | solution.py:345
  4.7 2.1 %collective-permute-done.inner = bf16[192,256]{1,0:T(8,128)(2,1)S(1)} collective-permute-done((bf16[192,256]{1,0:T(8,128)(2,1)S(1)}, bf16[192,256]{1,0:T(8,128)(2,1)S(1)}, u32[]{:S(2)}, u32[]{:S(2)}) %collective-permute-start) | collective-permute-done | bytes 98336 | tf_op jit(solution)/shard_map/ppermute | solution.py:327
  6.8 0.1 join.1
  6.9 2.0 %collective-permute-start.2 = (bf16[128,256]{1,0:T(8,128)(2,1)S(1)}, bf16[128,256]{1,0:T(8,128)(2,1)S(1)}, u32[]{:S(2)}, u32[]{:S(2)}) collective-permute-start(bf16[128,256]{1,0:T(8,128)(2,1)S(1)} %get-tuple-element.33), channel_id=1, source_target_pairs={{0,8},{4,12},{8,16},{12,20},{16,24},{20,28},{24,0},{28,4},{1,9},{5... | collective-permute-start | bytes 196616 | tf_op jit(solution)/shard_map/ppermute | solution.py:356
  8.8 2.6 %collective-permute-start.3 = (bf16[64,256]{1,0:T(8,128)(2,1)S(1)}, bf16[64,256]{1,0:T(8,128)(2,1)S(1)}, u32[]{:S(2)}, u32[]{:S(2)}) collective-permute-start(bf16[64,256]{1,0:T(8,128)(2,1)S(1)} %get-tuple-element.34), channel_id=1, source_target_pairs={{0,16},{4,20},{8,24},{12,28},{16,0},{20,4},{24,8},{28,12},{1,17},{... | collective-permute-start | bytes 98312 | tf_op jit(solution)/shard_map/ppermute | solution.py:327
  11.4 1.3 %collective-permute-start.4 = (bf16[128,256]{1,0:T(8,128)(2,1)S(1)}, bf16[128,256]{1,0:T(8,128)(2,1)S(1)}, u32[]{:S(2)}, u32[]{:S(2)}) collective-permute-start(bf16[128,256]{1,0:T(8,128)(2,1)S(1)} %get-tuple-element.37), channel_id=1, source_target_pairs={{8,0},{12,4},{16,8},{20,12},{24,16},{28,20},{0,24},{4,28},{9,1},{1... | collective-permute-start | bytes 196616 | tf_op jit(solution)/shard_map/ppermute | solution.py:357
  12.8 0.0 collective-permute-done.1.outer
  12.8 0.4 %near.1 = (f32[2,256,512]{2,1,0:T(8,128)S(1)}, bf16[2,512,128]{2,1,0:T(8,128)(2,1)S(1)}, bf16[64,256]{1,0:T(8,128)(2,1)S(1)}) custom-call(bf16[256,128]{1,0:T(8,128)(2,1)S(1)} %get-tuple-element.25.queries, bf16[256,256]{1,0:T(8,128)(2,1)S(1)} %get-tuple-element.26.own, bf16[192,256]{1,0:T(8,128)(2,1)S(1)} %collective-permute-done.inner, ...), custom_call_target="tpu_custom_call" | custom-call | flops 67108864 | bytes 1048576 | tf_op jit(solution)/shard_map/near/pallas_call | solution.py:362
  13.2 1.1 %collective-permute-done.3.rest_1_ = bf16[64,256]{1,0:T(8,128)(2,1)S(1)} collective-permute-done((bf16[64,256]{1,0:T(8,128)(2,1)S(1)}, bf16[64,256]{1,0:T(8,128)(2,1)S(1)}, u32[]{:S(2)}, u32[]{:S(2)}) %collective-permute-start.3) | collective-permute-done | bytes 32800 | tf_op jit(solution)/shard_map/ppermute | solution.py:327
  14.2 0.4 %collective-permute-done.2.rest_0_ = bf16[128,256]{1,0:T(8,128)(2,1)S(1)} collective-permute-done((bf16[128,256]{1,0:T(8,128)(2,1)S(1)}, bf16[128,256]{1,0:T(8,128)(2,1)S(1)}, u32[]{:S(2)}, u32[]{:S(2)}) %collective-permute-start.2) | collective-permute-done | bytes 65568 | tf_op jit(solution)/shard_map/ppermute | solution.py:356
  14.7 0.2 %mid.1 = (f32[2,256,256]{2,1,0:T(8,128)S(1)}, bf16[256,128]{1,0:T(8,128)(2,1)S(1)}) custom-call(bf16[256,128]{1,0:T(8,128)(2,1)S(1)} %get-tuple-element.25.queries, bf16[64,256]{1,0:T(8,128)(2,1)S(1)} %get-tuple-element.31.shared, bf16[128,256]{1,0:T(8,128)(2,1)S(1)} %collective-permute-done.2.rest_0_, bf16[64,256]{1,0:T(8,128)(2,1)S(1)} %collective-permute-done.3.rest_1_), custom_call_target="tpu_custom_call" | custom-call | flops 1000000000 | bytes 1048576 | tf_op jit(solution)/shard_map/mid/pallas_call | solution.py:376
  14.9 0.8 %collective-permute-done.4.rest_0_ = bf16[128,256]{1,0:T(8,128)(2,1)S(1)} collective-permute-done((bf16[128,256]{1,0:T(8,128)(2,1)S(1)}, bf16[128,256]{1,0:T(8,128)(2,1)S(1)}, u32[]{:S(2)}, u32[]{:S(2)}) %collective-permute-start.4) | collective-permute-done | bytes 65568 | tf_op jit(solution)/shard_map/ppermute | solution.py:357
  15.7 0.6 %leaves.1 = (bf16[80,128]{1,0:T(8,128)(2,1)S(1)}, bf16[80,128]{1,0:T(8,128)(2,1)S(1)}, bf16[128,128]{1,0:T(8,128)(2,1)S(1)}, bf16[128,128]{1,0:T(8,128)(2,1)S(1)}, f32[8,128]{1,0:T(8,128)S(1)}) custom-call(bf16[256,128]{1,0:T(8,128)(2,1)S(1)} %get-tuple-element.25.queries, f32[2,256,512]{2,1,0:T(8,128)S(1)} %get-tuple-element.29.near_scores, ...), custom_call_target="tpu_custom_call" | custom-call | flops 117440512 | bytes 1048576 | tf_op jit(solution)/shard_map/leaves/pallas_call | solution.py:388
  16.3 0.1 collective-permute-start.6
  16.3 1.6 %collective-permute-start.7 = (bf16[80,128]{1,0:T(8,128)(2,1)S(1)}, bf16[80,128]{1,0:T(8,128)(2,1)S(1)}, u32[]{:S(2)}, u32[]{:S(2)}) collective-permute-start(bf16[80,128]{1,0:T(8,128)(2,1)S(1)} %get-tuple-element.44), channel_id=1, source_target_pairs={{0,2},{1,3},{2,0},{3,1},{4,6},{5,7},{6,4},{7,5},{8,10},{9,11},{10,... | collective-permute-start | bytes 61448 | tf_op jit(solution)/shard_map/ppermute | solution.py:327
  17.9 0.0 copy-start
  17.9 0.6 %stays.1 = (bf16[64,128]{1,0:T(8,128)(2,1)S(1)}, bf16[64,128]{1,0:T(8,128)(2,1)S(1)}) custom-call(bf16[256,128]{1,0:T(8,128)(2,1)S(1)} %get-tuple-element.25.queries, f32[2,256,512]{2,1,0:T(8,128)S(1)} %get-tuple-element.29.near_scores, bf16[2,512,128]{2,1,0:T(8,128)(2,1)S(1)} %get-tuple-element.30.near_values, ...), custom_call_target="tpu_custom_call" | custom-call | flops 117440512 | bytes 1048576 | tf_op jit(solution)/shard_map/stays/pallas_call | solution.py:403
  18.5 0.3 %collective-permute-start.5 = (bf16[64,128]{1,0:T(8,128)(2,1)S(1)}, bf16[64,128]{1,0:T(8,128)(2,1)S(1)}, u32[]{:S(2)}, u32[]{:S(2)}) collective-permute-start(bf16[64,128]{1,0:T(8,128)(2,1)S(1)} %get-tuple-element.42), channel_id=1, source_target_pairs={{0,1},{1,0},{2,3},{3,2},{4,5},{5,4},{6,7},{7,6},{8,9},{9,8},{10,11... | collective-permute-start | bytes 49160 | tf_op jit(solution)/shard_map/ppermute | solution.py:327
  18.8 0.9 %collective-permute-done.5.other = bf16[64,128]{1,0:T(8,128)(2,1)S(1)} collective-permute-done((bf16[64,128]{1,0:T(8,128)(2,1)S(1)}, bf16[64,128]{1,0:T(8,128)(2,1)S(1)}, u32[]{:S(2)}, u32[]{:S(2)}) %collective-permute-start.5) | collective-permute-done | bytes 16416 | tf_op jit(solution)/shard_map/ppermute | solution.py:327
  19.7 0.0 copy-done
  19.7 0.2 begin.1.partial
  19.9 0.0 collective-permute-done.6.other
  19.9 0.3 %collective-permute-done.7.same = bf16[80,128]{1,0:T(8,128)(2,1)S(1)} collective-permute-done((bf16[80,128]{1,0:T(8,128)(2,1)S(1)}, bf16[80,128]{1,0:T(8,128)(2,1)S(1)}, u32[]{:S(2)}, u32[]{:S(2)}) %collective-permute-start.7) | collective-permute-done | bytes 20512 | tf_op jit(solution)/shard_map/ppermute | solution.py:327
  20.2 0.8 %project.1 = bf16[64,512]{1,0:T(8,128)(2,1)} custom-call(f32[64,512]{1,0:T(8,128)S(1)} %begin.1.partial, bf16[80,128]{1,0:T(8,128)(2,1)S(1)} %collective-permute-done.6.other, bf16[80,128]{1,0:T(8,128)(2,1)S(1)} %collective-permute-done.7.same, bf16[512,512]{1,0:T(8,128)(2,1)S(1)} %copy-done), custom_call_target="tpu_custom_call" | custom-call | bytes 1048576 | tf_op jit(solution)/shard_map/project/pallas_call | solution.py:416
Async XLA Ops:
  1.0 5.8 %collective-permute-start = (bf16[192,256]{1,0:T(8,128)(2,1)S(1)}, bf16[192,256]{1,0:T(8,128)(2,1)S(1)}, u32[]{:S(2)}, u32[]{:S(2)}) collective-permute-start(bf16[192,256]{1,0:T(8,128)(2,1)S(1)} %get-tuple-element.27), channel_id=1, source_target_pairs={{0,4},{4,0},{8,12},{12,8},{16,20},{20,16},{24,28},{28,24},{1,5},{5... | collective-permute-start | bytes 294920 | tf_op jit(solution)/shard_map/ppermute | solution.py:327
  4.0 8.8 %collective-permute-start.1 = (bf16[192,256]{1,0:T(8,128)(2,1)S(1)}, bf16[192,256]{1,0:T(8,128)(2,1)S(1)}, u32[]{:S(2)}, u32[]{:S(2)}) collective-permute-start(bf16[192,256]{1,0:T(8,128)(2,1)S(1)} %get-tuple-element.28), channel_id=1, source_target_pairs={{4,8},{8,4},{12,16},{16,12},{20,24},{24,20},{5,9},{9,5},{13,17},{1... | collective-permute-start | bytes 294920 | tf_op jit(solution)/shard_map/ppermute | solution.py:345
  6.9 7.8 %collective-permute-start.2 = (bf16[128,256]{1,0:T(8,128)(2,1)S(1)}, bf16[128,256]{1,0:T(8,128)(2,1)S(1)}, u32[]{:S(2)}, u32[]{:S(2)}) collective-permute-start(bf16[128,256]{1,0:T(8,128)(2,1)S(1)} %get-tuple-element.33), channel_id=1, source_target_pairs={{0,8},{4,12},{8,16},{12,20},{16,24},{20,28},{24,0},{28,4},{1,9},{5... | collective-permute-start | bytes 196616 | tf_op jit(solution)/shard_map/ppermute | solution.py:356
  8.8 5.4 %collective-permute-start.3 = (bf16[64,256]{1,0:T(8,128)(2,1)S(1)}, bf16[64,256]{1,0:T(8,128)(2,1)S(1)}, u32[]{:S(2)}, u32[]{:S(2)}) collective-permute-start(bf16[64,256]{1,0:T(8,128)(2,1)S(1)} %get-tuple-element.34), channel_id=1, source_target_pairs={{0,16},{4,20},{8,24},{12,28},{16,0},{20,4},{24,8},{28,12},{1,17},{... | collective-permute-start | bytes 98312 | tf_op jit(solution)/shard_map/ppermute | solution.py:327
  11.4 4.3 %collective-permute-start.4 = (bf16[128,256]{1,0:T(8,128)(2,1)S(1)}, bf16[128,256]{1,0:T(8,128)(2,1)S(1)}, u32[]{:S(2)}, u32[]{:S(2)}) collective-permute-start(bf16[128,256]{1,0:T(8,128)(2,1)S(1)} %get-tuple-element.37), channel_id=1, source_target_pairs={{8,0},{12,4},{16,8},{20,12},{24,16},{28,20},{0,24},{4,28},{9,1},{1... | collective-permute-start | bytes 196616 | tf_op jit(solution)/shard_map/ppermute | solution.py:357
  16.3 3.7 %collective-permute-start.6 = (bf16[80,128]{1,0:T(8,128)(2,1)S(1)}, bf16[80,128]{1,0:T(8,128)(2,1)S(1)}, u32[]{:S(2)}, u32[]{:S(2)}) collective-permute-start(bf16[80,128]{1,0:T(8,128)(2,1)S(1)} %get-tuple-element.43), channel_id=1, source_target_pairs={{0,3},{1,2},{2,1},{3,0},{4,7},{5,6},{6,5},{7,4},{8,11},{9,10},{10,... | collective-permute-start | bytes 61448 | tf_op jit(solution)/shard_map/ppermute | solution.py:327
  16.3 3.8 %collective-permute-start.7 = (bf16[80,128]{1,0:T(8,128)(2,1)S(1)}, bf16[80,128]{1,0:T(8,128)(2,1)S(1)}, u32[]{:S(2)}, u32[]{:S(2)}) collective-permute-start(bf16[80,128]{1,0:T(8,128)(2,1)S(1)} %get-tuple-element.44), channel_id=1, source_target_pairs={{0,2},{1,3},{2,0},{3,1},{4,6},{5,7},{6,4},{7,5},{8,10},{9,11},{10,... | collective-permute-start | bytes 61448 | tf_op jit(solution)/shard_map/ppermute | solution.py:327
  17.9 1.8 %copy-start = (bf16[512,512]{1,0:T(8,128)(2,1)S(1)}, bf16[512,512]{1,0:T(8,128)(2,1)}, u32[]{:S(2)}) copy-start(bf16[512,512]{1,0:T(8,128)(2,1)} %weight.3) | copy-start | bytes 1572868
  18.5 1.2 %collective-permute-start.5 = (bf16[64,128]{1,0:T(8,128)(2,1)S(1)}, bf16[64,128]{1,0:T(8,128)(2,1)S(1)}, u32[]{:S(2)}, u32[]{:S(2)}) collective-permute-start(bf16[64,128]{1,0:T(8,128)(2,1)S(1)} %get-tuple-element.42), channel_id=1, source_target_pairs={{0,1},{1,0},{2,3},{3,2},{4,5},{5,4},{6,7},{7,6},{8,9},{9,8},{10,11... | collective-permute-start | bytes 49160 | tf_op jit(solution)/shard_map/ppermute | solution.py:327

commit v17 on v16

--- a/solution.py
+++ b/solution.py
@@ -54,9 +54,10 @@
         quarter[...] = level_two
 
 
-def join_kernel(inner, quarter, upward, downward, eighth, wide):
+def join_kernel(inner, quarter, opening, downward, closing, eighth, wide):
     me = lax.axis_index("seq")
     odd = me & 1
+    pair = me >> 1
     edge_half = average_pairs(inner[:LEAF], wide)
     other_half = inner[LEAF:]
     theirs = jnp.concatenate(
@@ -66,10 +67,11 @@
     first = jnp.where(odd == 1, theirs, quarter[...])
     second = jnp.where(odd == 1, quarter[...], theirs)
     level_three = average_pairs(jnp.concatenate([first, second], axis=0), wide)
-    upward[:HALF] = jnp.where(me >= 6, level_three, first)
-    upward[HALF:] = second
-    downward[:HALF] = jnp.where(me < 2, level_three, first)
-    downward[HALF:] = second
+    opening[:HALF] = jnp.where(pair == 0, first, level_three)
+    downward[:HALF] = jnp.where(pair == 0, level_three, first)
+    closing[:HALF] = jnp.where(pair == 3, level_three, first)
+    for sent in (opening, downward, closing):
+        sent[HALF:] = second
     eighth[...] = level_three
 
 
@@ -79,7 +81,7 @@
 
 def last_row_count(seq_size, paired):
     if paired:
-        return LEAF
+        return 2 * LEAF
     rows = 0
     for far in range(1, seq_size.bit_length() - 1):
         if seq_size >> far == 2:
@@ -133,16 +135,21 @@
     return pieces
 
 
-def early_pieces(lower, eighth):
+def early_pieces(opening, eighth):
+    pair = lax.axis_index("seq") >> 1
+    return [(jnp.where(pair == 2, eighth[...], opening[:HALF]), None)]
+
+
+def late_pieces(opening, eighth, upper, closing):
     me = lax.axis_index("seq")
-    whole = ((me & 1) == 1) & (me >= 2)
-    return [(lower[:HALF], None), (lower[HALF:], bias_of(whole)), (eighth[...], None)]
-
-
-def late_pieces(upper):
-    me = lax.axis_index("seq")
-    whole = ((me & 1) == 0) | (me >= 6)
-    return [(upper[:HALF], bias_of(whole)), (upper[HALF:], bias_of(me < 6))]
+    odd = (me & 1) == 1
+    pair = me >> 1
+    return [
+        (jnp.where(pair == 0, eighth[...], closing[:HALF]), None),
+        (jnp.where(pair == 1, opening[HALF:], closing[HALF:]), bias_of(odd & (pair >= 1))),
+        (upper[:HALF], bias_of(jnp.logical_not(odd) | (pair == 3))),
+        (upper[HALF:], bias_of(pair <= 2)),
+    ]
 
 
 def place(pieces, values, keys):
@@ -246,8 +253,8 @@
 
 
 def leaves_kernel(seq_size, paired, queries, near_scores, near_values, mid_scores, mid_values, *rest):
-    late, same, other, keys, values, bias, wide = rest
-    pieces = late_pieces(late) if paired else gathered_pieces(seq_size, late, wide)
+    *late, same, other, keys, values, bias, wide = rest
+    pieces = late_pieces(*late) if paired else gathered_pieces(seq_size, late[0], wide)
     bias[...] = jnp.broadcast_to(place(pieces, values, keys), bias.shape)
     leaf = (lax.axis_index("head") >> 1) ^ 1
     scored = (near_scores, near_values, mid_scores, mid_values)
@@ -344,20 +351,24 @@
     others = [(i, i + 1 if i & 1 else i - 1) for i in range(1, seq_size - 1)]
     outer = lax.ppermute(outer, "seq", others)
     if paired:
-        upward, downward, eighth = kernel_call(
+        opening, downward, closing, eighth = kernel_call(
             join_kernel,
             "join",
             8,
             [VMEM] * 2,
-            [(LEAF, pair_width), (LEAF, pair_width), (HALF, pair_width)],
+            [(LEAF, pair_width)] * 3 + [(HALF, pair_width)],
             [wide],
         )(inner, quarter)
-        shift = [(i, (i + 2) % seq_size) for i in range(seq_size)]
-        early = (lax.ppermute(upward, "seq", shift), swap(eighth, 4))
-        late = lax.ppermute(downward, "seq", [(target, source) for source, target in shift])
+
+        def over_pairs(array, targets):
+            spans = [(2 * p + x, 2 * t + x) for p, t in enumerate(targets) for x in range(2)]
+            return lax.ppermute(array, "seq", spans)
+
+        early = (over_pairs(opening, (1, 3, 2, 0)), over_pairs(eighth, (2, 1, 0, 3)))
+        late = early + (over_pairs(downward, (3, 0, 1, 2)), over_pairs(closing, (0, 2, 3, 1)))
     else:
         early = ()
-        late = lax.all_to_all(quarter, "seq", split_axis=0, concat_axis=0)
+        late = (lax.all_to_all(quarter, "seq", split_axis=0, concat_axis=0),)
     share = tokens // head_size
     near_scores, near_values, shared = kernel_call(
         functools.partial(near_kernel, seq_size),
@@ -372,7 +383,7 @@
         [pltpu.VMEM((NEAR_ROWS, width), jnp.bfloat16), wide],
         flops=8 * LEAF * NEAR_ROWS * width,
     )(own_queries, own, inner, outer)
-    mid_rows = 4 * HALF if paired else HALF
+    mid_rows = LEAF if paired else HALF
     mid_scores, mid_values = kernel_call(
         mid_kernel,
         "mid",
@@ -389,7 +400,7 @@
         functools.partial(leaves_kernel, seq_size, paired),
         "leaves",
         24,
-        [VMEM] * 6,
+        [VMEM] * (5 + len(late)),
         [
             (share + PAD, width),
             (share + PAD, width),
@@ -399,7 +410,7 @@
         ],
         [wide],
         flops=leaf_flops,
-    )(own_queries, *scored, late)
+    )(own_queries, *scored, *late)
     share_0, share_1 = kernel_call(
         stays_kernel, "stays", 16, [VMEM] * 8, [(share, width)] * 2, [], flops=leaf_flops
     )(own_queries, *scored, far_keys, far_values, far_bias)

time: 21.2 us -> 25.2 us (1.19)
  the two profiles are of different devices: /device:TPU:0 before, /device:TPU:11 now
where the time goes in v17:
time: 25.2 us; the launch traced here: 25 us
  starting transfers between devices  17.1 us (68%)
  waiting for transfers between devices  3.93 us (16%)
  Pallas kernels  3.83 us (15%)
    ppermute x4, starting transfers between devices, over_pairs(): return lax.ppermute(array, 'seq', spans)  8.44 us
    ppermute x4, starting transfers between devices, swap(): lax.ppermute(array, axis, [(i, i ^ bit) for i in range(lax.axis_size(axis...  4.56 us
    ppermute x1, starting transfers between devices, shards(): outer = lax.ppermute(outer, 'seq', others)  4.12 us
    ppermute x4, waiting for transfers between devices, over_pairs(): return lax.ppermute(array, 'seq', spans)  2.6 us
    ppermute x4, waiting for transfers between devices, swap(): lax.ppermute(array, axis, [(i, i ^ bit) for i in range(lax.axis_size(axis...  1.32 us
    pallas_call x1, Pallas kernels, shards(): kernel_call(functools.partial(pack_kernel, not paired), 'pack', 16, [HBM]...  0.99 us
    pallas_call x1, Pallas kernels, shards(): kernel_call(project_kernel, 'project', 8, [VMEM] * 4, [(share, out_weight...  0.81 us
    pallas_call x1, Pallas kernels, shards(): kernel_call(functools.partial(leaves_kernel, seq_size, paired), 'leaves',...  0.62 us
  transfers between devices with their start and end apart: 9, of which 3 were waited for; matrix products, arithmetic and copies ran while one was open for 0% of the time, Pallas kernels for 6%

profile of v17, /device:TPU:11, one launch (start us, length us, event | category | flops | bytes accessed | tf_op | source)
XLA Modules:
  0.0 25.0 jit_solution(4107653383737043265)
XLA Ops:
  0.0 1.0 %pack.1 = (bf16[256,128]{1,0:T(8,128)(2,1)S(1)}, bf16[256,256]{1,0:T(8,128)(2,1)S(1)}, bf16[192,256]{1,0:T(8,128)(2,1)S(1)}, bf16[192,256]{1,0:T(8,128)(2,1)S(1)}, bf16[64,256]{1,0:T(8,128)(2,1)S(1)}) custom-call(bf16[256,128]{1,0:T(8,128)(2,1)} %queries.1, bf16[256,128]{1,0:T(8,128)(2,1)} %keys.1, bf16[256,128]{1,0:T(8,128)(2,1)} %values.1), custom_call_target="tpu_custom_call" | custom-call | bytes 1048576 | tf_op jit(solution)/shard_map/pack/pallas_call | solution.py:336
  1.0 0.3 %collective-permute-start = (bf16[192,256]{1,0:T(8,128)(2,1)S(1)}, bf16[192,256]{1,0:T(8,128)(2,1)S(1)}, u32[]{:S(2)}, u32[]{:S(2)}) collective-permute-start(bf16[192,256]{1,0:T(8,128)(2,1)S(1)} %get-tuple-element.28), channel_id=1, source_target_pairs={{0,4},{4,0},{8,12},{12,8},{16,20},{20,16},{24,28},{28,24},{1,5},{5... | collective-permute-start | bytes 294920 | tf_op jit(solution)/shard_map/ppermute | solution.py:334
  1.3 4.1 %collective-permute-start.1 = (bf16[192,256]{1,0:T(8,128)(2,1)S(1)}, bf16[192,256]{1,0:T(8,128)(2,1)S(1)}, u32[]{:S(2)}, u32[]{:S(2)}) collective-permute-start(bf16[192,256]{1,0:T(8,128)(2,1)S(1)} %get-tuple-element.29), channel_id=1, source_target_pairs={{4,8},{8,4},{12,16},{16,12},{20,24},{24,20},{5,9},{9,5},{13,17},{1... | collective-permute-start | bytes 294920 | tf_op jit(solution)/shard_map/ppermute | solution.py:352
  5.5 0.0 collective-permute-done.inner
  5.5 0.1 join.1
  5.5 3.3 %collective-permute-start.2 = (bf16[128,256]{1,0:T(8,128)(2,1)S(1)}, bf16[128,256]{1,0:T(8,128)(2,1)S(1)}, u32[]{:S(2)}, u32[]{:S(2)}) collective-permute-start(bf16[128,256]{1,0:T(8,128)(2,1)S(1)} %get-tuple-element.34), channel_id=1, source_target_pairs={{0,8},{4,12},{8,24},{12,28},{16,16},{20,20},{24,0},{28,4},{1,9},{5... | collective-permute-start | bytes 196616 | tf_op jit(solution)/shard_map/ppermute | solution.py:365
  8.8 0.7 %collective-permute-start.3 = (bf16[64,256]{1,0:T(8,128)(2,1)S(1)}, bf16[64,256]{1,0:T(8,128)(2,1)S(1)}, u32[]{:S(2)}, u32[]{:S(2)}) collective-permute-start(bf16[64,256]{1,0:T(8,128)(2,1)S(1)} %get-tuple-element.35), channel_id=1, source_target_pairs={{0,16},{4,20},{8,8},{12,12},{16,0},{20,4},{24,24},{28,28},{1,17},{... | collective-permute-start | bytes 98312 | tf_op jit(solution)/shard_map/ppermute | solution.py:365
  9.5 1.4 %collective-permute-start.4 = (bf16[128,256]{1,0:T(8,128)(2,1)S(1)}, bf16[128,256]{1,0:T(8,128)(2,1)S(1)}, u32[]{:S(2)}, u32[]{:S(2)}) collective-permute-start(bf16[128,256]{1,0:T(8,128)(2,1)S(1)} %get-tuple-element.38), channel_id=1, source_target_pairs={{0,24},{4,28},{8,0},{12,4},{16,8},{20,12},{24,16},{28,20},{1,25},{... | collective-permute-start | bytes 196616 | tf_op jit(solution)/shard_map/ppermute | solution.py:365
  10.9 3.1 %collective-permute-start.5 = (bf16[128,256]{1,0:T(8,128)(2,1)S(1)}, bf16[128,256]{1,0:T(8,128)(2,1)S(1)}, u32[]{:S(2)}, u32[]{:S(2)}) collective-permute-start(bf16[128,256]{1,0:T(8,128)(2,1)S(1)} %get-tuple-element.39), channel_id=1, source_target_pairs={{0,0},{4,4},{8,16},{12,20},{16,24},{20,28},{24,8},{28,12},{1,1},{5... | collective-permute-start | bytes 196616 | tf_op jit(solution)/shard_map/ppermute | solution.py:365
  14.0 0.0 collective-permute-done.1.outer
  14.0 0.4 %near.1 = (f32[2,256,512]{2,1,0:T(8,128)S(1)}, bf16[2,512,128]{2,1,0:T(8,128)(2,1)S(1)}, bf16[64,256]{1,0:T(8,128)(2,1)S(1)}) custom-call(bf16[256,128]{1,0:T(8,128)(2,1)S(1)} %get-tuple-element.26.queries, bf16[256,256]{1,0:T(8,128)(2,1)S(1)} %get-tuple-element.27.own, bf16[192,256]{1,0:T(8,128)(2,1)S(1)} %collective-permute-done.inner, ...), custom_call_target="tpu_custom_call" | custom-call | flops 67108864 | bytes 1048576 | tf_op jit(solution)/shard_map/near/pallas_call | solution.py:373
  14.4 0.0 collective-permute-done.3.rest_1_
  14.4 0.0 collective-permute-done.2.rest_0_
  14.4 0.2 mid.1
  14.6 0.0 collective-permute-done.4.rest_2_
  14.6 2.6 %collective-permute-done.5.rest_3_ = bf16[128,256]{1,0:T(8,128)(2,1)S(1)} collective-permute-done((bf16[128,256]{1,0:T(8,128)(2,1)S(1)}, bf16[128,256]{1,0:T(8,128)(2,1)S(1)}, u32[]{:S(2)}, u32[]{:S(2)}) %collective-permute-start.5) | collective-permute-done | bytes 65568 | tf_op jit(solution)/shard_map/ppermute | solution.py:365
  17.2 0.6 %leaves.1 = (bf16[80,128]{1,0:T(8,128)(2,1)S(1)}, bf16[80,128]{1,0:T(8,128)(2,1)S(1)}, bf16[256,128]{1,0:T(8,128)(2,1)S(1)}, bf16[256,128]{1,0:T(8,128)(2,1)S(1)}, f32[8,256]{1,0:T(8,128)S(1)}) custom-call(bf16[256,128]{1,0:T(8,128)(2,1)S(1)} %get-tuple-element.26.queries, f32[2,256,512]{2,1,0:T(8,128)S(1)} %get-tuple-element.30.near_scores, ...), custom_call_target="tpu_custom_call" | custom-call | flops 117440512 | bytes 1048576 | tf_op jit(solution)/shard_map/leaves/pallas_call | solution.py:399
  17.9 3.7 %collective-permute-start.7 = (bf16[80,128]{1,0:T(8,128)(2,1)S(1)}, bf16[80,128]{1,0:T(8,128)(2,1)S(1)}, u32[]{:S(2)}, u32[]{:S(2)}) collective-permute-start(bf16[80,128]{1,0:T(8,128)(2,1)S(1)} %get-tuple-element.45), channel_id=1, source_target_pairs={{0,3},{1,2},{2,1},{3,0},{4,7},{5,6},{6,5},{7,4},{8,11},{9,10},{10,... | collective-permute-start | bytes 61448 | tf_op jit(solution)/shard_map/ppermute | solution.py:334
  21.6 0.2 collective-permute-start.8
  21.8 0.0 copy-start
  21.8 0.6 %stays.1 = (bf16[64,128]{1,0:T(8,128)(2,1)S(1)}, bf16[64,128]{1,0:T(8,128)(2,1)S(1)}) custom-call(bf16[256,128]{1,0:T(8,128)(2,1)S(1)} %get-tuple-element.26.queries, f32[2,256,512]{2,1,0:T(8,128)S(1)} %get-tuple-element.30.near_scores, bf16[2,512,128]{2,1,0:T(8,128)(2,1)S(1)} %get-tuple-element.31.near_values, ...), custom_call_target="tpu_custom_call" | custom-call | flops 117440512 | bytes 1048576 | tf_op jit(solution)/shard_map/stays/pallas_call | solution.py:414
  22.4 0.3 %collective-permute-start.6 = (bf16[64,128]{1,0:T(8,128)(2,1)S(1)}, bf16[64,128]{1,0:T(8,128)(2,1)S(1)}, u32[]{:S(2)}, u32[]{:S(2)}) collective-permute-start(bf16[64,128]{1,0:T(8,128)(2,1)S(1)} %get-tuple-element.44), channel_id=1, source_target_pairs={{0,1},{1,0},{2,3},{3,2},{4,5},{5,4},{6,7},{7,6},{8,9},{9,8},{10,11... | collective-permute-start | bytes 49160 | tf_op jit(solution)/shard_map/ppermute | solution.py:334
  22.7 0.9 %collective-permute-done.6.other = bf16[64,128]{1,0:T(8,128)(2,1)S(1)} collective-permute-done((bf16[64,128]{1,0:T(8,128)(2,1)S(1)}, bf16[64,128]{1,0:T(8,128)(2,1)S(1)}, u32[]{:S(2)}, u32[]{:S(2)}) %collective-permute-start.6) | collective-permute-done | bytes 16416 | tf_op jit(solution)/shard_map/ppermute | solution.py:334
  23.6 0.0 copy-done
  23.6 0.2 begin.1.partial
  23.8 0.0 collective-permute-done.7.other
  23.8 0.4 %collective-permute-done.8.same = bf16[80,128]{1,0:T(8,128)(2,1)S(1)} collective-permute-done((bf16[80,128]{1,0:T(8,128)(2,1)S(1)}, bf16[80,128]{1,0:T(8,128)(2,1)S(1)}, u32[]{:S(2)}, u32[]{:S(2)}) %collective-permute-start.8) | collective-permute-done | bytes 20512 | tf_op jit(solution)/shard_map/ppermute | solution.py:334
  24.2 0.8 %project.1 = bf16[64,512]{1,0:T(8,128)(2,1)} custom-call(f32[64,512]{1,0:T(8,128)S(1)} %begin.1.partial, bf16[80,128]{1,0:T(8,128)(2,1)S(1)} %collective-permute-done.7.other, bf16[80,128]{1,0:T(8,128)(2,1)S(1)} %collective-permute-done.8.same, bf16[512,512]{1,0:T(8,128)(2,1)S(1)} %copy-done), custom_call_target="tpu_custom_call" | custom-call | bytes 1048576 | tf_op jit(solution)/shard_map/project/pallas_call | solution.py:427
Async XLA Ops:
  1.0 4.5 %collective-permute-start = (bf16[192,256]{1,0:T(8,128)(2,1)S(1)}, bf16[192,256]{1,0:T(8,128)(2,1)S(1)}, u32[]{:S(2)}, u32[]{:S(2)}) collective-permute-start(bf16[192,256]{1,0:T(8,128)(2,1)S(1)} %get-tuple-element.28), channel_id=1, source_target_pairs={{0,4},{4,0},{8,12},{12,8},{16,20},{20,16},{24,28},{28,24},{1,5},{5... | collective-permute-start | bytes 294920 | tf_op jit(solution)/shard_map/ppermute | solution.py:334
  1.3 12.7 %collective-permute-start.1 = (bf16[192,256]{1,0:T(8,128)(2,1)S(1)}, bf16[192,256]{1,0:T(8,128)(2,1)S(1)}, u32[]{:S(2)}, u32[]{:S(2)}) collective-permute-start(bf16[192,256]{1,0:T(8,128)(2,1)S(1)} %get-tuple-element.29), channel_id=1, source_target_pairs={{4,8},{8,4},{12,16},{16,12},{20,24},{24,20},{5,9},{9,5},{13,17},{1... | collective-permute-start | bytes 294920 | tf_op jit(solution)/shard_map/ppermute | solution.py:352
  5.5 8.9 %collective-permute-start.2 = (bf16[128,256]{1,0:T(8,128)(2,1)S(1)}, bf16[128,256]{1,0:T(8,128)(2,1)S(1)}, u32[]{:S(2)}, u32[]{:S(2)}) collective-permute-start(bf16[128,256]{1,0:T(8,128)(2,1)S(1)} %get-tuple-element.34), channel_id=1, source_target_pairs={{0,8},{4,12},{8,24},{12,28},{16,16},{20,20},{24,0},{28,4},{1,9},{5... | collective-permute-start | bytes 196616 | tf_op jit(solution)/shard_map/ppermute | solution.py:365
  8.8 5.6 %collective-permute-start.3 = (bf16[64,256]{1,0:T(8,128)(2,1)S(1)}, bf16[64,256]{1,0:T(8,128)(2,1)S(1)}, u32[]{:S(2)}, u32[]{:S(2)}) collective-permute-start(bf16[64,256]{1,0:T(8,128)(2,1)S(1)} %get-tuple-element.35), channel_id=1, source_target_pairs={{0,16},{4,20},{8,8},{12,12},{16,0},{20,4},{24,24},{28,28},{1,17},{... | collective-permute-start | bytes 98312 | tf_op jit(solution)/shard_map/ppermute | solution.py:365
  9.5 5.1 %collective-permute-start.4 = (bf16[128,256]{1,0:T(8,128)(2,1)S(1)}, bf16[128,256]{1,0:T(8,128)(2,1)S(1)}, u32[]{:S(2)}, u32[]{:S(2)}) collective-permute-start(bf16[128,256]{1,0:T(8,128)(2,1)S(1)} %get-tuple-element.38), channel_id=1, source_target_pairs={{0,24},{4,28},{8,0},{12,4},{16,8},{20,12},{24,16},{28,20},{1,25},{... | collective-permute-start | bytes 196616 | tf_op jit(solution)/shard_map/ppermute | solution.py:365
  10.9 6.3 %collective-permute-start.5 = (bf16[128,256]{1,0:T(8,128)(2,1)S(1)}, bf16[128,256]{1,0:T(8,128)(2,1)S(1)}, u32[]{:S(2)}, u32[]{:S(2)}) collective-permute-start(bf16[128,256]{1,0:T(8,128)(2,1)S(1)} %get-tuple-element.39), channel_id=1, source_target_pairs={{0,0},{4,4},{8,16},{12,20},{16,24},{20,28},{24,8},{28,12},{1,1},{5... | collective-permute-start | bytes 196616 | tf_op jit(solution)/shard_map/ppermute | solution.py:365
  17.9 5.9 %collective-permute-start.7 = (bf16[80,128]{1,0:T(8,128)(2,1)S(1)}, bf16[80,128]{1,0:T(8,128)(2,1)S(1)}, u32[]{:S(2)}, u32[]{:S(2)}) collective-permute-start(bf16[80,128]{1,0:T(8,128)(2,1)S(1)} %get-tuple-element.45), channel_id=1, source_target_pairs={{0,3},{1,2},{2,1},{3,0},{4,7},{5,6},{6,5},{7,4},{8,11},{9,10},{10,... | collective-permute-start | bytes 61448 | tf_op jit(solution)/shard_map/ppermute | solution.py:334
  21.6 2.6 %collective-permute-start.8 = (bf16[80,128]{1,0:T(8,128)(2,1)S(1)}, bf16[80,128]{1,0:T(8,128)(2,1)S(1)}, u32[]{:S(2)}, u32[]{:S(2)}) collective-permute-start(bf16[80,128]{1,0:T(8,128)(2,1)S(1)} %get-tuple-element.46), channel_id=1, source_target_pairs={{0,2},{1,3},{2,0},{3,1},{4,6},{5,7},{6,4},{7,5},{8,10},{9,11},{10,... | collective-permute-start | bytes 61448 | tf_op jit(solution)/shard_map/ppermute | solution.py:334
  21.8 1.8 %copy-start = (bf16[512,512]{1,0:T(8,128)(2,1)S(1)}, bf16[512,512]{1,0:T(8,128)(2,1)}, u32[]{:S(2)}) copy-start(bf16[512,512]{1,0:T(8,128)(2,1)} %weight.3) | copy-start | bytes 1572868
  22.4 1.2 %collective-permute-start.6 = (bf16[64,128]{1,0:T(8,128)(2,1)S(1)}, bf16[64,128]{1,0:T(8,128)(2,1)S(1)}, u32[]{:S(2)}, u32[]{:S(2)}) collective-permute-start(bf16[64,128]{1,0:T(8,128)(2,1)S(1)} %get-tuple-element.44), channel_id=1, source_target_pairs={{0,1},{1,0},{2,3},{3,2},{4,5},{5,4},{6,7},{7,6},{8,9},{9,8},{10,11... | collective-permute-start | bytes 49160 | tf_op jit(solution)/shard_map/ppermute | solution.py:334

commit v18 on v17

--- a/solution.py
+++ b/solution.py
@@ -348,8 +348,20 @@
         [wide, pltpu.SemaphoreType.DMA((3,))],
     )(*(pltpu.with_memory_space_constraint(array, pltpu.HBM) for array in (queries, keys, values)))
     inner = swap(inner, 1)
-    others = [(i, i + 1 if i & 1 else i - 1) for i in range(1, seq_size - 1)]
-    outer = lax.ppermute(outer, "seq", others)
+
+    def to_spans(array, targets):
+        return lax.ppermute(
+            array,
+            ("seq", "head"),
+            [
+                (s * head_size + h, t * head_size + (h if s != t else h ^ 1))
+                for s, t in enumerate(targets)
+                for h in range(head_size)
+            ],
+        )
+
+    last = seq_size - 1
+    outer = to_spans(outer, [s if s in (0, last) else s + 1 if s & 1 else s - 1 for s in range(seq_size)])
     if paired:
         opening, downward, closing, eighth = kernel_call(
             join_kernel,
@@ -361,8 +373,7 @@
         )(inner, quarter)
 
         def over_pairs(array, targets):
-            spans = [(2 * p + x, 2 * t + x) for p, t in enumerate(targets) for x in range(2)]
-            return lax.ppermute(array, "seq", spans)
+            return to_spans(array, [2 * t + x for t in targets for x in range(2)])
 
         early = (over_pairs(opening, (1, 3, 2, 0)), over_pairs(eighth, (2, 1, 0, 3)))
         late = early + (over_pairs(downward, (3, 0, 1, 2)), over_pairs(closing, (0, 2, 3, 1)))

time: 25.2 us -> 22.6 us (0.90)
  the two profiles are of different devices: /device:TPU:11 before, /device:TPU:0 now
where the time goes in v18:
time: 22.6 us; the launch traced here: 22.4 us
  waiting for transfers between devices  9.44 us (42%)
  starting transfers between devices  9.1 us (40%)
  Pallas kernels  3.84 us (17%)
    ppermute x4, waiting for transfers between devices, swap(): lax.ppermute(array, axis, [(i, i ^ bit) for i in range(lax.axis_size(axis...  6.18 us
    ppermute x4, starting transfers between devices, swap(): lax.ppermute(array, axis, [(i, i ^ bit) for i in range(lax.axis_size(axis...  5 us
    ppermute x5, starting transfers between devices, to_spans(): lax.ppermute(array, ('seq', 'head'), [(s * head_size + h, t * head_size +...  4.11 us
    ppermute x5, waiting for transfers between devices, to_spans(): lax.ppermute(array, ('seq', 'head'), [(s * head_size + h, t * head_size +...  3.26 us
    pallas_call x1, Pallas kernels, shards(): kernel_call(functools.partial(pack_kernel, not paired), 'pack', 16, [HBM]...  0.99 us
    pallas_call x1, Pallas kernels, shards(): kernel_call(project_kernel, 'project', 8, [VMEM] * 4, [(share, out_weight...  0.81 us
    pallas_call x1, Pallas kernels, shards(): kernel_call(functools.partial(leaves_kernel, seq_size, paired), 'leaves',...  0.62 us
    pallas_call x1, Pallas kernels, shards(): kernel_call(stays_kernel, 'stays', 16, [VMEM] * 8, [(share, width)] * 2,...  0.59 us
  transfers between devices with their start and end apart: 9, of which 5 were waited for; matrix products, arithmetic and copies ran while one was open for 0% of the time, Pallas kernels for 6%

profile of v18, /device:TPU:0, one launch (start us, length us, event | category | flops | bytes accessed | tf_op | source)
XLA Modules:
  0.0 22.4 jit_solution(7384448818864262369)
XLA Ops:
  0.0 1.0 %pack.1 = (bf16[256,128]{1,0:T(8,128)(2,1)S(1)}, bf16[256,256]{1,0:T(8,128)(2,1)S(1)}, bf16[192,256]{1,0:T(8,128)(2,1)S(1)}, bf16[192,256]{1,0:T(8,128)(2,1)S(1)}, bf16[64,256]{1,0:T(8,128)(2,1)S(1)}) custom-call(bf16[256,128]{1,0:T(8,128)(2,1)} %queries.1, bf16[256,128]{1,0:T(8,128)(2,1)} %keys.1, bf16[256,128]{1,0:T(8,128)(2,1)} %values.1), custom_call_target="tpu_custom_call" | custom-call | bytes 1048576 | tf_op jit(solution)/shard_map/pack/pallas_call | solution.py:336
  1.0 3.0 %collective-permute-start = (bf16[192,256]{1,0:T(8,128)(2,1)S(1)}, bf16[192,256]{1,0:T(8,128)(2,1)S(1)}, u32[]{:S(2)}, u32[]{:S(2)}) collective-permute-start(bf16[192,256]{1,0:T(8,128)(2,1)S(1)} %get-tuple-element.28), channel_id=1, source_target_pairs={{0,4},{4,0},{8,12},{12,8},{16,20},{20,16},{24,28},{28,24},{1,5},{5... | collective-permute-start | bytes 294920 | tf_op jit(solution)/shard_map/ppermute | solution.py:334
  4.0 0.0 collective-permute-start.1
  4.0 4.2 %collective-permute-done.inner = bf16[192,256]{1,0:T(8,128)(2,1)S(1)} collective-permute-done((bf16[192,256]{1,0:T(8,128)(2,1)S(1)}, bf16[192,256]{1,0:T(8,128)(2,1)S(1)}, u32[]{:S(2)}, u32[]{:S(2)}) %collective-permute-start) | collective-permute-done | bytes 98336 | tf_op jit(solution)/shard_map/ppermute | solution.py:334
  8.2 0.1 join.1
  8.2 1.7 %collective-permute-start.2 = (bf16[128,256]{1,0:T(8,128)(2,1)S(1)}, bf16[128,256]{1,0:T(8,128)(2,1)S(1)}, u32[]{:S(2)}, u32[]{:S(2)}) collective-permute-start(bf16[128,256]{1,0:T(8,128)(2,1)S(1)} %get-tuple-element.34), channel_id=1, source_target_pairs={{0,8},{1,9},{2,10},{3,11},{4,12},{5,13},{6,14},{7,15},{8,24},{9,25... | collective-permute-start | bytes 196616 | tf_op jit(solution)/shard_map/ppermute | solution.py:353
  10.0 1.1 %collective-permute-start.3 = (bf16[64,256]{1,0:T(8,128)(2,1)S(1)}, bf16[64,256]{1,0:T(8,128)(2,1)S(1)}, u32[]{:S(2)}, u32[]{:S(2)}) collective-permute-start(bf16[64,256]{1,0:T(8,128)(2,1)S(1)} %get-tuple-element.35), channel_id=1, source_target_pairs={{0,16},{1,17},{2,18},{3,19},{4,20},{5,21},{6,22},{7,23},{8,9},{9,8... | collective-permute-start | bytes 98312 | tf_op jit(solution)/shard_map/ppermute | solution.py:353
  11.1 1.0 %collective-permute-start.4 = (bf16[128,256]{1,0:T(8,128)(2,1)S(1)}, bf16[128,256]{1,0:T(8,128)(2,1)S(1)}, u32[]{:S(2)}, u32[]{:S(2)}) collective-permute-start(bf16[128,256]{1,0:T(8,128)(2,1)S(1)} %get-tuple-element.38), channel_id=1, source_target_pairs={{0,24},{1,25},{2,26},{3,27},{4,28},{5,29},{6,30},{7,31},{8,0},{9,1... | collective-permute-start | bytes 196616 | tf_op jit(solution)/shard_map/ppermute | solution.py:353
  12.1 0.2 %collective-permute-start.5 = (bf16[128,256]{1,0:T(8,128)(2,1)S(1)}, bf16[128,256]{1,0:T(8,128)(2,1)S(1)}, u32[]{:S(2)}, u32[]{:S(2)}) collective-permute-start(bf16[128,256]{1,0:T(8,128)(2,1)S(1)} %get-tuple-element.39), channel_id=1, source_target_pairs={{0,1},{1,0},{2,3},{3,2},{4,5},{5,4},{6,7},{7,6},{8,16},{9,17},{10,... | collective-permute-start | bytes 196616 | tf_op jit(solution)/shard_map/ppermute | solution.py:353
  12.4 0.0 collective-permute-done.1.outer
  12.4 0.4 %near.1 = (f32[2,256,512]{2,1,0:T(8,128)S(1)}, bf16[2,512,128]{2,1,0:T(8,128)(2,1)S(1)}, bf16[64,256]{1,0:T(8,128)(2,1)S(1)}) custom-call(bf16[256,128]{1,0:T(8,128)(2,1)S(1)} %get-tuple-element.26.queries, bf16[256,256]{1,0:T(8,128)(2,1)S(1)} %get-tuple-element.27.own, bf16[192,256]{1,0:T(8,128)(2,1)S(1)} %collective-permute-done.inner, ...), custom_call_target="tpu_custom_call" | custom-call | flops 67108864 | bytes 1048576 | tf_op jit(solution)/shard_map/near/pallas_call | solution.py:384
  12.7 2.7 %collective-permute-done.3.rest_1_ = bf16[64,256]{1,0:T(8,128)(2,1)S(1)} collective-permute-done((bf16[64,256]{1,0:T(8,128)(2,1)S(1)}, bf16[64,256]{1,0:T(8,128)(2,1)S(1)}, u32[]{:S(2)}, u32[]{:S(2)}) %collective-permute-start.3) | collective-permute-done | bytes 32800 | tf_op jit(solution)/shard_map/ppermute | solution.py:353
  15.5 0.0 collective-permute-done.2.rest_0_
  15.5 0.2 mid.1
  15.7 0.5 %collective-permute-done.4.rest_2_ = bf16[128,256]{1,0:T(8,128)(2,1)S(1)} collective-permute-done((bf16[128,256]{1,0:T(8,128)(2,1)S(1)}, bf16[128,256]{1,0:T(8,128)(2,1)S(1)}, u32[]{:S(2)}, u32[]{:S(2)}) %collective-permute-start.4) | collective-permute-done | bytes 65568 | tf_op jit(solution)/shard_map/ppermute | solution.py:353
  16.2 0.0 collective-permute-done.5.rest_3_
  16.2 0.6 %leaves.1 = (bf16[80,128]{1,0:T(8,128)(2,1)S(1)}, bf16[80,128]{1,0:T(8,128)(2,1)S(1)}, bf16[256,128]{1,0:T(8,128)(2,1)S(1)}, bf16[256,128]{1,0:T(8,128)(2,1)S(1)}, f32[8,256]{1,0:T(8,128)S(1)}) custom-call(bf16[256,128]{1,0:T(8,128)(2,1)S(1)} %get-tuple-element.26.queries, f32[2,256,512]{2,1,0:T(8,128)S(1)} %get-tuple-element.30.near_scores, ...), custom_call_target="tpu_custom_call" | custom-call | flops 117440512 | bytes 1048576 | tf_op jit(solution)/shard_map/leaves/pallas_call | solution.py:410
  16.8 1.0 %collective-permute-start.7 = (bf16[80,128]{1,0:T(8,128)(2,1)S(1)}, bf16[80,128]{1,0:T(8,128)(2,1)S(1)}, u32[]{:S(2)}, u32[]{:S(2)}) collective-permute-start(bf16[80,128]{1,0:T(8,128)(2,1)S(1)} %get-tuple-element.45), channel_id=1, source_target_pairs={{0,3},{1,2},{2,1},{3,0},{4,7},{5,6},{6,5},{7,4},{8,11},{9,10},{10,... | collective-permute-start | bytes 61448 | tf_op jit(solution)/shard_map/ppermute | solution.py:334
  17.8 0.7 %collective-permute-start.8 = (bf16[80,128]{1,0:T(8,128)(2,1)S(1)}, bf16[80,128]{1,0:T(8,128)(2,1)S(1)}, u32[]{:S(2)}, u32[]{:S(2)}) collective-permute-start(bf16[80,128]{1,0:T(8,128)(2,1)S(1)} %get-tuple-element.46), channel_id=1, source_target_pairs={{0,2},{1,3},{2,0},{3,1},{4,6},{5,7},{6,4},{7,5},{8,10},{9,11},{10,... | collective-permute-start | bytes 61448 | tf_op jit(solution)/shard_map/ppermute | solution.py:334
  18.6 0.0 copy-start
  18.6 0.6 %stays.1 = (bf16[64,128]{1,0:T(8,128)(2,1)S(1)}, bf16[64,128]{1,0:T(8,128)(2,1)S(1)}) custom-call(bf16[256,128]{1,0:T(8,128)(2,1)S(1)} %get-tuple-element.26.queries, f32[2,256,512]{2,1,0:T(8,128)S(1)} %get-tuple-element.30.near_scores, bf16[2,512,128]{2,1,0:T(8,128)(2,1)S(1)} %get-tuple-element.31.near_values, ...), custom_call_target="tpu_custom_call" | custom-call | flops 117440512 | bytes 1048576 | tf_op jit(solution)/shard_map/stays/pallas_call | solution.py:425
  19.2 0.3 %collective-permute-start.6 = (bf16[64,128]{1,0:T(8,128)(2,1)S(1)}, bf16[64,128]{1,0:T(8,128)(2,1)S(1)}, u32[]{:S(2)}, u32[]{:S(2)}) collective-permute-start(bf16[64,128]{1,0:T(8,128)(2,1)S(1)} %get-tuple-element.44), channel_id=1, source_target_pairs={{0,1},{1,0},{2,3},{3,2},{4,5},{5,4},{6,7},{7,6},{8,9},{9,8},{10,11... | collective-permute-start | bytes 49160 | tf_op jit(solution)/shard_map/ppermute | solution.py:334
  19.4 1.0 %collective-permute-done.6.other = bf16[64,128]{1,0:T(8,128)(2,1)S(1)} collective-permute-done((bf16[64,128]{1,0:T(8,128)(2,1)S(1)}, bf16[64,128]{1,0:T(8,128)(2,1)S(1)}, u32[]{:S(2)}, u32[]{:S(2)}) %collective-permute-start.6) | collective-permute-done | bytes 16416 | tf_op jit(solution)/shard_map/ppermute | solution.py:334
  20.4 0.0 copy-done
  20.4 0.2 begin.1.partial
  20.6 0.0 collective-permute-done.7.other
  20.6 1.0 %collective-permute-done.8.same = bf16[80,128]{1,0:T(8,128)(2,1)S(1)} collective-permute-done((bf16[80,128]{1,0:T(8,128)(2,1)S(1)}, bf16[80,128]{1,0:T(8,128)(2,1)S(1)}, u32[]{:S(2)}, u32[]{:S(2)}) %collective-permute-start.8) | collective-permute-done | bytes 20512 | tf_op jit(solution)/shard_map/ppermute | solution.py:334
  21.6 0.8 %project.1 = bf16[64,512]{1,0:T(8,128)(2,1)} custom-call(f32[64,512]{1,0:T(8,128)S(1)} %begin.1.partial, bf16[80,128]{1,0:T(8,128)(2,1)S(1)} %collective-permute-done.7.other, bf16[80,128]{1,0:T(8,128)(2,1)S(1)} %collective-permute-done.8.same, bf16[512,512]{1,0:T(8,128)(2,1)S(1)} %copy-done), custom_call_target="tpu_custom_call" | custom-call | bytes 1048576 | tf_op jit(solution)/shard_map/project/pallas_call | solution.py:438
Async XLA Ops:
  1.0 7.2 %collective-permute-start = (bf16[192,256]{1,0:T(8,128)(2,1)S(1)}, bf16[192,256]{1,0:T(8,128)(2,1)S(1)}, u32[]{:S(2)}, u32[]{:S(2)}) collective-permute-start(bf16[192,256]{1,0:T(8,128)(2,1)S(1)} %get-tuple-element.28), channel_id=1, source_target_pairs={{0,4},{4,0},{8,12},{12,8},{16,20},{20,16},{24,28},{28,24},{1,5},{5... | collective-permute-start | bytes 294920 | tf_op jit(solution)/shard_map/ppermute | solution.py:334
  4.0 8.4 %collective-permute-start.1 = (bf16[192,256]{1,0:T(8,128)(2,1)S(1)}, bf16[192,256]{1,0:T(8,128)(2,1)S(1)}, u32[]{:S(2)}, u32[]{:S(2)}) collective-permute-start(bf16[192,256]{1,0:T(8,128)(2,1)S(1)} %get-tuple-element.29), channel_id=1, source_target_pairs={{0,1},{1,0},{2,3},{3,2},{4,8},{5,9},{6,10},{7,11},{8,4},{9,5},{10,... | collective-permute-start | bytes 294920 | tf_op jit(solution)/shard_map/ppermute | solution.py:353
  8.2 7.2 %collective-permute-start.2 = (bf16[128,256]{1,0:T(8,128)(2,1)S(1)}, bf16[128,256]{1,0:T(8,128)(2,1)S(1)}, u32[]{:S(2)}, u32[]{:S(2)}) collective-permute-start(bf16[128,256]{1,0:T(8,128)(2,1)S(1)} %get-tuple-element.34), channel_id=1, source_target_pairs={{0,8},{1,9},{2,10},{3,11},{4,12},{5,13},{6,14},{7,15},{8,24},{9,25... | collective-permute-start | bytes 196616 | tf_op jit(solution)/shard_map/ppermute | solution.py:353
  10.0 5.5 %collective-permute-start.3 = (bf16[64,256]{1,0:T(8,128)(2,1)S(1)}, bf16[64,256]{1,0:T(8,128)(2,1)S(1)}, u32[]{:S(2)}, u32[]{:S(2)}) collective-permute-start(bf16[64,256]{1,0:T(8,128)(2,1)S(1)} %get-tuple-element.35), channel_id=1, source_target_pairs={{0,16},{1,17},{2,18},{3,19},{4,20},{5,21},{6,22},{7,23},{8,9},{9,8... | collective-permute-start | bytes 98312 | tf_op jit(solution)/shard_map/ppermute | solution.py:353
  11.1 5.1 %collective-permute-start.4 = (bf16[128,256]{1,0:T(8,128)(2,1)S(1)}, bf16[128,256]{1,0:T(8,128)(2,1)S(1)}, u32[]{:S(2)}, u32[]{:S(2)}) collective-permute-start(bf16[128,256]{1,0:T(8,128)(2,1)S(1)} %get-tuple-element.38), channel_id=1, source_target_pairs={{0,24},{1,25},{2,26},{3,27},{4,28},{5,29},{6,30},{7,31},{8,0},{9,1... | collective-permute-start | bytes 196616 | tf_op jit(solution)/shard_map/ppermute | solution.py:353
  12.1 4.1 %collective-permute-start.5 = (bf16[128,256]{1,0:T(8,128)(2,1)S(1)}, bf16[128,256]{1,0:T(8,128)(2,1)S(1)}, u32[]{:S(2)}, u32[]{:S(2)}) collective-permute-start(bf16[128,256]{1,0:T(8,128)(2,1)S(1)} %get-tuple-element.39), channel_id=1, source_target_pairs={{0,1},{1,0},{2,3},{3,2},{4,5},{5,4},{6,7},{7,6},{8,16},{9,17},{10,... | collective-permute-start | bytes 196616 | tf_op jit(solution)/shard_map/ppermute | solution.py:353
  16.8 3.7 %collective-permute-start.7 = (bf16[80,128]{1,0:T(8,128)(2,1)S(1)}, bf16[80,128]{1,0:T(8,128)(2,1)S(1)}, u32[]{:S(2)}, u32[]{:S(2)}) collective-permute-start(bf16[80,128]{1,0:T(8,128)(2,1)S(1)} %get-tuple-element.45), channel_id=1, source_target_pairs={{0,3},{1,2},{2,1},{3,0},{4,7},{5,6},{6,5},{7,4},{8,11},{9,10},{10,... | collective-permute-start | bytes 61448 | tf_op jit(solution)/shard_map/ppermute | solution.py:334
  17.8 3.8 %collective-permute-start.8 = (bf16[80,128]{1,0:T(8,128)(2,1)S(1)}, bf16[80,128]{1,0:T(8,128)(2,1)S(1)}, u32[]{:S(2)}, u32[]{:S(2)}) collective-permute-start(bf16[80,128]{1,0:T(8,128)(2,1)S(1)} %get-tuple-element.46), channel_id=1, source_target_pairs={{0,2},{1,3},{2,0},{3,1},{4,6},{5,7},{6,4},{7,5},{8,10},{9,11},{10,... | collective-permute-start | bytes 61448 | tf_op jit(solution)/shard_map/ppermute | solution.py:334
  18.6 1.8 %copy-start = (bf16[512,512]{1,0:T(8,128)(2,1)S(1)}, bf16[512,512]{1,0:T(8,128)(2,1)}, u32[]{:S(2)}) copy-start(bf16[512,512]{1,0:T(8,128)(2,1)} %weight.3) | copy-start | bytes 1572868
  19.2 1.2 %collective-permute-start.6 = (bf16[64,128]{1,0:T(8,128)(2,1)S(1)}, bf16[64,128]{1,0:T(8,128)(2,1)S(1)}, u32[]{:S(2)}, u32[]{:S(2)}) collective-permute-start(bf16[64,128]{1,0:T(8,128)(2,1)S(1)} %get-tuple-element.44), channel_id=1, source_target_pairs={{0,1},{1,0},{2,3},{3,2},{4,5},{5,4},{6,7},{7,6},{8,9},{9,8},{10,11... | collective-permute-start | bytes 49160 | tf_op jit(solution)/shard_map/ppermute | solution.py:334

commit v19 on v18

--- a/solution.py
+++ b/solution.py
@@ -54,18 +54,12 @@
         quarter[...] = level_two
 
 
-def join_kernel(inner, quarter, opening, downward, closing, eighth, wide):
+def join_kernel(theirs, quarter, opening, downward, closing, eighth, wide):
     me = lax.axis_index("seq")
     odd = me & 1
     pair = me >> 1
-    edge_half = average_pairs(inner[:LEAF], wide)
-    other_half = inner[LEAF:]
-    theirs = jnp.concatenate(
-        [jnp.where(odd == 1, other_half, edge_half), jnp.where(odd == 1, edge_half, other_half)], axis=0
-    )
-    theirs = average_pairs(theirs, wide)
-    first = jnp.where(odd == 1, theirs, quarter[...])
-    second = jnp.where(odd == 1, quarter[...], theirs)
+    first = jnp.where(odd == 1, theirs[...], quarter[...])
+    second = jnp.where(odd == 1, quarter[...], theirs[...])
     level_three = average_pairs(jnp.concatenate([first, second], axis=0), wide)
     opening[:HALF] = jnp.where(pair == 0, first, level_three)
     downward[:HALF] = jnp.where(pair == 0, level_three, first)
@@ -370,7 +364,8 @@
             [VMEM] * 2,
             [(LEAF, pair_width)] * 3 + [(HALF, pair_width)],
             [wide],
-        )(inner, quarter)
+            flops=3 * 10**8,
+        )(swap(quarter, 1), quarter)
 
         def over_pairs(array, targets):
             return to_spans(array, [2 * t + x for t in targets for x in range(2)])

time: 22.6 us -> 21.1 us (0.934)
  waiting for transfers between devices: 9.44 us -> 7.26 us
  starting transfers between devices: 9.1 us -> 9.84 us
    ppermute x4 -> x5, waiting for transfers between devices: 6.18 us -> 3.78 us  [swap(): lax.ppermute(array, axis, [(i, i ^ bit) for i in range(lax.axis_size(axis...]
    ppermute x5, starting transfers between devices: 4.11 us -> 4.76 us  [to_spans(): lax.ppermute(array, ('seq', 'head'), [(s * head_size + h, t * head_size +...]
    ppermute x4 -> x5, starting transfers between devices: 5 us -> 5.07 us  [swap(): lax.ppermute(array, axis, [(i, i ^ bit) for i in range(lax.axis_size(axis...]
  transfers between devices with their start and end apart: 9 -> 10, of which waited for: 5 -> 5; matrix products, arithmetic and copies ran while one was open for 0% -> 0% of each run, Pallas kernels for 6% -> 7%
where the time goes in v19:
time: 21.1 us; the launch traced here: 21 us
  starting transfers between devices  9.84 us (47%)
  waiting for transfers between devices  7.26 us (34%)
  Pallas kernels  3.8 us (18%)
    ppermute x5, starting transfers between devices, swap(): lax.ppermute(array, axis, [(i, i ^ bit) for i in range(lax.axis_size(axis...  5.07 us
    ppermute x5, starting transfers between devices, to_spans(): lax.ppermute(array, ('seq', 'head'), [(s * head_size + h, t * head_size +...  4.76 us
    ppermute x5, waiting for transfers between devices, swap(): lax.ppermute(array, axis, [(i, i ^ bit) for i in range(lax.axis_size(axis...  3.78 us
    ppermute x5, waiting for transfers between devices, to_spans(): lax.ppermute(array, ('seq', 'head'), [(s * head_size + h, t * head_size +...  3.48 us
    pallas_call x1, Pallas kernels, shards(): kernel_call(functools.partial(pack_kernel, not paired), 'pack', 16, [HBM]...  0.99 us
    pallas_call x1, Pallas kernels, shards(): kernel_call(project_kernel, 'project', 8, [VMEM] * 4, [(share, out_weight...  0.81 us
    pallas_call x1, Pallas kernels, shards(): kernel_call(functools.partial(leaves_kernel, seq_size, paired), 'leaves',...  0.62 us
    pallas_call x1, Pallas kernels, shards(): kernel_call(stays_kernel, 'stays', 16, [VMEM] * 8, [(share, width)] * 2,...  0.59 us
  transfers between devices with their start and end apart: 10, of which 5 were waited for; matrix products, arithmetic and copies ran while one was open for 0% of the time, Pallas kernels for 7%

profile of v19, /device:TPU:0, one launch (start us, length us, event | category | flops | bytes accessed | tf_op | source)
XLA Modules:
  0.0 21.0 jit_solution(12684739074137526124)
XLA Ops:
  0.0 1.0 %pack.1 = (bf16[256,128]{1,0:T(8,128)(2,1)S(1)}, bf16[256,256]{1,0:T(8,128)(2,1)S(1)}, bf16[192,256]{1,0:T(8,128)(2,1)S(1)}, bf16[192,256]{1,0:T(8,128)(2,1)S(1)}, bf16[64,256]{1,0:T(8,128)(2,1)S(1)}) custom-call(bf16[256,128]{1,0:T(8,128)(2,1)} %queries.1, bf16[256,128]{1,0:T(8,128)(2,1)} %keys.1, bf16[256,128]{1,0:T(8,128)(2,1)} %values.1), custom_call_target="tpu_custom_call" | custom-call | bytes 1048576 | tf_op jit(solution)/shard_map/pack/pallas_call | solution.py:330
  1.0 3.0 %collective-permute-start.2 = (bf16[64,256]{1,0:T(8,128)(2,1)S(1)}, bf16[64,256]{1,0:T(8,128)(2,1)S(1)}, u32[]{:S(2)}, u32[]{:S(2)}) collective-permute-start(bf16[64,256]{1,0:T(8,128)(2,1)S(1)} %get-tuple-element.33.quarter), channel_id=1, source_target_pairs={{0,4},{4,0},{8,12},{12,8},{16,20},{20,16},{24,28},{28,24},{1,5},{5... | collective-permute-start | bytes 98312 | tf_op jit(solution)/shard_map/ppermute | solution.py:328
  4.0 0.1 collective-permute-start
  4.1 0.0 collective-permute-start.1
  4.1 1.8 %collective-permute-done.2.theirs = bf16[64,256]{1,0:T(8,128)(2,1)S(1)} collective-permute-done((bf16[64,256]{1,0:T(8,128)(2,1)S(1)}, bf16[64,256]{1,0:T(8,128)(2,1)S(1)}, u32[]{:S(2)}, u32[]{:S(2)}) %collective-permute-start.2) | collective-permute-done | bytes 32800 | tf_op jit(solution)/shard_map/ppermute | solution.py:328
  5.9 2.4 %collective-permute-start.3 = (bf16[128,256]{1,0:T(8,128)(2,1)S(1)}, bf16[128,256]{1,0:T(8,128)(2,1)S(1)}, u32[]{:S(2)}, u32[]{:S(2)}) collective-permute-start(bf16[128,256]{1,0:T(8,128)(2,1)S(1)} %get-tuple-element.34), channel_id=1, source_target_pairs={{0,8},{1,9},{2,10},{3,11},{4,12},{5,13},{6,14},{7,15},{8,24},{9,25... | collective-permute-start | bytes 196616 | tf_op jit(solution)/shard_map/ppermute | solution.py:347
  8.4 1.1 %collective-permute-start.4 = (bf16[64,256]{1,0:T(8,128)(2,1)S(1)}, bf16[64,256]{1,0:T(8,128)(2,1)S(1)}, u32[]{:S(2)}, u32[]{:S(2)}) collective-permute-start(bf16[64,256]{1,0:T(8,128)(2,1)S(1)} %get-tuple-element.35), channel_id=1, source_target_pairs={{0,16},{1,17},{2,18},{3,19},{4,20},{5,21},{6,22},{7,23},{8,9},{9,8... | collective-permute-start | bytes 98312 | tf_op jit(solution)/shard_map/ppermute | solution.py:347
  9.5 1.1 %collective-permute-start.5 = (bf16[128,256]{1,0:T(8,128)(2,1)S(1)}, bf16[128,256]{1,0:T(8,128)(2,1)S(1)}, u32[]{:S(2)}, u32[]{:S(2)}) collective-permute-start(bf16[128,256]{1,0:T(8,128)(2,1)S(1)} %get-tuple-element.38), channel_id=1, source_target_pairs={{0,24},{1,25},{2,26},{3,27},{4,28},{5,29},{6,30},{7,31},{8,0},{9,1... | collective-permute-start | bytes 196616 | tf_op jit(solution)/shard_map/ppermute | solution.py:347
  10.5 0.0 collective-permute-done.inner
  10.5 0.2 collective-permute-start.6
  10.7 0.0 collective-permute-done.1.outer
  10.7 0.4 %near.1 = (f32[2,256,512]{2,1,0:T(8,128)S(1)}, bf16[2,512,128]{2,1,0:T(8,128)(2,1)S(1)}, bf16[64,256]{1,0:T(8,128)(2,1)S(1)}) custom-call(bf16[256,128]{1,0:T(8,128)(2,1)S(1)} %get-tuple-element.26.queries, bf16[256,256]{1,0:T(8,128)(2,1)S(1)} %get-tuple-element.27.own, bf16[192,256]{1,0:T(8,128)(2,1)S(1)} %collective-permute-done.inner, ...), custom_call_target="tpu_custom_call" | custom-call | flops 67108864 | bytes 1048576 | tf_op jit(solution)/shard_map/near/pallas_call | solution.py:379
  11.1 2.7 %collective-permute-done.4.rest_1_ = bf16[64,256]{1,0:T(8,128)(2,1)S(1)} collective-permute-done((bf16[64,256]{1,0:T(8,128)(2,1)S(1)}, bf16[64,256]{1,0:T(8,128)(2,1)S(1)}, u32[]{:S(2)}, u32[]{:S(2)}) %collective-permute-start.4) | collective-permute-done | bytes 32800 | tf_op jit(solution)/shard_map/ppermute | solution.py:347
  13.8 0.0 collective-permute-done.3.rest_0_
  13.9 0.2 mid.1
  14.1 0.7 %collective-permute-done.5.rest_2_ = bf16[128,256]{1,0:T(8,128)(2,1)S(1)} collective-permute-done((bf16[128,256]{1,0:T(8,128)(2,1)S(1)}, bf16[128,256]{1,0:T(8,128)(2,1)S(1)}, u32[]{:S(2)}, u32[]{:S(2)}) %collective-permute-start.5) | collective-permute-done | bytes 65568 | tf_op jit(solution)/shard_map/ppermute | solution.py:347
  14.8 0.0 collective-permute-done.6.rest_3_
  14.8 0.6 %leaves.1 = (bf16[80,128]{1,0:T(8,128)(2,1)S(1)}, bf16[80,128]{1,0:T(8,128)(2,1)S(1)}, bf16[256,128]{1,0:T(8,128)(2,1)S(1)}, bf16[256,128]{1,0:T(8,128)(2,1)S(1)}, f32[8,256]{1,0:T(8,128)S(1)}) custom-call(bf16[256,128]{1,0:T(8,128)(2,1)S(1)} %get-tuple-element.26.queries, f32[2,256,512]{2,1,0:T(8,128)S(1)} %get-tuple-element.30.near_scores, ...), custom_call_target="tpu_custom_call" | custom-call | flops 117440512 | bytes 1048576 | tf_op jit(solution)/shard_map/leaves/pallas_call | solution.py:405
  15.4 0.9 %collective-permute-start.8 = (bf16[80,128]{1,0:T(8,128)(2,1)S(1)}, bf16[80,128]{1,0:T(8,128)(2,1)S(1)}, u32[]{:S(2)}, u32[]{:S(2)}) collective-permute-start(bf16[80,128]{1,0:T(8,128)(2,1)S(1)} %get-tuple-element.45), channel_id=1, source_target_pairs={{0,3},{1,2},{2,1},{3,0},{4,7},{5,6},{6,5},{7,4},{8,11},{9,10},{10,... | collective-permute-start | bytes 61448 | tf_op jit(solution)/shard_map/ppermute | solution.py:328
  16.3 0.7 %collective-permute-start.9 = (bf16[80,128]{1,0:T(8,128)(2,1)S(1)}, bf16[80,128]{1,0:T(8,128)(2,1)S(1)}, u32[]{:S(2)}, u32[]{:S(2)}) collective-permute-start(bf16[80,128]{1,0:T(8,128)(2,1)S(1)} %get-tuple-element.46), channel_id=1, source_target_pairs={{0,2},{1,3},{2,0},{3,1},{4,6},{5,7},{6,4},{7,5},{8,10},{9,11},{10,... | collective-permute-start | bytes 61448 | tf_op jit(solution)/shard_map/ppermute | solution.py:328
  17.1 0.0 copy-start
  17.1 0.6 %stays.1 = (bf16[64,128]{1,0:T(8,128)(2,1)S(1)}, bf16[64,128]{1,0:T(8,128)(2,1)S(1)}) custom-call(bf16[256,128]{1,0:T(8,128)(2,1)S(1)} %get-tuple-element.26.queries, f32[2,256,512]{2,1,0:T(8,128)S(1)} %get-tuple-element.30.near_scores, bf16[2,512,128]{2,1,0:T(8,128)(2,1)S(1)} %get-tuple-element.31.near_values, ...), custom_call_target="tpu_custom_call" | custom-call | flops 117440512 | bytes 1048576 | tf_op jit(solution)/shard_map/stays/pallas_call | solution.py:420
  17.7 0.3 %collective-permute-start.7 = (bf16[64,128]{1,0:T(8,128)(2,1)S(1)}, bf16[64,128]{1,0:T(8,128)(2,1)S(1)}, u32[]{:S(2)}, u32[]{:S(2)}) collective-permute-start(bf16[64,128]{1,0:T(8,128)(2,1)S(1)} %get-tuple-element.44), channel_id=1, source_target_pairs={{0,1},{1,0},{2,3},{3,2},{4,5},{5,4},{6,7},{7,6},{8,9},{9,8},{10,11... | collective-permute-start | bytes 49160 | tf_op jit(solution)/shard_map/ppermute | solution.py:328
  18.0 0.9 %collective-permute-done.7.other = bf16[64,128]{1,0:T(8,128)(2,1)S(1)} collective-permute-done((bf16[64,128]{1,0:T(8,128)(2,1)S(1)}, bf16[64,128]{1,0:T(8,128)(2,1)S(1)}, u32[]{:S(2)}, u32[]{:S(2)}) %collective-permute-start.7) | collective-permute-done | bytes 16416 | tf_op jit(solution)/shard_map/ppermute | solution.py:328
  18.9 0.0 copy-done
  18.9 0.2 begin.1.partial
  19.1 0.0 collective-permute-done.8.other
  19.1 1.0 %collective-permute-done.9.same = bf16[80,128]{1,0:T(8,128)(2,1)S(1)} collective-permute-done((bf16[80,128]{1,0:T(8,128)(2,1)S(1)}, bf16[80,128]{1,0:T(8,128)(2,1)S(1)}, u32[]{:S(2)}, u32[]{:S(2)}) %collective-permute-start.9) | collective-permute-done | bytes 20512 | tf_op jit(solution)/shard_map/ppermute | solution.py:328
  20.1 0.8 %project.1 = bf16[64,512]{1,0:T(8,128)(2,1)} custom-call(f32[64,512]{1,0:T(8,128)S(1)} %begin.1.partial, bf16[80,128]{1,0:T(8,128)(2,1)S(1)} %collective-permute-done.8.other, bf16[80,128]{1,0:T(8,128)(2,1)S(1)} %collective-permute-done.9.same, bf16[512,512]{1,0:T(8,128)(2,1)S(1)} %copy-done), custom_call_target="tpu_custom_call" | custom-call | bytes 1048576 | tf_op jit(solution)/shard_map/project/pallas_call | solution.py:433
  (1 shorter events, 0.0 us)
Async XLA Ops:
  1.0 4.9 %collective-permute-start.2 = (bf16[64,256]{1,0:T(8,128)(2,1)S(1)}, bf16[64,256]{1,0:T(8,128)(2,1)S(1)}, u32[]{:S(2)}, u32[]{:S(2)}) collective-permute-start(bf16[64,256]{1,0:T(8,128)(2,1)S(1)} %get-tuple-element.33.quarter), channel_id=1, source_target_pairs={{0,4},{4,0},{8,12},{12,8},{16,20},{20,16},{24,28},{28,24},{1,5},{5... | collective-permute-start | bytes 98312 | tf_op jit(solution)/shard_map/ppermute | solution.py:328
  4.0 6.5 %collective-permute-start = (bf16[192,256]{1,0:T(8,128)(2,1)S(1)}, bf16[192,256]{1,0:T(8,128)(2,1)S(1)}, u32[]{:S(2)}, u32[]{:S(2)}) collective-permute-start(bf16[192,256]{1,0:T(8,128)(2,1)S(1)} %get-tuple-element.28), channel_id=1, source_target_pairs={{0,4},{4,0},{8,12},{12,8},{16,20},{20,16},{24,28},{28,24},{1,5},{5... | collective-permute-start | bytes 294920 | tf_op jit(solution)/shard_map/ppermute | solution.py:328
  4.1 6.6 %collective-permute-start.1 = (bf16[192,256]{1,0:T(8,128)(2,1)S(1)}, bf16[192,256]{1,0:T(8,128)(2,1)S(1)}, u32[]{:S(2)}, u32[]{:S(2)}) collective-permute-start(bf16[192,256]{1,0:T(8,128)(2,1)S(1)} %get-tuple-element.29), channel_id=1, source_target_pairs={{0,1},{1,0},{2,3},{3,2},{4,8},{5,9},{6,10},{7,11},{8,4},{9,5},{10,... | collective-permute-start | bytes 294920 | tf_op jit(solution)/shard_map/ppermute | solution.py:347
  5.9 7.9 %collective-permute-start.3 = (bf16[128,256]{1,0:T(8,128)(2,1)S(1)}, bf16[128,256]{1,0:T(8,128)(2,1)S(1)}, u32[]{:S(2)}, u32[]{:S(2)}) collective-permute-start(bf16[128,256]{1,0:T(8,128)(2,1)S(1)} %get-tuple-element.34), channel_id=1, source_target_pairs={{0,8},{1,9},{2,10},{3,11},{4,12},{5,13},{6,14},{7,15},{8,24},{9,25... | collective-permute-start | bytes 196616 | tf_op jit(solution)/shard_map/ppermute | solution.py:347
  8.4 5.5 %collective-permute-start.4 = (bf16[64,256]{1,0:T(8,128)(2,1)S(1)}, bf16[64,256]{1,0:T(8,128)(2,1)S(1)}, u32[]{:S(2)}, u32[]{:S(2)}) collective-permute-start(bf16[64,256]{1,0:T(8,128)(2,1)S(1)} %get-tuple-element.35), channel_id=1, source_target_pairs={{0,16},{1,17},{2,18},{3,19},{4,20},{5,21},{6,22},{7,23},{8,9},{9,8... | collective-permute-start | bytes 98312 | tf_op jit(solution)/shard_map/ppermute | solution.py:347
  9.5 5.3 %collective-permute-start.5 = (bf16[128,256]{1,0:T(8,128)(2,1)S(1)}, bf16[128,256]{1,0:T(8,128)(2,1)S(1)}, u32[]{:S(2)}, u32[]{:S(2)}) collective-permute-start(bf16[128,256]{1,0:T(8,128)(2,1)S(1)} %get-tuple-element.38), channel_id=1, source_target_pairs={{0,24},{1,25},{2,26},{3,27},{4,28},{5,29},{6,30},{7,31},{8,0},{9,1... | collective-permute-start | bytes 196616 | tf_op jit(solution)/shard_map/ppermute | solution.py:347
  10.5 4.2 %collective-permute-start.6 = (bf16[128,256]{1,0:T(8,128)(2,1)S(1)}, bf16[128,256]{1,0:T(8,128)(2,1)S(1)}, u32[]{:S(2)}, u32[]{:S(2)}) collective-permute-start(bf16[128,256]{1,0:T(8,128)(2,1)S(1)} %get-tuple-element.39), channel_id=1, source_target_pairs={{0,1},{1,0},{2,3},{3,2},{4,5},{5,4},{6,7},{7,6},{8,16},{9,17},{10,... | collective-permute-start | bytes 196616 | tf_op jit(solution)/shard_map/ppermute | solution.py:347
  15.4 3.7 %collective-permute-start.8 = (bf16[80,128]{1,0:T(8,128)(2,1)S(1)}, bf16[80,128]{1,0:T(8,128)(2,1)S(1)}, u32[]{:S(2)}, u32[]{:S(2)}) collective-permute-start(bf16[80,128]{1,0:T(8,128)(2,1)S(1)} %get-tuple-element.45), channel_id=1, source_target_pairs={{0,3},{1,2},{2,1},{3,0},{4,7},{5,6},{6,5},{7,4},{8,11},{9,10},{10,... | collective-permute-start | bytes 61448 | tf_op jit(solution)/shard_map/ppermute | solution.py:328
  16.3 3.8 %collective-permute-start.9 = (bf16[80,128]{1,0:T(8,128)(2,1)S(1)}, bf16[80,128]{1,0:T(8,128)(2,1)S(1)}, u32[]{:S(2)}, u32[]{:S(2)}) collective-permute-start(bf16[80,128]{1,0:T(8,128)(2,1)S(1)} %get-tuple-element.46), channel_id=1, source_target_pairs={{0,2},{1,3},{2,0},{3,1},{4,6},{5,7},{6,4},{7,5},{8,10},{9,11},{10,... | collective-permute-start | bytes 61448 | tf_op jit(solution)/shard_map/ppermute | solution.py:328
  17.1 1.8 %copy-start = (bf16[512,512]{1,0:T(8,128)(2,1)S(1)}, bf16[512,512]{1,0:T(8,128)(2,1)}, u32[]{:S(2)}) copy-start(bf16[512,512]{1,0:T(8,128)(2,1)} %weight.3) | copy-start | bytes 1572868
  17.7 1.2 %collective-permute-start.7 = (bf16[64,128]{1,0:T(8,128)(2,1)S(1)}, bf16[64,128]{1,0:T(8,128)(2,1)S(1)}, u32[]{:S(2)}, u32[]{:S(2)}) collective-permute-start(bf16[64,128]{1,0:T(8,128)(2,1)S(1)} %get-tuple-element.44), channel_id=1, source_target_pairs={{0,1},{1,0},{2,3},{3,2},{4,5},{5,4},{6,7},{7,6},{8,9},{9,8},{10,11... | collective-permute-start | bytes 49160 | tf_op jit(solution)/shard_map/ppermute | solution.py:328

commit v20 on v19

--- a/solution.py
+++ b/solution.py
@@ -348,7 +348,7 @@
             array,
             ("seq", "head"),
             [
-                (s * head_size + h, t * head_size + (h if s != t else h ^ 1))
+                (s * head_size + h, t * head_size + (h if s != t else h ^ 2))
                 for s, t in enumerate(targets)
                 for h in range(head_size)
             ],

time: 21.1 us -> 22 us (1.043)
  starting transfers between devices: 9.84 us -> 13.4 us
  waiting for transfers between devices: 7.26 us -> 4.51 us
    ppermute x5, starting transfers between devices: 4.76 us -> 8.37 us  [to_spans(): lax.ppermute(array, ('seq', 'head'), [(s * head_size + h, t * head_size +...]
    ppermute x5, waiting for transfers between devices: 3.78 us -> 1.2 us  [swap(): lax.ppermute(array, axis, [(i, i ^ bit) for i in range(lax.axis_size(axis...]
  transfers between devices with their start and end apart: 10 -> 10, of which waited for: 5 -> 5; matrix products, arithmetic and copies ran while one was open for 0% -> 0% of each run, Pallas kernels for 7% -> 6%
where the time goes in v20:
time: 22 us; the launch traced here: 21.8 us
  starting transfers between devices  13.4 us (61%)
  waiting for transfers between devices  4.51 us (20%)
  Pallas kernels  3.8 us (17%)
    ppermute x5, starting transfers between devices, to_spans(): lax.ppermute(array, ('seq', 'head'), [(s * head_size + h, t * head_size +...  8.37 us
    ppermute x5, starting transfers between devices, swap(): lax.ppermute(array, axis, [(i, i ^ bit) for i in range(lax.axis_size(axis...  5.07 us
    ppermute x5, waiting for transfers between devices, to_spans(): lax.ppermute(array, ('seq', 'head'), [(s * head_size + h, t * head_size +...  3.31 us
    ppermute x5, waiting for transfers between devices, swap(): lax.ppermute(array, axis, [(i, i ^ bit) for i in range(lax.axis_size(axis...  1.2 us
    pallas_call x1, Pallas kernels, shards(): kernel_call(functools.partial(pack_kernel, not paired), 'pack', 16, [HBM]...  0.99 us
    pallas_call x1, Pallas kernels, shards(): kernel_call(project_kernel, 'project', 8, [VMEM] * 4, [(share, out_weight...  0.81 us
    pallas_call x1, Pallas kernels, shards(): kernel_call(functools.partial(leaves_kernel, seq_size, paired), 'leaves',...  0.62 us
    pallas_call x1, Pallas kernels, shards(): kernel_call(stays_kernel, 'stays', 16, [VMEM] * 8, [(share, width)] * 2,...  0.59 us
  transfers between devices with their start and end apart: 10, of which 5 were waited for; matrix products, arithmetic and copies ran while one was open for 0% of the time, Pallas kernels for 6%

profile of v20, /device:TPU:0, one launch (start us, length us, event | category | flops | bytes accessed | tf_op | source)
XLA Modules:
  0.0 21.8 jit_solution(15469773743938541836)
XLA Ops:
  0.0 1.0 %pack.1 = (bf16[256,128]{1,0:T(8,128)(2,1)S(1)}, bf16[256,256]{1,0:T(8,128)(2,1)S(1)}, bf16[192,256]{1,0:T(8,128)(2,1)S(1)}, bf16[192,256]{1,0:T(8,128)(2,1)S(1)}, bf16[64,256]{1,0:T(8,128)(2,1)S(1)}) custom-call(bf16[256,128]{1,0:T(8,128)(2,1)} %queries.1, bf16[256,128]{1,0:T(8,128)(2,1)} %keys.1, bf16[256,128]{1,0:T(8,128)(2,1)} %values.1), custom_call_target="tpu_custom_call" | custom-call | bytes 1048576 | tf_op jit(solution)/shard_map/pack/pallas_call | solution.py:330
  1.0 3.0 %collective-permute-start.2 = (bf16[64,256]{1,0:T(8,128)(2,1)S(1)}, bf16[64,256]{1,0:T(8,128)(2,1)S(1)}, u32[]{:S(2)}, u32[]{:S(2)}) collective-permute-start(bf16[64,256]{1,0:T(8,128)(2,1)S(1)} %get-tuple-element.33.quarter), channel_id=1, source_target_pairs={{0,4},{4,0},{8,12},{12,8},{16,20},{20,16},{24,28},{28,24},{1,5},{5... | collective-permute-start | bytes 98312 | tf_op jit(solution)/shard_map/ppermute | solution.py:328
  4.0 0.1 collective-permute-start
  4.1 2.0 %collective-permute-start.1 = (bf16[192,256]{1,0:T(8,128)(2,1)S(1)}, bf16[192,256]{1,0:T(8,128)(2,1)S(1)}, u32[]{:S(2)}, u32[]{:S(2)}) collective-permute-start(bf16[192,256]{1,0:T(8,128)(2,1)S(1)} %get-tuple-element.29), channel_id=1, source_target_pairs={{0,2},{1,3},{2,0},{3,1},{4,8},{5,9},{6,10},{7,11},{8,4},{9,5},{10,... | collective-permute-start | bytes 294920 | tf_op jit(solution)/shard_map/ppermute | solution.py:347
  6.1 0.0 collective-permute-done.2.theirs
  6.1 2.3 %collective-permute-start.3 = (bf16[128,256]{1,0:T(8,128)(2,1)S(1)}, bf16[128,256]{1,0:T(8,128)(2,1)S(1)}, u32[]{:S(2)}, u32[]{:S(2)}) collective-permute-start(bf16[128,256]{1,0:T(8,128)(2,1)S(1)} %get-tuple-element.34), channel_id=1, source_target_pairs={{0,8},{1,9},{2,10},{3,11},{4,12},{5,13},{6,14},{7,15},{8,24},{9,25... | collective-permute-start | bytes 196616 | tf_op jit(solution)/shard_map/ppermute | solution.py:347
  8.4 2.5 %collective-permute-start.4 = (bf16[64,256]{1,0:T(8,128)(2,1)S(1)}, bf16[64,256]{1,0:T(8,128)(2,1)S(1)}, u32[]{:S(2)}, u32[]{:S(2)}) collective-permute-start(bf16[64,256]{1,0:T(8,128)(2,1)S(1)} %get-tuple-element.35), channel_id=1, source_target_pairs={{0,16},{1,17},{2,18},{3,19},{4,20},{5,21},{6,22},{7,23},{8,10},{9,... | collective-permute-start | bytes 98312 | tf_op jit(solution)/shard_map/ppermute | solution.py:347
  10.9 1.2 %collective-permute-start.5 = (bf16[128,256]{1,0:T(8,128)(2,1)S(1)}, bf16[128,256]{1,0:T(8,128)(2,1)S(1)}, u32[]{:S(2)}, u32[]{:S(2)}) collective-permute-start(bf16[128,256]{1,0:T(8,128)(2,1)S(1)} %get-tuple-element.38), channel_id=1, source_target_pairs={{0,24},{1,25},{2,26},{3,27},{4,28},{5,29},{6,30},{7,31},{8,0},{9,1... | collective-permute-start | bytes 196616 | tf_op jit(solution)/shard_map/ppermute | solution.py:347
  12.1 0.0 collective-permute-done.inner
  12.2 0.4 %collective-permute-start.6 = (bf16[128,256]{1,0:T(8,128)(2,1)S(1)}, bf16[128,256]{1,0:T(8,128)(2,1)S(1)}, u32[]{:S(2)}, u32[]{:S(2)}) collective-permute-start(bf16[128,256]{1,0:T(8,128)(2,1)S(1)} %get-tuple-element.39), channel_id=1, source_target_pairs={{0,2},{1,3},{2,0},{3,1},{4,6},{5,7},{6,4},{7,5},{8,16},{9,17},{10,... | collective-permute-start | bytes 196616 | tf_op jit(solution)/shard_map/ppermute | solution.py:347
  12.5 0.0 collective-permute-done.1.outer
  12.5 0.4 %near.1 = (f32[2,256,512]{2,1,0:T(8,128)S(1)}, bf16[2,512,128]{2,1,0:T(8,128)(2,1)S(1)}, bf16[64,256]{1,0:T(8,128)(2,1)S(1)}) custom-call(bf16[256,128]{1,0:T(8,128)(2,1)S(1)} %get-tuple-element.26.queries, bf16[256,256]{1,0:T(8,128)(2,1)S(1)} %get-tuple-element.27.own, bf16[192,256]{1,0:T(8,128)(2,1)S(1)} %collective-permute-done.inner, ...), custom_call_target="tpu_custom_call" | custom-call | flops 67108864 | bytes 1048576 | tf_op jit(solution)/shard_map/near/pallas_call | solution.py:379
  12.9 2.0 %collective-permute-done.4.rest_1_ = bf16[64,256]{1,0:T(8,128)(2,1)S(1)} collective-permute-done((bf16[64,256]{1,0:T(8,128)(2,1)S(1)}, bf16[64,256]{1,0:T(8,128)(2,1)S(1)}, u32[]{:S(2)}, u32[]{:S(2)}) %collective-permute-start.4) | collective-permute-done | bytes 32800 | tf_op jit(solution)/shard_map/ppermute | solution.py:347
  14.9 0.0 collective-permute-done.3.rest_0_
  14.9 0.2 mid.1
  15.1 0.2 %collective-permute-done.5.rest_2_ = bf16[128,256]{1,0:T(8,128)(2,1)S(1)} collective-permute-done((bf16[128,256]{1,0:T(8,128)(2,1)S(1)}, bf16[128,256]{1,0:T(8,128)(2,1)S(1)}, u32[]{:S(2)}, u32[]{:S(2)}) %collective-permute-start.5) | collective-permute-done | bytes 65568 | tf_op jit(solution)/shard_map/ppermute | solution.py:347
  15.4 1.0 %collective-permute-done.6.rest_3_ = bf16[128,256]{1,0:T(8,128)(2,1)S(1)} collective-permute-done((bf16[128,256]{1,0:T(8,128)(2,1)S(1)}, bf16[128,256]{1,0:T(8,128)(2,1)S(1)}, u32[]{:S(2)}, u32[]{:S(2)}) %collective-permute-start.6) | collective-permute-done | bytes 65568 | tf_op jit(solution)/shard_map/ppermute | solution.py:347
  16.4 0.6 %leaves.1 = (bf16[80,128]{1,0:T(8,128)(2,1)S(1)}, bf16[80,128]{1,0:T(8,128)(2,1)S(1)}, bf16[256,128]{1,0:T(8,128)(2,1)S(1)}, bf16[256,128]{1,0:T(8,128)(2,1)S(1)}, f32[8,256]{1,0:T(8,128)S(1)}) custom-call(bf16[256,128]{1,0:T(8,128)(2,1)S(1)} %get-tuple-element.26.queries, f32[2,256,512]{2,1,0:T(8,128)S(1)} %get-tuple-element.30.near_scores, ...), custom_call_target="tpu_custom_call" | custom-call | flops 117440512 | bytes 1048576 | tf_op jit(solution)/shard_map/leaves/pallas_call | solution.py:405
  17.0 0.1 collective-permute-start.8
  17.1 0.4 %collective-permute-start.9 = (bf16[80,128]{1,0:T(8,128)(2,1)S(1)}, bf16[80,128]{1,0:T(8,128)(2,1)S(1)}, u32[]{:S(2)}, u32[]{:S(2)}) collective-permute-start(bf16[80,128]{1,0:T(8,128)(2,1)S(1)} %get-tuple-element.46), channel_id=1, source_target_pairs={{0,2},{1,3},{2,0},{3,1},{4,6},{5,7},{6,4},{7,5},{8,10},{9,11},{10,... | collective-permute-start | bytes 61448 | tf_op jit(solution)/shard_map/ppermute | solution.py:328
  17.5 0.0 copy-start
  17.5 0.6 %stays.1 = (bf16[64,128]{1,0:T(8,128)(2,1)S(1)}, bf16[64,128]{1,0:T(8,128)(2,1)S(1)}) custom-call(bf16[256,128]{1,0:T(8,128)(2,1)S(1)} %get-tuple-element.26.queries, f32[2,256,512]{2,1,0:T(8,128)S(1)} %get-tuple-element.30.near_scores, bf16[2,512,128]{2,1,0:T(8,128)(2,1)S(1)} %get-tuple-element.31.near_values, ...), custom_call_target="tpu_custom_call" | custom-call | flops 117440512 | bytes 1048576 | tf_op jit(solution)/shard_map/stays/pallas_call | solution.py:420
  18.1 1.5 %collective-permute-start.7 = (bf16[64,128]{1,0:T(8,128)(2,1)S(1)}, bf16[64,128]{1,0:T(8,128)(2,1)S(1)}, u32[]{:S(2)}, u32[]{:S(2)}) collective-permute-start(bf16[64,128]{1,0:T(8,128)(2,1)S(1)} %get-tuple-element.44), channel_id=1, source_target_pairs={{0,1},{1,0},{2,3},{3,2},{4,5},{5,4},{6,7},{7,6},{8,9},{9,8},{10,11... | collective-permute-start | bytes 49160 | tf_op jit(solution)/shard_map/ppermute | solution.py:328
  19.6 0.8 %collective-permute-done.7.other = bf16[64,128]{1,0:T(8,128)(2,1)S(1)} collective-permute-done((bf16[64,128]{1,0:T(8,128)(2,1)S(1)}, bf16[64,128]{1,0:T(8,128)(2,1)S(1)}, u32[]{:S(2)}, u32[]{:S(2)}) %collective-permute-start.7) | collective-permute-done | bytes 16416 | tf_op jit(solution)/shard_map/ppermute | solution.py:328
  20.5 0.0 copy-done
  20.5 0.2 begin.1.partial
  20.6 0.0 collective-permute-done.8.other
  20.7 0.3 %collective-permute-done.9.same = bf16[80,128]{1,0:T(8,128)(2,1)S(1)} collective-permute-done((bf16[80,128]{1,0:T(8,128)(2,1)S(1)}, bf16[80,128]{1,0:T(8,128)(2,1)S(1)}, u32[]{:S(2)}, u32[]{:S(2)}) %collective-permute-start.9) | collective-permute-done | bytes 20512 | tf_op jit(solution)/shard_map/ppermute | solution.py:328
  21.0 0.8 %project.1 = bf16[64,512]{1,0:T(8,128)(2,1)} custom-call(f32[64,512]{1,0:T(8,128)S(1)} %begin.1.partial, bf16[80,128]{1,0:T(8,128)(2,1)S(1)} %collective-permute-done.8.other, bf16[80,128]{1,0:T(8,128)(2,1)S(1)} %collective-permute-done.9.same, bf16[512,512]{1,0:T(8,128)(2,1)S(1)} %copy-done), custom_call_target="tpu_custom_call" | custom-call | bytes 1048576 | tf_op jit(solution)/shard_map/project/pallas_call | solution.py:433
  (1 shorter events, 0.0 us)
Async XLA Ops:
  1.0 5.1 %collective-permute-start.2 = (bf16[64,256]{1,0:T(8,128)(2,1)S(1)}, bf16[64,256]{1,0:T(8,128)(2,1)S(1)}, u32[]{:S(2)}, u32[]{:S(2)}) collective-permute-start(bf16[64,256]{1,0:T(8,128)(2,1)S(1)} %get-tuple-element.33.quarter), channel_id=1, source_target_pairs={{0,4},{4,0},{8,12},{12,8},{16,20},{20,16},{24,28},{28,24},{1,5},{5... | collective-permute-start | bytes 98312 | tf_op jit(solution)/shard_map/ppermute | solution.py:328
  4.0 8.1 %collective-permute-start = (bf16[192,256]{1,0:T(8,128)(2,1)S(1)}, bf16[192,256]{1,0:T(8,128)(2,1)S(1)}, u32[]{:S(2)}, u32[]{:S(2)}) collective-permute-start(bf16[192,256]{1,0:T(8,128)(2,1)S(1)} %get-tuple-element.28), channel_id=1, source_target_pairs={{0,4},{4,0},{8,12},{12,8},{16,20},{20,16},{24,28},{28,24},{1,5},{5... | collective-permute-start | bytes 294920 | tf_op jit(solution)/shard_map/ppermute | solution.py:328
  4.1 8.4 %collective-permute-start.1 = (bf16[192,256]{1,0:T(8,128)(2,1)S(1)}, bf16[192,256]{1,0:T(8,128)(2,1)S(1)}, u32[]{:S(2)}, u32[]{:S(2)}) collective-permute-start(bf16[192,256]{1,0:T(8,128)(2,1)S(1)} %get-tuple-element.29), channel_id=1, source_target_pairs={{0,2},{1,3},{2,0},{3,1},{4,8},{5,9},{6,10},{7,11},{8,4},{9,5},{10,... | collective-permute-start | bytes 294920 | tf_op jit(solution)/shard_map/ppermute | solution.py:347
  6.1 8.8 %collective-permute-start.3 = (bf16[128,256]{1,0:T(8,128)(2,1)S(1)}, bf16[128,256]{1,0:T(8,128)(2,1)S(1)}, u32[]{:S(2)}, u32[]{:S(2)}) collective-permute-start(bf16[128,256]{1,0:T(8,128)(2,1)S(1)} %get-tuple-element.34), channel_id=1, source_target_pairs={{0,8},{1,9},{2,10},{3,11},{4,12},{5,13},{6,14},{7,15},{8,24},{9,25... | collective-permute-start | bytes 196616 | tf_op jit(solution)/shard_map/ppermute | solution.py:347
  8.4 6.5 %collective-permute-start.4 = (bf16[64,256]{1,0:T(8,128)(2,1)S(1)}, bf16[64,256]{1,0:T(8,128)(2,1)S(1)}, u32[]{:S(2)}, u32[]{:S(2)}) collective-permute-start(bf16[64,256]{1,0:T(8,128)(2,1)S(1)} %get-tuple-element.35), channel_id=1, source_target_pairs={{0,16},{1,17},{2,18},{3,19},{4,20},{5,21},{6,22},{7,23},{8,10},{9,... | collective-permute-start | bytes 98312 | tf_op jit(solution)/shard_map/ppermute | solution.py:347
  10.9 4.5 %collective-permute-start.5 = (bf16[128,256]{1,0:T(8,128)(2,1)S(1)}, bf16[128,256]{1,0:T(8,128)(2,1)S(1)}, u32[]{:S(2)}, u32[]{:S(2)}) collective-permute-start(bf16[128,256]{1,0:T(8,128)(2,1)S(1)} %get-tuple-element.38), channel_id=1, source_target_pairs={{0,24},{1,25},{2,26},{3,27},{4,28},{5,29},{6,30},{7,31},{8,0},{9,1... | collective-permute-start | bytes 196616 | tf_op jit(solution)/shard_map/ppermute | solution.py:347
  12.2 4.3 %collective-permute-start.6 = (bf16[128,256]{1,0:T(8,128)(2,1)S(1)}, bf16[128,256]{1,0:T(8,128)(2,1)S(1)}, u32[]{:S(2)}, u32[]{:S(2)}) collective-permute-start(bf16[128,256]{1,0:T(8,128)(2,1)S(1)} %get-tuple-element.39), channel_id=1, source_target_pairs={{0,2},{1,3},{2,0},{3,1},{4,6},{5,7},{6,4},{7,5},{8,16},{9,17},{10,... | collective-permute-start | bytes 196616 | tf_op jit(solution)/shard_map/ppermute | solution.py:347
  17.0 3.6 %collective-permute-start.8 = (bf16[80,128]{1,0:T(8,128)(2,1)S(1)}, bf16[80,128]{1,0:T(8,128)(2,1)S(1)}, u32[]{:S(2)}, u32[]{:S(2)}) collective-permute-start(bf16[80,128]{1,0:T(8,128)(2,1)S(1)} %get-tuple-element.45), channel_id=1, source_target_pairs={{0,3},{1,2},{2,1},{3,0},{4,7},{5,6},{6,5},{7,4},{8,11},{9,10},{10,... | collective-permute-start | bytes 61448 | tf_op jit(solution)/shard_map/ppermute | solution.py:328
  17.1 3.9 %collective-permute-start.9 = (bf16[80,128]{1,0:T(8,128)(2,1)S(1)}, bf16[80,128]{1,0:T(8,128)(2,1)S(1)}, u32[]{:S(2)}, u32[]{:S(2)}) collective-permute-start(bf16[80,128]{1,0:T(8,128)(2,1)S(1)} %get-tuple-element.46), channel_id=1, source_target_pairs={{0,2},{1,3},{2,0},{3,1},{4,6},{5,7},{6,4},{7,5},{8,10},{9,11},{10,... | collective-permute-start | bytes 61448 | tf_op jit(solution)/shard_map/ppermute | solution.py:328
  17.5 2.9 %copy-start = (bf16[512,512]{1,0:T(8,128)(2,1)S(1)}, bf16[512,512]{1,0:T(8,128)(2,1)}, u32[]{:S(2)}) copy-start(bf16[512,512]{1,0:T(8,128)(2,1)} %weight.3) | copy-start | bytes 1572868
  18.1 2.3 %collective-permute-start.7 = (bf16[64,128]{1,0:T(8,128)(2,1)S(1)}, bf16[64,128]{1,0:T(8,128)(2,1)S(1)}, u32[]{:S(2)}, u32[]{:S(2)}) collective-permute-start(bf16[64,128]{1,0:T(8,128)(2,1)S(1)} %get-tuple-element.44), channel_id=1, source_target_pairs={{0,1},{1,0},{2,3},{3,2},{4,5},{5,4},{6,7},{7,6},{8,9},{9,8},{10,11... | collective-permute-start | bytes 49160 | tf_op jit(solution)/shard_map/ppermute | solution.py:328

commit v21 on v16

--- a/solution.py
+++ b/solution.py
@@ -54,17 +54,11 @@
         quarter[...] = level_two
 
 
-def join_kernel(inner, quarter, upward, downward, eighth, wide):
+def join_kernel(theirs, quarter, upward, downward, eighth, wide):
     me = lax.axis_index("seq")
     odd = me & 1
-    edge_half = average_pairs(inner[:LEAF], wide)
-    other_half = inner[LEAF:]
-    theirs = jnp.concatenate(
-        [jnp.where(odd == 1, other_half, edge_half), jnp.where(odd == 1, edge_half, other_half)], axis=0
-    )
-    theirs = average_pairs(theirs, wide)
-    first = jnp.where(odd == 1, theirs, quarter[...])
-    second = jnp.where(odd == 1, quarter[...], theirs)
+    first = jnp.where(odd == 1, theirs[...], quarter[...])
+    second = jnp.where(odd == 1, quarter[...], theirs[...])
     level_three = average_pairs(jnp.concatenate([first, second], axis=0), wide)
     upward[:HALF] = jnp.where(me >= 6, level_three, first)
     upward[HALF:] = second
@@ -341,8 +335,20 @@
         [wide, pltpu.SemaphoreType.DMA((3,))],
     )(*(pltpu.with_memory_space_constraint(array, pltpu.HBM) for array in (queries, keys, values)))
     inner = swap(inner, 1)
-    others = [(i, i + 1 if i & 1 else i - 1) for i in range(1, seq_size - 1)]
-    outer = lax.ppermute(outer, "seq", others)
+
+    def to_spans(array, targets):
+        return lax.ppermute(
+            array,
+            ("seq", "head"),
+            [
+                (s * head_size + h, t * head_size + (h if s != t else h ^ 1))
+                for s, t in enumerate(targets)
+                for h in range(head_size)
+            ],
+        )
+
+    last = seq_size - 1
+    outer = to_spans(outer, [s if s in (0, last) else s + 1 if s & 1 else s - 1 for s in range(seq_size)])
     if paired:
         upward, downward, eighth = kernel_call(
             join_kernel,
@@ -351,7 +357,8 @@
             [VMEM] * 2,
             [(LEAF, pair_width), (LEAF, pair_width), (HALF, pair_width)],
             [wide],
-        )(inner, quarter)
+            flops=3 * 10**8,
+        )(swap(quarter, 1), quarter)
         shift = [(i, (i + 2) % seq_size) for i in range(seq_size)]
         early = (lax.ppermute(upward, "seq", shift), swap(eighth, 4))
         late = lax.ppermute(downward, "seq", [(target, source) for source, target in shift])

time: 21.2 us -> 20.7 us (0.976)
  waiting for transfers between devices: 5.6 us -> 5.32 us
    ppermute x1, starting transfers between devices: 0.65 us -> 0.01 us  [to_spans(): lax.ppermute(array, ('seq', 'head'), [(s * head_size + h, t * head_size +...]
    ppermute x1, starting transfers between devices: 1.96 us -> 2.43 us  [shards(): early = (lax.ppermute(upward, 'seq', shift), swap(eighth, 4))]
    ppermute x5 -> x6, waiting for transfers between devices: 4.39 us -> 4.86 us  [swap(): lax.ppermute(array, axis, [(i, i ^ bit) for i in range(lax.axis_size(axis...]
    ppermute x1, waiting for transfers between devices: 0.42 us -> 0.01 us  [shards(): early = (lax.ppermute(upward, 'seq', shift), swap(eighth, 4))]
    ppermute x1, waiting for transfers between devices: 0.79 us -> 0.45 us  [shards(): lax.ppermute(downward, 'seq', [(target, source) for source, target in shi...]
    ppermute x5 -> x6, starting transfers between devices: 7.58 us -> 7.65 us  [swap(): lax.ppermute(array, axis, [(i, i ^ bit) for i in range(lax.axis_size(axis...]
  transfers between devices with their start and end apart: 8 -> 9, of which waited for: 6 -> 5; matrix products, arithmetic and copies ran while one was open for 0% -> 0% of each run, Pallas kernels for 7% -> 7%
where the time goes in v21:
time: 20.7 us; the launch traced here: 20.6 us
  starting transfers between devices  11.4 us (55%)
  waiting for transfers between devices  5.32 us (26%)
  Pallas kernels  3.74 us (18%)
    ppermute x6, starting transfers between devices, swap(): lax.ppermute(array, axis, [(i, i ^ bit) for i in range(lax.axis_size(axis...  7.65 us
    ppermute x6, waiting for transfers between devices, swap(): lax.ppermute(array, axis, [(i, i ^ bit) for i in range(lax.axis_size(axis...  4.86 us
    ppermute x1, starting transfers between devices, shards(): early = (lax.ppermute(upward, 'seq', shift), swap(eighth, 4))  2.43 us
    ppermute x1, starting transfers between devices, shards(): lax.ppermute(downward, 'seq', [(target, source) for source, target in shi...  1.35 us
    pallas_call x1, Pallas kernels, shards(): kernel_call(functools.partial(pack_kernel, not paired), 'pack', 16, [HBM]...  0.99 us
    pallas_call x1, Pallas kernels, shards(): kernel_call(project_kernel, 'project', 8, [VMEM] * 4, [(share, out_weight...  0.81 us
    pallas_call x1, Pallas kernels, shards(): kernel_call(functools.partial(leaves_kernel, seq_size, paired), 'leaves',...  0.56 us
    pallas_call x1, Pallas kernels, shards(): kernel_call(stays_kernel, 'stays', 16, [VMEM] * 8, [(share, width)] * 2,...  0.55 us
  transfers between devices with their start and end apart: 9, of which 5 were waited for; matrix products, arithmetic and copies ran while one was open for 0% of the time, Pallas kernels for 7%

profile of v21, /device:TPU:0, one launch (start us, length us, event | category | flops | bytes accessed | tf_op | source)
XLA Modules:
  0.0 20.6 jit_solution(10137283787779825760)
XLA Ops:
  0.0 1.0 %pack.1 = (bf16[256,128]{1,0:T(8,128)(2,1)S(1)}, bf16[256,256]{1,0:T(8,128)(2,1)S(1)}, bf16[192,256]{1,0:T(8,128)(2,1)S(1)}, bf16[192,256]{1,0:T(8,128)(2,1)S(1)}, bf16[64,256]{1,0:T(8,128)(2,1)S(1)}) custom-call(bf16[256,128]{1,0:T(8,128)(2,1)} %queries.1, bf16[256,128]{1,0:T(8,128)(2,1)} %keys.1, bf16[256,128]{1,0:T(8,128)(2,1)} %values.1), custom_call_target="tpu_custom_call" | custom-call | bytes 1048576 | tf_op jit(solution)/shard_map/pack/pallas_call | solution.py:323
  1.0 3.0 %collective-permute-start.2 = (bf16[64,256]{1,0:T(8,128)(2,1)S(1)}, bf16[64,256]{1,0:T(8,128)(2,1)S(1)}, u32[]{:S(2)}, u32[]{:S(2)}) collective-permute-start(bf16[64,256]{1,0:T(8,128)(2,1)S(1)} %get-tuple-element.32.quarter), channel_id=1, source_target_pairs={{0,4},{4,0},{8,12},{12,8},{16,20},{20,16},{24,28},{28,24},{1,5},{5... | collective-permute-start | bytes 98312 | tf_op jit(solution)/shard_map/ppermute | solution.py:321
  4.0 0.1 collective-permute-start
  4.1 0.0 collective-permute-start.1
  4.1 1.8 %collective-permute-done.2.theirs = bf16[64,256]{1,0:T(8,128)(2,1)S(1)} collective-permute-done((bf16[64,256]{1,0:T(8,128)(2,1)S(1)}, bf16[64,256]{1,0:T(8,128)(2,1)S(1)}, u32[]{:S(2)}, u32[]{:S(2)}) %collective-permute-start.2) | collective-permute-done | bytes 32800 | tf_op jit(solution)/shard_map/ppermute | solution.py:321
  5.9 2.4 %collective-permute-start.3 = (bf16[128,256]{1,0:T(8,128)(2,1)S(1)}, bf16[128,256]{1,0:T(8,128)(2,1)S(1)}, u32[]{:S(2)}, u32[]{:S(2)}) collective-permute-start(bf16[128,256]{1,0:T(8,128)(2,1)S(1)} %get-tuple-element.33), channel_id=1, source_target_pairs={{0,8},{4,12},{8,16},{12,20},{16,24},{20,28},{24,0},{28,4},{1,9},{5... | collective-permute-start | bytes 196616 | tf_op jit(solution)/shard_map/ppermute | solution.py:363
  8.4 2.6 %collective-permute-start.4 = (bf16[64,256]{1,0:T(8,128)(2,1)S(1)}, bf16[64,256]{1,0:T(8,128)(2,1)S(1)}, u32[]{:S(2)}, u32[]{:S(2)}) collective-permute-start(bf16[64,256]{1,0:T(8,128)(2,1)S(1)} %get-tuple-element.34), channel_id=1, source_target_pairs={{0,16},{4,20},{8,24},{12,28},{16,0},{20,4},{24,8},{28,12},{1,17},{... | collective-permute-start | bytes 98312 | tf_op jit(solution)/shard_map/ppermute | solution.py:321
  11.0 1.3 %collective-permute-start.5 = (bf16[128,256]{1,0:T(8,128)(2,1)S(1)}, bf16[128,256]{1,0:T(8,128)(2,1)S(1)}, u32[]{:S(2)}, u32[]{:S(2)}) collective-permute-start(bf16[128,256]{1,0:T(8,128)(2,1)S(1)} %get-tuple-element.37), channel_id=1, source_target_pairs={{8,0},{12,4},{16,8},{20,12},{24,16},{28,20},{0,24},{4,28},{9,1},{1... | collective-permute-start | bytes 196616 | tf_op jit(solution)/shard_map/ppermute | solution.py:364
  12.3 0.0 collective-permute-done.inner
  12.3 0.0 collective-permute-done.1.outer
  12.3 0.4 %near.1 = (f32[2,256,512]{2,1,0:T(8,128)S(1)}, bf16[2,512,128]{2,1,0:T(8,128)(2,1)S(1)}, bf16[64,256]{1,0:T(8,128)(2,1)S(1)}) custom-call(bf16[256,128]{1,0:T(8,128)(2,1)S(1)} %get-tuple-element.25.queries, bf16[256,256]{1,0:T(8,128)(2,1)S(1)} %get-tuple-element.26.own, bf16[192,256]{1,0:T(8,128)(2,1)S(1)} %collective-permute-done.inner, ...), custom_call_target="tpu_custom_call" | custom-call | flops 67108864 | bytes 1048576 | tf_op jit(solution)/shard_map/near/pallas_call | solution.py:369
  12.7 1.9 %collective-permute-done.4.rest_1_ = bf16[64,256]{1,0:T(8,128)(2,1)S(1)} collective-permute-done((bf16[64,256]{1,0:T(8,128)(2,1)S(1)}, bf16[64,256]{1,0:T(8,128)(2,1)S(1)}, u32[]{:S(2)}, u32[]{:S(2)}) %collective-permute-start.4) | collective-permute-done | bytes 32800 | tf_op jit(solution)/shard_map/ppermute | solution.py:321
  14.6 0.0 collective-permute-done.3.rest_0_
  14.6 0.2 %mid.1 = (f32[2,256,256]{2,1,0:T(8,128)S(1)}, bf16[256,128]{1,0:T(8,128)(2,1)S(1)}) custom-call(bf16[256,128]{1,0:T(8,128)(2,1)S(1)} %get-tuple-element.25.queries, bf16[64,256]{1,0:T(8,128)(2,1)S(1)} %get-tuple-element.31.shared, bf16[128,256]{1,0:T(8,128)(2,1)S(1)} %collective-permute-done.3.rest_0_, bf16[64,256]{1,0:T(8,128)(2,1)S(1)} %collective-permute-done.4.rest_1_), custom_call_target="tpu_custom_call" | custom-call | flops 1000000000 | bytes 1048576 | tf_op jit(solution)/shard_map/mid/pallas_call | solution.py:383
  14.8 0.5 %collective-permute-done.5.rest_0_ = bf16[128,256]{1,0:T(8,128)(2,1)S(1)} collective-permute-done((bf16[128,256]{1,0:T(8,128)(2,1)S(1)}, bf16[128,256]{1,0:T(8,128)(2,1)S(1)}, u32[]{:S(2)}, u32[]{:S(2)}) %collective-permute-start.5) | collective-permute-done | bytes 65568 | tf_op jit(solution)/shard_map/ppermute | solution.py:364
  15.3 0.6 %leaves.1 = (bf16[80,128]{1,0:T(8,128)(2,1)S(1)}, bf16[80,128]{1,0:T(8,128)(2,1)S(1)}, bf16[128,128]{1,0:T(8,128)(2,1)S(1)}, bf16[128,128]{1,0:T(8,128)(2,1)S(1)}, f32[8,128]{1,0:T(8,128)S(1)}) custom-call(bf16[256,128]{1,0:T(8,128)(2,1)S(1)} %get-tuple-element.25.queries, f32[2,256,512]{2,1,0:T(8,128)S(1)} %get-tuple-element.29.near_scores, ...), custom_call_target="tpu_custom_call" | custom-call | flops 117440512 | bytes 1048576 | tf_op jit(solution)/shard_map/leaves/pallas_call | solution.py:395
  15.8 0.1 collective-permute-start.7
  15.9 1.6 %collective-permute-start.8 = (bf16[80,128]{1,0:T(8,128)(2,1)S(1)}, bf16[80,128]{1,0:T(8,128)(2,1)S(1)}, u32[]{:S(2)}, u32[]{:S(2)}) collective-permute-start(bf16[80,128]{1,0:T(8,128)(2,1)S(1)} %get-tuple-element.44), channel_id=1, source_target_pairs={{0,2},{1,3},{2,0},{3,1},{4,6},{5,7},{6,4},{7,5},{8,10},{9,11},{10,... | collective-permute-start | bytes 61448 | tf_op jit(solution)/shard_map/ppermute | solution.py:321
  17.5 0.0 copy-start
  17.5 0.6 %stays.1 = (bf16[64,128]{1,0:T(8,128)(2,1)S(1)}, bf16[64,128]{1,0:T(8,128)(2,1)S(1)}) custom-call(bf16[256,128]{1,0:T(8,128)(2,1)S(1)} %get-tuple-element.25.queries, f32[2,256,512]{2,1,0:T(8,128)S(1)} %get-tuple-element.29.near_scores, bf16[2,512,128]{2,1,0:T(8,128)(2,1)S(1)} %get-tuple-element.30.near_values, ...), custom_call_target="tpu_custom_call" | custom-call | flops 117440512 | bytes 1048576 | tf_op jit(solution)/shard_map/stays/pallas_call | solution.py:410
  18.1 0.3 %collective-permute-start.6 = (bf16[64,128]{1,0:T(8,128)(2,1)S(1)}, bf16[64,128]{1,0:T(8,128)(2,1)S(1)}, u32[]{:S(2)}, u32[]{:S(2)}) collective-permute-start(bf16[64,128]{1,0:T(8,128)(2,1)S(1)} %get-tuple-element.42), channel_id=1, source_target_pairs={{0,1},{1,0},{2,3},{3,2},{4,5},{5,4},{6,7},{7,6},{8,9},{9,8},{10,11... | collective-permute-start | bytes 49160 | tf_op jit(solution)/shard_map/ppermute | solution.py:321
  18.4 0.9 %collective-permute-done.6.other = bf16[64,128]{1,0:T(8,128)(2,1)S(1)} collective-permute-done((bf16[64,128]{1,0:T(8,128)(2,1)S(1)}, bf16[64,128]{1,0:T(8,128)(2,1)S(1)}, u32[]{:S(2)}, u32[]{:S(2)}) %collective-permute-start.6) | collective-permute-done | bytes 16416 | tf_op jit(solution)/shard_map/ppermute | solution.py:321
  19.3 0.0 copy-done
  19.3 0.2 begin.1.partial
  19.5 0.0 collective-permute-done.7.other
  19.5 0.3 %collective-permute-done.8.same = bf16[80,128]{1,0:T(8,128)(2,1)S(1)} collective-permute-done((bf16[80,128]{1,0:T(8,128)(2,1)S(1)}, bf16[80,128]{1,0:T(8,128)(2,1)S(1)}, u32[]{:S(2)}, u32[]{:S(2)}) %collective-permute-start.8) | collective-permute-done | bytes 20512 | tf_op jit(solution)/shard_map/ppermute | solution.py:321
  19.8 0.8 %project.1 = bf16[64,512]{1,0:T(8,128)(2,1)} custom-call(f32[64,512]{1,0:T(8,128)S(1)} %begin.1.partial, bf16[80,128]{1,0:T(8,128)(2,1)S(1)} %collective-permute-done.7.other, bf16[80,128]{1,0:T(8,128)(2,1)S(1)} %collective-permute-done.8.same, bf16[512,512]{1,0:T(8,128)(2,1)S(1)} %copy-done), custom_call_target="tpu_custom_call" | custom-call | bytes 1048576 | tf_op jit(solution)/shard_map/project/pallas_call | solution.py:423
  (1 shorter events, 0.0 us)
Async XLA Ops:
  1.0 4.9 %collective-permute-start.2 = (bf16[64,256]{1,0:T(8,128)(2,1)S(1)}, bf16[64,256]{1,0:T(8,128)(2,1)S(1)}, u32[]{:S(2)}, u32[]{:S(2)}) collective-permute-start(bf16[64,256]{1,0:T(8,128)(2,1)S(1)} %get-tuple-element.32.quarter), channel_id=1, source_target_pairs={{0,4},{4,0},{8,12},{12,8},{16,20},{20,16},{24,28},{28,24},{1,5},{5... | collective-permute-start | bytes 98312 | tf_op jit(solution)/shard_map/ppermute | solution.py:321
  4.0 8.3 %collective-permute-start = (bf16[192,256]{1,0:T(8,128)(2,1)S(1)}, bf16[192,256]{1,0:T(8,128)(2,1)S(1)}, u32[]{:S(2)}, u32[]{:S(2)}) collective-permute-start(bf16[192,256]{1,0:T(8,128)(2,1)S(1)} %get-tuple-element.27), channel_id=1, source_target_pairs={{0,4},{4,0},{8,12},{12,8},{16,20},{20,16},{24,28},{28,24},{1,5},{5... | collective-permute-start | bytes 294920 | tf_op jit(solution)/shard_map/ppermute | solution.py:321
  4.1 8.2 %collective-permute-start.1 = (bf16[192,256]{1,0:T(8,128)(2,1)S(1)}, bf16[192,256]{1,0:T(8,128)(2,1)S(1)}, u32[]{:S(2)}, u32[]{:S(2)}) collective-permute-start(bf16[192,256]{1,0:T(8,128)(2,1)S(1)} %get-tuple-element.28), channel_id=1, source_target_pairs={{0,1},{1,0},{2,3},{3,2},{4,8},{5,9},{6,10},{7,11},{8,4},{9,5},{10,... | collective-permute-start | bytes 294920 | tf_op jit(solution)/shard_map/ppermute | solution.py:340
  5.9 8.6 %collective-permute-start.3 = (bf16[128,256]{1,0:T(8,128)(2,1)S(1)}, bf16[128,256]{1,0:T(8,128)(2,1)S(1)}, u32[]{:S(2)}, u32[]{:S(2)}) collective-permute-start(bf16[128,256]{1,0:T(8,128)(2,1)S(1)} %get-tuple-element.33), channel_id=1, source_target_pairs={{0,8},{4,12},{8,16},{12,20},{16,24},{20,28},{24,0},{28,4},{1,9},{5... | collective-permute-start | bytes 196616 | tf_op jit(solution)/shard_map/ppermute | solution.py:363
  8.4 6.2 %collective-permute-start.4 = (bf16[64,256]{1,0:T(8,128)(2,1)S(1)}, bf16[64,256]{1,0:T(8,128)(2,1)S(1)}, u32[]{:S(2)}, u32[]{:S(2)}) collective-permute-start(bf16[64,256]{1,0:T(8,128)(2,1)S(1)} %get-tuple-element.34), channel_id=1, source_target_pairs={{0,16},{4,20},{8,24},{12,28},{16,0},{20,4},{24,8},{28,12},{1,17},{... | collective-permute-start | bytes 98312 | tf_op jit(solution)/shard_map/ppermute | solution.py:321
  11.0 4.3 %collective-permute-start.5 = (bf16[128,256]{1,0:T(8,128)(2,1)S(1)}, bf16[128,256]{1,0:T(8,128)(2,1)S(1)}, u32[]{:S(2)}, u32[]{:S(2)}) collective-permute-start(bf16[128,256]{1,0:T(8,128)(2,1)S(1)} %get-tuple-element.37), channel_id=1, source_target_pairs={{8,0},{12,4},{16,8},{20,12},{24,16},{28,20},{0,24},{4,28},{9,1},{1... | collective-permute-start | bytes 196616 | tf_op jit(solution)/shard_map/ppermute | solution.py:364
  15.8 3.7 %collective-permute-start.7 = (bf16[80,128]{1,0:T(8,128)(2,1)S(1)}, bf16[80,128]{1,0:T(8,128)(2,1)S(1)}, u32[]{:S(2)}, u32[]{:S(2)}) collective-permute-start(bf16[80,128]{1,0:T(8,128)(2,1)S(1)} %get-tuple-element.43), channel_id=1, source_target_pairs={{0,3},{1,2},{2,1},{3,0},{4,7},{5,6},{6,5},{7,4},{8,11},{9,10},{10,... | collective-permute-start | bytes 61448 | tf_op jit(solution)/shard_map/ppermute | solution.py:321
  15.9 3.8 %collective-permute-start.8 = (bf16[80,128]{1,0:T(8,128)(2,1)S(1)}, bf16[80,128]{1,0:T(8,128)(2,1)S(1)}, u32[]{:S(2)}, u32[]{:S(2)}) collective-permute-start(bf16[80,128]{1,0:T(8,128)(2,1)S(1)} %get-tuple-element.44), channel_id=1, source_target_pairs={{0,2},{1,3},{2,0},{3,1},{4,6},{5,7},{6,4},{7,5},{8,10},{9,11},{10,... | collective-permute-start | bytes 61448 | tf_op jit(solution)/shard_map/ppermute | solution.py:321
  17.5 1.8 %copy-start = (bf16[512,512]{1,0:T(8,128)(2,1)S(1)}, bf16[512,512]{1,0:T(8,128)(2,1)}, u32[]{:S(2)}) copy-start(bf16[512,512]{1,0:T(8,128)(2,1)} %weight.3) | copy-start | bytes 1572868
  18.1 1.2 %collective-permute-start.6 = (bf16[64,128]{1,0:T(8,128)(2,1)S(1)}, bf16[64,128]{1,0:T(8,128)(2,1)S(1)}, u32[]{:S(2)}, u32[]{:S(2)}) collective-permute-start(bf16[64,128]{1,0:T(8,128)(2,1)S(1)} %get-tuple-element.42), channel_id=1, source_target_pairs={{0,1},{1,0},{2,3},{3,2},{4,5},{5,4},{6,7},{7,6},{8,9},{9,8},{10,11... | collective-permute-start | bytes 49160 | tf_op jit(solution)/shard_map/ppermute | solution.py:321

commit v22 on v21

--- a/solution.py
+++ b/solution.py
@@ -17,10 +17,11 @@
 def average_pairs(rows, wide):
     count = rows.shape[0]
     halves = []
-    for low in range(0, rows.shape[1], LEAF):
-        wide[:count] = rows[:, low : low + LEAF].astype(jnp.float32)
-        even = wide[pl.ds(0, count // 2, stride=2), :]
-        odd = wide[pl.ds(1, count // 2, stride=2), :]
+    for half, low in enumerate(range(0, rows.shape[1], LEAF)):
+        wide[half, :count] = rows[:, low : low + LEAF].astype(jnp.float32)
+    for half in range(rows.shape[1] // LEAF):
+        even = wide[half, pl.ds(0, count // 2, stride=2), :]
+        odd = wide[half, pl.ds(1, count // 2, stride=2), :]
         halves.append((0.5 * (even + odd)).astype(jnp.bfloat16))
     return jnp.concatenate(halves, axis=1)
 
@@ -201,30 +202,33 @@
         scores[leaf] = scores_of(rows, keys) + bias
 
 
-def mid_kernel(queries, shared, *rest):
-    *early, scores, values, keys = rest
+def mid_kernel(queries, near_scores, shared, *rest):
+    *early, scores, values, peak, keys = rest
     pieces = [(shared, bias_of(lax.axis_index("seq") >= 1))]
     if early:
         pieces += early_pieces(*early)
     bias = place(pieces, values, keys)
     for leaf in range(2):
         rows = split_heads(queries[leaf * LEAF : (leaf + 1) * LEAF])
-        scores[leaf] = scores_of(rows, keys) + bias
+        found = scores_of(rows, keys) + bias
+        scores[leaf] = found
+        peak[leaf] = jnp.maximum(
+            jnp.max(near_scores[leaf], axis=1, keepdims=True), jnp.max(found, axis=1, keepdims=True)
+        )
 
 
 def attend_leaf(leaf, queries, scored, keys, values, bias, same, other):
     first_head = lax.broadcasted_iota(jnp.int32, (1, values.shape[1]), 1) < HD
     exponent = math.log2(math.e) / math.sqrt(HD)
     rows = split_heads(queries[pl.ds(pl.multiple_of(leaf * LEAF, LEAF), LEAF)])
-    near_scores, near_values, mid_scores, mid_values = scored
+    near_scores, near_values, mid_scores, mid_values, peaks = scored
+    last_scores = scores_of(rows, keys) + bias
     parts = [
         (near_scores[leaf], near_values[leaf]),
         (mid_scores[leaf], mid_values[...]),
-        (scores_of(rows, keys) + bias, values[...]),
+        (last_scores, values[...]),
     ]
-    peak = functools.reduce(
-        jnp.maximum, [jnp.max(scores, axis=1, keepdims=True) for scores, _ in parts]
-    )
+    peak = jnp.maximum(peaks[leaf], jnp.max(last_scores, axis=1, keepdims=True))
     total, numer = 0.0, 0.0
     for scores, part_values in parts:
         weights = jnp.exp2((scores - peak) * exponent)
@@ -239,22 +243,19 @@
     other[:HALF] = jnp.where(second, attended[:HALF], attended[HALF:])
 
 
-def leaves_kernel(seq_size, paired, queries, near_scores, near_values, mid_scores, mid_values, *rest):
-    late, same, other, keys, values, bias, wide = rest
+def leaves_kernel(seq_size, paired, queries, *rest):
+    scored, (late, same, other, keys, values, bias, wide) = rest[:5], rest[5:]
     pieces = late_pieces(late) if paired else gathered_pieces(seq_size, late, wide)
     bias[...] = jnp.broadcast_to(place(pieces, values, keys), bias.shape)
     leaf = (lax.axis_index("head") >> 1) ^ 1
-    scored = (near_scores, near_values, mid_scores, mid_values)
     attend_leaf(leaf, queries, scored, keys, values, bias[:1], same, other)
     for share in (same, other):
         share[HALF:] = jnp.zeros((PAD, share.shape[1]), share.dtype)
 
 
-def stays_kernel(
-    queries, near_scores, near_values, mid_scores, mid_values, keys, values, bias, same, other
-):
+def stays_kernel(queries, *rest):
+    scored, (keys, values, bias, same, other) = rest[:5], rest[5:]
     leaf = lax.axis_index("head") >> 1
-    scored = (near_scores, near_values, mid_scores, mid_values)
     attend_leaf(leaf, queries, scored, keys, values, bias[:1], same, other)
 
 
@@ -315,7 +316,7 @@
     pair_width = 2 * width
     paired = seq_size == 8
     wide_rows = 2 * LEAF if paired else max(2 * LEAF, seq_size // 2 * HALF)
-    wide = pltpu.VMEM((wide_rows, width), jnp.float32)
+    wide = pltpu.VMEM((2, wide_rows, width), jnp.float32)
 
     def swap(array, bit, axis="seq"):
         return lax.ppermute(array, axis, [(i, i ^ bit) for i in range(lax.axis_size(axis))])
@@ -380,23 +381,27 @@
         flops=8 * LEAF * NEAR_ROWS * width,
     )(own_queries, own, inner, outer)
     mid_rows = 4 * HALF if paired else HALF
-    mid_scores, mid_values = kernel_call(
+    mid_scores, mid_values, peaks = kernel_call(
         mid_kernel,
         "mid",
         8,
-        [VMEM] * (2 + len(early)),
-        [jax.ShapeDtypeStruct((2, 2 * LEAF, mid_rows), jnp.float32), (mid_rows, width)],
+        [VMEM] * (3 + len(early)),
+        [
+            jax.ShapeDtypeStruct((2, 2 * LEAF, mid_rows), jnp.float32),
+            (mid_rows, width),
+            jax.ShapeDtypeStruct((2, 2 * LEAF, 1), jnp.float32),
+        ],
         [pltpu.VMEM((mid_rows, width), jnp.bfloat16)],
         flops=10**9,
-    )(own_queries, shared, *early)
-    scored = (near_scores, near_values, mid_scores, mid_values)
+    )(own_queries, near_scores, shared, *early)
+    scored = (near_scores, near_values, mid_scores, mid_values, peaks)
     last_rows = last_row_count(seq_size, paired)
     leaf_flops = 8 * LEAF * (NEAR_ROWS + mid_rows + last_rows) * width
     share_2, share_3, far_keys, far_values, far_bias = kernel_call(
         functools.partial(leaves_kernel, seq_size, paired),
         "leaves",
         24,
-        [VMEM] * 6,
+        [VMEM] * 7,
         [
             (share + PAD, width),
             (share + PAD, width),
@@ -408,7 +413,7 @@
         flops=leaf_flops,
     )(own_queries, *scored, late)
     share_0, share_1 = kernel_call(
-        stays_kernel, "stays", 16, [VMEM] * 8, [(share, width)] * 2, [], flops=leaf_flops
+        stays_kernel, "stays", 16, [VMEM] * 9, [(share, width)] * 2, [], flops=leaf_flops
     )(own_queries, *scored, far_keys, far_values, far_bias)
     columns = pltpu.VMEM((share, pair_width), jnp.bfloat16)
     part_3, part_2 = swap(share_3, 3, "head"), swap(share_2, 2, "head")

time: 20.7 us -> 20.8 us (level)
  Pallas kernels: 3.74 us -> 4.04 us
  transfers between devices with their start and end apart: 9 -> 9, of which waited for: 5 -> 5; matrix products, arithmetic and copies ran while one was open for 0% -> 0% of each run, Pallas kernels for 7% -> 8%
where the time goes in v22:
time: 20.8 us; the launch traced here: 20.7 us
  starting transfers between devices  11.4 us (55%)
  waiting for transfers between devices  5.13 us (25%)
  Pallas kernels  4.04 us (19%)
    ppermute x6, starting transfers between devices, swap(): lax.ppermute(array, axis, [(i, i ^ bit) for i in range(lax.axis_size(axis...  7.66 us
    ppermute x6, waiting for transfers between devices, swap(): lax.ppermute(array, axis, [(i, i ^ bit) for i in range(lax.axis_size(axis...  4.76 us
    ppermute x1, starting transfers between devices, shards(): early = (lax.ppermute(upward, 'seq', shift), swap(eighth, 4))  2.43 us
    ppermute x1, starting transfers between devices, shards(): lax.ppermute(downward, 'seq', [(target, source) for source, target in shi...  1.35 us
    pallas_call x1, Pallas kernels, shards(): kernel_call(functools.partial(pack_kernel, not paired), 'pack', 16, [HBM]...  1 us
    pallas_call x1, Pallas kernels, shards(): kernel_call(project_kernel, 'project', 8, [VMEM] * 4, [(share, out_weight...  0.81 us
    pallas_call x1, Pallas kernels, shards(): kernel_call(functools.partial(leaves_kernel, seq_size, paired), 'leaves',...  0.67 us
    pallas_call x1, Pallas kernels, shards(): kernel_call(stays_kernel, 'stays', 16, [VMEM] * 9, [(share, width)] * 2,...  0.66 us
  transfers between devices with their start and end apart: 9, of which 5 were waited for; matrix products, arithmetic and copies ran while one was open for 0% of the time, Pallas kernels for 8%

profile of v22, /device:TPU:0, one launch (start us, length us, event | category | flops | bytes accessed | tf_op | source)
XLA Modules:
  0.0 20.7 jit_solution(16031476066214591731)
XLA Ops:
  0.0 1.0 %pack.1 = (bf16[256,128]{1,0:T(8,128)(2,1)S(1)}, bf16[256,256]{1,0:T(8,128)(2,1)S(1)}, bf16[192,256]{1,0:T(8,128)(2,1)S(1)}, bf16[192,256]{1,0:T(8,128)(2,1)S(1)}, bf16[64,256]{1,0:T(8,128)(2,1)S(1)}) custom-call(bf16[256,128]{1,0:T(8,128)(2,1)} %queries.1, bf16[256,128]{1,0:T(8,128)(2,1)} %keys.1, bf16[256,128]{1,0:T(8,128)(2,1)} %values.1), custom_call_target="tpu_custom_call" | custom-call | bytes 1048576 | tf_op jit(solution)/shard_map/pack/pallas_call | solution.py:324
  1.0 3.0 %collective-permute-start.2 = (bf16[64,256]{1,0:T(8,128)(2,1)S(1)}, bf16[64,256]{1,0:T(8,128)(2,1)S(1)}, u32[]{:S(2)}, u32[]{:S(2)}) collective-permute-start(bf16[64,256]{1,0:T(8,128)(2,1)S(1)} %get-tuple-element.33.quarter), channel_id=1, source_target_pairs={{0,4},{4,0},{8,12},{12,8},{16,20},{20,16},{24,28},{28,24},{1,5},{5... | collective-permute-start | bytes 98312 | tf_op jit(solution)/shard_map/ppermute | solution.py:322
  4.0 0.1 collective-permute-start
  4.1 0.0 collective-permute-start.1
  4.1 1.8 %collective-permute-done.2.theirs = bf16[64,256]{1,0:T(8,128)(2,1)S(1)} collective-permute-done((bf16[64,256]{1,0:T(8,128)(2,1)S(1)}, bf16[64,256]{1,0:T(8,128)(2,1)S(1)}, u32[]{:S(2)}, u32[]{:S(2)}) %collective-permute-start.2) | collective-permute-done | bytes 32800 | tf_op jit(solution)/shard_map/ppermute | solution.py:322
  5.9 2.4 %collective-permute-start.3 = (bf16[128,256]{1,0:T(8,128)(2,1)S(1)}, bf16[128,256]{1,0:T(8,128)(2,1)S(1)}, u32[]{:S(2)}, u32[]{:S(2)}) collective-permute-start(bf16[128,256]{1,0:T(8,128)(2,1)S(1)} %get-tuple-element.34), channel_id=1, source_target_pairs={{0,8},{4,12},{8,16},{12,20},{16,24},{20,28},{24,0},{28,4},{1,9},{5... | collective-permute-start | bytes 196616 | tf_op jit(solution)/shard_map/ppermute | solution.py:364
  8.4 2.6 %collective-permute-start.4 = (bf16[64,256]{1,0:T(8,128)(2,1)S(1)}, bf16[64,256]{1,0:T(8,128)(2,1)S(1)}, u32[]{:S(2)}, u32[]{:S(2)}) collective-permute-start(bf16[64,256]{1,0:T(8,128)(2,1)S(1)} %get-tuple-element.35), channel_id=1, source_target_pairs={{0,16},{4,20},{8,24},{12,28},{16,0},{20,4},{24,8},{28,12},{1,17},{... | collective-permute-start | bytes 98312 | tf_op jit(solution)/shard_map/ppermute | solution.py:322
  11.0 1.3 %collective-permute-start.5 = (bf16[128,256]{1,0:T(8,128)(2,1)S(1)}, bf16[128,256]{1,0:T(8,128)(2,1)S(1)}, u32[]{:S(2)}, u32[]{:S(2)}) collective-permute-start(bf16[128,256]{1,0:T(8,128)(2,1)S(1)} %get-tuple-element.39), channel_id=1, source_target_pairs={{8,0},{12,4},{16,8},{20,12},{24,16},{28,20},{0,24},{4,28},{9,1},{1... | collective-permute-start | bytes 196616 | tf_op jit(solution)/shard_map/ppermute | solution.py:365
  12.3 0.0 collective-permute-done.inner
  12.3 0.0 collective-permute-done.1.outer
  12.3 0.4 %near.1 = (f32[2,256,512]{2,1,0:T(8,128)S(1)}, bf16[2,512,128]{2,1,0:T(8,128)(2,1)S(1)}, bf16[64,256]{1,0:T(8,128)(2,1)S(1)}) custom-call(bf16[256,128]{1,0:T(8,128)(2,1)S(1)} %get-tuple-element.26.queries, bf16[256,256]{1,0:T(8,128)(2,1)S(1)} %get-tuple-element.27.own, bf16[192,256]{1,0:T(8,128)(2,1)S(1)} %collective-permute-done.inner, ...), custom_call_target="tpu_custom_call" | custom-call | flops 67108864 | bytes 1048576 | tf_op jit(solution)/shard_map/near/pallas_call | solution.py:370
  12.7 1.9 %collective-permute-done.4.rest_1_ = bf16[64,256]{1,0:T(8,128)(2,1)S(1)} collective-permute-done((bf16[64,256]{1,0:T(8,128)(2,1)S(1)}, bf16[64,256]{1,0:T(8,128)(2,1)S(1)}, u32[]{:S(2)}, u32[]{:S(2)}) %collective-permute-start.4) | collective-permute-done | bytes 32800 | tf_op jit(solution)/shard_map/ppermute | solution.py:322
  14.6 0.0 collective-permute-done.3.rest_0_
  14.6 0.3 %mid.1 = (f32[2,256,256]{2,1,0:T(8,128)S(1)}, bf16[256,128]{1,0:T(8,128)(2,1)S(1)}, f32[2,256,1]{2,1,0:T(8,128)S(1)}) custom-call(bf16[256,128]{1,0:T(8,128)(2,1)S(1)} %get-tuple-element.26.queries, f32[2,256,512]{2,1,0:T(8,128)S(1)} %get-tuple-element.30.near_scores.rest_0_, bf16[64,256]{1,0:T(8,128)(2,1)S(1)} %get-tuple-element.32.shared, ...), custom_call_target="tpu_custom_call" | custom-call | flops 1000000000 | bytes 1048576 | tf_op jit(solution)/shard_map/mid/pallas_call | solution.py:384
  14.9 0.4 %collective-permute-done.5.rest_5_ = bf16[128,256]{1,0:T(8,128)(2,1)S(1)} collective-permute-done((bf16[128,256]{1,0:T(8,128)(2,1)S(1)}, bf16[128,256]{1,0:T(8,128)(2,1)S(1)}, u32[]{:S(2)}, u32[]{:S(2)}) %collective-permute-start.5) | collective-permute-done | bytes 65568 | tf_op jit(solution)/shard_map/ppermute | solution.py:365
  15.3 0.7 %leaves.1 = (bf16[80,128]{1,0:T(8,128)(2,1)S(1)}, bf16[80,128]{1,0:T(8,128)(2,1)S(1)}, bf16[128,128]{1,0:T(8,128)(2,1)S(1)}, bf16[128,128]{1,0:T(8,128)(2,1)S(1)}, f32[8,128]{1,0:T(8,128)S(1)}) custom-call(bf16[256,128]{1,0:T(8,128)(2,1)S(1)} %get-tuple-element.26.queries, f32[2,256,512]{2,1,0:T(8,128)S(1)} %get-tuple-element.30.near_scores.rest_0_, ...), custom_call_target="tpu_custom_call" | custom-call | flops 117440512 | bytes 1048576 | tf_op jit(solution)/shard_map/leaves/pallas_call | solution.py:400
  15.9 0.1 collective-permute-start.7
  16.0 1.6 %collective-permute-start.8 = (bf16[80,128]{1,0:T(8,128)(2,1)S(1)}, bf16[80,128]{1,0:T(8,128)(2,1)S(1)}, u32[]{:S(2)}, u32[]{:S(2)}) collective-permute-start(bf16[80,128]{1,0:T(8,128)(2,1)S(1)} %get-tuple-element.46), channel_id=1, source_target_pairs={{0,2},{1,3},{2,0},{3,1},{4,6},{5,7},{6,4},{7,5},{8,10},{9,11},{10,... | collective-permute-start | bytes 61448 | tf_op jit(solution)/shard_map/ppermute | solution.py:322
  17.6 0.0 copy-start
  17.6 0.7 %stays.1 = (bf16[64,128]{1,0:T(8,128)(2,1)S(1)}, bf16[64,128]{1,0:T(8,128)(2,1)S(1)}) custom-call(bf16[256,128]{1,0:T(8,128)(2,1)S(1)} %get-tuple-element.26.queries, f32[2,256,512]{2,1,0:T(8,128)S(1)} %get-tuple-element.30.near_scores.rest_0_, bf16[2,512,128]{2,1,0:T(8,128)(2,1)S(1)} %get-tuple-element.31.rest_1_, ...), custom_call_target="tpu_custom_call" | custom-call | flops 117440512 | bytes 1048576 | tf_op jit(solution)/shard_map/stays/pallas_call | solution.py:415
  18.3 0.3 %collective-permute-start.6 = (bf16[64,128]{1,0:T(8,128)(2,1)S(1)}, bf16[64,128]{1,0:T(8,128)(2,1)S(1)}, u32[]{:S(2)}, u32[]{:S(2)}) collective-permute-start(bf16[64,128]{1,0:T(8,128)(2,1)S(1)} %get-tuple-element.44), channel_id=1, source_target_pairs={{0,1},{1,0},{2,3},{3,2},{4,5},{5,4},{6,7},{7,6},{8,9},{9,8},{10,11... | collective-permute-start | bytes 49160 | tf_op jit(solution)/shard_map/ppermute | solution.py:322
  18.6 0.9 %collective-permute-done.6.other = bf16[64,128]{1,0:T(8,128)(2,1)S(1)} collective-permute-done((bf16[64,128]{1,0:T(8,128)(2,1)S(1)}, bf16[64,128]{1,0:T(8,128)(2,1)S(1)}, u32[]{:S(2)}, u32[]{:S(2)}) %collective-permute-start.6) | collective-permute-done | bytes 16416 | tf_op jit(solution)/shard_map/ppermute | solution.py:322
  19.5 0.0 copy-done
  19.5 0.2 begin.1.partial
  19.7 0.0 collective-permute-done.7.other
  19.7 0.2 collective-permute-done.8.same
  19.9 0.8 %project.1 = bf16[64,512]{1,0:T(8,128)(2,1)} custom-call(f32[64,512]{1,0:T(8,128)S(1)} %begin.1.partial, bf16[80,128]{1,0:T(8,128)(2,1)S(1)} %collective-permute-done.7.other, bf16[80,128]{1,0:T(8,128)(2,1)S(1)} %collective-permute-done.8.same, bf16[512,512]{1,0:T(8,128)(2,1)S(1)} %copy-done), custom_call_target="tpu_custom_call" | custom-call | bytes 1048576 | tf_op jit(solution)/shard_map/project/pallas_call | solution.py:428
  (1 shorter events, 0.0 us)
Async XLA Ops:
  1.0 4.9 %collective-permute-start.2 = (bf16[64,256]{1,0:T(8,128)(2,1)S(1)}, bf16[64,256]{1,0:T(8,128)(2,1)S(1)}, u32[]{:S(2)}, u32[]{:S(2)}) collective-permute-start(bf16[64,256]{1,0:T(8,128)(2,1)S(1)} %get-tuple-element.33.quarter), channel_id=1, source_target_pairs={{0,4},{4,0},{8,12},{12,8},{16,20},{20,16},{24,28},{28,24},{1,5},{5... | collective-permute-start | bytes 98312 | tf_op jit(solution)/shard_map/ppermute | solution.py:322
  4.0 8.3 %collective-permute-start = (bf16[192,256]{1,0:T(8,128)(2,1)S(1)}, bf16[192,256]{1,0:T(8,128)(2,1)S(1)}, u32[]{:S(2)}, u32[]{:S(2)}) collective-permute-start(bf16[192,256]{1,0:T(8,128)(2,1)S(1)} %get-tuple-element.28), channel_id=1, source_target_pairs={{0,4},{4,0},{8,12},{12,8},{16,20},{20,16},{24,28},{28,24},{1,5},{5... | collective-permute-start | bytes 294920 | tf_op jit(solution)/shard_map/ppermute | solution.py:322
  4.1 8.2 %collective-permute-start.1 = (bf16[192,256]{1,0:T(8,128)(2,1)S(1)}, bf16[192,256]{1,0:T(8,128)(2,1)S(1)}, u32[]{:S(2)}, u32[]{:S(2)}) collective-permute-start(bf16[192,256]{1,0:T(8,128)(2,1)S(1)} %get-tuple-element.29), channel_id=1, source_target_pairs={{0,1},{1,0},{2,3},{3,2},{4,8},{5,9},{6,10},{7,11},{8,4},{9,5},{10,... | collective-permute-start | bytes 294920 | tf_op jit(solution)/shard_map/ppermute | solution.py:341
  5.9 8.6 %collective-permute-start.3 = (bf16[128,256]{1,0:T(8,128)(2,1)S(1)}, bf16[128,256]{1,0:T(8,128)(2,1)S(1)}, u32[]{:S(2)}, u32[]{:S(2)}) collective-permute-start(bf16[128,256]{1,0:T(8,128)(2,1)S(1)} %get-tuple-element.34), channel_id=1, source_target_pairs={{0,8},{4,12},{8,16},{12,20},{16,24},{20,28},{24,0},{28,4},{1,9},{5... | collective-permute-start | bytes 196616 | tf_op jit(solution)/shard_map/ppermute | solution.py:364
  8.4 6.2 %collective-permute-start.4 = (bf16[64,256]{1,0:T(8,128)(2,1)S(1)}, bf16[64,256]{1,0:T(8,128)(2,1)S(1)}, u32[]{:S(2)}, u32[]{:S(2)}) collective-permute-start(bf16[64,256]{1,0:T(8,128)(2,1)S(1)} %get-tuple-element.35), channel_id=1, source_target_pairs={{0,16},{4,20},{8,24},{12,28},{16,0},{20,4},{24,8},{28,12},{1,17},{... | collective-permute-start | bytes 98312 | tf_op jit(solution)/shard_map/ppermute | solution.py:322
  11.0 4.3 %collective-permute-start.5 = (bf16[128,256]{1,0:T(8,128)(2,1)S(1)}, bf16[128,256]{1,0:T(8,128)(2,1)S(1)}, u32[]{:S(2)}, u32[]{:S(2)}) collective-permute-start(bf16[128,256]{1,0:T(8,128)(2,1)S(1)} %get-tuple-element.39), channel_id=1, source_target_pairs={{8,0},{12,4},{16,8},{20,12},{24,16},{28,20},{0,24},{4,28},{9,1},{1... | collective-permute-start | bytes 196616 | tf_op jit(solution)/shard_map/ppermute | solution.py:365
  15.9 3.8 %collective-permute-start.7 = (bf16[80,128]{1,0:T(8,128)(2,1)S(1)}, bf16[80,128]{1,0:T(8,128)(2,1)S(1)}, u32[]{:S(2)}, u32[]{:S(2)}) collective-permute-start(bf16[80,128]{1,0:T(8,128)(2,1)S(1)} %get-tuple-element.45), channel_id=1, source_target_pairs={{0,3},{1,2},{2,1},{3,0},{4,7},{5,6},{6,5},{7,4},{8,11},{9,10},{10,... | collective-permute-start | bytes 61448 | tf_op jit(solution)/shard_map/ppermute | solution.py:322
  16.0 3.8 %collective-permute-start.8 = (bf16[80,128]{1,0:T(8,128)(2,1)S(1)}, bf16[80,128]{1,0:T(8,128)(2,1)S(1)}, u32[]{:S(2)}, u32[]{:S(2)}) collective-permute-start(bf16[80,128]{1,0:T(8,128)(2,1)S(1)} %get-tuple-element.46), channel_id=1, source_target_pairs={{0,2},{1,3},{2,0},{3,1},{4,6},{5,7},{6,4},{7,5},{8,10},{9,11},{10,... | collective-permute-start | bytes 61448 | tf_op jit(solution)/shard_map/ppermute | solution.py:322
  17.6 1.9 %copy-start = (bf16[512,512]{1,0:T(8,128)(2,1)S(1)}, bf16[512,512]{1,0:T(8,128)(2,1)}, u32[]{:S(2)}) copy-start(bf16[512,512]{1,0:T(8,128)(2,1)} %weight.3) | copy-start | bytes 1572868
  18.3 1.2 %collective-permute-start.6 = (bf16[64,128]{1,0:T(8,128)(2,1)S(1)}, bf16[64,128]{1,0:T(8,128)(2,1)S(1)}, u32[]{:S(2)}, u32[]{:S(2)}) collective-permute-start(bf16[64,128]{1,0:T(8,128)(2,1)S(1)} %get-tuple-element.44), channel_id=1, source_target_pairs={{0,1},{1,0},{2,3},{3,2},{4,5},{5,4},{6,7},{7,6},{8,9},{9,8},{10,11... | collective-permute-start | bytes 49160 | tf_op jit(solution)/shard_map/ppermute | solution.py:322

commit v23 on v19

--- a/solution.py
+++ b/solution.py
@@ -370,7 +370,7 @@
         def over_pairs(array, targets):
             return to_spans(array, [2 * t + x for t in targets for x in range(2)])
 
-        early = (over_pairs(opening, (1, 3, 2, 0)), over_pairs(eighth, (2, 1, 0, 3)))
+        early = (over_pairs(opening, (1, 3, 2, 0)), over_pairs(eighth, (2, 3, 0, 1)))
         late = early + (over_pairs(downward, (3, 0, 1, 2)), over_pairs(closing, (0, 2, 3, 1)))
     else:
         early = ()

time: 21.1 us -> 21.5 us (1.019)
  starting transfers between devices: 9.84 us -> 12.5 us
  waiting for transfers between devices: 7.26 us -> 5.01 us
    ppermute x5, starting transfers between devices: 4.76 us -> 7.38 us  [to_spans(): lax.ppermute(array, ('seq', 'head'), [(s * head_size + h, t * head_size +...]
    ppermute x5, waiting for transfers between devices: 3.48 us -> 1.3 us  [to_spans(): lax.ppermute(array, ('seq', 'head'), [(s * head_size + h, t * head_size +...]
  transfers between devices with their start and end apart: 10 -> 10, of which waited for: 5 -> 5; matrix products, arithmetic and copies ran while one was open for 0% -> 0% of each run, Pallas kernels for 7% -> 6%
where the time goes in v23:
time: 21.5 us; the launch traced here: 21.3 us
  starting transfers between devices  12.5 us (58%)
  waiting for transfers between devices  5.01 us (23%)
  Pallas kernels  3.8 us (18%)
    ppermute x5, starting transfers between devices, to_spans(): lax.ppermute(array, ('seq', 'head'), [(s * head_size + h, t * head_size +...  7.38 us
    ppermute x5, starting transfers between devices, swap(): lax.ppermute(array, axis, [(i, i ^ bit) for i in range(lax.axis_size(axis...  5.07 us
    ppermute x5, waiting for transfers between devices, swap(): lax.ppermute(array, axis, [(i, i ^ bit) for i in range(lax.axis_size(axis...  3.7 us
    ppermute x5, waiting for transfers between devices, to_spans(): lax.ppermute(array, ('seq', 'head'), [(s * head_size + h, t * head_size +...  1.3 us
    pallas_call x1, Pallas kernels, shards(): kernel_call(functools.partial(pack_kernel, not paired), 'pack', 16, [HBM]...  0.99 us
    pallas_call x1, Pallas kernels, shards(): kernel_call(project_kernel, 'project', 8, [VMEM] * 4, [(share, out_weight...  0.81 us
    pallas_call x1, Pallas kernels, shards(): kernel_call(functools.partial(leaves_kernel, seq_size, paired), 'leaves',...  0.62 us
    pallas_call x1, Pallas kernels, shards(): kernel_call(stays_kernel, 'stays', 16, [VMEM] * 8, [(share, width)] * 2,...  0.59 us
  transfers between devices with their start and end apart: 10, of which 5 were waited for; matrix products, arithmetic and copies ran while one was open for 0% of the time, Pallas kernels for 6%

profile of v23, /device:TPU:0, one launch (start us, length us, event | category | flops | bytes accessed | tf_op | source)
XLA Modules:
  0.0 21.3 jit_solution(10596207005864966597)
XLA Ops:
  0.0 1.0 %pack.1 = (bf16[256,128]{1,0:T(8,128)(2,1)S(1)}, bf16[256,256]{1,0:T(8,128)(2,1)S(1)}, bf16[192,256]{1,0:T(8,128)(2,1)S(1)}, bf16[192,256]{1,0:T(8,128)(2,1)S(1)}, bf16[64,256]{1,0:T(8,128)(2,1)S(1)}) custom-call(bf16[256,128]{1,0:T(8,128)(2,1)} %queries.1, bf16[256,128]{1,0:T(8,128)(2,1)} %keys.1, bf16[256,128]{1,0:T(8,128)(2,1)} %values.1), custom_call_target="tpu_custom_call" | custom-call | bytes 1048576 | tf_op jit(solution)/shard_map/pack/pallas_call | solution.py:330
  1.0 3.0 %collective-permute-start.2 = (bf16[64,256]{1,0:T(8,128)(2,1)S(1)}, bf16[64,256]{1,0:T(8,128)(2,1)S(1)}, u32[]{:S(2)}, u32[]{:S(2)}) collective-permute-start(bf16[64,256]{1,0:T(8,128)(2,1)S(1)} %get-tuple-element.33.quarter), channel_id=1, source_target_pairs={{0,4},{4,0},{8,12},{12,8},{16,20},{20,16},{24,28},{28,24},{1,5},{5... | collective-permute-start | bytes 98312 | tf_op jit(solution)/shard_map/ppermute | solution.py:328
  4.0 0.1 collective-permute-start
  4.1 0.0 collective-permute-start.1
  4.1 1.8 %collective-permute-done.2.theirs = bf16[64,256]{1,0:T(8,128)(2,1)S(1)} collective-permute-done((bf16[64,256]{1,0:T(8,128)(2,1)S(1)}, bf16[64,256]{1,0:T(8,128)(2,1)S(1)}, u32[]{:S(2)}, u32[]{:S(2)}) %collective-permute-start.2) | collective-permute-done | bytes 32800 | tf_op jit(solution)/shard_map/ppermute | solution.py:328
  5.9 2.4 %collective-permute-start.3 = (bf16[128,256]{1,0:T(8,128)(2,1)S(1)}, bf16[128,256]{1,0:T(8,128)(2,1)S(1)}, u32[]{:S(2)}, u32[]{:S(2)}) collective-permute-start(bf16[128,256]{1,0:T(8,128)(2,1)S(1)} %get-tuple-element.34), channel_id=1, source_target_pairs={{0,8},{1,9},{2,10},{3,11},{4,12},{5,13},{6,14},{7,15},{8,24},{9,25... | collective-permute-start | bytes 196616 | tf_op jit(solution)/shard_map/ppermute | solution.py:347
  8.4 1.1 %collective-permute-start.4 = (bf16[64,256]{1,0:T(8,128)(2,1)S(1)}, bf16[64,256]{1,0:T(8,128)(2,1)S(1)}, u32[]{:S(2)}, u32[]{:S(2)}) collective-permute-start(bf16[64,256]{1,0:T(8,128)(2,1)S(1)} %get-tuple-element.35), channel_id=1, source_target_pairs={{0,16},{1,17},{2,18},{3,19},{4,20},{5,21},{6,22},{7,23},{8,24},{9,... | collective-permute-start | bytes 98312 | tf_op jit(solution)/shard_map/ppermute | solution.py:347
  9.5 3.9 %collective-permute-start.5 = (bf16[128,256]{1,0:T(8,128)(2,1)S(1)}, bf16[128,256]{1,0:T(8,128)(2,1)S(1)}, u32[]{:S(2)}, u32[]{:S(2)}) collective-permute-start(bf16[128,256]{1,0:T(8,128)(2,1)S(1)} %get-tuple-element.38), channel_id=1, source_target_pairs={{0,24},{1,25},{2,26},{3,27},{4,28},{5,29},{6,30},{7,31},{8,0},{9,1... | collective-permute-start | bytes 196616 | tf_op jit(solution)/shard_map/ppermute | solution.py:347
  13.3 0.0 collective-permute-done.inner
  13.3 0.0 collective-permute-start.6
  13.3 0.0 collective-permute-done.1.outer
  13.3 0.4 %near.1 = (f32[2,256,512]{2,1,0:T(8,128)S(1)}, bf16[2,512,128]{2,1,0:T(8,128)(2,1)S(1)}, bf16[64,256]{1,0:T(8,128)(2,1)S(1)}) custom-call(bf16[256,128]{1,0:T(8,128)(2,1)S(1)} %get-tuple-element.26.queries, bf16[256,256]{1,0:T(8,128)(2,1)S(1)} %get-tuple-element.27.own, bf16[192,256]{1,0:T(8,128)(2,1)S(1)} %collective-permute-done.inner, ...), custom_call_target="tpu_custom_call" | custom-call | flops 67108864 | bytes 1048576 | tf_op jit(solution)/shard_map/near/pallas_call | solution.py:379
  13.7 0.4 %collective-permute-done.4.rest_1_ = bf16[64,256]{1,0:T(8,128)(2,1)S(1)} collective-permute-done((bf16[64,256]{1,0:T(8,128)(2,1)S(1)}, bf16[64,256]{1,0:T(8,128)(2,1)S(1)}, u32[]{:S(2)}, u32[]{:S(2)}) %collective-permute-start.4) | collective-permute-done | bytes 32800 | tf_op jit(solution)/shard_map/ppermute | solution.py:347
  14.1 0.0 collective-permute-done.3.rest_0_
  14.1 0.2 mid.1
  14.3 0.9 %collective-permute-done.5.rest_2_ = bf16[128,256]{1,0:T(8,128)(2,1)S(1)} collective-permute-done((bf16[128,256]{1,0:T(8,128)(2,1)S(1)}, bf16[128,256]{1,0:T(8,128)(2,1)S(1)}, u32[]{:S(2)}, u32[]{:S(2)}) %collective-permute-start.5) | collective-permute-done | bytes 65568 | tf_op jit(solution)/shard_map/ppermute | solution.py:347
  15.2 0.0 collective-permute-done.6.rest_3_
  15.2 0.6 %leaves.1 = (bf16[80,128]{1,0:T(8,128)(2,1)S(1)}, bf16[80,128]{1,0:T(8,128)(2,1)S(1)}, bf16[256,128]{1,0:T(8,128)(2,1)S(1)}, bf16[256,128]{1,0:T(8,128)(2,1)S(1)}, f32[8,256]{1,0:T(8,128)S(1)}) custom-call(bf16[256,128]{1,0:T(8,128)(2,1)S(1)} %get-tuple-element.26.queries, f32[2,256,512]{2,1,0:T(8,128)S(1)} %get-tuple-element.30.near_scores, ...), custom_call_target="tpu_custom_call" | custom-call | flops 117440512 | bytes 1048576 | tf_op jit(solution)/shard_map/leaves/pallas_call | solution.py:405
  15.9 0.7 %collective-permute-start.8 = (bf16[80,128]{1,0:T(8,128)(2,1)S(1)}, bf16[80,128]{1,0:T(8,128)(2,1)S(1)}, u32[]{:S(2)}, u32[]{:S(2)}) collective-permute-start(bf16[80,128]{1,0:T(8,128)(2,1)S(1)} %get-tuple-element.45), channel_id=1, source_target_pairs={{0,3},{1,2},{2,1},{3,0},{4,7},{5,6},{6,5},{7,4},{8,11},{9,10},{10,... | collective-permute-start | bytes 61448 | tf_op jit(solution)/shard_map/ppermute | solution.py:328
  16.6 1.0 %collective-permute-start.9 = (bf16[80,128]{1,0:T(8,128)(2,1)S(1)}, bf16[80,128]{1,0:T(8,128)(2,1)S(1)}, u32[]{:S(2)}, u32[]{:S(2)}) collective-permute-start(bf16[80,128]{1,0:T(8,128)(2,1)S(1)} %get-tuple-element.46), channel_id=1, source_target_pairs={{0,2},{1,3},{2,0},{3,1},{4,6},{5,7},{6,4},{7,5},{8,10},{9,11},{10,... | collective-permute-start | bytes 61448 | tf_op jit(solution)/shard_map/ppermute | solution.py:328
  17.5 0.0 copy-start
  17.5 0.6 %stays.1 = (bf16[64,128]{1,0:T(8,128)(2,1)S(1)}, bf16[64,128]{1,0:T(8,128)(2,1)S(1)}) custom-call(bf16[256,128]{1,0:T(8,128)(2,1)S(1)} %get-tuple-element.26.queries, f32[2,256,512]{2,1,0:T(8,128)S(1)} %get-tuple-element.30.near_scores, bf16[2,512,128]{2,1,0:T(8,128)(2,1)S(1)} %get-tuple-element.31.near_values, ...), custom_call_target="tpu_custom_call" | custom-call | flops 117440512 | bytes 1048576 | tf_op jit(solution)/shard_map/stays/pallas_call | solution.py:420
  18.1 0.3 %collective-permute-start.7 = (bf16[64,128]{1,0:T(8,128)(2,1)S(1)}, bf16[64,128]{1,0:T(8,128)(2,1)S(1)}, u32[]{:S(2)}, u32[]{:S(2)}) collective-permute-start(bf16[64,128]{1,0:T(8,128)(2,1)S(1)} %get-tuple-element.44), channel_id=1, source_target_pairs={{0,1},{1,0},{2,3},{3,2},{4,5},{5,4},{6,7},{7,6},{8,9},{9,8},{10,11... | collective-permute-start | bytes 49160 | tf_op jit(solution)/shard_map/ppermute | solution.py:328
  18.4 0.9 %collective-permute-done.7.other = bf16[64,128]{1,0:T(8,128)(2,1)S(1)} collective-permute-done((bf16[64,128]{1,0:T(8,128)(2,1)S(1)}, bf16[64,128]{1,0:T(8,128)(2,1)S(1)}, u32[]{:S(2)}, u32[]{:S(2)}) %collective-permute-start.7) | collective-permute-done | bytes 16416 | tf_op jit(solution)/shard_map/ppermute | solution.py:328
  19.4 0.0 copy-done
  19.4 0.2 begin.1.partial
  19.5 0.0 collective-permute-done.8.other
  19.6 1.0 %collective-permute-done.9.same = bf16[80,128]{1,0:T(8,128)(2,1)S(1)} collective-permute-done((bf16[80,128]{1,0:T(8,128)(2,1)S(1)}, bf16[80,128]{1,0:T(8,128)(2,1)S(1)}, u32[]{:S(2)}, u32[]{:S(2)}) %collective-permute-start.9) | collective-permute-done | bytes 20512 | tf_op jit(solution)/shard_map/ppermute | solution.py:328
  20.5 0.8 %project.1 = bf16[64,512]{1,0:T(8,128)(2,1)} custom-call(f32[64,512]{1,0:T(8,128)S(1)} %begin.1.partial, bf16[80,128]{1,0:T(8,128)(2,1)S(1)} %collective-permute-done.8.other, bf16[80,128]{1,0:T(8,128)(2,1)S(1)} %collective-permute-done.9.same, bf16[512,512]{1,0:T(8,128)(2,1)S(1)} %copy-done), custom_call_target="tpu_custom_call" | custom-call | bytes 1048576 | tf_op jit(solution)/shard_map/project/pallas_call | solution.py:433
  (1 shorter events, 0.0 us)
Async XLA Ops:
  1.0 4.9 %collective-permute-start.2 = (bf16[64,256]{1,0:T(8,128)(2,1)S(1)}, bf16[64,256]{1,0:T(8,128)(2,1)S(1)}, u32[]{:S(2)}, u32[]{:S(2)}) collective-permute-start(bf16[64,256]{1,0:T(8,128)(2,1)S(1)} %get-tuple-element.33.quarter), channel_id=1, source_target_pairs={{0,4},{4,0},{8,12},{12,8},{16,20},{20,16},{24,28},{28,24},{1,5},{5... | collective-permute-start | bytes 98312 | tf_op jit(solution)/shard_map/ppermute | solution.py:328
  4.0 9.3 %collective-permute-start = (bf16[192,256]{1,0:T(8,128)(2,1)S(1)}, bf16[192,256]{1,0:T(8,128)(2,1)S(1)}, u32[]{:S(2)}, u32[]{:S(2)}) collective-permute-start(bf16[192,256]{1,0:T(8,128)(2,1)S(1)} %get-tuple-element.28), channel_id=1, source_target_pairs={{0,4},{4,0},{8,12},{12,8},{16,20},{20,16},{24,28},{28,24},{1,5},{5... | collective-permute-start | bytes 294920 | tf_op jit(solution)/shard_map/ppermute | solution.py:328
  4.1 9.2 %collective-permute-start.1 = (bf16[192,256]{1,0:T(8,128)(2,1)S(1)}, bf16[192,256]{1,0:T(8,128)(2,1)S(1)}, u32[]{:S(2)}, u32[]{:S(2)}) collective-permute-start(bf16[192,256]{1,0:T(8,128)(2,1)S(1)} %get-tuple-element.29), channel_id=1, source_target_pairs={{0,1},{1,0},{2,3},{3,2},{4,8},{5,9},{6,10},{7,11},{8,4},{9,5},{10,... | collective-permute-start | bytes 294920 | tf_op jit(solution)/shard_map/ppermute | solution.py:347
  5.9 8.2 %collective-permute-start.3 = (bf16[128,256]{1,0:T(8,128)(2,1)S(1)}, bf16[128,256]{1,0:T(8,128)(2,1)S(1)}, u32[]{:S(2)}, u32[]{:S(2)}) collective-permute-start(bf16[128,256]{1,0:T(8,128)(2,1)S(1)} %get-tuple-element.34), channel_id=1, source_target_pairs={{0,8},{1,9},{2,10},{3,11},{4,12},{5,13},{6,14},{7,15},{8,24},{9,25... | collective-permute-start | bytes 196616 | tf_op jit(solution)/shard_map/ppermute | solution.py:347
  8.4 5.8 %collective-permute-start.4 = (bf16[64,256]{1,0:T(8,128)(2,1)S(1)}, bf16[64,256]{1,0:T(8,128)(2,1)S(1)}, u32[]{:S(2)}, u32[]{:S(2)}) collective-permute-start(bf16[64,256]{1,0:T(8,128)(2,1)S(1)} %get-tuple-element.35), channel_id=1, source_target_pairs={{0,16},{1,17},{2,18},{3,19},{4,20},{5,21},{6,22},{7,23},{8,24},{9,... | collective-permute-start | bytes 98312 | tf_op jit(solution)/shard_map/ppermute | solution.py:347
  9.5 5.8 %collective-permute-start.5 = (bf16[128,256]{1,0:T(8,128)(2,1)S(1)}, bf16[128,256]{1,0:T(8,128)(2,1)S(1)}, u32[]{:S(2)}, u32[]{:S(2)}) collective-permute-start(bf16[128,256]{1,0:T(8,128)(2,1)S(1)} %get-tuple-element.38), channel_id=1, source_target_pairs={{0,24},{1,25},{2,26},{3,27},{4,28},{5,29},{6,30},{7,31},{8,0},{9,1... | collective-permute-start | bytes 196616 | tf_op jit(solution)/shard_map/ppermute | solution.py:347
  13.3 1.9 %collective-permute-start.6 = (bf16[128,256]{1,0:T(8,128)(2,1)S(1)}, bf16[128,256]{1,0:T(8,128)(2,1)S(1)}, u32[]{:S(2)}, u32[]{:S(2)}) collective-permute-start(bf16[128,256]{1,0:T(8,128)(2,1)S(1)} %get-tuple-element.39), channel_id=1, source_target_pairs={{0,1},{1,0},{2,3},{3,2},{4,5},{5,4},{6,7},{7,6},{8,16},{9,17},{10,... | collective-permute-start | bytes 196616 | tf_op jit(solution)/shard_map/ppermute | solution.py:347
  15.9 3.7 %collective-permute-start.8 = (bf16[80,128]{1,0:T(8,128)(2,1)S(1)}, bf16[80,128]{1,0:T(8,128)(2,1)S(1)}, u32[]{:S(2)}, u32[]{:S(2)}) collective-permute-start(bf16[80,128]{1,0:T(8,128)(2,1)S(1)} %get-tuple-element.45), channel_id=1, source_target_pairs={{0,3},{1,2},{2,1},{3,0},{4,7},{5,6},{6,5},{7,4},{8,11},{9,10},{10,... | collective-permute-start | bytes 61448 | tf_op jit(solution)/shard_map/ppermute | solution.py:328
  16.6 4.0 %collective-permute-start.9 = (bf16[80,128]{1,0:T(8,128)(2,1)S(1)}, bf16[80,128]{1,0:T(8,128)(2,1)S(1)}, u32[]{:S(2)}, u32[]{:S(2)}) collective-permute-start(bf16[80,128]{1,0:T(8,128)(2,1)S(1)} %get-tuple-element.46), channel_id=1, source_target_pairs={{0,2},{1,3},{2,0},{3,1},{4,6},{5,7},{6,4},{7,5},{8,10},{9,11},{10,... | collective-permute-start | bytes 61448 | tf_op jit(solution)/shard_map/ppermute | solution.py:328
  17.5 1.8 %copy-start = (bf16[512,512]{1,0:T(8,128)(2,1)S(1)}, bf16[512,512]{1,0:T(8,128)(2,1)}, u32[]{:S(2)}) copy-start(bf16[512,512]{1,0:T(8,128)(2,1)} %weight.3) | copy-start | bytes 1572868
  18.1 1.2 %collective-permute-start.7 = (bf16[64,128]{1,0:T(8,128)(2,1)S(1)}, bf16[64,128]{1,0:T(8,128)(2,1)S(1)}, u32[]{:S(2)}, u32[]{:S(2)}) collective-permute-start(bf16[64,128]{1,0:T(8,128)(2,1)S(1)} %get-tuple-element.44), channel_id=1, source_target_pairs={{0,1},{1,0},{2,3},{3,2},{4,5},{5,4},{6,7},{7,6},{8,9},{9,8},{10,11... | collective-permute-start | bytes 49160 | tf_op jit(solution)/shard_map/ppermute | solution.py:328

commit v24 on v21

--- a/solution.py
+++ b/solution.py
@@ -169,7 +169,7 @@
     )
 
 
-def near_kernel(seq_size, queries, own, inner, outer, scores, values, shared, keys, wide):
+def near_kernel(seq_size, queries, own, outer, inner, scores, values, shared, keys, wide):
     me = lax.axis_index("seq")
     odd = me & 1
     from_inner, from_outer = inner[...], outer[...]
@@ -378,7 +378,7 @@
         ],
         [pltpu.VMEM((NEAR_ROWS, width), jnp.bfloat16), wide],
         flops=8 * LEAF * NEAR_ROWS * width,
-    )(own_queries, own, inner, outer)
+    )(own_queries, own, outer, inner)
     mid_rows = 4 * HALF if paired else HALF
     mid_scores, mid_values = kernel_call(
         mid_kernel,

time: 20.7 us -> 20.5 us (level)
  waiting for transfers between devices: 5.32 us -> 3.43 us
  starting transfers between devices: 11.4 us -> 13.1 us
    ppermute x6, starting transfers between devices: 7.65 us -> 10.1 us  [swap(): lax.ppermute(array, axis, [(i, i ^ bit) for i in range(lax.axis_size(axis...]
    ppermute x6, waiting for transfers between devices: 4.86 us -> 2.64 us  [swap(): lax.ppermute(array, axis, [(i, i ^ bit) for i in range(lax.axis_size(axis...]
    ppermute x1, starting transfers between devices: 2.43 us -> 1.18 us  [shards(): early = (lax.ppermute(upward, 'seq', shift), swap(eighth, 4))]
    ppermute x1, starting transfers between devices: 1.35 us -> 1.84 us  [shards(): lax.ppermute(downward, 'seq', [(target, source) for source, target in shi...]
    ppermute x1, waiting for transfers between devices: 0.45 us -> 0.79 us  [shards(): lax.ppermute(downward, 'seq', [(target, source) for source, target in shi...]
where the time goes in v24:
time: 20.5 us; the launch traced here: 20.4 us
  starting transfers between devices  13.1 us (64%)
  Pallas kernels  3.74 us (18%)
  waiting for transfers between devices  3.43 us (17%)
    ppermute x6, starting transfers between devices, swap(): lax.ppermute(array, axis, [(i, i ^ bit) for i in range(lax.axis_size(axis...  10.1 us
    ppermute x6, waiting for transfers between devices, swap(): lax.ppermute(array, axis, [(i, i ^ bit) for i in range(lax.axis_size(axis...  2.64 us
    ppermute x1, starting transfers between devices, shards(): lax.ppermute(downward, 'seq', [(target, source) for source, target in shi...  1.84 us
    ppermute x1, starting transfers between devices, shards(): early = (lax.ppermute(upward, 'seq', shift), swap(eighth, 4))  1.18 us
    pallas_call x1, Pallas kernels, shards(): kernel_call(functools.partial(pack_kernel, not paired), 'pack', 16, [HBM]...  0.99 us
    pallas_call x1, Pallas kernels, shards(): kernel_call(project_kernel, 'project', 8, [VMEM] * 4, [(share, out_weight...  0.81 us
    ppermute x1, waiting for transfers between devices, shards(): lax.ppermute(downward, 'seq', [(target, source) for source, target in shi...  0.79 us
    pallas_call x1, Pallas kernels, shards(): kernel_call(functools.partial(leaves_kernel, seq_size, paired), 'leaves',...  0.56 us
  transfers between devices with their start and end apart: 9, of which 5 were waited for; matrix products, arithmetic and copies ran while one was open for 0% of the time, Pallas kernels for 7%

profile of v24, /device:TPU:0, one launch (start us, length us, event | category | flops | bytes accessed | tf_op | source)
XLA Modules:
  0.0 20.4 jit_solution(16790004774356675614)
XLA Ops:
  0.0 1.0 %pack.1 = (bf16[256,128]{1,0:T(8,128)(2,1)S(1)}, bf16[256,256]{1,0:T(8,128)(2,1)S(1)}, bf16[192,256]{1,0:T(8,128)(2,1)S(1)}, bf16[192,256]{1,0:T(8,128)(2,1)S(1)}, bf16[64,256]{1,0:T(8,128)(2,1)S(1)}) custom-call(bf16[256,128]{1,0:T(8,128)(2,1)} %queries.1, bf16[256,128]{1,0:T(8,128)(2,1)} %keys.1, bf16[256,128]{1,0:T(8,128)(2,1)} %values.1), custom_call_target="tpu_custom_call" | custom-call | bytes 1048576 | tf_op jit(solution)/shard_map/pack/pallas_call | solution.py:323
  1.0 3.0 %collective-permute-start.2 = (bf16[64,256]{1,0:T(8,128)(2,1)S(1)}, bf16[64,256]{1,0:T(8,128)(2,1)S(1)}, u32[]{:S(2)}, u32[]{:S(2)}) collective-permute-start(bf16[64,256]{1,0:T(8,128)(2,1)S(1)} %get-tuple-element.32.quarter), channel_id=1, source_target_pairs={{0,4},{4,0},{8,12},{12,8},{16,20},{20,16},{24,28},{28,24},{1,5},{5... | collective-permute-start | bytes 98312 | tf_op jit(solution)/shard_map/ppermute | solution.py:321
  4.0 0.0 collective-permute-start
  4.0 3.0 %collective-permute-start.1 = (bf16[192,256]{1,0:T(8,128)(2,1)S(1)}, bf16[192,256]{1,0:T(8,128)(2,1)S(1)}, u32[]{:S(2)}, u32[]{:S(2)}) collective-permute-start(bf16[192,256]{1,0:T(8,128)(2,1)S(1)} %get-tuple-element.28), channel_id=1, source_target_pairs={{0,4},{4,0},{8,12},{12,8},{16,20},{20,16},{24,28},{28,24},{1,5},{5... | collective-permute-start | bytes 294920 | tf_op jit(solution)/shard_map/ppermute | solution.py:321
  7.0 0.5 %collective-permute-done.2.theirs = bf16[64,256]{1,0:T(8,128)(2,1)S(1)} collective-permute-done((bf16[64,256]{1,0:T(8,128)(2,1)S(1)}, bf16[64,256]{1,0:T(8,128)(2,1)S(1)}, u32[]{:S(2)}, u32[]{:S(2)}) %collective-permute-start.2) | collective-permute-done | bytes 32800 | tf_op jit(solution)/shard_map/ppermute | solution.py:321
  7.5 1.2 %collective-permute-start.3 = (bf16[128,256]{1,0:T(8,128)(2,1)S(1)}, bf16[128,256]{1,0:T(8,128)(2,1)S(1)}, u32[]{:S(2)}, u32[]{:S(2)}) collective-permute-start(bf16[128,256]{1,0:T(8,128)(2,1)S(1)} %get-tuple-element.33), channel_id=1, source_target_pairs={{0,8},{4,12},{8,16},{12,20},{16,24},{20,28},{24,0},{28,4},{1,9},{5... | collective-permute-start | bytes 196616 | tf_op jit(solution)/shard_map/ppermute | solution.py:363
  8.7 2.1 %collective-permute-start.4 = (bf16[64,256]{1,0:T(8,128)(2,1)S(1)}, bf16[64,256]{1,0:T(8,128)(2,1)S(1)}, u32[]{:S(2)}, u32[]{:S(2)}) collective-permute-start(bf16[64,256]{1,0:T(8,128)(2,1)S(1)} %get-tuple-element.34), channel_id=1, source_target_pairs={{0,16},{4,20},{8,24},{12,28},{16,0},{20,4},{24,8},{28,12},{1,17},{... | collective-permute-start | bytes 98312 | tf_op jit(solution)/shard_map/ppermute | solution.py:321
  10.8 1.8 %collective-permute-start.5 = (bf16[128,256]{1,0:T(8,128)(2,1)S(1)}, bf16[128,256]{1,0:T(8,128)(2,1)S(1)}, u32[]{:S(2)}, u32[]{:S(2)}) collective-permute-start(bf16[128,256]{1,0:T(8,128)(2,1)S(1)} %get-tuple-element.37), channel_id=1, source_target_pairs={{8,0},{12,4},{16,8},{20,12},{24,16},{28,20},{0,24},{4,28},{9,1},{1... | collective-permute-start | bytes 196616 | tf_op jit(solution)/shard_map/ppermute | solution.py:364
  12.7 0.0 collective-permute-done.outer
  12.7 0.0 collective-permute-done.1.inner
  12.7 0.4 %near.1 = (f32[2,256,512]{2,1,0:T(8,128)S(1)}, bf16[2,512,128]{2,1,0:T(8,128)(2,1)S(1)}, bf16[64,256]{1,0:T(8,128)(2,1)S(1)}) custom-call(bf16[256,128]{1,0:T(8,128)(2,1)S(1)} %get-tuple-element.25.queries, bf16[256,256]{1,0:T(8,128)(2,1)S(1)} %get-tuple-element.26.own, bf16[192,256]{1,0:T(8,128)(2,1)S(1)} %collective-permute-done.outer, ...), custom_call_target="tpu_custom_call" | custom-call | flops 67108864 | bytes 1048576 | tf_op jit(solution)/shard_map/near/pallas_call | solution.py:369
  13.1 1.0 %collective-permute-done.4.rest_1_ = bf16[64,256]{1,0:T(8,128)(2,1)S(1)} collective-permute-done((bf16[64,256]{1,0:T(8,128)(2,1)S(1)}, bf16[64,256]{1,0:T(8,128)(2,1)S(1)}, u32[]{:S(2)}, u32[]{:S(2)}) %collective-permute-start.4) | collective-permute-done | bytes 32800 | tf_op jit(solution)/shard_map/ppermute | solution.py:321
  14.0 0.0 collective-permute-done.3.rest_0_
  14.1 0.2 %mid.1 = (f32[2,256,256]{2,1,0:T(8,128)S(1)}, bf16[256,128]{1,0:T(8,128)(2,1)S(1)}) custom-call(bf16[256,128]{1,0:T(8,128)(2,1)S(1)} %get-tuple-element.25.queries, bf16[64,256]{1,0:T(8,128)(2,1)S(1)} %get-tuple-element.31.shared, bf16[128,256]{1,0:T(8,128)(2,1)S(1)} %collective-permute-done.3.rest_0_, bf16[64,256]{1,0:T(8,128)(2,1)S(1)} %collective-permute-done.4.rest_1_), custom_call_target="tpu_custom_call" | custom-call | flops 1000000000 | bytes 1048576 | tf_op jit(solution)/shard_map/mid/pallas_call | solution.py:383
  14.3 0.8 %collective-permute-done.5.rest_0_ = bf16[128,256]{1,0:T(8,128)(2,1)S(1)} collective-permute-done((bf16[128,256]{1,0:T(8,128)(2,1)S(1)}, bf16[128,256]{1,0:T(8,128)(2,1)S(1)}, u32[]{:S(2)}, u32[]{:S(2)}) %collective-permute-start.5) | collective-permute-done | bytes 65568 | tf_op jit(solution)/shard_map/ppermute | solution.py:364
  15.1 0.6 %leaves.1 = (bf16[80,128]{1,0:T(8,128)(2,1)S(1)}, bf16[80,128]{1,0:T(8,128)(2,1)S(1)}, bf16[128,128]{1,0:T(8,128)(2,1)S(1)}, bf16[128,128]{1,0:T(8,128)(2,1)S(1)}, f32[8,128]{1,0:T(8,128)S(1)}) custom-call(bf16[256,128]{1,0:T(8,128)(2,1)S(1)} %get-tuple-element.25.queries, f32[2,256,512]{2,1,0:T(8,128)S(1)} %get-tuple-element.29.near_scores, ...), custom_call_target="tpu_custom_call" | custom-call | flops 117440512 | bytes 1048576 | tf_op jit(solution)/shard_map/leaves/pallas_call | solution.py:395
  15.7 0.1 collective-permute-start.7
  15.7 1.6 %collective-permute-start.8 = (bf16[80,128]{1,0:T(8,128)(2,1)S(1)}, bf16[80,128]{1,0:T(8,128)(2,1)S(1)}, u32[]{:S(2)}, u32[]{:S(2)}) collective-permute-start(bf16[80,128]{1,0:T(8,128)(2,1)S(1)} %get-tuple-element.44), channel_id=1, source_target_pairs={{0,2},{1,3},{2,0},{3,1},{4,6},{5,7},{6,4},{7,5},{8,10},{9,11},{10,... | collective-permute-start | bytes 61448 | tf_op jit(solution)/shard_map/ppermute | solution.py:321
  17.3 0.0 copy-start
  17.3 0.6 %stays.1 = (bf16[64,128]{1,0:T(8,128)(2,1)S(1)}, bf16[64,128]{1,0:T(8,128)(2,1)S(1)}) custom-call(bf16[256,128]{1,0:T(8,128)(2,1)S(1)} %get-tuple-element.25.queries, f32[2,256,512]{2,1,0:T(8,128)S(1)} %get-tuple-element.29.near_scores, bf16[2,512,128]{2,1,0:T(8,128)(2,1)S(1)} %get-tuple-element.30.near_values, ...), custom_call_target="tpu_custom_call" | custom-call | flops 117440512 | bytes 1048576 | tf_op jit(solution)/shard_map/stays/pallas_call | solution.py:410
  17.9 0.3 %collective-permute-start.6 = (bf16[64,128]{1,0:T(8,128)(2,1)S(1)}, bf16[64,128]{1,0:T(8,128)(2,1)S(1)}, u32[]{:S(2)}, u32[]{:S(2)}) collective-permute-start(bf16[64,128]{1,0:T(8,128)(2,1)S(1)} %get-tuple-element.42), channel_id=1, source_target_pairs={{0,1},{1,0},{2,3},{3,2},{4,5},{5,4},{6,7},{7,6},{8,9},{9,8},{10,11... | collective-permute-start | bytes 49160 | tf_op jit(solution)/shard_map/ppermute | solution.py:321
  18.2 0.9 %collective-permute-done.6.other = bf16[64,128]{1,0:T(8,128)(2,1)S(1)} collective-permute-done((bf16[64,128]{1,0:T(8,128)(2,1)S(1)}, bf16[64,128]{1,0:T(8,128)(2,1)S(1)}, u32[]{:S(2)}, u32[]{:S(2)}) %collective-permute-start.6) | collective-permute-done | bytes 16416 | tf_op jit(solution)/shard_map/ppermute | solution.py:321
  19.1 0.0 copy-done
  19.1 0.2 begin.1.partial
  19.3 0.0 collective-permute-done.7.other
  19.3 0.3 %collective-permute-done.8.same = bf16[80,128]{1,0:T(8,128)(2,1)S(1)} collective-permute-done((bf16[80,128]{1,0:T(8,128)(2,1)S(1)}, bf16[80,128]{1,0:T(8,128)(2,1)S(1)}, u32[]{:S(2)}, u32[]{:S(2)}) %collective-permute-start.8) | collective-permute-done | bytes 20512 | tf_op jit(solution)/shard_map/ppermute | solution.py:321
  19.6 0.8 %project.1 = bf16[64,512]{1,0:T(8,128)(2,1)} custom-call(f32[64,512]{1,0:T(8,128)S(1)} %begin.1.partial, bf16[80,128]{1,0:T(8,128)(2,1)S(1)} %collective-permute-done.7.other, bf16[80,128]{1,0:T(8,128)(2,1)S(1)} %collective-permute-done.8.same, bf16[512,512]{1,0:T(8,128)(2,1)S(1)} %copy-done), custom_call_target="tpu_custom_call" | custom-call | bytes 1048576 | tf_op jit(solution)/shard_map/project/pallas_call | solution.py:423
  (1 shorter events, 0.0 us)
Async XLA Ops:
  1.0 6.5 %collective-permute-start.2 = (bf16[64,256]{1,0:T(8,128)(2,1)S(1)}, bf16[64,256]{1,0:T(8,128)(2,1)S(1)}, u32[]{:S(2)}, u32[]{:S(2)}) collective-permute-start(bf16[64,256]{1,0:T(8,128)(2,1)S(1)} %get-tuple-element.32.quarter), channel_id=1, source_target_pairs={{0,4},{4,0},{8,12},{12,8},{16,20},{20,16},{24,28},{28,24},{1,5},{5... | collective-permute-start | bytes 98312 | tf_op jit(solution)/shard_map/ppermute | solution.py:321
  4.0 8.7 %collective-permute-start = (bf16[192,256]{1,0:T(8,128)(2,1)S(1)}, bf16[192,256]{1,0:T(8,128)(2,1)S(1)}, u32[]{:S(2)}, u32[]{:S(2)}) collective-permute-start(bf16[192,256]{1,0:T(8,128)(2,1)S(1)} %get-tuple-element.27), channel_id=1, source_target_pairs={{0,1},{1,0},{2,3},{3,2},{4,8},{5,9},{6,10},{7,11},{8,4},{9,5},{10,... | collective-permute-start | bytes 294920 | tf_op jit(solution)/shard_map/ppermute | solution.py:340
  4.0 8.7 %collective-permute-start.1 = (bf16[192,256]{1,0:T(8,128)(2,1)S(1)}, bf16[192,256]{1,0:T(8,128)(2,1)S(1)}, u32[]{:S(2)}, u32[]{:S(2)}) collective-permute-start(bf16[192,256]{1,0:T(8,128)(2,1)S(1)} %get-tuple-element.28), channel_id=1, source_target_pairs={{0,4},{4,0},{8,12},{12,8},{16,20},{20,16},{24,28},{28,24},{1,5},{5... | collective-permute-start | bytes 294920 | tf_op jit(solution)/shard_map/ppermute | solution.py:321
  7.5 6.5 %collective-permute-start.3 = (bf16[128,256]{1,0:T(8,128)(2,1)S(1)}, bf16[128,256]{1,0:T(8,128)(2,1)S(1)}, u32[]{:S(2)}, u32[]{:S(2)}) collective-permute-start(bf16[128,256]{1,0:T(8,128)(2,1)S(1)} %get-tuple-element.33), channel_id=1, source_target_pairs={{0,8},{4,12},{8,16},{12,20},{16,24},{20,28},{24,0},{28,4},{1,9},{5... | collective-permute-start | bytes 196616 | tf_op jit(solution)/shard_map/ppermute | solution.py:363
  8.7 5.3 %collective-permute-start.4 = (bf16[64,256]{1,0:T(8,128)(2,1)S(1)}, bf16[64,256]{1,0:T(8,128)(2,1)S(1)}, u32[]{:S(2)}, u32[]{:S(2)}) collective-permute-start(bf16[64,256]{1,0:T(8,128)(2,1)S(1)} %get-tuple-element.34), channel_id=1, source_target_pairs={{0,16},{4,20},{8,24},{12,28},{16,0},{20,4},{24,8},{28,12},{1,17},{... | collective-permute-start | bytes 98312 | tf_op jit(solution)/shard_map/ppermute | solution.py:321
  10.8 4.3 %collective-permute-start.5 = (bf16[128,256]{1,0:T(8,128)(2,1)S(1)}, bf16[128,256]{1,0:T(8,128)(2,1)S(1)}, u32[]{:S(2)}, u32[]{:S(2)}) collective-permute-start(bf16[128,256]{1,0:T(8,128)(2,1)S(1)} %get-tuple-element.37), channel_id=1, source_target_pairs={{8,0},{12,4},{16,8},{20,12},{24,16},{28,20},{0,24},{4,28},{9,1},{1... | collective-permute-start | bytes 196616 | tf_op jit(solution)/shard_map/ppermute | solution.py:364
  15.7 3.7 %collective-permute-start.7 = (bf16[80,128]{1,0:T(8,128)(2,1)S(1)}, bf16[80,128]{1,0:T(8,128)(2,1)S(1)}, u32[]{:S(2)}, u32[]{:S(2)}) collective-permute-start(bf16[80,128]{1,0:T(8,128)(2,1)S(1)} %get-tuple-element.43), channel_id=1, source_target_pairs={{0,3},{1,2},{2,1},{3,0},{4,7},{5,6},{6,5},{7,4},{8,11},{9,10},{10,... | collective-permute-start | bytes 61448 | tf_op jit(solution)/shard_map/ppermute | solution.py:321
  15.7 3.8 %collective-permute-start.8 = (bf16[80,128]{1,0:T(8,128)(2,1)S(1)}, bf16[80,128]{1,0:T(8,128)(2,1)S(1)}, u32[]{:S(2)}, u32[]{:S(2)}) collective-permute-start(bf16[80,128]{1,0:T(8,128)(2,1)S(1)} %get-tuple-element.44), channel_id=1, source_target_pairs={{0,2},{1,3},{2,0},{3,1},{4,6},{5,7},{6,4},{7,5},{8,10},{9,11},{10,... | collective-permute-start | bytes 61448 | tf_op jit(solution)/shard_map/ppermute | solution.py:321
  17.3 1.8 %copy-start = (bf16[512,512]{1,0:T(8,128)(2,1)S(1)}, bf16[512,512]{1,0:T(8,128)(2,1)}, u32[]{:S(2)}) copy-start(bf16[512,512]{1,0:T(8,128)(2,1)} %weight.3) | copy-start | bytes 1572868
  17.9 1.2 %collective-permute-start.6 = (bf16[64,128]{1,0:T(8,128)(2,1)S(1)}, bf16[64,128]{1,0:T(8,128)(2,1)S(1)}, u32[]{:S(2)}, u32[]{:S(2)}) collective-permute-start(bf16[64,128]{1,0:T(8,128)(2,1)S(1)} %get-tuple-element.42), channel_id=1, source_target_pairs={{0,1},{1,0},{2,3},{3,2},{4,5},{5,4},{6,7},{7,6},{8,9},{9,8},{10,11... | collective-permute-start | bytes 49160 | tf_op jit(solution)/shard_map/ppermute | solution.py:321

commit v25 on v21

--- a/solution.py
+++ b/solution.py
@@ -60,10 +60,8 @@
     first = jnp.where(odd == 1, theirs[...], quarter[...])
     second = jnp.where(odd == 1, quarter[...], theirs[...])
     level_three = average_pairs(jnp.concatenate([first, second], axis=0), wide)
-    upward[:HALF] = jnp.where(me >= 6, level_three, first)
-    upward[HALF:] = second
-    downward[:HALF] = jnp.where(me < 2, level_three, first)
-    downward[HALF:] = second
+    upward[...] = jnp.where(me >= 6, level_three, first)
+    downward[...] = jnp.where(me < 2, level_three, second)
     eighth[...] = level_three
 
 
@@ -73,7 +71,7 @@
 
 def last_row_count(seq_size, paired):
     if paired:
-        return LEAF
+        return HALF
     rows = 0
     for far in range(1, seq_size.bit_length() - 1):
         if seq_size >> far == 2:
@@ -127,16 +125,10 @@
     return pieces
 
 
-def early_pieces(lower, eighth):
+def early_pieces(beside, lower, eighth):
     me = lax.axis_index("seq")
-    whole = ((me & 1) == 1) & (me >= 2)
-    return [(lower[:HALF], None), (lower[HALF:], bias_of(whole)), (eighth[...], None)]
-
-
-def late_pieces(upper):
-    me = lax.axis_index("seq")
-    whole = ((me & 1) == 0) | (me >= 6)
-    return [(upper[:HALF], bias_of(whole)), (upper[HALF:], bias_of(me < 6))]
+    has_beside = jnp.where((me & 1) == 1, me >= 2, me < 6)
+    return [(beside, bias_of(has_beside)), (lower, None), (eighth, None)]
 
 
 def place(pieces, values, keys):
@@ -241,7 +233,7 @@
 
 def leaves_kernel(seq_size, paired, queries, near_scores, near_values, mid_scores, mid_values, *rest):
     late, same, other, keys, values, bias, wide = rest
-    pieces = late_pieces(late) if paired else gathered_pieces(seq_size, late, wide)
+    pieces = [(late, None)] if paired else gathered_pieces(seq_size, late, wide)
     bias[...] = jnp.broadcast_to(place(pieces, values, keys), bias.shape)
     leaf = (lax.axis_index("head") >> 1) ^ 1
     scored = (near_scores, near_values, mid_scores, mid_values)
@@ -355,12 +347,15 @@
             "join",
             8,
             [VMEM] * 2,
-            [(LEAF, pair_width), (LEAF, pair_width), (HALF, pair_width)],
+            [(HALF, pair_width)] * 3,
             [wide],
-            flops=3 * 10**8,
+            flops=2 * 10**9,
         )(swap(quarter, 1), quarter)
         shift = [(i, (i + 2) % seq_size) for i in range(seq_size)]
-        early = (lax.ppermute(upward, "seq", shift), swap(eighth, 4))
+        cycle = [(i, i + 2 if i & 1 else i - 2) for i in range(1, seq_size - 1)]
+        cycle += [(0, 1), (seq_size - 1, seq_size - 2)]
+        beside = lax.ppermute(quarter, "seq", cycle)
+        early = (beside, lax.ppermute(upward, "seq", shift), swap(eighth, 4))
         late = lax.ppermute(downward, "seq", [(target, source) for source, target in shift])
     else:
         early = ()

time: 20.7 us -> 20.9 us (level)
  starting transfers between devices: 11.4 us -> 14.8 us
  waiting for transfers between devices: 5.32 us -> 2.15 us
    ppermute x6, waiting for transfers between devices: 4.86 us -> 1.22 us  [swap(): lax.ppermute(array, axis, [(i, i ^ bit) for i in range(lax.axis_size(axis...]
    ppermute x6, starting transfers between devices: 7.65 us -> 9.8 us  [swap(): lax.ppermute(array, axis, [(i, i ^ bit) for i in range(lax.axis_size(axis...]
    ppermute x1, starting transfers between devices: 1.35 us -> 2.93 us  [shards(): lax.ppermute(downward, 'seq', [(target, source) for source, target in shi...]
    ppermute x1, waiting for transfers between devices: 0.45 us -> 0.93 us  [shards(): lax.ppermute(downward, 'seq', [(target, source) for source, target in shi...]
    ppermute x1 -> x2, starting transfers between devices: 2.43 us -> 2.1 us  [the longest x1 2.04 us: shards(): early = (beside, lax.ppermute(upward, 'seq', shift), swap(eighth, 4))]
  transfers between devices with their start and end apart: 9 -> 10, of which waited for: 5 -> 3; matrix products, arithmetic and copies ran while one was open for 0% -> 0% of each run, Pallas kernels for 7% -> 7%
where the time goes in v25:
time: 20.9 us; the launch traced here: 20.8 us
  starting transfers between devices  14.8 us (71%)
  Pallas kernels  3.69 us (18%)
  waiting for transfers between devices  2.15 us (10%)
    ppermute x6, starting transfers between devices, swap(): lax.ppermute(array, axis, [(i, i ^ bit) for i in range(lax.axis_size(axis...  9.8 us
    ppermute x1, starting transfers between devices, shards(): lax.ppermute(downward, 'seq', [(target, source) for source, target in shi...  2.93 us
    ppermute x1, starting transfers between devices, shards(): early = (beside, lax.ppermute(upward, 'seq', shift), swap(eighth, 4))  2.04 us
    ppermute x6, waiting for transfers between devices, swap(): lax.ppermute(array, axis, [(i, i ^ bit) for i in range(lax.axis_size(axis...  1.22 us
    pallas_call x1, Pallas kernels, shards(): kernel_call(functools.partial(pack_kernel, not paired), 'pack', 16, [HBM]...  0.99 us
    ppermute x1, waiting for transfers between devices, shards(): lax.ppermute(downward, 'seq', [(target, source) for source, target in shi...  0.93 us
    pallas_call x1, Pallas kernels, shards(): kernel_call(project_kernel, 'project', 8, [VMEM] * 4, [(share, out_weight...  0.81 us
    pallas_call x1, Pallas kernels, shards(): kernel_call(functools.partial(leaves_kernel, seq_size, paired), 'leaves',...  0.53 us
  transfers between devices with their start and end apart: 10, of which 3 were waited for; matrix products, arithmetic and copies ran while one was open for 0% of the time, Pallas kernels for 7%

profile of v25, /device:TPU:0, one launch (start us, length us, event | category | flops | bytes accessed | tf_op | source)
XLA Modules:
  0.0 20.8 jit_solution(8322306027618972159)
XLA Ops:
  0.0 1.0 %pack.1 = (bf16[256,128]{1,0:T(8,128)(2,1)S(1)}, bf16[256,256]{1,0:T(8,128)(2,1)S(1)}, bf16[192,256]{1,0:T(8,128)(2,1)S(1)}, bf16[192,256]{1,0:T(8,128)(2,1)S(1)}, bf16[64,256]{1,0:T(8,128)(2,1)S(1)}) custom-call(bf16[256,128]{1,0:T(8,128)(2,1)} %queries.1, bf16[256,128]{1,0:T(8,128)(2,1)} %keys.1, bf16[256,128]{1,0:T(8,128)(2,1)} %values.1), custom_call_target="tpu_custom_call" | custom-call | bytes 1048576 | tf_op jit(solution)/shard_map/pack/pallas_call | solution.py:315
  1.0 3.0 %collective-permute-start.3 = (bf16[64,256]{1,0:T(8,128)(2,1)S(1)}, bf16[64,256]{1,0:T(8,128)(2,1)S(1)}, u32[]{:S(2)}, u32[]{:S(2)}) collective-permute-start(bf16[64,256]{1,0:T(8,128)(2,1)S(1)} %get-tuple-element.32.quarter), channel_id=1, source_target_pairs={{0,4},{4,0},{8,12},{12,8},{16,20},{20,16},{24,28},{28,24},{1,5},{5... | collective-permute-start | bytes 98312 | tf_op jit(solution)/shard_map/ppermute | solution.py:313
  4.0 0.1 collective-permute-start.2
  4.1 2.0 %collective-permute-start = (bf16[192,256]{1,0:T(8,128)(2,1)S(1)}, bf16[192,256]{1,0:T(8,128)(2,1)S(1)}, u32[]{:S(2)}, u32[]{:S(2)}) collective-permute-start(bf16[192,256]{1,0:T(8,128)(2,1)S(1)} %get-tuple-element.27), channel_id=1, source_target_pairs={{0,4},{4,0},{8,12},{12,8},{16,20},{20,16},{24,28},{28,24},{1,5},{5... | collective-permute-start | bytes 294920 | tf_op jit(solution)/shard_map/ppermute | solution.py:313
  6.1 0.0 collective-permute-start.1
  6.1 0.0 collective-permute-done.3.theirs
  6.2 2.0 %collective-permute-start.4 = (bf16[64,256]{1,0:T(8,128)(2,1)S(1)}, bf16[64,256]{1,0:T(8,128)(2,1)S(1)}, u32[]{:S(2)}, u32[]{:S(2)}) collective-permute-start(bf16[64,256]{1,0:T(8,128)(2,1)S(1)} %get-tuple-element.33), channel_id=1, source_target_pairs={{0,8},{4,12},{8,16},{12,20},{16,24},{20,28},{24,0},{28,4},{1,9},{5... | collective-permute-start | bytes 98312 | tf_op jit(solution)/shard_map/ppermute | solution.py:358
  8.2 2.8 %collective-permute-start.5 = (bf16[64,256]{1,0:T(8,128)(2,1)S(1)}, bf16[64,256]{1,0:T(8,128)(2,1)S(1)}, u32[]{:S(2)}, u32[]{:S(2)}) collective-permute-start(bf16[64,256]{1,0:T(8,128)(2,1)S(1)} %get-tuple-element.34), channel_id=1, source_target_pairs={{0,16},{4,20},{8,24},{12,28},{16,0},{20,4},{24,8},{28,12},{1,17},{... | collective-permute-start | bytes 98312 | tf_op jit(solution)/shard_map/ppermute | solution.py:313
  11.0 0.0 collective-permute-done.inner
  11.0 2.9 %collective-permute-start.6 = (bf16[64,256]{1,0:T(8,128)(2,1)S(1)}, bf16[64,256]{1,0:T(8,128)(2,1)S(1)}, u32[]{:S(2)}, u32[]{:S(2)}) collective-permute-start(bf16[64,256]{1,0:T(8,128)(2,1)S(1)} %get-tuple-element.37), channel_id=1, source_target_pairs={{8,0},{12,4},{16,8},{20,12},{24,16},{28,20},{0,24},{4,28},{9,1},{1... | collective-permute-start | bytes 98312 | tf_op jit(solution)/shard_map/ppermute | solution.py:359
  13.9 0.0 collective-permute-done.1.outer
  13.9 0.4 %near.1 = (f32[2,256,512]{2,1,0:T(8,128)S(1)}, bf16[2,512,128]{2,1,0:T(8,128)(2,1)S(1)}, bf16[64,256]{1,0:T(8,128)(2,1)S(1)}) custom-call(bf16[256,128]{1,0:T(8,128)(2,1)S(1)} %get-tuple-element.25.queries, bf16[256,256]{1,0:T(8,128)(2,1)S(1)} %get-tuple-element.26.own, bf16[192,256]{1,0:T(8,128)(2,1)S(1)} %collective-permute-done.inner, ...), custom_call_target="tpu_custom_call" | custom-call | flops 67108864 | bytes 1048576 | tf_op jit(solution)/shard_map/near/pallas_call | solution.py:364
  14.3 0.0 collective-permute-done.2.rest_0_
  14.3 0.0 collective-permute-done.4.rest_1_
  14.3 0.0 collective-permute-done.5.rest_2_
  14.3 0.2 %mid.1 = (f32[2,256,256]{2,1,0:T(8,128)S(1)}, bf16[256,128]{1,0:T(8,128)(2,1)S(1)}) custom-call(bf16[256,128]{1,0:T(8,128)(2,1)S(1)} %get-tuple-element.25.queries, bf16[64,256]{1,0:T(8,128)(2,1)S(1)} %get-tuple-element.31.shared, bf16[64,256]{1,0:T(8,128)(2,1)S(1)} %collective-permute-done.2.rest_0_, bf16[64,256]{1,0:T(8,128)(2,1)S(1)} %collective-permute-done.4.rest_1_, ...), custom_call_target="tpu_custom_call" | custom-call | flops 1000000000 | bytes 1048576 | tf_op jit(solution)/shard_map/mid/pallas_call | solution.py:378
  14.6 0.9 %collective-permute-done.6.rest_0_ = bf16[64,256]{1,0:T(8,128)(2,1)S(1)} collective-permute-done((bf16[64,256]{1,0:T(8,128)(2,1)S(1)}, bf16[64,256]{1,0:T(8,128)(2,1)S(1)}, u32[]{:S(2)}, u32[]{:S(2)}) %collective-permute-start.6) | collective-permute-done | bytes 32800 | tf_op jit(solution)/shard_map/ppermute | solution.py:359
  15.5 0.5 %leaves.1 = (bf16[80,128]{1,0:T(8,128)(2,1)S(1)}, bf16[80,128]{1,0:T(8,128)(2,1)S(1)}, bf16[64,128]{1,0:T(8,128)(2,1)S(1)}, bf16[64,128]{1,0:T(8,128)(2,1)S(1)}, f32[8,64]{1,0:T(8,128)S(1)}) custom-call(bf16[256,128]{1,0:T(8,128)(2,1)S(1)} %get-tuple-element.25.queries, f32[2,256,512]{2,1,0:T(8,128)S(1)} %get-tuple-element.29.near_scores, ...), custom_call_target="tpu_custom_call" | custom-call | flops 109051904 | bytes 1048576 | tf_op jit(solution)/shard_map/leaves/pallas_call | solution.py:390
  16.0 0.1 collective-permute-start.8
  16.1 1.6 %collective-permute-start.9 = (bf16[80,128]{1,0:T(8,128)(2,1)S(1)}, bf16[80,128]{1,0:T(8,128)(2,1)S(1)}, u32[]{:S(2)}, u32[]{:S(2)}) collective-permute-start(bf16[80,128]{1,0:T(8,128)(2,1)S(1)} %get-tuple-element.44), channel_id=1, source_target_pairs={{0,2},{1,3},{2,0},{3,1},{4,6},{5,7},{6,4},{7,5},{8,10},{9,11},{10,... | collective-permute-start | bytes 61448 | tf_op jit(solution)/shard_map/ppermute | solution.py:313
  17.7 0.0 copy-start
  17.7 0.5 %stays.1 = (bf16[64,128]{1,0:T(8,128)(2,1)S(1)}, bf16[64,128]{1,0:T(8,128)(2,1)S(1)}) custom-call(bf16[256,128]{1,0:T(8,128)(2,1)S(1)} %get-tuple-element.25.queries, f32[2,256,512]{2,1,0:T(8,128)S(1)} %get-tuple-element.29.near_scores, bf16[2,512,128]{2,1,0:T(8,128)(2,1)S(1)} %get-tuple-element.30.near_values, ...), custom_call_target="tpu_custom_call" | custom-call | flops 109051904 | bytes 1048576 | tf_op jit(solution)/shard_map/stays/pallas_call | solution.py:405
  18.2 0.3 %collective-permute-start.7 = (bf16[64,128]{1,0:T(8,128)(2,1)S(1)}, bf16[64,128]{1,0:T(8,128)(2,1)S(1)}, u32[]{:S(2)}, u32[]{:S(2)}) collective-permute-start(bf16[64,128]{1,0:T(8,128)(2,1)S(1)} %get-tuple-element.42), channel_id=1, source_target_pairs={{0,1},{1,0},{2,3},{3,2},{4,5},{5,4},{6,7},{7,6},{8,9},{9,8},{10,11... | collective-permute-start | bytes 49160 | tf_op jit(solution)/shard_map/ppermute | solution.py:313
  18.6 0.9 %collective-permute-done.7.other = bf16[64,128]{1,0:T(8,128)(2,1)S(1)} collective-permute-done((bf16[64,128]{1,0:T(8,128)(2,1)S(1)}, bf16[64,128]{1,0:T(8,128)(2,1)S(1)}, u32[]{:S(2)}, u32[]{:S(2)}) %collective-permute-start.7) | collective-permute-done | bytes 16416 | tf_op jit(solution)/shard_map/ppermute | solution.py:313
  19.5 0.0 copy-done
  19.5 0.2 begin.1.partial
  19.7 0.0 collective-permute-done.8.other
  19.7 0.3 %collective-permute-done.9.same = bf16[80,128]{1,0:T(8,128)(2,1)S(1)} collective-permute-done((bf16[80,128]{1,0:T(8,128)(2,1)S(1)}, bf16[80,128]{1,0:T(8,128)(2,1)S(1)}, u32[]{:S(2)}, u32[]{:S(2)}) %collective-permute-start.9) | collective-permute-done | bytes 20512 | tf_op jit(solution)/shard_map/ppermute | solution.py:313
  20.0 0.8 %project.1 = bf16[64,512]{1,0:T(8,128)(2,1)} custom-call(f32[64,512]{1,0:T(8,128)S(1)} %begin.1.partial, bf16[80,128]{1,0:T(8,128)(2,1)S(1)} %collective-permute-done.8.other, bf16[80,128]{1,0:T(8,128)(2,1)S(1)} %collective-permute-done.9.same, bf16[512,512]{1,0:T(8,128)(2,1)S(1)} %copy-done), custom_call_target="tpu_custom_call" | custom-call | bytes 1048576 | tf_op jit(solution)/shard_map/project/pallas_call | solution.py:418
  (1 shorter events, 0.0 us)
Async XLA Ops:
  1.0 5.1 %collective-permute-start.3 = (bf16[64,256]{1,0:T(8,128)(2,1)S(1)}, bf16[64,256]{1,0:T(8,128)(2,1)S(1)}, u32[]{:S(2)}, u32[]{:S(2)}) collective-permute-start(bf16[64,256]{1,0:T(8,128)(2,1)S(1)} %get-tuple-element.32.quarter), channel_id=1, source_target_pairs={{0,4},{4,0},{8,12},{12,8},{16,20},{20,16},{24,28},{28,24},{1,5},{5... | collective-permute-start | bytes 98312 | tf_op jit(solution)/shard_map/ppermute | solution.py:313
  4.0 10.3 %collective-permute-start.2 = (bf16[64,256]{1,0:T(8,128)(2,1)S(1)}, bf16[64,256]{1,0:T(8,128)(2,1)S(1)}, u32[]{:S(2)}, u32[]{:S(2)}) collective-permute-start(bf16[64,256]{1,0:T(8,128)(2,1)S(1)} %get-tuple-element.32.quarter), channel_id=1, source_target_pairs={{4,12},{8,0},{12,20},{16,8},{20,28},{24,16},{0,4},{28,24},{5,13},{... | collective-permute-start | bytes 98312 | tf_op jit(solution)/shard_map/ppermute | solution.py:357
  4.1 6.9 %collective-permute-start = (bf16[192,256]{1,0:T(8,128)(2,1)S(1)}, bf16[192,256]{1,0:T(8,128)(2,1)S(1)}, u32[]{:S(2)}, u32[]{:S(2)}) collective-permute-start(bf16[192,256]{1,0:T(8,128)(2,1)S(1)} %get-tuple-element.27), channel_id=1, source_target_pairs={{0,4},{4,0},{8,12},{12,8},{16,20},{20,16},{24,28},{28,24},{1,5},{5... | collective-permute-start | bytes 294920 | tf_op jit(solution)/shard_map/ppermute | solution.py:313
  6.1 7.8 %collective-permute-start.1 = (bf16[192,256]{1,0:T(8,128)(2,1)S(1)}, bf16[192,256]{1,0:T(8,128)(2,1)S(1)}, u32[]{:S(2)}, u32[]{:S(2)}) collective-permute-start(bf16[192,256]{1,0:T(8,128)(2,1)S(1)} %get-tuple-element.28), channel_id=1, source_target_pairs={{0,1},{1,0},{2,3},{3,2},{4,8},{5,9},{6,10},{7,11},{8,4},{9,5},{10,... | collective-permute-start | bytes 294920 | tf_op jit(solution)/shard_map/ppermute | solution.py:332
  6.2 8.1 %collective-permute-start.4 = (bf16[64,256]{1,0:T(8,128)(2,1)S(1)}, bf16[64,256]{1,0:T(8,128)(2,1)S(1)}, u32[]{:S(2)}, u32[]{:S(2)}) collective-permute-start(bf16[64,256]{1,0:T(8,128)(2,1)S(1)} %get-tuple-element.33), channel_id=1, source_target_pairs={{0,8},{4,12},{8,16},{12,20},{16,24},{20,28},{24,0},{28,4},{1,9},{5... | collective-permute-start | bytes 98312 | tf_op jit(solution)/shard_map/ppermute | solution.py:358
  8.2 6.1 %collective-permute-start.5 = (bf16[64,256]{1,0:T(8,128)(2,1)S(1)}, bf16[64,256]{1,0:T(8,128)(2,1)S(1)}, u32[]{:S(2)}, u32[]{:S(2)}) collective-permute-start(bf16[64,256]{1,0:T(8,128)(2,1)S(1)} %get-tuple-element.34), channel_id=1, source_target_pairs={{0,16},{4,20},{8,24},{12,28},{16,0},{20,4},{24,8},{28,12},{1,17},{... | collective-permute-start | bytes 98312 | tf_op jit(solution)/shard_map/ppermute | solution.py:313
  11.0 4.5 %collective-permute-start.6 = (bf16[64,256]{1,0:T(8,128)(2,1)S(1)}, bf16[64,256]{1,0:T(8,128)(2,1)S(1)}, u32[]{:S(2)}, u32[]{:S(2)}) collective-permute-start(bf16[64,256]{1,0:T(8,128)(2,1)S(1)} %get-tuple-element.37), channel_id=1, source_target_pairs={{8,0},{12,4},{16,8},{20,12},{24,16},{28,20},{0,24},{4,28},{9,1},{1... | collective-permute-start | bytes 98312 | tf_op jit(solution)/shard_map/ppermute | solution.py:359
  16.0 3.6 %collective-permute-start.8 = (bf16[80,128]{1,0:T(8,128)(2,1)S(1)}, bf16[80,128]{1,0:T(8,128)(2,1)S(1)}, u32[]{:S(2)}, u32[]{:S(2)}) collective-permute-start(bf16[80,128]{1,0:T(8,128)(2,1)S(1)} %get-tuple-element.43), channel_id=1, source_target_pairs={{0,3},{1,2},{2,1},{3,0},{4,7},{5,6},{6,5},{7,4},{8,11},{9,10},{10,... | collective-permute-start | bytes 61448 | tf_op jit(solution)/shard_map/ppermute | solution.py:313
  16.1 3.8 %collective-permute-start.9 = (bf16[80,128]{1,0:T(8,128)(2,1)S(1)}, bf16[80,128]{1,0:T(8,128)(2,1)S(1)}, u32[]{:S(2)}, u32[]{:S(2)}) collective-permute-start(bf16[80,128]{1,0:T(8,128)(2,1)S(1)} %get-tuple-element.44), channel_id=1, source_target_pairs={{0,2},{1,3},{2,0},{3,1},{4,6},{5,7},{6,4},{7,5},{8,10},{9,11},{10,... | collective-permute-start | bytes 61448 | tf_op jit(solution)/shard_map/ppermute | solution.py:313
  17.7 1.8 %copy-start = (bf16[512,512]{1,0:T(8,128)(2,1)S(1)}, bf16[512,512]{1,0:T(8,128)(2,1)}, u32[]{:S(2)}) copy-start(bf16[512,512]{1,0:T(8,128)(2,1)} %weight.3) | copy-start | bytes 1572868
  18.2 1.2 %collective-permute-start.7 = (bf16[64,128]{1,0:T(8,128)(2,1)S(1)}, bf16[64,128]{1,0:T(8,128)(2,1)S(1)}, u32[]{:S(2)}, u32[]{:S(2)}) collective-permute-start(bf16[64,128]{1,0:T(8,128)(2,1)S(1)} %get-tuple-element.42), channel_id=1, source_target_pairs={{0,1},{1,0},{2,3},{3,2},{4,5},{5,4},{6,7},{7,6},{8,9},{9,8},{10,11... | collective-permute-start | bytes 49160 | tf_op jit(solution)/shard_map/ppermute | solution.py:313

commit v26 on v25

--- a/solution.py
+++ b/solution.py
@@ -161,7 +161,8 @@
     )
 
 
-def near_kernel(seq_size, queries, own, inner, outer, scores, values, shared, keys, wide):
+def near_kernel(seq_size, queries, own, inner, outer, *rest):
+    *beside, scores, values, shared, keys, wide = rest
     me = lax.axis_index("seq")
     odd = me & 1
     from_inner, from_outer = inner[...], outer[...]
@@ -169,7 +170,9 @@
     after = jnp.where(odd == 1, from_outer, from_inner)
     edge_before, edge_after = before[:LEAF], after[:LEAF]
     far_half_after = after[LEAF:]
-    shared[...] = before[LEAF:]
+    shared[:HALF] = before[LEAF:]
+    for rows in beside:
+        shared[HALF:] = rows[...]
     near_half_before = average_pairs(edge_before, wide)
     near_half_after = average_pairs(edge_after, wide)
     has_before, has_after = bias_of(me >= 1), bias_of(me + 1 < seq_size)
@@ -195,9 +198,9 @@
 
 def mid_kernel(queries, shared, *rest):
     *early, scores, values, keys = rest
-    pieces = [(shared, bias_of(lax.axis_index("seq") >= 1))]
+    pieces = [(shared[:HALF], bias_of(lax.axis_index("seq") >= 1))]
     if early:
-        pieces += early_pieces(*early)
+        pieces += early_pieces(shared[HALF:], *early)
     bias = place(pieces, values, keys)
     for leaf in range(2):
         rows = split_heads(queries[leaf * LEAF : (leaf + 1) * LEAF])
@@ -354,26 +357,26 @@
         shift = [(i, (i + 2) % seq_size) for i in range(seq_size)]
         cycle = [(i, i + 2 if i & 1 else i - 2) for i in range(1, seq_size - 1)]
         cycle += [(0, 1), (seq_size - 1, seq_size - 2)]
-        beside = lax.ppermute(quarter, "seq", cycle)
-        early = (beside, lax.ppermute(upward, "seq", shift), swap(eighth, 4))
+        beside = (lax.ppermute(quarter, "seq", cycle),)
+        early = (lax.ppermute(upward, "seq", shift), swap(eighth, 4))
         late = lax.ppermute(downward, "seq", [(target, source) for source, target in shift])
     else:
-        early = ()
+        beside, early = (), ()
         late = lax.all_to_all(quarter, "seq", split_axis=0, concat_axis=0)
     share = tokens // head_size
     near_scores, near_values, shared = kernel_call(
         functools.partial(near_kernel, seq_size),
         "near",
         16,
-        [VMEM] * 4,
+        [VMEM] * (4 + len(beside)),
         [
             jax.ShapeDtypeStruct((2, 2 * LEAF, NEAR_ROWS), jnp.float32),
             (2, NEAR_ROWS, width),
-            (HALF, pair_width),
+            (HALF * (1 + len(beside)), pair_width),
         ],
         [pltpu.VMEM((NEAR_ROWS, width), jnp.bfloat16), wide],
         flops=8 * LEAF * NEAR_ROWS * width,
-    )(own_queries, own, inner, outer)
+    )(own_queries, own, inner, outer, *beside)
     mid_rows = 4 * HALF if paired else HALF
     mid_scores, mid_values = kernel_call(
         mid_kernel,

time: 20.9 us -> 20.3 us (0.971)
  starting transfers between devices: 14.8 us -> 13.1 us
  waiting for transfers between devices: 2.15 us -> 3.32 us
    ppermute x1, starting transfers between devices: 2.93 us -> 1.18 us  [shards(): lax.ppermute(downward, 'seq', [(target, source) for source, target in shi...]
    ppermute x2, waiting for transfers between devices: 0.01 us -> 1.1 us  [the longest x1 1.1 us: shards(): early = (lax.ppermute(upward, 'seq', shift), swap(eighth, 4))]
  transfers between devices with their start and end apart: 10 -> 10, of which waited for: 3 -> 4; matrix products, arithmetic and copies ran while one was open for 0% -> 0% of each run, Pallas kernels for 7% -> 7%
where the time goes in v26:
time: 20.3 us; the launch traced here: 20.2 us
  starting transfers between devices  13.1 us (65%)
  Pallas kernels  3.69 us (18%)
  waiting for transfers between devices  3.32 us (16%)
    ppermute x6, starting transfers between devices, swap(): lax.ppermute(array, axis, [(i, i ^ bit) for i in range(lax.axis_size(axis...  9.79 us
    ppermute x1, starting transfers between devices, shards(): early = (lax.ppermute(upward, 'seq', shift), swap(eighth, 4))  2.04 us
    ppermute x6, waiting for transfers between devices, swap(): lax.ppermute(array, axis, [(i, i ^ bit) for i in range(lax.axis_size(axis...  1.22 us
    ppermute x1, starting transfers between devices, shards(): lax.ppermute(downward, 'seq', [(target, source) for source, target in shi...  1.18 us
    ppermute x1, waiting for transfers between devices, shards(): early = (lax.ppermute(upward, 'seq', shift), swap(eighth, 4))  1.1 us
    ppermute x1, waiting for transfers between devices, shards(): lax.ppermute(downward, 'seq', [(target, source) for source, target in shi...  1 us
    pallas_call x1, Pallas kernels, shards(): kernel_call(functools.partial(pack_kernel, not paired), 'pack', 16, [HBM]...  0.99 us
    pallas_call x1, Pallas kernels, shards(): kernel_call(project_kernel, 'project', 8, [VMEM] * 4, [(share, out_weight...  0.81 us
  transfers between devices with their start and end apart: 10, of which 4 were waited for; matrix products, arithmetic and copies ran while one was open for 0% of the time, Pallas kernels for 7%

profile of v26, /device:TPU:0, one launch (start us, length us, event | category | flops | bytes accessed | tf_op | source)
XLA Modules:
  0.0 20.2 jit_solution(9541961094999292613)
XLA Ops:
  0.0 1.0 %pack.1 = (bf16[256,128]{1,0:T(8,128)(2,1)S(1)}, bf16[256,256]{1,0:T(8,128)(2,1)S(1)}, bf16[192,256]{1,0:T(8,128)(2,1)S(1)}, bf16[192,256]{1,0:T(8,128)(2,1)S(1)}, bf16[64,256]{1,0:T(8,128)(2,1)S(1)}) custom-call(bf16[256,128]{1,0:T(8,128)(2,1)} %queries.1, bf16[256,128]{1,0:T(8,128)(2,1)} %keys.1, bf16[256,128]{1,0:T(8,128)(2,1)} %values.1), custom_call_target="tpu_custom_call" | custom-call | bytes 1048576 | tf_op jit(solution)/shard_map/pack/pallas_call | solution.py:318
  1.0 3.0 %collective-permute-start.3 = (bf16[64,256]{1,0:T(8,128)(2,1)S(1)}, bf16[64,256]{1,0:T(8,128)(2,1)S(1)}, u32[]{:S(2)}, u32[]{:S(2)}) collective-permute-start(bf16[64,256]{1,0:T(8,128)(2,1)S(1)} %get-tuple-element.29.quarter), channel_id=1, source_target_pairs={{0,4},{4,0},{8,12},{12,8},{16,20},{20,16},{24,28},{28,24},{1,5},{5... | collective-permute-start | bytes 98312 | tf_op jit(solution)/shard_map/ppermute | solution.py:316
  4.0 0.1 collective-permute-start.2
  4.1 2.0 %collective-permute-start = (bf16[192,256]{1,0:T(8,128)(2,1)S(1)}, bf16[192,256]{1,0:T(8,128)(2,1)S(1)}, u32[]{:S(2)}, u32[]{:S(2)}) collective-permute-start(bf16[192,256]{1,0:T(8,128)(2,1)S(1)} %get-tuple-element.27), channel_id=1, source_target_pairs={{0,4},{4,0},{8,12},{12,8},{16,20},{20,16},{24,28},{28,24},{1,5},{5... | collective-permute-start | bytes 294920 | tf_op jit(solution)/shard_map/ppermute | solution.py:316
  6.1 0.0 collective-permute-start.1
  6.1 0.0 collective-permute-done.3.theirs
  6.2 2.0 %collective-permute-start.4 = (bf16[64,256]{1,0:T(8,128)(2,1)S(1)}, bf16[64,256]{1,0:T(8,128)(2,1)S(1)}, u32[]{:S(2)}, u32[]{:S(2)}) collective-permute-start(bf16[64,256]{1,0:T(8,128)(2,1)S(1)} %get-tuple-element.33), channel_id=1, source_target_pairs={{0,8},{4,12},{8,16},{12,20},{16,24},{20,28},{24,0},{28,4},{1,9},{5... | collective-permute-start | bytes 98312 | tf_op jit(solution)/shard_map/ppermute | solution.py:361
  8.2 2.8 %collective-permute-start.5 = (bf16[64,256]{1,0:T(8,128)(2,1)S(1)}, bf16[64,256]{1,0:T(8,128)(2,1)S(1)}, u32[]{:S(2)}, u32[]{:S(2)}) collective-permute-start(bf16[64,256]{1,0:T(8,128)(2,1)S(1)} %get-tuple-element.34), channel_id=1, source_target_pairs={{0,16},{4,20},{8,24},{12,28},{16,0},{20,4},{24,8},{28,12},{1,17},{... | collective-permute-start | bytes 98312 | tf_op jit(solution)/shard_map/ppermute | solution.py:316
  11.0 0.0 collective-permute-done.2.rest_0_
  11.0 1.2 %collective-permute-start.6 = (bf16[64,256]{1,0:T(8,128)(2,1)S(1)}, bf16[64,256]{1,0:T(8,128)(2,1)S(1)}, u32[]{:S(2)}, u32[]{:S(2)}) collective-permute-start(bf16[64,256]{1,0:T(8,128)(2,1)S(1)} %get-tuple-element.37), channel_id=1, source_target_pairs={{8,0},{12,4},{16,8},{20,12},{24,16},{28,20},{0,24},{4,28},{9,1},{1... | collective-permute-start | bytes 98312 | tf_op jit(solution)/shard_map/ppermute | solution.py:362
  12.1 0.0 collective-permute-done.inner
  12.1 0.0 collective-permute-done.1.outer
  12.2 0.4 %near.1 = (f32[2,256,512]{2,1,0:T(8,128)S(1)}, bf16[2,512,128]{2,1,0:T(8,128)(2,1)S(1)}, bf16[128,256]{1,0:T(8,128)(2,1)S(1)}) custom-call(bf16[256,128]{1,0:T(8,128)(2,1)S(1)} %get-tuple-element.25.queries, bf16[256,256]{1,0:T(8,128)(2,1)S(1)} %get-tuple-element.26.own, bf16[192,256]{1,0:T(8,128)(2,1)S(1)} %collective-permute-done.inner, ...), custom_call_target="tpu_custom_call" | custom-call | flops 67108864 | bytes 1048576 | tf_op jit(solution)/shard_map/near/pallas_call | solution.py:367
  12.5 1.1 %collective-permute-done.4.rest_0_ = bf16[64,256]{1,0:T(8,128)(2,1)S(1)} collective-permute-done((bf16[64,256]{1,0:T(8,128)(2,1)S(1)}, bf16[64,256]{1,0:T(8,128)(2,1)S(1)}, u32[]{:S(2)}, u32[]{:S(2)}) %collective-permute-start.4) | collective-permute-done | bytes 32800 | tf_op jit(solution)/shard_map/ppermute | solution.py:361
  13.6 0.0 collective-permute-done.5.rest_1_
  13.6 0.2 %mid.1 = (f32[2,256,256]{2,1,0:T(8,128)S(1)}, bf16[256,128]{1,0:T(8,128)(2,1)S(1)}) custom-call(bf16[256,128]{1,0:T(8,128)(2,1)S(1)} %get-tuple-element.25.queries, bf16[128,256]{1,0:T(8,128)(2,1)S(1)} %get-tuple-element.32.shared, bf16[64,256]{1,0:T(8,128)(2,1)S(1)} %collective-permute-done.4.rest_0_, bf16[64,256]{1,0:T(8,128)(2,1)S(1)} %collective-permute-done.5.rest_1_), custom_call_target="tpu_custom_call" | custom-call | flops 1000000000 | bytes 1048576 | tf_op jit(solution)/shard_map/mid/pallas_call | solution.py:381
  13.9 1.0 %collective-permute-done.6.rest_0_ = bf16[64,256]{1,0:T(8,128)(2,1)S(1)} collective-permute-done((bf16[64,256]{1,0:T(8,128)(2,1)S(1)}, bf16[64,256]{1,0:T(8,128)(2,1)S(1)}, u32[]{:S(2)}, u32[]{:S(2)}) %collective-permute-start.6) | collective-permute-done | bytes 32800 | tf_op jit(solution)/shard_map/ppermute | solution.py:362
  14.9 0.5 %leaves.1 = (bf16[80,128]{1,0:T(8,128)(2,1)S(1)}, bf16[80,128]{1,0:T(8,128)(2,1)S(1)}, bf16[64,128]{1,0:T(8,128)(2,1)S(1)}, bf16[64,128]{1,0:T(8,128)(2,1)S(1)}, f32[8,64]{1,0:T(8,128)S(1)}) custom-call(bf16[256,128]{1,0:T(8,128)(2,1)S(1)} %get-tuple-element.25.queries, f32[2,256,512]{2,1,0:T(8,128)S(1)} %get-tuple-element.30.near_scores, ...), custom_call_target="tpu_custom_call" | custom-call | flops 109051904 | bytes 1048576 | tf_op jit(solution)/shard_map/leaves/pallas_call | solution.py:393
  15.4 0.1 collective-permute-start.8
  15.5 1.6 %collective-permute-start.9 = (bf16[80,128]{1,0:T(8,128)(2,1)S(1)}, bf16[80,128]{1,0:T(8,128)(2,1)S(1)}, u32[]{:S(2)}, u32[]{:S(2)}) collective-permute-start(bf16[80,128]{1,0:T(8,128)(2,1)S(1)} %get-tuple-element.44), channel_id=1, source_target_pairs={{0,2},{1,3},{2,0},{3,1},{4,6},{5,7},{6,4},{7,5},{8,10},{9,11},{10,... | collective-permute-start | bytes 61448 | tf_op jit(solution)/shard_map/ppermute | solution.py:316
  17.1 0.0 copy-start
  17.1 0.5 %stays.1 = (bf16[64,128]{1,0:T(8,128)(2,1)S(1)}, bf16[64,128]{1,0:T(8,128)(2,1)S(1)}) custom-call(bf16[256,128]{1,0:T(8,128)(2,1)S(1)} %get-tuple-element.25.queries, f32[2,256,512]{2,1,0:T(8,128)S(1)} %get-tuple-element.30.near_scores, bf16[2,512,128]{2,1,0:T(8,128)(2,1)S(1)} %get-tuple-element.31.near_values, ...), custom_call_target="tpu_custom_call" | custom-call | flops 109051904 | bytes 1048576 | tf_op jit(solution)/shard_map/stays/pallas_call | solution.py:408
  17.6 0.3 %collective-permute-start.7 = (bf16[64,128]{1,0:T(8,128)(2,1)S(1)}, bf16[64,128]{1,0:T(8,128)(2,1)S(1)}, u32[]{:S(2)}, u32[]{:S(2)}) collective-permute-start(bf16[64,128]{1,0:T(8,128)(2,1)S(1)} %get-tuple-element.42), channel_id=1, source_target_pairs={{0,1},{1,0},{2,3},{3,2},{4,5},{5,4},{6,7},{7,6},{8,9},{9,8},{10,11... | collective-permute-start | bytes 49160 | tf_op jit(solution)/shard_map/ppermute | solution.py:316
  18.0 0.9 %collective-permute-done.7.other = bf16[64,128]{1,0:T(8,128)(2,1)S(1)} collective-permute-done((bf16[64,128]{1,0:T(8,128)(2,1)S(1)}, bf16[64,128]{1,0:T(8,128)(2,1)S(1)}, u32[]{:S(2)}, u32[]{:S(2)}) %collective-permute-start.7) | collective-permute-done | bytes 16416 | tf_op jit(solution)/shard_map/ppermute | solution.py:316
  18.9 0.0 copy-done
  18.9 0.2 begin.1.partial
  19.0 0.0 collective-permute-done.8.other
  19.1 0.3 %collective-permute-done.9.same = bf16[80,128]{1,0:T(8,128)(2,1)S(1)} collective-permute-done((bf16[80,128]{1,0:T(8,128)(2,1)S(1)}, bf16[80,128]{1,0:T(8,128)(2,1)S(1)}, u32[]{:S(2)}, u32[]{:S(2)}) %collective-permute-start.9) | collective-permute-done | bytes 20512 | tf_op jit(solution)/shard_map/ppermute | solution.py:316
  19.3 0.8 %project.1 = bf16[64,512]{1,0:T(8,128)(2,1)} custom-call(f32[64,512]{1,0:T(8,128)S(1)} %begin.1.partial, bf16[80,128]{1,0:T(8,128)(2,1)S(1)} %collective-permute-done.8.other, bf16[80,128]{1,0:T(8,128)(2,1)S(1)} %collective-permute-done.9.same, bf16[512,512]{1,0:T(8,128)(2,1)S(1)} %copy-done), custom_call_target="tpu_custom_call" | custom-call | bytes 1048576 | tf_op jit(solution)/shard_map/project/pallas_call | solution.py:421
  (1 shorter events, 0.0 us)
Async XLA Ops:
  1.0 5.1 %collective-permute-start.3 = (bf16[64,256]{1,0:T(8,128)(2,1)S(1)}, bf16[64,256]{1,0:T(8,128)(2,1)S(1)}, u32[]{:S(2)}, u32[]{:S(2)}) collective-permute-start(bf16[64,256]{1,0:T(8,128)(2,1)S(1)} %get-tuple-element.29.quarter), channel_id=1, source_target_pairs={{0,4},{4,0},{8,12},{12,8},{16,20},{20,16},{24,28},{28,24},{1,5},{5... | collective-permute-start | bytes 98312 | tf_op jit(solution)/shard_map/ppermute | solution.py:316
  4.0 7.0 %collective-permute-start.2 = (bf16[64,256]{1,0:T(8,128)(2,1)S(1)}, bf16[64,256]{1,0:T(8,128)(2,1)S(1)}, u32[]{:S(2)}, u32[]{:S(2)}) collective-permute-start(bf16[64,256]{1,0:T(8,128)(2,1)S(1)} %get-tuple-element.29.quarter), channel_id=1, source_target_pairs={{4,12},{8,0},{12,20},{16,8},{20,28},{24,16},{0,4},{28,24},{5,13},{... | collective-permute-start | bytes 98312 | tf_op jit(solution)/shard_map/ppermute | solution.py:360
  4.1 8.1 %collective-permute-start = (bf16[192,256]{1,0:T(8,128)(2,1)S(1)}, bf16[192,256]{1,0:T(8,128)(2,1)S(1)}, u32[]{:S(2)}, u32[]{:S(2)}) collective-permute-start(bf16[192,256]{1,0:T(8,128)(2,1)S(1)} %get-tuple-element.27), channel_id=1, source_target_pairs={{0,4},{4,0},{8,12},{12,8},{16,20},{20,16},{24,28},{28,24},{1,5},{5... | collective-permute-start | bytes 294920 | tf_op jit(solution)/shard_map/ppermute | solution.py:316
  6.1 6.0 %collective-permute-start.1 = (bf16[192,256]{1,0:T(8,128)(2,1)S(1)}, bf16[192,256]{1,0:T(8,128)(2,1)S(1)}, u32[]{:S(2)}, u32[]{:S(2)}) collective-permute-start(bf16[192,256]{1,0:T(8,128)(2,1)S(1)} %get-tuple-element.28), channel_id=1, source_target_pairs={{0,1},{1,0},{2,3},{3,2},{4,8},{5,9},{6,10},{7,11},{8,4},{9,5},{10,... | collective-permute-start | bytes 294920 | tf_op jit(solution)/shard_map/ppermute | solution.py:335
  6.2 7.5 %collective-permute-start.4 = (bf16[64,256]{1,0:T(8,128)(2,1)S(1)}, bf16[64,256]{1,0:T(8,128)(2,1)S(1)}, u32[]{:S(2)}, u32[]{:S(2)}) collective-permute-start(bf16[64,256]{1,0:T(8,128)(2,1)S(1)} %get-tuple-element.33), channel_id=1, source_target_pairs={{0,8},{4,12},{8,16},{12,20},{16,24},{20,28},{24,0},{28,4},{1,9},{5... | collective-permute-start | bytes 98312 | tf_op jit(solution)/shard_map/ppermute | solution.py:361
  8.2 5.4 %collective-permute-start.5 = (bf16[64,256]{1,0:T(8,128)(2,1)S(1)}, bf16[64,256]{1,0:T(8,128)(2,1)S(1)}, u32[]{:S(2)}, u32[]{:S(2)}) collective-permute-start(bf16[64,256]{1,0:T(8,128)(2,1)S(1)} %get-tuple-element.34), channel_id=1, source_target_pairs={{0,16},{4,20},{8,24},{12,28},{16,0},{20,4},{24,8},{28,12},{1,17},{... | collective-permute-start | bytes 98312 | tf_op jit(solution)/shard_map/ppermute | solution.py:316
  11.0 3.9 %collective-permute-start.6 = (bf16[64,256]{1,0:T(8,128)(2,1)S(1)}, bf16[64,256]{1,0:T(8,128)(2,1)S(1)}, u32[]{:S(2)}, u32[]{:S(2)}) collective-permute-start(bf16[64,256]{1,0:T(8,128)(2,1)S(1)} %get-tuple-element.37), channel_id=1, source_target_pairs={{8,0},{12,4},{16,8},{20,12},{24,16},{28,20},{0,24},{4,28},{9,1},{1... | collective-permute-start | bytes 98312 | tf_op jit(solution)/shard_map/ppermute | solution.py:362
  15.4 3.6 %collective-permute-start.8 = (bf16[80,128]{1,0:T(8,128)(2,1)S(1)}, bf16[80,128]{1,0:T(8,128)(2,1)S(1)}, u32[]{:S(2)}, u32[]{:S(2)}) collective-permute-start(bf16[80,128]{1,0:T(8,128)(2,1)S(1)} %get-tuple-element.43), channel_id=1, source_target_pairs={{0,3},{1,2},{2,1},{3,0},{4,7},{5,6},{6,5},{7,4},{8,11},{9,10},{10,... | collective-permute-start | bytes 61448 | tf_op jit(solution)/shard_map/ppermute | solution.py:316
  15.5 3.8 %collective-permute-start.9 = (bf16[80,128]{1,0:T(8,128)(2,1)S(1)}, bf16[80,128]{1,0:T(8,128)(2,1)S(1)}, u32[]{:S(2)}, u32[]{:S(2)}) collective-permute-start(bf16[80,128]{1,0:T(8,128)(2,1)S(1)} %get-tuple-element.44), channel_id=1, source_target_pairs={{0,2},{1,3},{2,0},{3,1},{4,6},{5,7},{6,4},{7,5},{8,10},{9,11},{10,... | collective-permute-start | bytes 61448 | tf_op jit(solution)/shard_map/ppermute | solution.py:316
  17.1 1.8 %copy-start = (bf16[512,512]{1,0:T(8,128)(2,1)S(1)}, bf16[512,512]{1,0:T(8,128)(2,1)}, u32[]{:S(2)}) copy-start(bf16[512,512]{1,0:T(8,128)(2,1)} %weight.3) | copy-start | bytes 1572868
  17.6 1.2 %collective-permute-start.7 = (bf16[64,128]{1,0:T(8,128)(2,1)S(1)}, bf16[64,128]{1,0:T(8,128)(2,1)S(1)}, u32[]{:S(2)}, u32[]{:S(2)}) collective-permute-start(bf16[64,128]{1,0:T(8,128)(2,1)S(1)} %get-tuple-element.42), channel_id=1, source_target_pairs={{0,1},{1,0},{2,3},{3,2},{4,5},{5,4},{6,7},{7,6},{8,9},{9,8},{10,11... | collective-permute-start | bytes 49160 | tf_op jit(solution)/shard_map/ppermute | solution.py:316

commit v27 on v26

--- a/solution.py
+++ b/solution.py
@@ -161,7 +161,7 @@
     )
 
 
-def near_kernel(seq_size, queries, own, inner, outer, *rest):
+def near_kernel(seq_size, queries, own, outer, inner, *rest):
     *beside, scores, values, shared, keys, wide = rest
     me = lax.axis_index("seq")
     odd = me & 1
@@ -376,7 +376,7 @@
         ],
         [pltpu.VMEM((NEAR_ROWS, width), jnp.bfloat16), wide],
         flops=8 * LEAF * NEAR_ROWS * width,
-    )(own_queries, own, inner, outer, *beside)
+    )(own_queries, own, outer, inner, *beside)
     mid_rows = 4 * HALF if paired else HALF
     mid_scores, mid_values = kernel_call(
         mid_kernel,

time: 20.3 us -> 20.3 us (level)
  waiting for transfers between devices: 3.32 us -> 2.35 us
  starting transfers between devices: 13.1 us -> 14 us
    ppermute x1, waiting for transfers between devices: 1.1 us -> 0.01 us  [shards(): early = (lax.ppermute(upward, 'seq', shift), swap(eighth, 4))]
    ppermute x1, starting transfers between devices: 1.18 us -> 2.14 us  [shards(): lax.ppermute(downward, 'seq', [(target, source) for source, target in shi...]
    ppermute x6, waiting for transfers between devices: 1.22 us -> 1.68 us  [swap(): lax.ppermute(array, axis, [(i, i ^ bit) for i in range(lax.axis_size(axis...]
    ppermute x6, starting transfers between devices: 9.79 us -> 10.2 us  [swap(): lax.ppermute(array, axis, [(i, i ^ bit) for i in range(lax.axis_size(axis...]
    ppermute x1, starting transfers between devices: 2.04 us -> 1.63 us  [shards(): early = (lax.ppermute(upward, 'seq', shift), swap(eighth, 4))]
    ppermute x1, waiting for transfers between devices: 1 us -> 0.66 us  [shards(): lax.ppermute(downward, 'seq', [(target, source) for source, target in shi...]
where the time goes in v27:
time: 20.3 us; the launch traced here: 20.2 us
  starting transfers between devices  14 us (69%)
  Pallas kernels  3.69 us (18%)
  waiting for transfers between devices  2.35 us (12%)
    ppermute x6, starting transfers between devices, swap(): lax.ppermute(array, axis, [(i, i ^ bit) for i in range(lax.axis_size(axis...  10.2 us
    ppermute x1, starting transfers between devices, shards(): lax.ppermute(downward, 'seq', [(target, source) for source, target in shi...  2.14 us
    ppermute x6, waiting for transfers between devices, swap(): lax.ppermute(array, axis, [(i, i ^ bit) for i in range(lax.axis_size(axis...  1.68 us
    ppermute x1, starting transfers between devices, shards(): early = (lax.ppermute(upward, 'seq', shift), swap(eighth, 4))  1.63 us
    pallas_call x1, Pallas kernels, shards(): kernel_call(functools.partial(pack_kernel, not paired), 'pack', 16, [HBM]...  0.99 us
    pallas_call x1, Pallas kernels, shards(): kernel_call(project_kernel, 'project', 8, [VMEM] * 4, [(share, out_weight...  0.81 us
    ppermute x1, waiting for transfers between devices, shards(): lax.ppermute(downward, 'seq', [(target, source) for source, target in shi...  0.66 us
    pallas_call x1, Pallas kernels, shards(): kernel_call(functools.partial(leaves_kernel, seq_size, paired), 'leaves',...  0.53 us
  transfers between devices with their start and end apart: 10, of which 4 were waited for; matrix products, arithmetic and copies ran while one was open for 0% of the time, Pallas kernels for 7%

profile of v27, /device:TPU:0, one launch (start us, length us, event | category | flops | bytes accessed | tf_op | source)
XLA Modules:
  0.0 20.2 jit_solution(12266835816897705412)
XLA Ops:
  0.0 1.0 %pack.1 = (bf16[256,128]{1,0:T(8,128)(2,1)S(1)}, bf16[256,256]{1,0:T(8,128)(2,1)S(1)}, bf16[192,256]{1,0:T(8,128)(2,1)S(1)}, bf16[192,256]{1,0:T(8,128)(2,1)S(1)}, bf16[64,256]{1,0:T(8,128)(2,1)S(1)}) custom-call(bf16[256,128]{1,0:T(8,128)(2,1)} %queries.1, bf16[256,128]{1,0:T(8,128)(2,1)} %keys.1, bf16[256,128]{1,0:T(8,128)(2,1)} %values.1), custom_call_target="tpu_custom_call" | custom-call | bytes 1048576 | tf_op jit(solution)/shard_map/pack/pallas_call | solution.py:318
  1.0 3.0 %collective-permute-start.3 = (bf16[64,256]{1,0:T(8,128)(2,1)S(1)}, bf16[64,256]{1,0:T(8,128)(2,1)S(1)}, u32[]{:S(2)}, u32[]{:S(2)}) collective-permute-start(bf16[64,256]{1,0:T(8,128)(2,1)S(1)} %get-tuple-element.29.quarter), channel_id=1, source_target_pairs={{0,4},{4,0},{8,12},{12,8},{16,20},{20,16},{24,28},{28,24},{1,5},{5... | collective-permute-start | bytes 98312 | tf_op jit(solution)/shard_map/ppermute | solution.py:316
  4.0 0.1 collective-permute-start.2
  4.1 0.0 collective-permute-start
  4.1 3.4 %collective-permute-start.1 = (bf16[192,256]{1,0:T(8,128)(2,1)S(1)}, bf16[192,256]{1,0:T(8,128)(2,1)S(1)}, u32[]{:S(2)}, u32[]{:S(2)}) collective-permute-start(bf16[192,256]{1,0:T(8,128)(2,1)S(1)} %get-tuple-element.28), channel_id=1, source_target_pairs={{0,4},{4,0},{8,12},{12,8},{16,20},{20,16},{24,28},{28,24},{1,5},{5... | collective-permute-start | bytes 294920 | tf_op jit(solution)/shard_map/ppermute | solution.py:316
  7.5 0.0 collective-permute-done.3.theirs
  7.5 1.6 %collective-permute-start.4 = (bf16[64,256]{1,0:T(8,128)(2,1)S(1)}, bf16[64,256]{1,0:T(8,128)(2,1)S(1)}, u32[]{:S(2)}, u32[]{:S(2)}) collective-permute-start(bf16[64,256]{1,0:T(8,128)(2,1)S(1)} %get-tuple-element.33), channel_id=1, source_target_pairs={{0,8},{4,12},{8,16},{12,20},{16,24},{20,28},{24,0},{28,4},{1,9},{5... | collective-permute-start | bytes 98312 | tf_op jit(solution)/shard_map/ppermute | solution.py:361
  9.2 1.8 %collective-permute-start.5 = (bf16[64,256]{1,0:T(8,128)(2,1)S(1)}, bf16[64,256]{1,0:T(8,128)(2,1)S(1)}, u32[]{:S(2)}, u32[]{:S(2)}) collective-permute-start(bf16[64,256]{1,0:T(8,128)(2,1)S(1)} %get-tuple-element.34), channel_id=1, source_target_pairs={{0,16},{4,20},{8,24},{12,28},{16,0},{20,4},{24,8},{28,12},{1,17},{... | collective-permute-start | bytes 98312 | tf_op jit(solution)/shard_map/ppermute | solution.py:316
  11.0 0.0 collective-permute-done.2.rest_0_
  11.0 2.1 %collective-permute-start.6 = (bf16[64,256]{1,0:T(8,128)(2,1)S(1)}, bf16[64,256]{1,0:T(8,128)(2,1)S(1)}, u32[]{:S(2)}, u32[]{:S(2)}) collective-permute-start(bf16[64,256]{1,0:T(8,128)(2,1)S(1)} %get-tuple-element.37), channel_id=1, source_target_pairs={{8,0},{12,4},{16,8},{20,12},{24,16},{28,20},{0,24},{4,28},{9,1},{1... | collective-permute-start | bytes 98312 | tf_op jit(solution)/shard_map/ppermute | solution.py:362
  13.1 0.0 collective-permute-done.outer
  13.1 0.0 collective-permute-done.1.inner
  13.1 0.4 %near.1 = (f32[2,256,512]{2,1,0:T(8,128)S(1)}, bf16[2,512,128]{2,1,0:T(8,128)(2,1)S(1)}, bf16[128,256]{1,0:T(8,128)(2,1)S(1)}) custom-call(bf16[256,128]{1,0:T(8,128)(2,1)S(1)} %get-tuple-element.25.queries, bf16[256,256]{1,0:T(8,128)(2,1)S(1)} %get-tuple-element.26.own, bf16[192,256]{1,0:T(8,128)(2,1)S(1)} %collective-permute-done.outer, ...), custom_call_target="tpu_custom_call" | custom-call | flops 67108864 | bytes 1048576 | tf_op jit(solution)/shard_map/near/pallas_call | solution.py:367
  13.5 0.0 collective-permute-done.4.rest_0_
  13.5 0.5 %collective-permute-done.5.rest_1_ = bf16[64,256]{1,0:T(8,128)(2,1)S(1)} collective-permute-done((bf16[64,256]{1,0:T(8,128)(2,1)S(1)}, bf16[64,256]{1,0:T(8,128)(2,1)S(1)}, u32[]{:S(2)}, u32[]{:S(2)}) %collective-permute-start.5) | collective-permute-done | bytes 32800 | tf_op jit(solution)/shard_map/ppermute | solution.py:316
  14.0 0.2 %mid.1 = (f32[2,256,256]{2,1,0:T(8,128)S(1)}, bf16[256,128]{1,0:T(8,128)(2,1)S(1)}) custom-call(bf16[256,128]{1,0:T(8,128)(2,1)S(1)} %get-tuple-element.25.queries, bf16[128,256]{1,0:T(8,128)(2,1)S(1)} %get-tuple-element.32.shared, bf16[64,256]{1,0:T(8,128)(2,1)S(1)} %collective-permute-done.4.rest_0_, bf16[64,256]{1,0:T(8,128)(2,1)S(1)} %collective-permute-done.5.rest_1_), custom_call_target="tpu_custom_call" | custom-call | flops 1000000000 | bytes 1048576 | tf_op jit(solution)/shard_map/mid/pallas_call | solution.py:381
  14.2 0.7 %collective-permute-done.6.rest_0_ = bf16[64,256]{1,0:T(8,128)(2,1)S(1)} collective-permute-done((bf16[64,256]{1,0:T(8,128)(2,1)S(1)}, bf16[64,256]{1,0:T(8,128)(2,1)S(1)}, u32[]{:S(2)}, u32[]{:S(2)}) %collective-permute-start.6) | collective-permute-done | bytes 32800 | tf_op jit(solution)/shard_map/ppermute | solution.py:362
  14.9 0.5 %leaves.1 = (bf16[80,128]{1,0:T(8,128)(2,1)S(1)}, bf16[80,128]{1,0:T(8,128)(2,1)S(1)}, bf16[64,128]{1,0:T(8,128)(2,1)S(1)}, bf16[64,128]{1,0:T(8,128)(2,1)S(1)}, f32[8,64]{1,0:T(8,128)S(1)}) custom-call(bf16[256,128]{1,0:T(8,128)(2,1)S(1)} %get-tuple-element.25.queries, f32[2,256,512]{2,1,0:T(8,128)S(1)} %get-tuple-element.30.near_scores, ...), custom_call_target="tpu_custom_call" | custom-call | flops 109051904 | bytes 1048576 | tf_op jit(solution)/shard_map/leaves/pallas_call | solution.py:393
  15.4 0.1 collective-permute-start.8
  15.5 1.6 %collective-permute-start.9 = (bf16[80,128]{1,0:T(8,128)(2,1)S(1)}, bf16[80,128]{1,0:T(8,128)(2,1)S(1)}, u32[]{:S(2)}, u32[]{:S(2)}) collective-permute-start(bf16[80,128]{1,0:T(8,128)(2,1)S(1)} %get-tuple-element.44), channel_id=1, source_target_pairs={{0,2},{1,3},{2,0},{3,1},{4,6},{5,7},{6,4},{7,5},{8,10},{9,11},{10,... | collective-permute-start | bytes 61448 | tf_op jit(solution)/shard_map/ppermute | solution.py:316
  17.1 0.0 copy-start
  17.1 0.5 %stays.1 = (bf16[64,128]{1,0:T(8,128)(2,1)S(1)}, bf16[64,128]{1,0:T(8,128)(2,1)S(1)}) custom-call(bf16[256,128]{1,0:T(8,128)(2,1)S(1)} %get-tuple-element.25.queries, f32[2,256,512]{2,1,0:T(8,128)S(1)} %get-tuple-element.30.near_scores, bf16[2,512,128]{2,1,0:T(8,128)(2,1)S(1)} %get-tuple-element.31.near_values, ...), custom_call_target="tpu_custom_call" | custom-call | flops 109051904 | bytes 1048576 | tf_op jit(solution)/shard_map/stays/pallas_call | solution.py:408
  17.6 0.3 %collective-permute-start.7 = (bf16[64,128]{1,0:T(8,128)(2,1)S(1)}, bf16[64,128]{1,0:T(8,128)(2,1)S(1)}, u32[]{:S(2)}, u32[]{:S(2)}) collective-permute-start(bf16[64,128]{1,0:T(8,128)(2,1)S(1)} %get-tuple-element.42), channel_id=1, source_target_pairs={{0,1},{1,0},{2,3},{3,2},{4,5},{5,4},{6,7},{7,6},{8,9},{9,8},{10,11... | collective-permute-start | bytes 49160 | tf_op jit(solution)/shard_map/ppermute | solution.py:316
  18.0 0.9 %collective-permute-done.7.other = bf16[64,128]{1,0:T(8,128)(2,1)S(1)} collective-permute-done((bf16[64,128]{1,0:T(8,128)(2,1)S(1)}, bf16[64,128]{1,0:T(8,128)(2,1)S(1)}, u32[]{:S(2)}, u32[]{:S(2)}) %collective-permute-start.7) | collective-permute-done | bytes 16416 | tf_op jit(solution)/shard_map/ppermute | solution.py:316
  18.9 0.0 copy-done
  18.9 0.2 begin.1.partial
  19.0 0.0 collective-permute-done.8.other
  19.1 0.3 %collective-permute-done.9.same = bf16[80,128]{1,0:T(8,128)(2,1)S(1)} collective-permute-done((bf16[80,128]{1,0:T(8,128)(2,1)S(1)}, bf16[80,128]{1,0:T(8,128)(2,1)S(1)}, u32[]{:S(2)}, u32[]{:S(2)}) %collective-permute-start.9) | collective-permute-done | bytes 20512 | tf_op jit(solution)/shard_map/ppermute | solution.py:316
  19.3 0.8 %project.1 = bf16[64,512]{1,0:T(8,128)(2,1)} custom-call(f32[64,512]{1,0:T(8,128)S(1)} %begin.1.partial, bf16[80,128]{1,0:T(8,128)(2,1)S(1)} %collective-permute-done.8.other, bf16[80,128]{1,0:T(8,128)(2,1)S(1)} %collective-permute-done.9.same, bf16[512,512]{1,0:T(8,128)(2,1)S(1)} %copy-done), custom_call_target="tpu_custom_call" | custom-call | bytes 1048576 | tf_op jit(solution)/shard_map/project/pallas_call | solution.py:421
  (1 shorter events, 0.0 us)
Async XLA Ops:
  1.0 6.5 %collective-permute-start.3 = (bf16[64,256]{1,0:T(8,128)(2,1)S(1)}, bf16[64,256]{1,0:T(8,128)(2,1)S(1)}, u32[]{:S(2)}, u32[]{:S(2)}) collective-permute-start(bf16[64,256]{1,0:T(8,128)(2,1)S(1)} %get-tuple-element.29.quarter), channel_id=1, source_target_pairs={{0,4},{4,0},{8,12},{12,8},{16,20},{20,16},{24,28},{28,24},{1,5},{5... | collective-permute-start | bytes 98312 | tf_op jit(solution)/shard_map/ppermute | solution.py:316
  4.0 7.0 %collective-permute-start.2 = (bf16[64,256]{1,0:T(8,128)(2,1)S(1)}, bf16[64,256]{1,0:T(8,128)(2,1)S(1)}, u32[]{:S(2)}, u32[]{:S(2)}) collective-permute-start(bf16[64,256]{1,0:T(8,128)(2,1)S(1)} %get-tuple-element.29.quarter), channel_id=1, source_target_pairs={{4,12},{8,0},{12,20},{16,8},{20,28},{24,16},{0,4},{28,24},{5,13},{... | collective-permute-start | bytes 98312 | tf_op jit(solution)/shard_map/ppermute | solution.py:360
  4.1 9.0 %collective-permute-start = (bf16[192,256]{1,0:T(8,128)(2,1)S(1)}, bf16[192,256]{1,0:T(8,128)(2,1)S(1)}, u32[]{:S(2)}, u32[]{:S(2)}) collective-permute-start(bf16[192,256]{1,0:T(8,128)(2,1)S(1)} %get-tuple-element.27), channel_id=1, source_target_pairs={{0,1},{1,0},{2,3},{3,2},{4,8},{5,9},{6,10},{7,11},{8,4},{9,5},{10,... | collective-permute-start | bytes 294920 | tf_op jit(solution)/shard_map/ppermute | solution.py:335
  4.1 9.0 %collective-permute-start.1 = (bf16[192,256]{1,0:T(8,128)(2,1)S(1)}, bf16[192,256]{1,0:T(8,128)(2,1)S(1)}, u32[]{:S(2)}, u32[]{:S(2)}) collective-permute-start(bf16[192,256]{1,0:T(8,128)(2,1)S(1)} %get-tuple-element.28), channel_id=1, source_target_pairs={{0,4},{4,0},{8,12},{12,8},{16,20},{20,16},{24,28},{28,24},{1,5},{5... | collective-permute-start | bytes 294920 | tf_op jit(solution)/shard_map/ppermute | solution.py:316
  7.5 6.0 %collective-permute-start.4 = (bf16[64,256]{1,0:T(8,128)(2,1)S(1)}, bf16[64,256]{1,0:T(8,128)(2,1)S(1)}, u32[]{:S(2)}, u32[]{:S(2)}) collective-permute-start(bf16[64,256]{1,0:T(8,128)(2,1)S(1)} %get-tuple-element.33), channel_id=1, source_target_pairs={{0,8},{4,12},{8,16},{12,20},{16,24},{20,28},{24,0},{28,4},{1,9},{5... | collective-permute-start | bytes 98312 | tf_op jit(solution)/shard_map/ppermute | solution.py:361
  9.2 4.8 %collective-permute-start.5 = (bf16[64,256]{1,0:T(8,128)(2,1)S(1)}, bf16[64,256]{1,0:T(8,128)(2,1)S(1)}, u32[]{:S(2)}, u32[]{:S(2)}) collective-permute-start(bf16[64,256]{1,0:T(8,128)(2,1)S(1)} %get-tuple-element.34), channel_id=1, source_target_pairs={{0,16},{4,20},{8,24},{12,28},{16,0},{20,4},{24,8},{28,12},{1,17},{... | collective-permute-start | bytes 98312 | tf_op jit(solution)/shard_map/ppermute | solution.py:316
  11.0 3.9 %collective-permute-start.6 = (bf16[64,256]{1,0:T(8,128)(2,1)S(1)}, bf16[64,256]{1,0:T(8,128)(2,1)S(1)}, u32[]{:S(2)}, u32[]{:S(2)}) collective-permute-start(bf16[64,256]{1,0:T(8,128)(2,1)S(1)} %get-tuple-element.37), channel_id=1, source_target_pairs={{8,0},{12,4},{16,8},{20,12},{24,16},{28,20},{0,24},{4,28},{9,1},{1... | collective-permute-start | bytes 98312 | tf_op jit(solution)/shard_map/ppermute | solution.py:362
  15.4 3.6 %collective-permute-start.8 = (bf16[80,128]{1,0:T(8,128)(2,1)S(1)}, bf16[80,128]{1,0:T(8,128)(2,1)S(1)}, u32[]{:S(2)}, u32[]{:S(2)}) collective-permute-start(bf16[80,128]{1,0:T(8,128)(2,1)S(1)} %get-tuple-element.43), channel_id=1, source_target_pairs={{0,3},{1,2},{2,1},{3,0},{4,7},{5,6},{6,5},{7,4},{8,11},{9,10},{10,... | collective-permute-start | bytes 61448 | tf_op jit(solution)/shard_map/ppermute | solution.py:316
  15.5 3.8 %collective-permute-start.9 = (bf16[80,128]{1,0:T(8,128)(2,1)S(1)}, bf16[80,128]{1,0:T(8,128)(2,1)S(1)}, u32[]{:S(2)}, u32[]{:S(2)}) collective-permute-start(bf16[80,128]{1,0:T(8,128)(2,1)S(1)} %get-tuple-element.44), channel_id=1, source_target_pairs={{0,2},{1,3},{2,0},{3,1},{4,6},{5,7},{6,4},{7,5},{8,10},{9,11},{10,... | collective-permute-start | bytes 61448 | tf_op jit(solution)/shard_map/ppermute | solution.py:316
  17.1 1.8 %copy-start = (bf16[512,512]{1,0:T(8,128)(2,1)S(1)}, bf16[512,512]{1,0:T(8,128)(2,1)}, u32[]{:S(2)}) copy-start(bf16[512,512]{1,0:T(8,128)(2,1)} %weight.3) | copy-start | bytes 1572868
  17.6 1.2 %collective-permute-start.7 = (bf16[64,128]{1,0:T(8,128)(2,1)S(1)}, bf16[64,128]{1,0:T(8,128)(2,1)S(1)}, u32[]{:S(2)}, u32[]{:S(2)}) collective-permute-start(bf16[64,128]{1,0:T(8,128)(2,1)S(1)} %get-tuple-element.42), channel_id=1, source_target_pairs={{0,1},{1,0},{2,3},{3,2},{4,5},{5,4},{6,7},{7,6},{8,9},{9,8},{10,11... | collective-permute-start | bytes 49160 | tf_op jit(solution)/shard_map/ppermute | solution.py:316

commit v28 on v26

--- a/solution.py
+++ b/solution.py
@@ -54,14 +54,16 @@
         quarter[...] = level_two
 
 
-def join_kernel(theirs, quarter, upward, downward, eighth, wide):
+def join_kernel(theirs, quarter, upward, third, fourth, eighth, wide):
     me = lax.axis_index("seq")
     odd = me & 1
+    pair = me >> 1
     first = jnp.where(odd == 1, theirs[...], quarter[...])
     second = jnp.where(odd == 1, quarter[...], theirs[...])
     level_three = average_pairs(jnp.concatenate([first, second], axis=0), wide)
-    upward[...] = jnp.where(me >= 6, level_three, first)
-    downward[...] = jnp.where(me < 2, level_three, second)
+    upward[...] = jnp.where(pair == 3, level_three, first)
+    third[...] = jnp.where(pair == 1, second, level_three)
+    fourth[...] = jnp.where(pair == 1, level_three, second)
     eighth[...] = level_three
 
 
@@ -71,7 +73,7 @@
 
 def last_row_count(seq_size, paired):
     if paired:
-        return HALF
+        return LEAF
     rows = 0
     for far in range(1, seq_size.bit_length() - 1):
         if seq_size >> far == 2:
@@ -125,10 +127,18 @@
     return pieces
 
 
-def early_pieces(beside, lower, eighth):
+def early_pieces(beside, lower):
     me = lax.axis_index("seq")
     has_beside = jnp.where((me & 1) == 1, me >= 2, me < 6)
-    return [(beside, bias_of(has_beside)), (lower, None), (eighth, None)]
+    return [(beside, bias_of(has_beside)), (lower, None)]
+
+
+def late_pieces(second, third, fourth):
+    pair = lax.axis_index("seq") >> 1
+    return [
+        (jnp.where(pair == 2, third[...], second[...]), None),
+        (jnp.where(pair == 0, third[...], fourth[...]), None),
+    ]
 
 
 def place(pieces, values, keys):
@@ -235,8 +245,8 @@
 
 
 def leaves_kernel(seq_size, paired, queries, near_scores, near_values, mid_scores, mid_values, *rest):
-    late, same, other, keys, values, bias, wide = rest
-    pieces = [(late, None)] if paired else gathered_pieces(seq_size, late, wide)
+    *late, same, other, keys, values, bias, wide = rest
+    pieces = late_pieces(*late) if paired else gathered_pieces(seq_size, late[0], wide)
     bias[...] = jnp.broadcast_to(place(pieces, values, keys), bias.shape)
     leaf = (lax.axis_index("head") >> 1) ^ 1
     scored = (near_scores, near_values, mid_scores, mid_values)
@@ -345,24 +355,31 @@
     last = seq_size - 1
     outer = to_spans(outer, [s if s in (0, last) else s + 1 if s & 1 else s - 1 for s in range(seq_size)])
     if paired:
-        upward, downward, eighth = kernel_call(
+        upward, third, fourth, eighth = kernel_call(
             join_kernel,
             "join",
             8,
             [VMEM] * 2,
-            [(HALF, pair_width)] * 3,
+            [(HALF, pair_width)] * 4,
             [wide],
             flops=2 * 10**9,
         )(swap(quarter, 1), quarter)
-        shift = [(i, (i + 2) % seq_size) for i in range(seq_size)]
+
+        def over_pairs(array, targets):
+            return to_spans(array, [2 * t + x for t in targets for x in range(2)])
+
         cycle = [(i, i + 2 if i & 1 else i - 2) for i in range(1, seq_size - 1)]
         cycle += [(0, 1), (seq_size - 1, seq_size - 2)]
         beside = (lax.ppermute(quarter, "seq", cycle),)
-        early = (lax.ppermute(upward, "seq", shift), swap(eighth, 4))
-        late = lax.ppermute(downward, "seq", [(target, source) for source, target in shift])
+        early = (over_pairs(upward, (1, 2, 3, 0)),)
+        late = (
+            over_pairs(eighth, (3, 2, 0, 1)),
+            over_pairs(third, (2, 0, 3, 1)),
+            over_pairs(fourth, (0, 3, 1, 2)),
+        )
     else:
         beside, early = (), ()
-        late = lax.all_to_all(quarter, "seq", split_axis=0, concat_axis=0)
+        late = (lax.all_to_all(quarter, "seq", split_axis=0, concat_axis=0),)
     share = tokens // head_size
     near_scores, near_values, shared = kernel_call(
         functools.partial(near_kernel, seq_size),
@@ -377,7 +394,7 @@
         [pltpu.VMEM((NEAR_ROWS, width), jnp.bfloat16), wide],
         flops=8 * LEAF * NEAR_ROWS * width,
     )(own_queries, own, inner, outer, *beside)
-    mid_rows = 4 * HALF if paired else HALF
+    mid_rows = 3 * HALF if paired else HALF
     mid_scores, mid_values = kernel_call(
         mid_kernel,
         "mid",
@@ -394,7 +411,7 @@
         functools.partial(leaves_kernel, seq_size, paired),
         "leaves",
         24,
-        [VMEM] * 6,
+        [VMEM] * (5 + len(late)),
         [
             (share + PAD, width),
             (share + PAD, width),
@@ -404,7 +421,7 @@
         ],
         [wide],
         flops=leaf_flops,
-    )(own_queries, *scored, late)
+    )(own_queries, *scored, *late)
     share_0, share_1 = kernel_call(
         stays_kernel, "stays", 16, [VMEM] * 8, [(share, width)] * 2, [], flops=leaf_flops
     )(own_queries, *scored, far_keys, far_values, far_bias)

time: 20.3 us -> 20.5 us (level)
  the two profiles are of different devices: /device:TPU:0 before, /device:TPU:11 now
where the time goes in v28:
time: 20.5 us; the launch traced here: 20.4 us
  starting transfers between devices  13.7 us (67%)
  Pallas kernels  3.75 us (18%)
  waiting for transfers between devices  2.9 us (14%)
    ppermute x5, starting transfers between devices, to_spans(): lax.ppermute(array, ('seq', 'head'), [(s * head_size + h, t * head_size +...  6.53 us
    ppermute x5, starting transfers between devices, swap(): lax.ppermute(array, axis, [(i, i ^ bit) for i in range(lax.axis_size(axis...  5.84 us
    ppermute x5, waiting for transfers between devices, to_spans(): lax.ppermute(array, ('seq', 'head'), [(s * head_size + h, t * head_size +...  1.54 us
    ppermute x5, waiting for transfers between devices, swap(): lax.ppermute(array, axis, [(i, i ^ bit) for i in range(lax.axis_size(axis...  1.36 us
    ppermute x1, starting transfers between devices, shards(): beside = (lax.ppermute(quarter, 'seq', cycle),)  1.3 us
    pallas_call x1, Pallas kernels, shards(): kernel_call(functools.partial(pack_kernel, not paired), 'pack', 16, [HBM]...  0.99 us
    pallas_call x1, Pallas kernels, shards(): kernel_call(project_kernel, 'project', 8, [VMEM] * 4, [(share, out_weight...  0.81 us
    pallas_call x1, Pallas kernels, shards(): kernel_call(functools.partial(leaves_kernel, seq_size, paired), 'leaves',...  0.56 us
  transfers between devices with their start and end apart: 11, of which 5 were waited for; matrix products, arithmetic and copies ran while one was open for 0% of the time, Pallas kernels for 7%

profile of v28, /device:TPU:11, one launch (start us, length us, event | category | flops | bytes accessed | tf_op | source)
XLA Modules:
  0.0 20.4 jit_solution(11609243750344605222)
XLA Ops:
  0.0 1.0 %pack.1 = (bf16[256,128]{1,0:T(8,128)(2,1)S(1)}, bf16[256,256]{1,0:T(8,128)(2,1)S(1)}, bf16[192,256]{1,0:T(8,128)(2,1)S(1)}, bf16[192,256]{1,0:T(8,128)(2,1)S(1)}, bf16[64,256]{1,0:T(8,128)(2,1)S(1)}) custom-call(bf16[256,128]{1,0:T(8,128)(2,1)} %queries.1, bf16[256,128]{1,0:T(8,128)(2,1)} %keys.1, bf16[256,128]{1,0:T(8,128)(2,1)} %values.1), custom_call_target="tpu_custom_call" | custom-call | bytes 1048576 | tf_op jit(solution)/shard_map/pack/pallas_call | solution.py:328
  1.0 0.3 %collective-permute-start.3 = (bf16[64,256]{1,0:T(8,128)(2,1)S(1)}, bf16[64,256]{1,0:T(8,128)(2,1)S(1)}, u32[]{:S(2)}, u32[]{:S(2)}) collective-permute-start(bf16[64,256]{1,0:T(8,128)(2,1)S(1)} %get-tuple-element.30.quarter), channel_id=1, source_target_pairs={{0,4},{4,0},{8,12},{12,8},{16,20},{20,16},{24,28},{28,24},{1,5},{5... | collective-permute-start | bytes 98312 | tf_op jit(solution)/shard_map/ppermute | solution.py:326
  1.3 1.3 %collective-permute-start.2 = (bf16[64,256]{1,0:T(8,128)(2,1)S(1)}, bf16[64,256]{1,0:T(8,128)(2,1)S(1)}, u32[]{:S(2)}, u32[]{:S(2)}) collective-permute-start(bf16[64,256]{1,0:T(8,128)(2,1)S(1)} %get-tuple-element.30.quarter), channel_id=1, source_target_pairs={{4,12},{8,0},{12,20},{16,8},{20,28},{24,16},{0,4},{28,24},{5,13},{... | collective-permute-start | bytes 98312 | tf_op jit(solution)/shard_map/ppermute | solution.py:373
  2.6 0.1 collective-permute-start
  2.7 2.4 %collective-permute-start.1 = (bf16[192,256]{1,0:T(8,128)(2,1)S(1)}, bf16[192,256]{1,0:T(8,128)(2,1)S(1)}, u32[]{:S(2)}, u32[]{:S(2)}) collective-permute-start(bf16[192,256]{1,0:T(8,128)(2,1)S(1)} %get-tuple-element.29), channel_id=1, source_target_pairs={{0,1},{1,0},{2,3},{3,2},{4,8},{5,9},{6,10},{7,11},{8,4},{9,5},{10,... | collective-permute-start | bytes 294920 | tf_op jit(solution)/shard_map/ppermute | solution.py:345
  5.1 0.0 collective-permute-done.3.theirs
  5.1 1.3 %collective-permute-start.4 = (bf16[64,256]{1,0:T(8,128)(2,1)S(1)}, bf16[64,256]{1,0:T(8,128)(2,1)S(1)}, u32[]{:S(2)}, u32[]{:S(2)}) collective-permute-start(bf16[64,256]{1,0:T(8,128)(2,1)S(1)} %get-tuple-element.34), channel_id=1, source_target_pairs={{0,8},{1,9},{2,10},{3,11},{4,12},{5,13},{6,14},{7,15},{8,16},{9,17... | collective-permute-start | bytes 98312 | tf_op jit(solution)/shard_map/ppermute | solution.py:345
  6.4 0.5 %collective-permute-start.5 = (bf16[64,256]{1,0:T(8,128)(2,1)S(1)}, bf16[64,256]{1,0:T(8,128)(2,1)S(1)}, u32[]{:S(2)}, u32[]{:S(2)}) collective-permute-start(bf16[64,256]{1,0:T(8,128)(2,1)S(1)} %get-tuple-element.37), channel_id=1, source_target_pairs={{0,24},{1,25},{2,26},{3,27},{4,28},{5,29},{6,30},{7,31},{8,16},{9,... | collective-permute-start | bytes 98312 | tf_op jit(solution)/shard_map/ppermute | solution.py:345
  6.9 0.0 collective-permute-done.2.rest_0_
  6.9 1.7 %collective-permute-start.6 = (bf16[64,256]{1,0:T(8,128)(2,1)S(1)}, bf16[64,256]{1,0:T(8,128)(2,1)S(1)}, u32[]{:S(2)}, u32[]{:S(2)}) collective-permute-start(bf16[64,256]{1,0:T(8,128)(2,1)S(1)} %get-tuple-element.38), channel_id=1, source_target_pairs={{0,16},{1,17},{2,18},{3,19},{4,20},{5,21},{6,22},{7,23},{8,0},{9,1... | collective-permute-start | bytes 98312 | tf_op jit(solution)/shard_map/ppermute | solution.py:345
  8.6 0.0 collective-permute-done.inner
  8.6 0.6 %collective-permute-start.7 = (bf16[64,256]{1,0:T(8,128)(2,1)S(1)}, bf16[64,256]{1,0:T(8,128)(2,1)S(1)}, u32[]{:S(2)}, u32[]{:S(2)}) collective-permute-start(bf16[64,256]{1,0:T(8,128)(2,1)S(1)} %get-tuple-element.39), channel_id=1, source_target_pairs={{0,1},{1,0},{2,3},{3,2},{4,5},{5,4},{6,7},{7,6},{8,24},{9,25},{10,... | collective-permute-start | bytes 98312 | tf_op jit(solution)/shard_map/ppermute | solution.py:345
  9.3 0.0 collective-permute-done.1.outer
  9.3 0.4 %near.1 = (f32[2,256,512]{2,1,0:T(8,128)S(1)}, bf16[2,512,128]{2,1,0:T(8,128)(2,1)S(1)}, bf16[128,256]{1,0:T(8,128)(2,1)S(1)}) custom-call(bf16[256,128]{1,0:T(8,128)(2,1)S(1)} %get-tuple-element.26.queries, bf16[256,256]{1,0:T(8,128)(2,1)S(1)} %get-tuple-element.27.own, bf16[192,256]{1,0:T(8,128)(2,1)S(1)} %collective-permute-done.inner, ...), custom_call_target="tpu_custom_call" | custom-call | flops 67108864 | bytes 1048576 | tf_op jit(solution)/shard_map/near/pallas_call | solution.py:384
  9.7 0.0 collective-permute-done.4.rest_0_
  9.7 0.2 %mid.1 = (f32[2,256,192]{2,1,0:T(8,128)S(1)}, bf16[192,128]{1,0:T(8,128)(2,1)S(1)}) custom-call(bf16[256,128]{1,0:T(8,128)(2,1)S(1)} %get-tuple-element.26.queries, bf16[128,256]{1,0:T(8,128)(2,1)S(1)} %get-tuple-element.33.shared, bf16[64,256]{1,0:T(8,128)(2,1)S(1)} %collective-permute-done.4.rest_0_), custom_call_target="tpu_custom_call" | custom-call | flops 1000000000 | bytes 1048576 | tf_op jit(solution)/shard_map/mid/pallas_call | solution.py:398
  9.9 0.3 %collective-permute-done.5.rest_0_ = bf16[64,256]{1,0:T(8,128)(2,1)S(1)} collective-permute-done((bf16[64,256]{1,0:T(8,128)(2,1)S(1)}, bf16[64,256]{1,0:T(8,128)(2,1)S(1)}, u32[]{:S(2)}, u32[]{:S(2)}) %collective-permute-start.5) | collective-permute-done | bytes 32800 | tf_op jit(solution)/shard_map/ppermute | solution.py:345
  10.3 0.3 %collective-permute-done.6.rest_1_ = bf16[64,256]{1,0:T(8,128)(2,1)S(1)} collective-permute-done((bf16[64,256]{1,0:T(8,128)(2,1)S(1)}, bf16[64,256]{1,0:T(8,128)(2,1)S(1)}, u32[]{:S(2)}, u32[]{:S(2)}) %collective-permute-start.6) | collective-permute-done | bytes 32800 | tf_op jit(solution)/shard_map/ppermute | solution.py:345
  10.6 0.9 %collective-permute-done.7.rest_2_ = bf16[64,256]{1,0:T(8,128)(2,1)S(1)} collective-permute-done((bf16[64,256]{1,0:T(8,128)(2,1)S(1)}, bf16[64,256]{1,0:T(8,128)(2,1)S(1)}, u32[]{:S(2)}, u32[]{:S(2)}) %collective-permute-start.7) | collective-permute-done | bytes 32800 | tf_op jit(solution)/shard_map/ppermute | solution.py:345
  11.5 0.6 %leaves.1 = (bf16[80,128]{1,0:T(8,128)(2,1)S(1)}, bf16[80,128]{1,0:T(8,128)(2,1)S(1)}, bf16[128,128]{1,0:T(8,128)(2,1)S(1)}, bf16[128,128]{1,0:T(8,128)(2,1)S(1)}, f32[8,128]{1,0:T(8,128)S(1)}) custom-call(bf16[256,128]{1,0:T(8,128)(2,1)S(1)} %get-tuple-element.26.queries, f32[2,256,512]{2,1,0:T(8,128)S(1)} %get-tuple-element.31.near_scores, ...), custom_call_target="tpu_custom_call" | custom-call | flops 109051904 | bytes 1048576 | tf_op jit(solution)/shard_map/leaves/pallas_call | solution.py:410
  12.0 4.9 %collective-permute-start.9 = (bf16[80,128]{1,0:T(8,128)(2,1)S(1)}, bf16[80,128]{1,0:T(8,128)(2,1)S(1)}, u32[]{:S(2)}, u32[]{:S(2)}) collective-permute-start(bf16[80,128]{1,0:T(8,128)(2,1)S(1)} %get-tuple-element.45), channel_id=1, source_target_pairs={{0,3},{1,2},{2,1},{3,0},{4,7},{5,6},{6,5},{7,4},{8,11},{9,10},{10,... | collective-permute-start | bytes 61448 | tf_op jit(solution)/shard_map/ppermute | solution.py:326
  16.9 0.2 %collective-permute-start.10 = (bf16[80,128]{1,0:T(8,128)(2,1)S(1)}, bf16[80,128]{1,0:T(8,128)(2,1)S(1)}, u32[]{:S(2)}, u32[]{:S(2)}) collective-permute-start(bf16[80,128]{1,0:T(8,128)(2,1)S(1)} %get-tuple-element.46), channel_id=1, source_target_pairs={{0,2},{1,3},{2,0},{3,1},{4,6},{5,7},{6,4},{7,5},{8,10},{9,11},{10,... | collective-permute-start | bytes 61448 | tf_op jit(solution)/shard_map/ppermute | solution.py:326
  17.2 0.0 copy-start
  17.2 0.5 %stays.1 = (bf16[64,128]{1,0:T(8,128)(2,1)S(1)}, bf16[64,128]{1,0:T(8,128)(2,1)S(1)}) custom-call(bf16[256,128]{1,0:T(8,128)(2,1)S(1)} %get-tuple-element.26.queries, f32[2,256,512]{2,1,0:T(8,128)S(1)} %get-tuple-element.31.near_scores, bf16[2,512,128]{2,1,0:T(8,128)(2,1)S(1)} %get-tuple-element.32.near_values, ...), custom_call_target="tpu_custom_call" | custom-call | flops 109051904 | bytes 1048576 | tf_op jit(solution)/shard_map/stays/pallas_call | solution.py:425
  17.7 0.3 %collective-permute-start.8 = (bf16[64,128]{1,0:T(8,128)(2,1)S(1)}, bf16[64,128]{1,0:T(8,128)(2,1)S(1)}, u32[]{:S(2)}, u32[]{:S(2)}) collective-permute-start(bf16[64,128]{1,0:T(8,128)(2,1)S(1)} %get-tuple-element.44), channel_id=1, source_target_pairs={{0,1},{1,0},{2,3},{3,2},{4,5},{5,4},{6,7},{7,6},{8,9},{9,8},{10,11... | collective-permute-start | bytes 49160 | tf_op jit(solution)/shard_map/ppermute | solution.py:326
  18.0 0.9 %collective-permute-done.8.other = bf16[64,128]{1,0:T(8,128)(2,1)S(1)} collective-permute-done((bf16[64,128]{1,0:T(8,128)(2,1)S(1)}, bf16[64,128]{1,0:T(8,128)(2,1)S(1)}, u32[]{:S(2)}, u32[]{:S(2)}) %collective-permute-start.8) | collective-permute-done | bytes 16416 | tf_op jit(solution)/shard_map/ppermute | solution.py:326
  19.0 0.0 copy-done
  19.0 0.2 begin.1.partial
  19.2 0.0 collective-permute-done.9.other
  19.2 0.4 %collective-permute-done.10.same = bf16[80,128]{1,0:T(8,128)(2,1)S(1)} collective-permute-done((bf16[80,128]{1,0:T(8,128)(2,1)S(1)}, bf16[80,128]{1,0:T(8,128)(2,1)S(1)}, u32[]{:S(2)}, u32[]{:S(2)}) %collective-permute-start.10) | collective-permute-done | bytes 20512 | tf_op jit(solution)/shard_map/ppermute | solution.py:326
  19.6 0.8 %project.1 = bf16[64,512]{1,0:T(8,128)(2,1)} custom-call(f32[64,512]{1,0:T(8,128)S(1)} %begin.1.partial, bf16[80,128]{1,0:T(8,128)(2,1)S(1)} %collective-permute-done.9.other, bf16[80,128]{1,0:T(8,128)(2,1)S(1)} %collective-permute-done.10.same, bf16[512,512]{1,0:T(8,128)(2,1)S(1)} %copy-done), custom_call_target="tpu_custom_call" | custom-call | bytes 1048576 | tf_op jit(solution)/shard_map/project/pallas_call | solution.py:438
  (1 shorter events, 0.0 us)
Async XLA Ops:
  1.0 4.1 %collective-permute-start.3 = (bf16[64,256]{1,0:T(8,128)(2,1)S(1)}, bf16[64,256]{1,0:T(8,128)(2,1)S(1)}, u32[]{:S(2)}, u32[]{:S(2)}) collective-permute-start(bf16[64,256]{1,0:T(8,128)(2,1)S(1)} %get-tuple-element.30.quarter), channel_id=1, source_target_pairs={{0,4},{4,0},{8,12},{12,8},{16,20},{20,16},{24,28},{28,24},{1,5},{5... | collective-permute-start | bytes 98312 | tf_op jit(solution)/shard_map/ppermute | solution.py:326
  1.3 5.6 %collective-permute-start.2 = (bf16[64,256]{1,0:T(8,128)(2,1)S(1)}, bf16[64,256]{1,0:T(8,128)(2,1)S(1)}, u32[]{:S(2)}, u32[]{:S(2)}) collective-permute-start(bf16[64,256]{1,0:T(8,128)(2,1)S(1)} %get-tuple-element.30.quarter), channel_id=1, source_target_pairs={{4,12},{8,0},{12,20},{16,8},{20,28},{24,16},{0,4},{28,24},{5,13},{... | collective-permute-start | bytes 98312 | tf_op jit(solution)/shard_map/ppermute | solution.py:373
  2.6 6.0 %collective-permute-start = (bf16[192,256]{1,0:T(8,128)(2,1)S(1)}, bf16[192,256]{1,0:T(8,128)(2,1)S(1)}, u32[]{:S(2)}, u32[]{:S(2)}) collective-permute-start(bf16[192,256]{1,0:T(8,128)(2,1)S(1)} %get-tuple-element.28), channel_id=1, source_target_pairs={{0,4},{4,0},{8,12},{12,8},{16,20},{20,16},{24,28},{28,24},{1,5},{5... | collective-permute-start | bytes 294920 | tf_op jit(solution)/shard_map/ppermute | solution.py:326
  2.7 6.6 %collective-permute-start.1 = (bf16[192,256]{1,0:T(8,128)(2,1)S(1)}, bf16[192,256]{1,0:T(8,128)(2,1)S(1)}, u32[]{:S(2)}, u32[]{:S(2)}) collective-permute-start(bf16[192,256]{1,0:T(8,128)(2,1)S(1)} %get-tuple-element.29), channel_id=1, source_target_pairs={{0,1},{1,0},{2,3},{3,2},{4,8},{5,9},{6,10},{7,11},{8,4},{9,5},{10,... | collective-permute-start | bytes 294920 | tf_op jit(solution)/shard_map/ppermute | solution.py:345
  5.1 4.5 %collective-permute-start.4 = (bf16[64,256]{1,0:T(8,128)(2,1)S(1)}, bf16[64,256]{1,0:T(8,128)(2,1)S(1)}, u32[]{:S(2)}, u32[]{:S(2)}) collective-permute-start(bf16[64,256]{1,0:T(8,128)(2,1)S(1)} %get-tuple-element.34), channel_id=1, source_target_pairs={{0,8},{1,9},{2,10},{3,11},{4,12},{5,13},{6,14},{7,15},{8,16},{9,17... | collective-permute-start | bytes 98312 | tf_op jit(solution)/shard_map/ppermute | solution.py:345
  6.4 3.9 %collective-permute-start.5 = (bf16[64,256]{1,0:T(8,128)(2,1)S(1)}, bf16[64,256]{1,0:T(8,128)(2,1)S(1)}, u32[]{:S(2)}, u32[]{:S(2)}) collective-permute-start(bf16[64,256]{1,0:T(8,128)(2,1)S(1)} %get-tuple-element.37), channel_id=1, source_target_pairs={{0,24},{1,25},{2,26},{3,27},{4,28},{5,29},{6,30},{7,31},{8,16},{9,... | collective-permute-start | bytes 98312 | tf_op jit(solution)/shard_map/ppermute | solution.py:345
  6.9 3.7 %collective-permute-start.6 = (bf16[64,256]{1,0:T(8,128)(2,1)S(1)}, bf16[64,256]{1,0:T(8,128)(2,1)S(1)}, u32[]{:S(2)}, u32[]{:S(2)}) collective-permute-start(bf16[64,256]{1,0:T(8,128)(2,1)S(1)} %get-tuple-element.38), channel_id=1, source_target_pairs={{0,16},{1,17},{2,18},{3,19},{4,20},{5,21},{6,22},{7,23},{8,0},{9,1... | collective-permute-start | bytes 98312 | tf_op jit(solution)/shard_map/ppermute | solution.py:345
  8.6 2.8 %collective-permute-start.7 = (bf16[64,256]{1,0:T(8,128)(2,1)S(1)}, bf16[64,256]{1,0:T(8,128)(2,1)S(1)}, u32[]{:S(2)}, u32[]{:S(2)}) collective-permute-start(bf16[64,256]{1,0:T(8,128)(2,1)S(1)} %get-tuple-element.39), channel_id=1, source_target_pairs={{0,1},{1,0},{2,3},{3,2},{4,5},{5,4},{6,7},{7,6},{8,24},{9,25},{10,... | collective-permute-start | bytes 98312 | tf_op jit(solution)/shard_map/ppermute | solution.py:345
  12.0 7.1 %collective-permute-start.9 = (bf16[80,128]{1,0:T(8,128)(2,1)S(1)}, bf16[80,128]{1,0:T(8,128)(2,1)S(1)}, u32[]{:S(2)}, u32[]{:S(2)}) collective-permute-start(bf16[80,128]{1,0:T(8,128)(2,1)S(1)} %get-tuple-element.45), channel_id=1, source_target_pairs={{0,3},{1,2},{2,1},{3,0},{4,7},{5,6},{6,5},{7,4},{8,11},{9,10},{10,... | collective-permute-start | bytes 61448 | tf_op jit(solution)/shard_map/ppermute | solution.py:326
  16.9 2.6 %collective-permute-start.10 = (bf16[80,128]{1,0:T(8,128)(2,1)S(1)}, bf16[80,128]{1,0:T(8,128)(2,1)S(1)}, u32[]{:S(2)}, u32[]{:S(2)}) collective-permute-start(bf16[80,128]{1,0:T(8,128)(2,1)S(1)} %get-tuple-element.46), channel_id=1, source_target_pairs={{0,2},{1,3},{2,0},{3,1},{4,6},{5,7},{6,4},{7,5},{8,10},{9,11},{10,... | collective-permute-start | bytes 61448 | tf_op jit(solution)/shard_map/ppermute | solution.py:326
  17.2 1.8 %copy-start = (bf16[512,512]{1,0:T(8,128)(2,1)S(1)}, bf16[512,512]{1,0:T(8,128)(2,1)}, u32[]{:S(2)}) copy-start(bf16[512,512]{1,0:T(8,128)(2,1)} %weight.3) | copy-start | bytes 1572868
  17.7 1.2 %collective-permute-start.8 = (bf16[64,128]{1,0:T(8,128)(2,1)S(1)}, bf16[64,128]{1,0:T(8,128)(2,1)S(1)}, u32[]{:S(2)}, u32[]{:S(2)}) collective-permute-start(bf16[64,128]{1,0:T(8,128)(2,1)S(1)} %get-tuple-element.44), channel_id=1, source_target_pairs={{0,1},{1,0},{2,3},{3,2},{4,5},{5,4},{6,7},{7,6},{8,9},{9,8},{10,11... | collective-permute-start | bytes 49160 | tf_op jit(solution)/shard_map/ppermute | solution.py:326

commit v29 on v28

--- a/solution.py
+++ b/solution.py
@@ -362,7 +362,7 @@
             [VMEM] * 2,
             [(HALF, pair_width)] * 4,
             [wide],
-            flops=2 * 10**9,
+            flops=55 * 10**7,
         )(swap(quarter, 1), quarter)
 
         def over_pairs(array, targets):

time: 20.5 us -> 21.5 us (1.049)
  the two profiles are of different devices: /device:TPU:11 before, /device:TPU:0 now
where the time goes in v29:
time: 21.5 us; the launch traced here: 21.3 us
  starting transfers between devices  14.4 us (67%)
  Pallas kernels  3.76 us (17%)
  waiting for transfers between devices  3.06 us (14%)
    ppermute x5, starting transfers between devices, to_spans(): lax.ppermute(array, ('seq', 'head'), [(s * head_size + h, t * head_size +...  5.86 us
    ppermute x5, starting transfers between devices, swap(): lax.ppermute(array, axis, [(i, i ^ bit) for i in range(lax.axis_size(axis...  5.07 us
    ppermute x1, starting transfers between devices, shards(): beside = (lax.ppermute(quarter, 'seq', cycle),)  3.49 us
    ppermute x5, waiting for transfers between devices, swap(): lax.ppermute(array, axis, [(i, i ^ bit) for i in range(lax.axis_size(axis...  1.8 us
    ppermute x5, waiting for transfers between devices, to_spans(): lax.ppermute(array, ('seq', 'head'), [(s * head_size + h, t * head_size +...  1.26 us
    pallas_call x1, Pallas kernels, shards(): kernel_call(functools.partial(pack_kernel, not paired), 'pack', 16, [HBM]...  0.99 us
    pallas_call x1, Pallas kernels, shards(): kernel_call(project_kernel, 'project', 8, [VMEM] * 4, [(share, out_weight...  0.81 us
    pallas_call x1, Pallas kernels, shards(): kernel_call(functools.partial(leaves_kernel, seq_size, paired), 'leaves',...  0.56 us
  transfers between devices with their start and end apart: 11, of which 3 were waited for; matrix products, arithmetic and copies ran while one was open for 0% of the time, Pallas kernels for 7%

profile of v29, /device:TPU:0, one launch (start us, length us, event | category | flops | bytes accessed | tf_op | source)
XLA Modules:
  0.0 21.3 jit_solution(5866922764211071257)
XLA Ops:
  0.0 1.0 %pack.1 = (bf16[256,128]{1,0:T(8,128)(2,1)S(1)}, bf16[256,256]{1,0:T(8,128)(2,1)S(1)}, bf16[192,256]{1,0:T(8,128)(2,1)S(1)}, bf16[192,256]{1,0:T(8,128)(2,1)S(1)}, bf16[64,256]{1,0:T(8,128)(2,1)S(1)}) custom-call(bf16[256,128]{1,0:T(8,128)(2,1)} %queries.1, bf16[256,128]{1,0:T(8,128)(2,1)} %keys.1, bf16[256,128]{1,0:T(8,128)(2,1)} %values.1), custom_call_target="tpu_custom_call" | custom-call | bytes 1048576 | tf_op jit(solution)/shard_map/pack/pallas_call | solution.py:328
  1.0 3.0 %collective-permute-start.3 = (bf16[64,256]{1,0:T(8,128)(2,1)S(1)}, bf16[64,256]{1,0:T(8,128)(2,1)S(1)}, u32[]{:S(2)}, u32[]{:S(2)}) collective-permute-start(bf16[64,256]{1,0:T(8,128)(2,1)S(1)} %get-tuple-element.30.quarter), channel_id=1, source_target_pairs={{0,4},{4,0},{8,12},{12,8},{16,20},{20,16},{24,28},{28,24},{1,5},{5... | collective-permute-start | bytes 98312 | tf_op jit(solution)/shard_map/ppermute | solution.py:326
  4.0 0.1 collective-permute-start
  4.1 0.0 collective-permute-start.1
  4.1 3.5 %collective-permute-start.2 = (bf16[64,256]{1,0:T(8,128)(2,1)S(1)}, bf16[64,256]{1,0:T(8,128)(2,1)S(1)}, u32[]{:S(2)}, u32[]{:S(2)}) collective-permute-start(bf16[64,256]{1,0:T(8,128)(2,1)S(1)} %get-tuple-element.30.quarter), channel_id=1, source_target_pairs={{4,12},{8,0},{12,20},{16,8},{20,28},{24,16},{0,4},{28,24},{5,13},{... | collective-permute-start | bytes 98312 | tf_op jit(solution)/shard_map/ppermute | solution.py:373
  7.6 0.0 collective-permute-done.3.theirs
  7.6 0.7 %collective-permute-start.4 = (bf16[64,256]{1,0:T(8,128)(2,1)S(1)}, bf16[64,256]{1,0:T(8,128)(2,1)S(1)}, u32[]{:S(2)}, u32[]{:S(2)}) collective-permute-start(bf16[64,256]{1,0:T(8,128)(2,1)S(1)} %get-tuple-element.34), channel_id=1, source_target_pairs={{0,8},{1,9},{2,10},{3,11},{4,12},{5,13},{6,14},{7,15},{8,16},{9,17... | collective-permute-start | bytes 98312 | tf_op jit(solution)/shard_map/ppermute | solution.py:345
  8.4 3.1 %collective-permute-start.5 = (bf16[64,256]{1,0:T(8,128)(2,1)S(1)}, bf16[64,256]{1,0:T(8,128)(2,1)S(1)}, u32[]{:S(2)}, u32[]{:S(2)}) collective-permute-start(bf16[64,256]{1,0:T(8,128)(2,1)S(1)} %get-tuple-element.37), channel_id=1, source_target_pairs={{0,24},{1,25},{2,26},{3,27},{4,28},{5,29},{6,30},{7,31},{8,16},{9,... | collective-permute-start | bytes 98312 | tf_op jit(solution)/shard_map/ppermute | solution.py:345
  11.5 0.0 collective-permute-done.2.rest_0_
  11.5 2.0 %collective-permute-start.6 = (bf16[64,256]{1,0:T(8,128)(2,1)S(1)}, bf16[64,256]{1,0:T(8,128)(2,1)S(1)}, u32[]{:S(2)}, u32[]{:S(2)}) collective-permute-start(bf16[64,256]{1,0:T(8,128)(2,1)S(1)} %get-tuple-element.38), channel_id=1, source_target_pairs={{0,16},{1,17},{2,18},{3,19},{4,20},{5,21},{6,22},{7,23},{8,0},{9,1... | collective-permute-start | bytes 98312 | tf_op jit(solution)/shard_map/ppermute | solution.py:345
  13.5 0.0 collective-permute-done.inner
  13.5 0.0 collective-permute-start.7
  13.5 0.0 collective-permute-done.1.outer
  13.5 0.4 %near.1 = (f32[2,256,512]{2,1,0:T(8,128)S(1)}, bf16[2,512,128]{2,1,0:T(8,128)(2,1)S(1)}, bf16[128,256]{1,0:T(8,128)(2,1)S(1)}) custom-call(bf16[256,128]{1,0:T(8,128)(2,1)S(1)} %get-tuple-element.26.queries, bf16[256,256]{1,0:T(8,128)(2,1)S(1)} %get-tuple-element.27.own, bf16[192,256]{1,0:T(8,128)(2,1)S(1)} %collective-permute-done.inner, ...), custom_call_target="tpu_custom_call" | custom-call | flops 67108864 | bytes 1048576 | tf_op jit(solution)/shard_map/near/pallas_call | solution.py:384
  13.9 0.0 collective-permute-done.4.rest_0_
  13.9 0.3 %mid.1 = (f32[2,256,192]{2,1,0:T(8,128)S(1)}, bf16[192,128]{1,0:T(8,128)(2,1)S(1)}) custom-call(bf16[256,128]{1,0:T(8,128)(2,1)S(1)} %get-tuple-element.26.queries, bf16[128,256]{1,0:T(8,128)(2,1)S(1)} %get-tuple-element.33.shared, bf16[64,256]{1,0:T(8,128)(2,1)S(1)} %collective-permute-done.4.rest_0_), custom_call_target="tpu_custom_call" | custom-call | flops 1000000000 | bytes 1048576 | tf_op jit(solution)/shard_map/mid/pallas_call | solution.py:398
  14.2 0.0 collective-permute-done.5.rest_0_
  14.2 1.3 %collective-permute-done.6.rest_1_ = bf16[64,256]{1,0:T(8,128)(2,1)S(1)} collective-permute-done((bf16[64,256]{1,0:T(8,128)(2,1)S(1)}, bf16[64,256]{1,0:T(8,128)(2,1)S(1)}, u32[]{:S(2)}, u32[]{:S(2)}) %collective-permute-start.6) | collective-permute-done | bytes 32800 | tf_op jit(solution)/shard_map/ppermute | solution.py:345
  15.4 0.0 collective-permute-done.7.rest_2_
  15.4 0.6 %leaves.1 = (bf16[80,128]{1,0:T(8,128)(2,1)S(1)}, bf16[80,128]{1,0:T(8,128)(2,1)S(1)}, bf16[128,128]{1,0:T(8,128)(2,1)S(1)}, bf16[128,128]{1,0:T(8,128)(2,1)S(1)}, f32[8,128]{1,0:T(8,128)S(1)}) custom-call(bf16[256,128]{1,0:T(8,128)(2,1)S(1)} %get-tuple-element.26.queries, f32[2,256,512]{2,1,0:T(8,128)S(1)} %get-tuple-element.31.near_scores, ...), custom_call_target="tpu_custom_call" | custom-call | flops 109051904 | bytes 1048576 | tf_op jit(solution)/shard_map/leaves/pallas_call | solution.py:410
  16.0 0.6 %collective-permute-start.9 = (bf16[80,128]{1,0:T(8,128)(2,1)S(1)}, bf16[80,128]{1,0:T(8,128)(2,1)S(1)}, u32[]{:S(2)}, u32[]{:S(2)}) collective-permute-start(bf16[80,128]{1,0:T(8,128)(2,1)S(1)} %get-tuple-element.45), channel_id=1, source_target_pairs={{0,3},{1,2},{2,1},{3,0},{4,7},{5,6},{6,5},{7,4},{8,11},{9,10},{10,... | collective-permute-start | bytes 61448 | tf_op jit(solution)/shard_map/ppermute | solution.py:326
  16.6 1.0 %collective-permute-start.10 = (bf16[80,128]{1,0:T(8,128)(2,1)S(1)}, bf16[80,128]{1,0:T(8,128)(2,1)S(1)}, u32[]{:S(2)}, u32[]{:S(2)}) collective-permute-start(bf16[80,128]{1,0:T(8,128)(2,1)S(1)} %get-tuple-element.46), channel_id=1, source_target_pairs={{0,2},{1,3},{2,0},{3,1},{4,6},{5,7},{6,4},{7,5},{8,10},{9,11},{10,... | collective-permute-start | bytes 61448 | tf_op jit(solution)/shard_map/ppermute | solution.py:326
  17.7 0.0 copy-start
  17.7 0.5 %stays.1 = (bf16[64,128]{1,0:T(8,128)(2,1)S(1)}, bf16[64,128]{1,0:T(8,128)(2,1)S(1)}) custom-call(bf16[256,128]{1,0:T(8,128)(2,1)S(1)} %get-tuple-element.26.queries, f32[2,256,512]{2,1,0:T(8,128)S(1)} %get-tuple-element.31.near_scores, bf16[2,512,128]{2,1,0:T(8,128)(2,1)S(1)} %get-tuple-element.32.near_values, ...), custom_call_target="tpu_custom_call" | custom-call | flops 109051904 | bytes 1048576 | tf_op jit(solution)/shard_map/stays/pallas_call | solution.py:425
  18.2 0.3 %collective-permute-start.8 = (bf16[64,128]{1,0:T(8,128)(2,1)S(1)}, bf16[64,128]{1,0:T(8,128)(2,1)S(1)}, u32[]{:S(2)}, u32[]{:S(2)}) collective-permute-start(bf16[64,128]{1,0:T(8,128)(2,1)S(1)} %get-tuple-element.44), channel_id=1, source_target_pairs={{0,1},{1,0},{2,3},{3,2},{4,5},{5,4},{6,7},{7,6},{8,9},{9,8},{10,11... | collective-permute-start | bytes 49160 | tf_op jit(solution)/shard_map/ppermute | solution.py:326
  18.5 0.9 %collective-permute-done.8.other = bf16[64,128]{1,0:T(8,128)(2,1)S(1)} collective-permute-done((bf16[64,128]{1,0:T(8,128)(2,1)S(1)}, bf16[64,128]{1,0:T(8,128)(2,1)S(1)}, u32[]{:S(2)}, u32[]{:S(2)}) %collective-permute-start.8) | collective-permute-done | bytes 16416 | tf_op jit(solution)/shard_map/ppermute | solution.py:326
  19.5 0.0 copy-done
  19.5 0.2 begin.1.partial
  19.6 0.0 collective-permute-done.9.other
  19.7 0.9 %collective-permute-done.10.same = bf16[80,128]{1,0:T(8,128)(2,1)S(1)} collective-permute-done((bf16[80,128]{1,0:T(8,128)(2,1)S(1)}, bf16[80,128]{1,0:T(8,128)(2,1)S(1)}, u32[]{:S(2)}, u32[]{:S(2)}) %collective-permute-start.10) | collective-permute-done | bytes 20512 | tf_op jit(solution)/shard_map/ppermute | solution.py:326
  20.5 0.8 %project.1 = bf16[64,512]{1,0:T(8,128)(2,1)} custom-call(f32[64,512]{1,0:T(8,128)S(1)} %begin.1.partial, bf16[80,128]{1,0:T(8,128)(2,1)S(1)} %collective-permute-done.9.other, bf16[80,128]{1,0:T(8,128)(2,1)S(1)} %collective-permute-done.10.same, bf16[512,512]{1,0:T(8,128)(2,1)S(1)} %copy-done), custom_call_target="tpu_custom_call" | custom-call | bytes 1048576 | tf_op jit(solution)/shard_map/project/pallas_call | solution.py:438
  (1 shorter events, 0.0 us)
Async XLA Ops:
  1.0 6.6 %collective-permute-start.3 = (bf16[64,256]{1,0:T(8,128)(2,1)S(1)}, bf16[64,256]{1,0:T(8,128)(2,1)S(1)}, u32[]{:S(2)}, u32[]{:S(2)}) collective-permute-start(bf16[64,256]{1,0:T(8,128)(2,1)S(1)} %get-tuple-element.30.quarter), channel_id=1, source_target_pairs={{0,4},{4,0},{8,12},{12,8},{16,20},{20,16},{24,28},{28,24},{1,5},{5... | collective-permute-start | bytes 98312 | tf_op jit(solution)/shard_map/ppermute | solution.py:326
  4.0 9.5 %collective-permute-start = (bf16[192,256]{1,0:T(8,128)(2,1)S(1)}, bf16[192,256]{1,0:T(8,128)(2,1)S(1)}, u32[]{:S(2)}, u32[]{:S(2)}) collective-permute-start(bf16[192,256]{1,0:T(8,128)(2,1)S(1)} %get-tuple-element.28), channel_id=1, source_target_pairs={{0,4},{4,0},{8,12},{12,8},{16,20},{20,16},{24,28},{28,24},{1,5},{5... | collective-permute-start | bytes 294920 | tf_op jit(solution)/shard_map/ppermute | solution.py:326
  4.1 9.4 %collective-permute-start.1 = (bf16[192,256]{1,0:T(8,128)(2,1)S(1)}, bf16[192,256]{1,0:T(8,128)(2,1)S(1)}, u32[]{:S(2)}, u32[]{:S(2)}) collective-permute-start(bf16[192,256]{1,0:T(8,128)(2,1)S(1)} %get-tuple-element.29), channel_id=1, source_target_pairs={{0,1},{1,0},{2,3},{3,2},{4,8},{5,9},{6,10},{7,11},{8,4},{9,5},{10,... | collective-permute-start | bytes 294920 | tf_op jit(solution)/shard_map/ppermute | solution.py:345
  4.1 7.4 %collective-permute-start.2 = (bf16[64,256]{1,0:T(8,128)(2,1)S(1)}, bf16[64,256]{1,0:T(8,128)(2,1)S(1)}, u32[]{:S(2)}, u32[]{:S(2)}) collective-permute-start(bf16[64,256]{1,0:T(8,128)(2,1)S(1)} %get-tuple-element.30.quarter), channel_id=1, source_target_pairs={{4,12},{8,0},{12,20},{16,8},{20,28},{24,16},{0,4},{28,24},{5,13},{... | collective-permute-start | bytes 98312 | tf_op jit(solution)/shard_map/ppermute | solution.py:373
  7.6 6.3 %collective-permute-start.4 = (bf16[64,256]{1,0:T(8,128)(2,1)S(1)}, bf16[64,256]{1,0:T(8,128)(2,1)S(1)}, u32[]{:S(2)}, u32[]{:S(2)}) collective-permute-start(bf16[64,256]{1,0:T(8,128)(2,1)S(1)} %get-tuple-element.34), channel_id=1, source_target_pairs={{0,8},{1,9},{2,10},{3,11},{4,12},{5,13},{6,14},{7,15},{8,16},{9,17... | collective-permute-start | bytes 98312 | tf_op jit(solution)/shard_map/ppermute | solution.py:345
  8.4 5.8 %collective-permute-start.5 = (bf16[64,256]{1,0:T(8,128)(2,1)S(1)}, bf16[64,256]{1,0:T(8,128)(2,1)S(1)}, u32[]{:S(2)}, u32[]{:S(2)}) collective-permute-start(bf16[64,256]{1,0:T(8,128)(2,1)S(1)} %get-tuple-element.37), channel_id=1, source_target_pairs={{0,24},{1,25},{2,26},{3,27},{4,28},{5,29},{6,30},{7,31},{8,16},{9,... | collective-permute-start | bytes 98312 | tf_op jit(solution)/shard_map/ppermute | solution.py:345
  11.5 3.9 %collective-permute-start.6 = (bf16[64,256]{1,0:T(8,128)(2,1)S(1)}, bf16[64,256]{1,0:T(8,128)(2,1)S(1)}, u32[]{:S(2)}, u32[]{:S(2)}) collective-permute-start(bf16[64,256]{1,0:T(8,128)(2,1)S(1)} %get-tuple-element.38), channel_id=1, source_target_pairs={{0,16},{1,17},{2,18},{3,19},{4,20},{5,21},{6,22},{7,23},{8,0},{9,1... | collective-permute-start | bytes 98312 | tf_op jit(solution)/shard_map/ppermute | solution.py:345
  13.5 1.9 %collective-permute-start.7 = (bf16[64,256]{1,0:T(8,128)(2,1)S(1)}, bf16[64,256]{1,0:T(8,128)(2,1)S(1)}, u32[]{:S(2)}, u32[]{:S(2)}) collective-permute-start(bf16[64,256]{1,0:T(8,128)(2,1)S(1)} %get-tuple-element.39), channel_id=1, source_target_pairs={{0,1},{1,0},{2,3},{3,2},{4,5},{5,4},{6,7},{7,6},{8,24},{9,25},{10,... | collective-permute-start | bytes 98312 | tf_op jit(solution)/shard_map/ppermute | solution.py:345
  16.0 3.7 %collective-permute-start.9 = (bf16[80,128]{1,0:T(8,128)(2,1)S(1)}, bf16[80,128]{1,0:T(8,128)(2,1)S(1)}, u32[]{:S(2)}, u32[]{:S(2)}) collective-permute-start(bf16[80,128]{1,0:T(8,128)(2,1)S(1)} %get-tuple-element.45), channel_id=1, source_target_pairs={{0,3},{1,2},{2,1},{3,0},{4,7},{5,6},{6,5},{7,4},{8,11},{9,10},{10,... | collective-permute-start | bytes 61448 | tf_op jit(solution)/shard_map/ppermute | solution.py:326
  16.6 3.9 %collective-permute-start.10 = (bf16[80,128]{1,0:T(8,128)(2,1)S(1)}, bf16[80,128]{1,0:T(8,128)(2,1)S(1)}, u32[]{:S(2)}, u32[]{:S(2)}) collective-permute-start(bf16[80,128]{1,0:T(8,128)(2,1)S(1)} %get-tuple-element.46), channel_id=1, source_target_pairs={{0,2},{1,3},{2,0},{3,1},{4,6},{5,7},{6,4},{7,5},{8,10},{9,11},{10,... | collective-permute-start | bytes 61448 | tf_op jit(solution)/shard_map/ppermute | solution.py:326
  17.7 1.8 %copy-start = (bf16[512,512]{1,0:T(8,128)(2,1)S(1)}, bf16[512,512]{1,0:T(8,128)(2,1)}, u32[]{:S(2)}) copy-start(bf16[512,512]{1,0:T(8,128)(2,1)} %weight.3) | copy-start | bytes 1572868
  18.2 1.2 %collective-permute-start.8 = (bf16[64,128]{1,0:T(8,128)(2,1)S(1)}, bf16[64,128]{1,0:T(8,128)(2,1)S(1)}, u32[]{:S(2)}, u32[]{:S(2)}) collective-permute-start(bf16[64,128]{1,0:T(8,128)(2,1)S(1)} %get-tuple-element.44), channel_id=1, source_target_pairs={{0,1},{1,0},{2,3},{3,2},{4,5},{5,4},{6,7},{7,6},{8,9},{9,8},{10,11... | collective-permute-start | bytes 49160 | tf_op jit(solution)/shard_map/ppermute | solution.py:326

commit v30 on v28

--- a/solution.py
+++ b/solution.py
@@ -171,7 +171,7 @@
     )
 
 
-def near_kernel(seq_size, queries, own, inner, outer, *rest):
+def near_kernel(seq_size, queries, own, outer, inner, *rest):
     *beside, scores, values, shared, keys, wide = rest
     me = lax.axis_index("seq")
     odd = me & 1
@@ -393,7 +393,7 @@
         ],
         [pltpu.VMEM((NEAR_ROWS, width), jnp.bfloat16), wide],
         flops=8 * LEAF * NEAR_ROWS * width,
-    )(own_queries, own, inner, outer, *beside)
+    )(own_queries, own, outer, inner, *beside)
     mid_rows = 3 * HALF if paired else HALF
     mid_scores, mid_values = kernel_call(
         mid_kernel,

time: 20.5 us -> 20.8 us (1.015)
  the two profiles are of different devices: /device:TPU:11 before, /device:TPU:0 now
where the time goes in v30:
time: 20.8 us; the launch traced here: 20.6 us
  starting transfers between devices  13 us (62%)
  waiting for transfers between devices  3.79 us (18%)
  Pallas kernels  3.76 us (18%)
    ppermute x5, starting transfers between devices, swap(): lax.ppermute(array, axis, [(i, i ^ bit) for i in range(lax.axis_size(axis...  8.4 us
    ppermute x5, starting transfers between devices, to_spans(): lax.ppermute(array, ('seq', 'head'), [(s * head_size + h, t * head_size +...  4.56 us
    ppermute x5, waiting for transfers between devices, to_spans(): lax.ppermute(array, ('seq', 'head'), [(s * head_size + h, t * head_size +...  2.58 us
    ppermute x5, waiting for transfers between devices, swap(): lax.ppermute(array, axis, [(i, i ^ bit) for i in range(lax.axis_size(axis...  1.2 us
    pallas_call x1, Pallas kernels, shards(): kernel_call(functools.partial(pack_kernel, not paired), 'pack', 16, [HBM]...  0.99 us
    pallas_call x1, Pallas kernels, shards(): kernel_call(project_kernel, 'project', 8, [VMEM] * 4, [(share, out_weight...  0.81 us
    pallas_call x1, Pallas kernels, shards(): kernel_call(functools.partial(leaves_kernel, seq_size, paired), 'leaves',...  0.56 us
    pallas_call x1, Pallas kernels, shards(): kernel_call(stays_kernel, 'stays', 16, [VMEM] * 8, [(share, width)] * 2,...  0.55 us
  transfers between devices with their start and end apart: 11, of which 5 were waited for; matrix products, arithmetic and copies ran while one was open for 0% of the time, Pallas kernels for 7%

profile of v30, /device:TPU:0, one launch (start us, length us, event | category | flops | bytes accessed | tf_op | source)
XLA Modules:
  0.0 20.6 jit_solution(14422134192621245626)
XLA Ops:
  0.0 1.0 %pack.1 = (bf16[256,128]{1,0:T(8,128)(2,1)S(1)}, bf16[256,256]{1,0:T(8,128)(2,1)S(1)}, bf16[192,256]{1,0:T(8,128)(2,1)S(1)}, bf16[192,256]{1,0:T(8,128)(2,1)S(1)}, bf16[64,256]{1,0:T(8,128)(2,1)S(1)}) custom-call(bf16[256,128]{1,0:T(8,128)(2,1)} %queries.1, bf16[256,128]{1,0:T(8,128)(2,1)} %keys.1, bf16[256,128]{1,0:T(8,128)(2,1)} %values.1), custom_call_target="tpu_custom_call" | custom-call | bytes 1048576 | tf_op jit(solution)/shard_map/pack/pallas_call | solution.py:328
  1.0 3.0 %collective-permute-start.3 = (bf16[64,256]{1,0:T(8,128)(2,1)S(1)}, bf16[64,256]{1,0:T(8,128)(2,1)S(1)}, u32[]{:S(2)}, u32[]{:S(2)}) collective-permute-start(bf16[64,256]{1,0:T(8,128)(2,1)S(1)} %get-tuple-element.30.quarter), channel_id=1, source_target_pairs={{0,4},{4,0},{8,12},{12,8},{16,20},{20,16},{24,28},{28,24},{1,5},{5... | collective-permute-start | bytes 98312 | tf_op jit(solution)/shard_map/ppermute | solution.py:326
  4.0 0.1 collective-permute-start.2
  4.1 0.0 collective-permute-start
  4.1 3.4 %collective-permute-start.1 = (bf16[192,256]{1,0:T(8,128)(2,1)S(1)}, bf16[192,256]{1,0:T(8,128)(2,1)S(1)}, u32[]{:S(2)}, u32[]{:S(2)}) collective-permute-start(bf16[192,256]{1,0:T(8,128)(2,1)S(1)} %get-tuple-element.29), channel_id=1, source_target_pairs={{0,4},{4,0},{8,12},{12,8},{16,20},{20,16},{24,28},{28,24},{1,5},{5... | collective-permute-start | bytes 294920 | tf_op jit(solution)/shard_map/ppermute | solution.py:326
  7.5 0.0 collective-permute-done.3.theirs
  7.5 1.6 %collective-permute-start.4 = (bf16[64,256]{1,0:T(8,128)(2,1)S(1)}, bf16[64,256]{1,0:T(8,128)(2,1)S(1)}, u32[]{:S(2)}, u32[]{:S(2)}) collective-permute-start(bf16[64,256]{1,0:T(8,128)(2,1)S(1)} %get-tuple-element.34), channel_id=1, source_target_pairs={{0,8},{1,9},{2,10},{3,11},{4,12},{5,13},{6,14},{7,15},{8,16},{9,17... | collective-permute-start | bytes 98312 | tf_op jit(solution)/shard_map/ppermute | solution.py:345
  9.2 2.2 %collective-permute-start.5 = (bf16[64,256]{1,0:T(8,128)(2,1)S(1)}, bf16[64,256]{1,0:T(8,128)(2,1)S(1)}, u32[]{:S(2)}, u32[]{:S(2)}) collective-permute-start(bf16[64,256]{1,0:T(8,128)(2,1)S(1)} %get-tuple-element.37), channel_id=1, source_target_pairs={{0,24},{1,25},{2,26},{3,27},{4,28},{5,29},{6,30},{7,31},{8,16},{9,... | collective-permute-start | bytes 98312 | tf_op jit(solution)/shard_map/ppermute | solution.py:345
  11.4 0.0 collective-permute-done.2.rest_0_
  11.4 0.7 %collective-permute-start.6 = (bf16[64,256]{1,0:T(8,128)(2,1)S(1)}, bf16[64,256]{1,0:T(8,128)(2,1)S(1)}, u32[]{:S(2)}, u32[]{:S(2)}) collective-permute-start(bf16[64,256]{1,0:T(8,128)(2,1)S(1)} %get-tuple-element.38), channel_id=1, source_target_pairs={{0,16},{1,17},{2,18},{3,19},{4,20},{5,21},{6,22},{7,23},{8,0},{9,1... | collective-permute-start | bytes 98312 | tf_op jit(solution)/shard_map/ppermute | solution.py:345
  12.1 0.0 collective-permute-done.outer
  12.1 0.0 collective-permute-start.7
  12.1 0.0 collective-permute-done.1.inner
  12.1 0.4 %near.1 = (f32[2,256,512]{2,1,0:T(8,128)S(1)}, bf16[2,512,128]{2,1,0:T(8,128)(2,1)S(1)}, bf16[128,256]{1,0:T(8,128)(2,1)S(1)}) custom-call(bf16[256,128]{1,0:T(8,128)(2,1)S(1)} %get-tuple-element.26.queries, bf16[256,256]{1,0:T(8,128)(2,1)S(1)} %get-tuple-element.27.own, bf16[192,256]{1,0:T(8,128)(2,1)S(1)} %collective-permute-done.outer, ...), custom_call_target="tpu_custom_call" | custom-call | flops 67108864 | bytes 1048576 | tf_op jit(solution)/shard_map/near/pallas_call | solution.py:384
  12.5 0.8 %collective-permute-done.4.rest_0_ = bf16[64,256]{1,0:T(8,128)(2,1)S(1)} collective-permute-done((bf16[64,256]{1,0:T(8,128)(2,1)S(1)}, bf16[64,256]{1,0:T(8,128)(2,1)S(1)}, u32[]{:S(2)}, u32[]{:S(2)}) %collective-permute-start.4) | collective-permute-done | bytes 32800 | tf_op jit(solution)/shard_map/ppermute | solution.py:345
  13.3 0.3 %mid.1 = (f32[2,256,192]{2,1,0:T(8,128)S(1)}, bf16[192,128]{1,0:T(8,128)(2,1)S(1)}) custom-call(bf16[256,128]{1,0:T(8,128)(2,1)S(1)} %get-tuple-element.26.queries, bf16[128,256]{1,0:T(8,128)(2,1)S(1)} %get-tuple-element.33.shared, bf16[64,256]{1,0:T(8,128)(2,1)S(1)} %collective-permute-done.4.rest_0_), custom_call_target="tpu_custom_call" | custom-call | flops 1000000000 | bytes 1048576 | tf_op jit(solution)/shard_map/mid/pallas_call | solution.py:398
  13.6 1.0 %collective-permute-done.5.rest_0_ = bf16[64,256]{1,0:T(8,128)(2,1)S(1)} collective-permute-done((bf16[64,256]{1,0:T(8,128)(2,1)S(1)}, bf16[64,256]{1,0:T(8,128)(2,1)S(1)}, u32[]{:S(2)}, u32[]{:S(2)}) %collective-permute-start.5) | collective-permute-done | bytes 32800 | tf_op jit(solution)/shard_map/ppermute | solution.py:345
  14.5 0.8 %collective-permute-done.6.rest_1_ = bf16[64,256]{1,0:T(8,128)(2,1)S(1)} collective-permute-done((bf16[64,256]{1,0:T(8,128)(2,1)S(1)}, bf16[64,256]{1,0:T(8,128)(2,1)S(1)}, u32[]{:S(2)}, u32[]{:S(2)}) %collective-permute-start.6) | collective-permute-done | bytes 32800 | tf_op jit(solution)/shard_map/ppermute | solution.py:345
  15.3 0.0 collective-permute-done.7.rest_2_
  15.3 0.6 %leaves.1 = (bf16[80,128]{1,0:T(8,128)(2,1)S(1)}, bf16[80,128]{1,0:T(8,128)(2,1)S(1)}, bf16[128,128]{1,0:T(8,128)(2,1)S(1)}, bf16[128,128]{1,0:T(8,128)(2,1)S(1)}, f32[8,128]{1,0:T(8,128)S(1)}) custom-call(bf16[256,128]{1,0:T(8,128)(2,1)S(1)} %get-tuple-element.26.queries, f32[2,256,512]{2,1,0:T(8,128)S(1)} %get-tuple-element.31.near_scores, ...), custom_call_target="tpu_custom_call" | custom-call | flops 109051904 | bytes 1048576 | tf_op jit(solution)/shard_map/leaves/pallas_call | solution.py:410
  15.9 0.1 collective-permute-start.9
  16.0 1.6 %collective-permute-start.10 = (bf16[80,128]{1,0:T(8,128)(2,1)S(1)}, bf16[80,128]{1,0:T(8,128)(2,1)S(1)}, u32[]{:S(2)}, u32[]{:S(2)}) collective-permute-start(bf16[80,128]{1,0:T(8,128)(2,1)S(1)} %get-tuple-element.46), channel_id=1, source_target_pairs={{0,2},{1,3},{2,0},{3,1},{4,6},{5,7},{6,4},{7,5},{8,10},{9,11},{10,... | collective-permute-start | bytes 61448 | tf_op jit(solution)/shard_map/ppermute | solution.py:326
  17.6 0.0 copy-start
  17.6 0.6 %stays.1 = (bf16[64,128]{1,0:T(8,128)(2,1)S(1)}, bf16[64,128]{1,0:T(8,128)(2,1)S(1)}) custom-call(bf16[256,128]{1,0:T(8,128)(2,1)S(1)} %get-tuple-element.26.queries, f32[2,256,512]{2,1,0:T(8,128)S(1)} %get-tuple-element.31.near_scores, bf16[2,512,128]{2,1,0:T(8,128)(2,1)S(1)} %get-tuple-element.32.near_values, ...), custom_call_target="tpu_custom_call" | custom-call | flops 109051904 | bytes 1048576 | tf_op jit(solution)/shard_map/stays/pallas_call | solution.py:425
  18.1 0.3 %collective-permute-start.8 = (bf16[64,128]{1,0:T(8,128)(2,1)S(1)}, bf16[64,128]{1,0:T(8,128)(2,1)S(1)}, u32[]{:S(2)}, u32[]{:S(2)}) collective-permute-start(bf16[64,128]{1,0:T(8,128)(2,1)S(1)} %get-tuple-element.44), channel_id=1, source_target_pairs={{0,1},{1,0},{2,3},{3,2},{4,5},{5,4},{6,7},{7,6},{8,9},{9,8},{10,11... | collective-permute-start | bytes 49160 | tf_op jit(solution)/shard_map/ppermute | solution.py:326
  18.5 0.9 %collective-permute-done.8.other = bf16[64,128]{1,0:T(8,128)(2,1)S(1)} collective-permute-done((bf16[64,128]{1,0:T(8,128)(2,1)S(1)}, bf16[64,128]{1,0:T(8,128)(2,1)S(1)}, u32[]{:S(2)}, u32[]{:S(2)}) %collective-permute-start.8) | collective-permute-done | bytes 16416 | tf_op jit(solution)/shard_map/ppermute | solution.py:326
  19.4 0.0 copy-done
  19.4 0.2 begin.1.partial
  19.6 0.0 collective-permute-done.9.other
  19.6 0.3 %collective-permute-done.10.same = bf16[80,128]{1,0:T(8,128)(2,1)S(1)} collective-permute-done((bf16[80,128]{1,0:T(8,128)(2,1)S(1)}, bf16[80,128]{1,0:T(8,128)(2,1)S(1)}, u32[]{:S(2)}, u32[]{:S(2)}) %collective-permute-start.10) | collective-permute-done | bytes 20512 | tf_op jit(solution)/shard_map/ppermute | solution.py:326
  19.8 0.8 %project.1 = bf16[64,512]{1,0:T(8,128)(2,1)} custom-call(f32[64,512]{1,0:T(8,128)S(1)} %begin.1.partial, bf16[80,128]{1,0:T(8,128)(2,1)S(1)} %collective-permute-done.9.other, bf16[80,128]{1,0:T(8,128)(2,1)S(1)} %collective-permute-done.10.same, bf16[512,512]{1,0:T(8,128)(2,1)S(1)} %copy-done), custom_call_target="tpu_custom_call" | custom-call | bytes 1048576 | tf_op jit(solution)/shard_map/project/pallas_call | solution.py:438
  (1 shorter events, 0.0 us)
Async XLA Ops:
  1.0 6.5 %collective-permute-start.3 = (bf16[64,256]{1,0:T(8,128)(2,1)S(1)}, bf16[64,256]{1,0:T(8,128)(2,1)S(1)}, u32[]{:S(2)}, u32[]{:S(2)}) collective-permute-start(bf16[64,256]{1,0:T(8,128)(2,1)S(1)} %get-tuple-element.30.quarter), channel_id=1, source_target_pairs={{0,4},{4,0},{8,12},{12,8},{16,20},{20,16},{24,28},{28,24},{1,5},{5... | collective-permute-start | bytes 98312 | tf_op jit(solution)/shard_map/ppermute | solution.py:326
  4.0 7.4 %collective-permute-start.2 = (bf16[64,256]{1,0:T(8,128)(2,1)S(1)}, bf16[64,256]{1,0:T(8,128)(2,1)S(1)}, u32[]{:S(2)}, u32[]{:S(2)}) collective-permute-start(bf16[64,256]{1,0:T(8,128)(2,1)S(1)} %get-tuple-element.30.quarter), channel_id=1, source_target_pairs={{4,12},{8,0},{12,20},{16,8},{20,28},{24,16},{0,4},{28,24},{5,13},{... | collective-permute-start | bytes 98312 | tf_op jit(solution)/shard_map/ppermute | solution.py:373
  4.1 8.0 %collective-permute-start = (bf16[192,256]{1,0:T(8,128)(2,1)S(1)}, bf16[192,256]{1,0:T(8,128)(2,1)S(1)}, u32[]{:S(2)}, u32[]{:S(2)}) collective-permute-start(bf16[192,256]{1,0:T(8,128)(2,1)S(1)} %get-tuple-element.28), channel_id=1, source_target_pairs={{0,1},{1,0},{2,3},{3,2},{4,8},{5,9},{6,10},{7,11},{8,4},{9,5},{10,... | collective-permute-start | bytes 294920 | tf_op jit(solution)/shard_map/ppermute | solution.py:345
  4.1 8.0 %collective-permute-start.1 = (bf16[192,256]{1,0:T(8,128)(2,1)S(1)}, bf16[192,256]{1,0:T(8,128)(2,1)S(1)}, u32[]{:S(2)}, u32[]{:S(2)}) collective-permute-start(bf16[192,256]{1,0:T(8,128)(2,1)S(1)} %get-tuple-element.29), channel_id=1, source_target_pairs={{0,4},{4,0},{8,12},{12,8},{16,20},{20,16},{24,28},{28,24},{1,5},{5... | collective-permute-start | bytes 294920 | tf_op jit(solution)/shard_map/ppermute | solution.py:326
  7.5 5.8 %collective-permute-start.4 = (bf16[64,256]{1,0:T(8,128)(2,1)S(1)}, bf16[64,256]{1,0:T(8,128)(2,1)S(1)}, u32[]{:S(2)}, u32[]{:S(2)}) collective-permute-start(bf16[64,256]{1,0:T(8,128)(2,1)S(1)} %get-tuple-element.34), channel_id=1, source_target_pairs={{0,8},{1,9},{2,10},{3,11},{4,12},{5,13},{6,14},{7,15},{8,16},{9,17... | collective-permute-start | bytes 98312 | tf_op jit(solution)/shard_map/ppermute | solution.py:345
  9.2 5.3 %collective-permute-start.5 = (bf16[64,256]{1,0:T(8,128)(2,1)S(1)}, bf16[64,256]{1,0:T(8,128)(2,1)S(1)}, u32[]{:S(2)}, u32[]{:S(2)}) collective-permute-start(bf16[64,256]{1,0:T(8,128)(2,1)S(1)} %get-tuple-element.37), channel_id=1, source_target_pairs={{0,24},{1,25},{2,26},{3,27},{4,28},{5,29},{6,30},{7,31},{8,16},{9,... | collective-permute-start | bytes 98312 | tf_op jit(solution)/shard_map/ppermute | solution.py:345
  11.4 3.9 %collective-permute-start.6 = (bf16[64,256]{1,0:T(8,128)(2,1)S(1)}, bf16[64,256]{1,0:T(8,128)(2,1)S(1)}, u32[]{:S(2)}, u32[]{:S(2)}) collective-permute-start(bf16[64,256]{1,0:T(8,128)(2,1)S(1)} %get-tuple-element.38), channel_id=1, source_target_pairs={{0,16},{1,17},{2,18},{3,19},{4,20},{5,21},{6,22},{7,23},{8,0},{9,1... | collective-permute-start | bytes 98312 | tf_op jit(solution)/shard_map/ppermute | solution.py:345
  12.1 3.2 %collective-permute-start.7 = (bf16[64,256]{1,0:T(8,128)(2,1)S(1)}, bf16[64,256]{1,0:T(8,128)(2,1)S(1)}, u32[]{:S(2)}, u32[]{:S(2)}) collective-permute-start(bf16[64,256]{1,0:T(8,128)(2,1)S(1)} %get-tuple-element.39), channel_id=1, source_target_pairs={{0,1},{1,0},{2,3},{3,2},{4,5},{5,4},{6,7},{7,6},{8,24},{9,25},{10,... | collective-permute-start | bytes 98312 | tf_op jit(solution)/shard_map/ppermute | solution.py:345
  15.9 3.7 %collective-permute-start.9 = (bf16[80,128]{1,0:T(8,128)(2,1)S(1)}, bf16[80,128]{1,0:T(8,128)(2,1)S(1)}, u32[]{:S(2)}, u32[]{:S(2)}) collective-permute-start(bf16[80,128]{1,0:T(8,128)(2,1)S(1)} %get-tuple-element.45), channel_id=1, source_target_pairs={{0,3},{1,2},{2,1},{3,0},{4,7},{5,6},{6,5},{7,4},{8,11},{9,10},{10,... | collective-permute-start | bytes 61448 | tf_op jit(solution)/shard_map/ppermute | solution.py:326
  16.0 3.8 %collective-permute-start.10 = (bf16[80,128]{1,0:T(8,128)(2,1)S(1)}, bf16[80,128]{1,0:T(8,128)(2,1)S(1)}, u32[]{:S(2)}, u32[]{:S(2)}) collective-permute-start(bf16[80,128]{1,0:T(8,128)(2,1)S(1)} %get-tuple-element.46), channel_id=1, source_target_pairs={{0,2},{1,3},{2,0},{3,1},{4,6},{5,7},{6,4},{7,5},{8,10},{9,11},{10,... | collective-permute-start | bytes 61448 | tf_op jit(solution)/shard_map/ppermute | solution.py:326
  17.6 1.8 %copy-start = (bf16[512,512]{1,0:T(8,128)(2,1)S(1)}, bf16[512,512]{1,0:T(8,128)(2,1)}, u32[]{:S(2)}) copy-start(bf16[512,512]{1,0:T(8,128)(2,1)} %weight.3) | copy-start | bytes 1572868
  18.1 1.2 %collective-permute-start.8 = (bf16[64,128]{1,0:T(8,128)(2,1)S(1)}, bf16[64,128]{1,0:T(8,128)(2,1)S(1)}, u32[]{:S(2)}, u32[]{:S(2)}) collective-permute-start(bf16[64,128]{1,0:T(8,128)(2,1)S(1)} %get-tuple-element.44), channel_id=1, source_target_pairs={{0,1},{1,0},{2,3},{3,2},{4,5},{5,4},{6,7},{7,6},{8,9},{9,8},{10,11... | collective-permute-start | bytes 49160 | tf_op jit(solution)/shard_map/ppermute | solution.py:326

commit v31 on v26

--- a/solution.py
+++ b/solution.py
@@ -25,7 +25,7 @@
     return jnp.concatenate(halves, axis=1)
 
 
-def pack_kernel(far_shares, queries, keys, values, own_queries, own, inner, outer, quarter, wide, arrived):
+def pack_kernel(far_shares, queries, keys, values, own_queries, own, level_one, quarter, wide, arrived):
     width = keys.shape[1]
     copies = [
         pltpu.make_async_copy(keys, own.at[:, :width], arrived.at[0]),
@@ -34,24 +34,25 @@
     ]
     for copy in copies:
         copy.start()
-    me = lax.axis_index("seq")
-    odd = me & 1
     for copy in copies:
         copy.wait()
-    rows = own[...]
-    low, high = rows[:LEAF], rows[LEAF:]
-    level_one = average_pairs(rows, wide)
-    level_two = average_pairs(level_one, wide)
+    level_one[...] = average_pairs(own[...], wide)
+    level_two = average_pairs(level_one[...], wide)
+    if far_shares:
+        for peer in range(quarter.shape[0]):
+            quarter[peer] = level_two
+    else:
+        quarter[...] = level_two
+
+
+def edges_kernel(own, level_one, inner, outer):
+    odd = lax.axis_index("seq") & 1
+    low, high = own[:LEAF], own[LEAF:]
     first, second = level_one[:HALF], level_one[HALF:]
     inner[:LEAF] = jnp.where(odd == 1, low, high)
     inner[LEAF:] = jnp.where(odd == 1, second, first)
     outer[:LEAF] = jnp.where(odd == 1, high, low)
     outer[LEAF:] = jnp.where(odd == 1, first, second)
-    if far_shares:
-        for peer in range(quarter.shape[0]):
-            quarter[peer] = level_two
-    else:
-        quarter[...] = level_two
 
 
 def join_kernel(theirs, quarter, upward, downward, eighth, wide):
@@ -315,7 +316,7 @@
     def swap(array, bit, axis="seq"):
         return lax.ppermute(array, axis, [(i, i ^ bit) for i in range(lax.axis_size(axis))])
 
-    own_queries, own, inner, outer, quarter = kernel_call(
+    own_queries, own, level_one, quarter = kernel_call(
         functools.partial(pack_kernel, not paired),
         "pack",
         16,
@@ -323,12 +324,14 @@
         [
             (tokens, width),
             (tokens, pair_width),
-            (LEAF + HALF, pair_width),
-            (LEAF + HALF, pair_width),
+            (LEAF, pair_width),
             (HALF, pair_width) if paired else (seq_size, HALF, pair_width),
         ],
         [wide, pltpu.SemaphoreType.DMA((3,))],
     )(*(pltpu.with_memory_space_constraint(array, pltpu.HBM) for array in (queries, keys, values)))
+    inner, outer = kernel_call(
+        edges_kernel, "edges", 8, [VMEM] * 2, [(LEAF + HALF, pair_width)] * 2, []
+    )(own, level_one)
     inner = swap(inner, 1)
 
     def to_spans(array, targets):

time: 20.3 us -> 20.3 us (level)
  no operation moved by 1% of the time
where the time goes in v31:
time: 20.3 us; the launch traced here: 20.1 us
  starting transfers between devices  13 us (64%)
  Pallas kernels  3.7 us (18%)
  waiting for transfers between devices  3.39 us (17%)
    ppermute x6, starting transfers between devices, swap(): lax.ppermute(array, axis, [(i, i ^ bit) for i in range(lax.axis_size(axis...  9.95 us
    ppermute x1, starting transfers between devices, shards(): early = (lax.ppermute(upward, 'seq', shift), swap(eighth, 4))  1.85 us
    ppermute x6, waiting for transfers between devices, swap(): lax.ppermute(array, axis, [(i, i ^ bit) for i in range(lax.axis_size(axis...  1.22 us
    ppermute x1, waiting for transfers between devices, shards(): early = (lax.ppermute(upward, 'seq', shift), swap(eighth, 4))  1.19 us
    ppermute x1, starting transfers between devices, shards(): lax.ppermute(downward, 'seq', [(target, source) for source, target in shi...  1.11 us
    pallas_call x1, Pallas kernels, shards(): kernel_call(functools.partial(pack_kernel, not paired), 'pack', 16, [HBM]...  0.98 us
    ppermute x1, waiting for transfers between devices, shards(): lax.ppermute(downward, 'seq', [(target, source) for source, target in shi...  0.97 us
    pallas_call x1, Pallas kernels, shards(): kernel_call(project_kernel, 'project', 8, [VMEM] * 4, [(share, out_weight...  0.81 us
  transfers between devices with their start and end apart: 10, of which 4 were waited for; matrix products, arithmetic and copies ran while one was open for 0% of the time, Pallas kernels for 7%

profile of v31, /device:TPU:0, one launch (start us, length us, event | category | flops | bytes accessed | tf_op | source)
XLA Modules:
  0.0 20.1 jit_solution(13974018261842417821)
XLA Ops:
  0.0 1.0 %pack.1 = (bf16[256,128]{1,0:T(8,128)(2,1)S(1)}, bf16[256,256]{1,0:T(8,128)(2,1)S(1)}, bf16[128,256]{1,0:T(8,128)(2,1)S(1)}, bf16[64,256]{1,0:T(8,128)(2,1)S(1)}) custom-call(bf16[256,128]{1,0:T(8,128)(2,1)} %queries.1, bf16[256,128]{1,0:T(8,128)(2,1)} %keys.1, bf16[256,128]{1,0:T(8,128)(2,1)} %values.1), custom_call_target="tpu_custom_call" | custom-call | bytes 1048576 | tf_op jit(solution)/shard_map/pack/pallas_call | solution.py:319
  1.0 3.0 %collective-permute-start.3 = (bf16[64,256]{1,0:T(8,128)(2,1)S(1)}, bf16[64,256]{1,0:T(8,128)(2,1)S(1)}, u32[]{:S(2)}, u32[]{:S(2)}) collective-permute-start(bf16[64,256]{1,0:T(8,128)(2,1)S(1)} %get-tuple-element.31.quarter), channel_id=1, source_target_pairs={{0,4},{4,0},{8,12},{12,8},{16,20},{20,16},{24,28},{28,24},{1,5},{5... | collective-permute-start | bytes 98312 | tf_op jit(solution)/shard_map/ppermute | solution.py:317
  4.0 0.1 collective-permute-start.2
  4.1 2.1 %collective-permute-start = (bf16[192,256]{1,0:T(8,128)(2,1)S(1)}, bf16[192,256]{1,0:T(8,128)(2,1)S(1)}, u32[]{:S(2)}, u32[]{:S(2)}) collective-permute-start(bf16[192,256]{1,0:T(8,128)(2,1)S(1)} %get-tuple-element.29), channel_id=1, source_target_pairs={{0,4},{4,0},{8,12},{12,8},{16,20},{20,16},{24,28},{28,24},{1,5},{5... | collective-permute-start | bytes 294920 | tf_op jit(solution)/shard_map/ppermute | solution.py:317
  6.2 0.0 collective-permute-start.1
  6.2 0.0 collective-permute-done.3.theirs
  6.2 1.9 %collective-permute-start.4 = (bf16[64,256]{1,0:T(8,128)(2,1)S(1)}, bf16[64,256]{1,0:T(8,128)(2,1)S(1)}, u32[]{:S(2)}, u32[]{:S(2)}) collective-permute-start(bf16[64,256]{1,0:T(8,128)(2,1)S(1)} %get-tuple-element.35), channel_id=1, source_target_pairs={{0,8},{4,12},{8,16},{12,20},{16,24},{20,28},{24,0},{28,4},{1,9},{5... | collective-permute-start | bytes 98312 | tf_op jit(solution)/shard_map/ppermute | solution.py:364
  8.1 2.9 %collective-permute-start.5 = (bf16[64,256]{1,0:T(8,128)(2,1)S(1)}, bf16[64,256]{1,0:T(8,128)(2,1)S(1)}, u32[]{:S(2)}, u32[]{:S(2)}) collective-permute-start(bf16[64,256]{1,0:T(8,128)(2,1)S(1)} %get-tuple-element.36), channel_id=1, source_target_pairs={{0,16},{4,20},{8,24},{12,28},{16,0},{20,4},{24,8},{28,12},{1,17},{... | collective-permute-start | bytes 98312 | tf_op jit(solution)/shard_map/ppermute | solution.py:317
  11.0 0.0 collective-permute-done.2.rest_0_
  11.0 1.1 %collective-permute-start.6 = (bf16[64,256]{1,0:T(8,128)(2,1)S(1)}, bf16[64,256]{1,0:T(8,128)(2,1)S(1)}, u32[]{:S(2)}, u32[]{:S(2)}) collective-permute-start(bf16[64,256]{1,0:T(8,128)(2,1)S(1)} %get-tuple-element.39), channel_id=1, source_target_pairs={{8,0},{12,4},{16,8},{20,12},{24,16},{28,20},{0,24},{4,28},{9,1},{1... | collective-permute-start | bytes 98312 | tf_op jit(solution)/shard_map/ppermute | solution.py:365
  12.1 0.0 collective-permute-done.inner
  12.1 0.0 collective-permute-done.1.outer
  12.1 0.4 %near.1 = (f32[2,256,512]{2,1,0:T(8,128)S(1)}, bf16[2,512,128]{2,1,0:T(8,128)(2,1)S(1)}, bf16[128,256]{1,0:T(8,128)(2,1)S(1)}) custom-call(bf16[256,128]{1,0:T(8,128)(2,1)S(1)} %get-tuple-element.26.queries, bf16[256,256]{1,0:T(8,128)(2,1)S(1)} %get-tuple-element.27.own, bf16[192,256]{1,0:T(8,128)(2,1)S(1)} %collective-permute-done.inner, ...), custom_call_target="tpu_custom_call" | custom-call | flops 67108864 | bytes 1048576 | tf_op jit(solution)/shard_map/near/pallas_call | solution.py:370
  12.5 1.2 %collective-permute-done.4.rest_0_ = bf16[64,256]{1,0:T(8,128)(2,1)S(1)} collective-permute-done((bf16[64,256]{1,0:T(8,128)(2,1)S(1)}, bf16[64,256]{1,0:T(8,128)(2,1)S(1)}, u32[]{:S(2)}, u32[]{:S(2)}) %collective-permute-start.4) | collective-permute-done | bytes 32800 | tf_op jit(solution)/shard_map/ppermute | solution.py:364
  13.7 0.0 collective-permute-done.5.rest_1_
  13.7 0.2 %mid.1 = (f32[2,256,256]{2,1,0:T(8,128)S(1)}, bf16[256,128]{1,0:T(8,128)(2,1)S(1)}) custom-call(bf16[256,128]{1,0:T(8,128)(2,1)S(1)} %get-tuple-element.26.queries, bf16[128,256]{1,0:T(8,128)(2,1)S(1)} %get-tuple-element.34.shared, bf16[64,256]{1,0:T(8,128)(2,1)S(1)} %collective-permute-done.4.rest_0_, bf16[64,256]{1,0:T(8,128)(2,1)S(1)} %collective-permute-done.5.rest_1_), custom_call_target="tpu_custom_call" | custom-call | flops 1000000000 | bytes 1048576 | tf_op jit(solution)/shard_map/mid/pallas_call | solution.py:384
  13.9 1.0 %collective-permute-done.6.rest_0_ = bf16[64,256]{1,0:T(8,128)(2,1)S(1)} collective-permute-done((bf16[64,256]{1,0:T(8,128)(2,1)S(1)}, bf16[64,256]{1,0:T(8,128)(2,1)S(1)}, u32[]{:S(2)}, u32[]{:S(2)}) %collective-permute-start.6) | collective-permute-done | bytes 32800 | tf_op jit(solution)/shard_map/ppermute | solution.py:365
  14.9 0.5 %leaves.1 = (bf16[80,128]{1,0:T(8,128)(2,1)S(1)}, bf16[80,128]{1,0:T(8,128)(2,1)S(1)}, bf16[64,128]{1,0:T(8,128)(2,1)S(1)}, bf16[64,128]{1,0:T(8,128)(2,1)S(1)}, f32[8,64]{1,0:T(8,128)S(1)}) custom-call(bf16[256,128]{1,0:T(8,128)(2,1)S(1)} %get-tuple-element.26.queries, f32[2,256,512]{2,1,0:T(8,128)S(1)} %get-tuple-element.32.near_scores, ...), custom_call_target="tpu_custom_call" | custom-call | flops 109051904 | bytes 1048576 | tf_op jit(solution)/shard_map/leaves/pallas_call | solution.py:396
  15.4 0.1 collective-permute-start.8
  15.5 1.6 %collective-permute-start.9 = (bf16[80,128]{1,0:T(8,128)(2,1)S(1)}, bf16[80,128]{1,0:T(8,128)(2,1)S(1)}, u32[]{:S(2)}, u32[]{:S(2)}) collective-permute-start(bf16[80,128]{1,0:T(8,128)(2,1)S(1)} %get-tuple-element.46), channel_id=1, source_target_pairs={{0,2},{1,3},{2,0},{3,1},{4,6},{5,7},{6,4},{7,5},{8,10},{9,11},{10,... | collective-permute-start | bytes 61448 | tf_op jit(solution)/shard_map/ppermute | solution.py:317
  17.1 0.0 copy-start
  17.1 0.5 %stays.1 = (bf16[64,128]{1,0:T(8,128)(2,1)S(1)}, bf16[64,128]{1,0:T(8,128)(2,1)S(1)}) custom-call(bf16[256,128]{1,0:T(8,128)(2,1)S(1)} %get-tuple-element.26.queries, f32[2,256,512]{2,1,0:T(8,128)S(1)} %get-tuple-element.32.near_scores, bf16[2,512,128]{2,1,0:T(8,128)(2,1)S(1)} %get-tuple-element.33.near_values, ...), custom_call_target="tpu_custom_call" | custom-call | flops 109051904 | bytes 1048576 | tf_op jit(solution)/shard_map/stays/pallas_call | solution.py:411
  17.6 0.3 %collective-permute-start.7 = (bf16[64,128]{1,0:T(8,128)(2,1)S(1)}, bf16[64,128]{1,0:T(8,128)(2,1)S(1)}, u32[]{:S(2)}, u32[]{:S(2)}) collective-permute-start(bf16[64,128]{1,0:T(8,128)(2,1)S(1)} %get-tuple-element.44), channel_id=1, source_target_pairs={{0,1},{1,0},{2,3},{3,2},{4,5},{5,4},{6,7},{7,6},{8,9},{9,8},{10,11... | collective-permute-start | bytes 49160 | tf_op jit(solution)/shard_map/ppermute | solution.py:317
  17.9 0.9 %collective-permute-done.7.other = bf16[64,128]{1,0:T(8,128)(2,1)S(1)} collective-permute-done((bf16[64,128]{1,0:T(8,128)(2,1)S(1)}, bf16[64,128]{1,0:T(8,128)(2,1)S(1)}, u32[]{:S(2)}, u32[]{:S(2)}) %collective-permute-start.7) | collective-permute-done | bytes 16416 | tf_op jit(solution)/shard_map/ppermute | solution.py:317
  18.9 0.0 copy-done
  18.9 0.2 begin.1.partial
  19.0 0.0 collective-permute-done.8.other
  19.0 0.3 %collective-permute-done.9.same = bf16[80,128]{1,0:T(8,128)(2,1)S(1)} collective-permute-done((bf16[80,128]{1,0:T(8,128)(2,1)S(1)}, bf16[80,128]{1,0:T(8,128)(2,1)S(1)}, u32[]{:S(2)}, u32[]{:S(2)}) %collective-permute-start.9) | collective-permute-done | bytes 20512 | tf_op jit(solution)/shard_map/ppermute | solution.py:317
  19.3 0.8 %project.1 = bf16[64,512]{1,0:T(8,128)(2,1)} custom-call(f32[64,512]{1,0:T(8,128)S(1)} %begin.1.partial, bf16[80,128]{1,0:T(8,128)(2,1)S(1)} %collective-permute-done.8.other, bf16[80,128]{1,0:T(8,128)(2,1)S(1)} %collective-permute-done.9.same, bf16[512,512]{1,0:T(8,128)(2,1)S(1)} %copy-done), custom_call_target="tpu_custom_call" | custom-call | bytes 1048576 | tf_op jit(solution)/shard_map/project/pallas_call | solution.py:424
  (2 shorter events, 0.1 us)
Async XLA Ops:
  1.0 5.2 %collective-permute-start.3 = (bf16[64,256]{1,0:T(8,128)(2,1)S(1)}, bf16[64,256]{1,0:T(8,128)(2,1)S(1)}, u32[]{:S(2)}, u32[]{:S(2)}) collective-permute-start(bf16[64,256]{1,0:T(8,128)(2,1)S(1)} %get-tuple-element.31.quarter), channel_id=1, source_target_pairs={{0,4},{4,0},{8,12},{12,8},{16,20},{20,16},{24,28},{28,24},{1,5},{5... | collective-permute-start | bytes 98312 | tf_op jit(solution)/shard_map/ppermute | solution.py:317
  4.0 7.0 %collective-permute-start.2 = (bf16[64,256]{1,0:T(8,128)(2,1)S(1)}, bf16[64,256]{1,0:T(8,128)(2,1)S(1)}, u32[]{:S(2)}, u32[]{:S(2)}) collective-permute-start(bf16[64,256]{1,0:T(8,128)(2,1)S(1)} %get-tuple-element.31.quarter), channel_id=1, source_target_pairs={{4,12},{8,0},{12,20},{16,8},{20,28},{24,16},{0,4},{28,24},{5,13},{... | collective-permute-start | bytes 98312 | tf_op jit(solution)/shard_map/ppermute | solution.py:363
  4.1 8.0 %collective-permute-start = (bf16[192,256]{1,0:T(8,128)(2,1)S(1)}, bf16[192,256]{1,0:T(8,128)(2,1)S(1)}, u32[]{:S(2)}, u32[]{:S(2)}) collective-permute-start(bf16[192,256]{1,0:T(8,128)(2,1)S(1)} %get-tuple-element.29), channel_id=1, source_target_pairs={{0,4},{4,0},{8,12},{12,8},{16,20},{20,16},{24,28},{28,24},{1,5},{5... | collective-permute-start | bytes 294920 | tf_op jit(solution)/shard_map/ppermute | solution.py:317
  6.2 5.9 %collective-permute-start.1 = (bf16[192,256]{1,0:T(8,128)(2,1)S(1)}, bf16[192,256]{1,0:T(8,128)(2,1)S(1)}, u32[]{:S(2)}, u32[]{:S(2)}) collective-permute-start(bf16[192,256]{1,0:T(8,128)(2,1)S(1)} %get-tuple-element.30), channel_id=1, source_target_pairs={{0,1},{1,0},{2,3},{3,2},{4,8},{5,9},{6,10},{7,11},{8,4},{9,5},{10,... | collective-permute-start | bytes 294920 | tf_op jit(solution)/shard_map/ppermute | solution.py:338
  6.2 7.4 %collective-permute-start.4 = (bf16[64,256]{1,0:T(8,128)(2,1)S(1)}, bf16[64,256]{1,0:T(8,128)(2,1)S(1)}, u32[]{:S(2)}, u32[]{:S(2)}) collective-permute-start(bf16[64,256]{1,0:T(8,128)(2,1)S(1)} %get-tuple-element.35), channel_id=1, source_target_pairs={{0,8},{4,12},{8,16},{12,20},{16,24},{20,28},{24,0},{28,4},{1,9},{5... | collective-permute-start | bytes 98312 | tf_op jit(solution)/shard_map/ppermute | solution.py:364
  8.1 5.6 %collective-permute-start.5 = (bf16[64,256]{1,0:T(8,128)(2,1)S(1)}, bf16[64,256]{1,0:T(8,128)(2,1)S(1)}, u32[]{:S(2)}, u32[]{:S(2)}) collective-permute-start(bf16[64,256]{1,0:T(8,128)(2,1)S(1)} %get-tuple-element.36), channel_id=1, source_target_pairs={{0,16},{4,20},{8,24},{12,28},{16,0},{20,4},{24,8},{28,12},{1,17},{... | collective-permute-start | bytes 98312 | tf_op jit(solution)/shard_map/ppermute | solution.py:317
  11.0 3.9 %collective-permute-start.6 = (bf16[64,256]{1,0:T(8,128)(2,1)S(1)}, bf16[64,256]{1,0:T(8,128)(2,1)S(1)}, u32[]{:S(2)}, u32[]{:S(2)}) collective-permute-start(bf16[64,256]{1,0:T(8,128)(2,1)S(1)} %get-tuple-element.39), channel_id=1, source_target_pairs={{8,0},{12,4},{16,8},{20,12},{24,16},{28,20},{0,24},{4,28},{9,1},{1... | collective-permute-start | bytes 98312 | tf_op jit(solution)/shard_map/ppermute | solution.py:365
  15.4 3.6 %collective-permute-start.8 = (bf16[80,128]{1,0:T(8,128)(2,1)S(1)}, bf16[80,128]{1,0:T(8,128)(2,1)S(1)}, u32[]{:S(2)}, u32[]{:S(2)}) collective-permute-start(bf16[80,128]{1,0:T(8,128)(2,1)S(1)} %get-tuple-element.45), channel_id=1, source_target_pairs={{0,3},{1,2},{2,1},{3,0},{4,7},{5,6},{6,5},{7,4},{8,11},{9,10},{10,... | collective-permute-start | bytes 61448 | tf_op jit(solution)/shard_map/ppermute | solution.py:317
  15.5 3.8 %collective-permute-start.9 = (bf16[80,128]{1,0:T(8,128)(2,1)S(1)}, bf16[80,128]{1,0:T(8,128)(2,1)S(1)}, u32[]{:S(2)}, u32[]{:S(2)}) collective-permute-start(bf16[80,128]{1,0:T(8,128)(2,1)S(1)} %get-tuple-element.46), channel_id=1, source_target_pairs={{0,2},{1,3},{2,0},{3,1},{4,6},{5,7},{6,4},{7,5},{8,10},{9,11},{10,... | collective-permute-start | bytes 61448 | tf_op jit(solution)/shard_map/ppermute | solution.py:317
  17.1 1.8 %copy-start = (bf16[512,512]{1,0:T(8,128)(2,1)S(1)}, bf16[512,512]{1,0:T(8,128)(2,1)}, u32[]{:S(2)}) copy-start(bf16[512,512]{1,0:T(8,128)(2,1)} %weight.3) | copy-start | bytes 1572868
  17.6 1.2 %collective-permute-start.7 = (bf16[64,128]{1,0:T(8,128)(2,1)S(1)}, bf16[64,128]{1,0:T(8,128)(2,1)S(1)}, u32[]{:S(2)}, u32[]{:S(2)}) collective-permute-start(bf16[64,128]{1,0:T(8,128)(2,1)S(1)} %get-tuple-element.44), channel_id=1, source_target_pairs={{0,1},{1,0},{2,3},{3,2},{4,5},{5,4},{6,7},{7,6},{8,9},{9,8},{10,11... | collective-permute-start | bytes 49160 | tf_op jit(solution)/shard_map/ppermute | solution.py:317

commit v32 on v26

--- a/solution.py
+++ b/solution.py
@@ -273,13 +273,22 @@
     )
 
 
-def project_kernel(partial, other, same, weight, mixed, columns):
+def project_kernel(partial, other, same, weight, mixed, columns, held, sent):
     chip = (lax.axis_index("head") >> 1) ^ 1
-    shares = side_by_side(same, other, partial.shape[0], columns)
-    total = partial[...] + jnp.dot(
-        shares, chip_rows(weight, chip, columns.shape[1]), preferred_element_type=jnp.float32
-    )
-    mixed[...] = total.astype(mixed.dtype)
+    count, width = partial.shape
+    shares = side_by_side(same, other, count, columns)
+    rows = pl.ds(pl.multiple_of(chip * columns.shape[1], columns.shape[1]), columns.shape[1])
+    copies = []
+    for half in range(2):
+        span = slice(half * width // 2, (half + 1) * width // 2)
+        total = partial[:, span] + jnp.dot(
+            shares, weight[rows, span], preferred_element_type=jnp.float32
+        )
+        held[:, span] = total.astype(mixed.dtype)
+        copies.append(pltpu.make_async_copy(held.at[:, span], mixed.at[:, span], sent.at[half]))
+        copies[-1].start()
+    for copy in copies:
+        copy.wait()
 
 
 VMEM = pl.BlockSpec(memory_space=pltpu.VMEM)
@@ -418,10 +427,20 @@
         [jax.ShapeDtypeStruct((share, out_weight.shape[1]), jnp.float32)],
         [columns],
     )(share_0, swap(share_1, 1, "head"), out_weight)
-    (mixed,) = kernel_call(
-        project_kernel, "project", 8, [VMEM] * 4, [(share, out_weight.shape[1])], [columns]
+    out_shape = (share, out_weight.shape[1])
+    return pl.pallas_call(
+        project_kernel,
+        out_shape=jax.ShapeDtypeStruct(out_shape, jnp.bfloat16),
+        in_specs=[VMEM] * 4,
+        out_specs=HBM,
+        scratch_shapes=[
+            columns,
+            pltpu.VMEM(out_shape, jnp.bfloat16),
+            pltpu.SemaphoreType.DMA((2,)),
+        ],
+        compiler_params=pltpu.CompilerParams(vmem_limit_bytes=8 << 20),
+        name="project",
     )(partial, part_3, part_2, out_weight)
-    return mixed
 
 
 def solution(mesh):

time: 20.3 us -> 20.3 us (level)
  no operation moved by 1% of the time
where the time goes in v32:
time: 20.3 us; the launch traced here: 20.2 us
  starting transfers between devices  13.1 us (65%)
  Pallas kernels  3.71 us (18%)
  waiting for transfers between devices  3.32 us (16%)
    ppermute x6, starting transfers between devices, swap(): lax.ppermute(array, axis, [(i, i ^ bit) for i in range(lax.axis_size(axis...  9.79 us
    ppermute x1, starting transfers between devices, shards(): early = (lax.ppermute(upward, 'seq', shift), swap(eighth, 4))  2.04 us
    ppermute x6, waiting for transfers between devices, swap(): lax.ppermute(array, axis, [(i, i ^ bit) for i in range(lax.axis_size(axis...  1.22 us
    ppermute x1, starting transfers between devices, shards(): lax.ppermute(downward, 'seq', [(target, source) for source, target in shi...  1.18 us
    ppermute x1, waiting for transfers between devices, shards(): early = (lax.ppermute(upward, 'seq', shift), swap(eighth, 4))  1.1 us
    ppermute x1, waiting for transfers between devices, shards(): lax.ppermute(downward, 'seq', [(target, source) for source, target in shi...  1 us
    pallas_call x1, Pallas kernels, shards(): kernel_call(functools.partial(pack_kernel, not paired), 'pack', 16, [HBM]...  0.99 us
    pallas_call x1, Pallas kernels, shards(): pl.pallas_call(project_kernel, out_shape=jax.ShapeDtypeStruct(out_shape,...  0.83 us
  transfers between devices with their start and end apart: 10, of which 4 were waited for; matrix products, arithmetic and copies ran while one was open for 0% of the time, Pallas kernels for 7%

profile of v32, /device:TPU:0, one launch (start us, length us, event | category | flops | bytes accessed | tf_op | source)
XLA Modules:
  0.0 20.2 jit_solution(4400420068308216254)
XLA Ops:
  0.0 1.0 %pack.1 = (bf16[256,128]{1,0:T(8,128)(2,1)S(1)}, bf16[256,256]{1,0:T(8,128)(2,1)S(1)}, bf16[192,256]{1,0:T(8,128)(2,1)S(1)}, bf16[192,256]{1,0:T(8,128)(2,1)S(1)}, bf16[64,256]{1,0:T(8,128)(2,1)S(1)}) custom-call(bf16[256,128]{1,0:T(8,128)(2,1)} %queries.1, bf16[256,128]{1,0:T(8,128)(2,1)} %keys.1, bf16[256,128]{1,0:T(8,128)(2,1)} %values.1), custom_call_target="tpu_custom_call" | custom-call | bytes 1048576 | tf_op jit(solution)/shard_map/pack/pallas_call | solution.py:327
  1.0 3.0 %collective-permute-start.3 = (bf16[64,256]{1,0:T(8,128)(2,1)S(1)}, bf16[64,256]{1,0:T(8,128)(2,1)S(1)}, u32[]{:S(2)}, u32[]{:S(2)}) collective-permute-start(bf16[64,256]{1,0:T(8,128)(2,1)S(1)} %get-tuple-element.29.quarter), channel_id=1, source_target_pairs={{0,4},{4,0},{8,12},{12,8},{16,20},{20,16},{24,28},{28,24},{1,5},{5... | collective-permute-start | bytes 98312 | tf_op jit(solution)/shard_map/ppermute | solution.py:325
  4.0 0.1 collective-permute-start.2
  4.1 2.0 %collective-permute-start = (bf16[192,256]{1,0:T(8,128)(2,1)S(1)}, bf16[192,256]{1,0:T(8,128)(2,1)S(1)}, u32[]{:S(2)}, u32[]{:S(2)}) collective-permute-start(bf16[192,256]{1,0:T(8,128)(2,1)S(1)} %get-tuple-element.27), channel_id=1, source_target_pairs={{0,4},{4,0},{8,12},{12,8},{16,20},{20,16},{24,28},{28,24},{1,5},{5... | collective-permute-start | bytes 294920 | tf_op jit(solution)/shard_map/ppermute | solution.py:325
  6.1 0.0 collective-permute-start.1
  6.1 0.0 collective-permute-done.3.theirs
  6.2 2.0 %collective-permute-start.4 = (bf16[64,256]{1,0:T(8,128)(2,1)S(1)}, bf16[64,256]{1,0:T(8,128)(2,1)S(1)}, u32[]{:S(2)}, u32[]{:S(2)}) collective-permute-start(bf16[64,256]{1,0:T(8,128)(2,1)S(1)} %get-tuple-element.33), channel_id=1, source_target_pairs={{0,8},{4,12},{8,16},{12,20},{16,24},{20,28},{24,0},{28,4},{1,9},{5... | collective-permute-start | bytes 98312 | tf_op jit(solution)/shard_map/ppermute | solution.py:370
  8.2 2.8 %collective-permute-start.5 = (bf16[64,256]{1,0:T(8,128)(2,1)S(1)}, bf16[64,256]{1,0:T(8,128)(2,1)S(1)}, u32[]{:S(2)}, u32[]{:S(2)}) collective-permute-start(bf16[64,256]{1,0:T(8,128)(2,1)S(1)} %get-tuple-element.34), channel_id=1, source_target_pairs={{0,16},{4,20},{8,24},{12,28},{16,0},{20,4},{24,8},{28,12},{1,17},{... | collective-permute-start | bytes 98312 | tf_op jit(solution)/shard_map/ppermute | solution.py:325
  11.0 0.0 collective-permute-done.2.rest_0_
  11.0 1.2 %collective-permute-start.6 = (bf16[64,256]{1,0:T(8,128)(2,1)S(1)}, bf16[64,256]{1,0:T(8,128)(2,1)S(1)}, u32[]{:S(2)}, u32[]{:S(2)}) collective-permute-start(bf16[64,256]{1,0:T(8,128)(2,1)S(1)} %get-tuple-element.37), channel_id=1, source_target_pairs={{8,0},{12,4},{16,8},{20,12},{24,16},{28,20},{0,24},{4,28},{9,1},{1... | collective-permute-start | bytes 98312 | tf_op jit(solution)/shard_map/ppermute | solution.py:371
  12.1 0.0 collective-permute-done.inner
  12.1 0.0 collective-permute-done.1.outer
  12.2 0.4 %near.1 = (f32[2,256,512]{2,1,0:T(8,128)S(1)}, bf16[2,512,128]{2,1,0:T(8,128)(2,1)S(1)}, bf16[128,256]{1,0:T(8,128)(2,1)S(1)}) custom-call(bf16[256,128]{1,0:T(8,128)(2,1)S(1)} %get-tuple-element.25.queries, bf16[256,256]{1,0:T(8,128)(2,1)S(1)} %get-tuple-element.26.own, bf16[192,256]{1,0:T(8,128)(2,1)S(1)} %collective-permute-done.inner, ...), custom_call_target="tpu_custom_call" | custom-call | flops 67108864 | bytes 1048576 | tf_op jit(solution)/shard_map/near/pallas_call | solution.py:376
  12.5 1.1 %collective-permute-done.4.rest_0_ = bf16[64,256]{1,0:T(8,128)(2,1)S(1)} collective-permute-done((bf16[64,256]{1,0:T(8,128)(2,1)S(1)}, bf16[64,256]{1,0:T(8,128)(2,1)S(1)}, u32[]{:S(2)}, u32[]{:S(2)}) %collective-permute-start.4) | collective-permute-done | bytes 32800 | tf_op jit(solution)/shard_map/ppermute | solution.py:370
  13.6 0.0 collective-permute-done.5.rest_1_
  13.6 0.2 %mid.1 = (f32[2,256,256]{2,1,0:T(8,128)S(1)}, bf16[256,128]{1,0:T(8,128)(2,1)S(1)}) custom-call(bf16[256,128]{1,0:T(8,128)(2,1)S(1)} %get-tuple-element.25.queries, bf16[128,256]{1,0:T(8,128)(2,1)S(1)} %get-tuple-element.32.shared, bf16[64,256]{1,0:T(8,128)(2,1)S(1)} %collective-permute-done.4.rest_0_, bf16[64,256]{1,0:T(8,128)(2,1)S(1)} %collective-permute-done.5.rest_1_), custom_call_target="tpu_custom_call" | custom-call | flops 1000000000 | bytes 1048576 | tf_op jit(solution)/shard_map/mid/pallas_call | solution.py:390
  13.9 1.0 %collective-permute-done.6.rest_0_ = bf16[64,256]{1,0:T(8,128)(2,1)S(1)} collective-permute-done((bf16[64,256]{1,0:T(8,128)(2,1)S(1)}, bf16[64,256]{1,0:T(8,128)(2,1)S(1)}, u32[]{:S(2)}, u32[]{:S(2)}) %collective-permute-start.6) | collective-permute-done | bytes 32800 | tf_op jit(solution)/shard_map/ppermute | solution.py:371
  14.9 0.5 %leaves.1 = (bf16[80,128]{1,0:T(8,128)(2,1)S(1)}, bf16[80,128]{1,0:T(8,128)(2,1)S(1)}, bf16[64,128]{1,0:T(8,128)(2,1)S(1)}, bf16[64,128]{1,0:T(8,128)(2,1)S(1)}, f32[8,64]{1,0:T(8,128)S(1)}) custom-call(bf16[256,128]{1,0:T(8,128)(2,1)S(1)} %get-tuple-element.25.queries, f32[2,256,512]{2,1,0:T(8,128)S(1)} %get-tuple-element.30.near_scores, ...), custom_call_target="tpu_custom_call" | custom-call | flops 109051904 | bytes 1048576 | tf_op jit(solution)/shard_map/leaves/pallas_call | solution.py:402
  15.4 0.1 collective-permute-start.8
  15.5 1.6 %collective-permute-start.9 = (bf16[80,128]{1,0:T(8,128)(2,1)S(1)}, bf16[80,128]{1,0:T(8,128)(2,1)S(1)}, u32[]{:S(2)}, u32[]{:S(2)}) collective-permute-start(bf16[80,128]{1,0:T(8,128)(2,1)S(1)} %get-tuple-element.44), channel_id=1, source_target_pairs={{0,2},{1,3},{2,0},{3,1},{4,6},{5,7},{6,4},{7,5},{8,10},{9,11},{10,... | collective-permute-start | bytes 61448 | tf_op jit(solution)/shard_map/ppermute | solution.py:325
  17.1 0.0 copy-start
  17.1 0.5 %stays.1 = (bf16[64,128]{1,0:T(8,128)(2,1)S(1)}, bf16[64,128]{1,0:T(8,128)(2,1)S(1)}) custom-call(bf16[256,128]{1,0:T(8,128)(2,1)S(1)} %get-tuple-element.25.queries, f32[2,256,512]{2,1,0:T(8,128)S(1)} %get-tuple-element.30.near_scores, bf16[2,512,128]{2,1,0:T(8,128)(2,1)S(1)} %get-tuple-element.31.near_values, ...), custom_call_target="tpu_custom_call" | custom-call | flops 109051904 | bytes 1048576 | tf_op jit(solution)/shard_map/stays/pallas_call | solution.py:417
  17.6 0.3 %collective-permute-start.7 = (bf16[64,128]{1,0:T(8,128)(2,1)S(1)}, bf16[64,128]{1,0:T(8,128)(2,1)S(1)}, u32[]{:S(2)}, u32[]{:S(2)}) collective-permute-start(bf16[64,128]{1,0:T(8,128)(2,1)S(1)} %get-tuple-element.42), channel_id=1, source_target_pairs={{0,1},{1,0},{2,3},{3,2},{4,5},{5,4},{6,7},{7,6},{8,9},{9,8},{10,11... | collective-permute-start | bytes 49160 | tf_op jit(solution)/shard_map/ppermute | solution.py:325
  18.0 0.9 %collective-permute-done.7.other = bf16[64,128]{1,0:T(8,128)(2,1)S(1)} collective-permute-done((bf16[64,128]{1,0:T(8,128)(2,1)S(1)}, bf16[64,128]{1,0:T(8,128)(2,1)S(1)}, u32[]{:S(2)}, u32[]{:S(2)}) %collective-permute-start.7) | collective-permute-done | bytes 16416 | tf_op jit(solution)/shard_map/ppermute | solution.py:325
  18.9 0.0 copy-done
  18.9 0.2 begin.1.partial
  19.0 0.0 collective-permute-done.8.other
  19.1 0.3 %collective-permute-done.9.same = bf16[80,128]{1,0:T(8,128)(2,1)S(1)} collective-permute-done((bf16[80,128]{1,0:T(8,128)(2,1)S(1)}, bf16[80,128]{1,0:T(8,128)(2,1)S(1)}, u32[]{:S(2)}, u32[]{:S(2)}) %collective-permute-start.9) | collective-permute-done | bytes 20512 | tf_op jit(solution)/shard_map/ppermute | solution.py:325
  19.3 0.8 %project.1 = bf16[64,512]{1,0:T(8,128)(2,1)} custom-call(f32[64,512]{1,0:T(8,128)S(1)} %begin.1.partial, bf16[80,128]{1,0:T(8,128)(2,1)S(1)} %collective-permute-done.8.other, bf16[80,128]{1,0:T(8,128)(2,1)S(1)} %collective-permute-done.9.same, bf16[512,512]{1,0:T(8,128)(2,1)S(1)} %copy-done), custom_call_target="tpu_custom_call" | custom-call | tf_op jit(solution)/shard_map/project/pallas_call | solution.py:431
  (1 shorter events, 0.0 us)
Async XLA Ops:
  1.0 5.1 %collective-permute-start.3 = (bf16[64,256]{1,0:T(8,128)(2,1)S(1)}, bf16[64,256]{1,0:T(8,128)(2,1)S(1)}, u32[]{:S(2)}, u32[]{:S(2)}) collective-permute-start(bf16[64,256]{1,0:T(8,128)(2,1)S(1)} %get-tuple-element.29.quarter), channel_id=1, source_target_pairs={{0,4},{4,0},{8,12},{12,8},{16,20},{20,16},{24,28},{28,24},{1,5},{5... | collective-permute-start | bytes 98312 | tf_op jit(solution)/shard_map/ppermute | solution.py:325
  4.0 7.0 %collective-permute-start.2 = (bf16[64,256]{1,0:T(8,128)(2,1)S(1)}, bf16[64,256]{1,0:T(8,128)(2,1)S(1)}, u32[]{:S(2)}, u32[]{:S(2)}) collective-permute-start(bf16[64,256]{1,0:T(8,128)(2,1)S(1)} %get-tuple-element.29.quarter), channel_id=1, source_target_pairs={{4,12},{8,0},{12,20},{16,8},{20,28},{24,16},{0,4},{28,24},{5,13},{... | collective-permute-start | bytes 98312 | tf_op jit(solution)/shard_map/ppermute | solution.py:369
  4.1 8.1 %collective-permute-start = (bf16[192,256]{1,0:T(8,128)(2,1)S(1)}, bf16[192,256]{1,0:T(8,128)(2,1)S(1)}, u32[]{:S(2)}, u32[]{:S(2)}) collective-permute-start(bf16[192,256]{1,0:T(8,128)(2,1)S(1)} %get-tuple-element.27), channel_id=1, source_target_pairs={{0,4},{4,0},{8,12},{12,8},{16,20},{20,16},{24,28},{28,24},{1,5},{5... | collective-permute-start | bytes 294920 | tf_op jit(solution)/shard_map/ppermute | solution.py:325
  6.1 6.0 %collective-permute-start.1 = (bf16[192,256]{1,0:T(8,128)(2,1)S(1)}, bf16[192,256]{1,0:T(8,128)(2,1)S(1)}, u32[]{:S(2)}, u32[]{:S(2)}) collective-permute-start(bf16[192,256]{1,0:T(8,128)(2,1)S(1)} %get-tuple-element.28), channel_id=1, source_target_pairs={{0,1},{1,0},{2,3},{3,2},{4,8},{5,9},{6,10},{7,11},{8,4},{9,5},{10,... | collective-permute-start | bytes 294920 | tf_op jit(solution)/shard_map/ppermute | solution.py:344
  6.2 7.5 %collective-permute-start.4 = (bf16[64,256]{1,0:T(8,128)(2,1)S(1)}, bf16[64,256]{1,0:T(8,128)(2,1)S(1)}, u32[]{:S(2)}, u32[]{:S(2)}) collective-permute-start(bf16[64,256]{1,0:T(8,128)(2,1)S(1)} %get-tuple-element.33), channel_id=1, source_target_pairs={{0,8},{4,12},{8,16},{12,20},{16,24},{20,28},{24,0},{28,4},{1,9},{5... | collective-permute-start | bytes 98312 | tf_op jit(solution)/shard_map/ppermute | solution.py:370
  8.2 5.4 %collective-permute-start.5 = (bf16[64,256]{1,0:T(8,128)(2,1)S(1)}, bf16[64,256]{1,0:T(8,128)(2,1)S(1)}, u32[]{:S(2)}, u32[]{:S(2)}) collective-permute-start(bf16[64,256]{1,0:T(8,128)(2,1)S(1)} %get-tuple-element.34), channel_id=1, source_target_pairs={{0,16},{4,20},{8,24},{12,28},{16,0},{20,4},{24,8},{28,12},{1,17},{... | collective-permute-start | bytes 98312 | tf_op jit(solution)/shard_map/ppermute | solution.py:325
  11.0 3.9 %collective-permute-start.6 = (bf16[64,256]{1,0:T(8,128)(2,1)S(1)}, bf16[64,256]{1,0:T(8,128)(2,1)S(1)}, u32[]{:S(2)}, u32[]{:S(2)}) collective-permute-start(bf16[64,256]{1,0:T(8,128)(2,1)S(1)} %get-tuple-element.37), channel_id=1, source_target_pairs={{8,0},{12,4},{16,8},{20,12},{24,16},{28,20},{0,24},{4,28},{9,1},{1... | collective-permute-start | bytes 98312 | tf_op jit(solution)/shard_map/ppermute | solution.py:371
  15.4 3.6 %collective-permute-start.8 = (bf16[80,128]{1,0:T(8,128)(2,1)S(1)}, bf16[80,128]{1,0:T(8,128)(2,1)S(1)}, u32[]{:S(2)}, u32[]{:S(2)}) collective-permute-start(bf16[80,128]{1,0:T(8,128)(2,1)S(1)} %get-tuple-element.43), channel_id=1, source_target_pairs={{0,3},{1,2},{2,1},{3,0},{4,7},{5,6},{6,5},{7,4},{8,11},{9,10},{10,... | collective-permute-start | bytes 61448 | tf_op jit(solution)/shard_map/ppermute | solution.py:325
  15.5 3.8 %collective-permute-start.9 = (bf16[80,128]{1,0:T(8,128)(2,1)S(1)}, bf16[80,128]{1,0:T(8,128)(2,1)S(1)}, u32[]{:S(2)}, u32[]{:S(2)}) collective-permute-start(bf16[80,128]{1,0:T(8,128)(2,1)S(1)} %get-tuple-element.44), channel_id=1, source_target_pairs={{0,2},{1,3},{2,0},{3,1},{4,6},{5,7},{6,4},{7,5},{8,10},{9,11},{10,... | collective-permute-start | bytes 61448 | tf_op jit(solution)/shard_map/ppermute | solution.py:325
  17.1 1.8 %copy-start = (bf16[512,512]{1,0:T(8,128)(2,1)S(1)}, bf16[512,512]{1,0:T(8,128)(2,1)}, u32[]{:S(2)}) copy-start(bf16[512,512]{1,0:T(8,128)(2,1)} %weight.3) | copy-start | bytes 1572868
  17.6 1.2 %collective-permute-start.7 = (bf16[64,128]{1,0:T(8,128)(2,1)S(1)}, bf16[64,128]{1,0:T(8,128)(2,1)S(1)}, u32[]{:S(2)}, u32[]{:S(2)}) collective-permute-start(bf16[64,128]{1,0:T(8,128)(2,1)S(1)} %get-tuple-element.42), channel_id=1, source_target_pairs={{0,1},{1,0},{2,3},{3,2},{4,5},{5,4},{6,7},{7,6},{8,9},{9,8},{10,11... | collective-permute-start | bytes 49160 | tf_op jit(solution)/shard_map/ppermute | solution.py:325

commit v33 on v26

--- a/solution.py
+++ b/solution.py
@@ -227,8 +227,9 @@
         numer = numer + jnp.dot(
             weights.astype(jnp.bfloat16), part_values, preferred_element_type=jnp.float32
         )
-    mean = numer / total
-    attended = jnp.where(first_head, mean[:LEAF], mean[LEAF:]).astype(jnp.bfloat16)
+    own_numer = jnp.where(first_head, numer[:LEAF], numer[LEAF:])
+    own_total = jnp.where(first_head, total[:LEAF], total[LEAF:])
+    attended = (own_numer / own_total).astype(jnp.bfloat16)
     second = (lax.axis_index("head") & 1) == 1
     same[:HALF] = jnp.where(second, attended[HALF:], attended[:HALF])
     other[:HALF] = jnp.where(second, attended[:HALF], attended[HALF:])

time: 20.3 us -> 20.3 us (level)
  no operation moved by 1% of the time
where the time goes in v33:
time: 20.3 us; the launch traced here: 20.2 us
  starting transfers between devices  13.1 us (65%)
  Pallas kernels  3.69 us (18%)
  waiting for transfers between devices  3.32 us (16%)
    ppermute x6, starting transfers between devices, swap(): lax.ppermute(array, axis, [(i, i ^ bit) for i in range(lax.axis_size(axis...  9.79 us
    ppermute x1, starting transfers between devices, shards(): early = (lax.ppermute(upward, 'seq', shift), swap(eighth, 4))  2.04 us
    ppermute x6, waiting for transfers between devices, swap(): lax.ppermute(array, axis, [(i, i ^ bit) for i in range(lax.axis_size(axis...  1.22 us
    ppermute x1, starting transfers between devices, shards(): lax.ppermute(downward, 'seq', [(target, source) for source, target in shi...  1.18 us
    ppermute x1, waiting for transfers between devices, shards(): early = (lax.ppermute(upward, 'seq', shift), swap(eighth, 4))  1.1 us
    ppermute x1, waiting for transfers between devices, shards(): lax.ppermute(downward, 'seq', [(target, source) for source, target in shi...  1 us
    pallas_call x1, Pallas kernels, shards(): kernel_call(functools.partial(pack_kernel, not paired), 'pack', 16, [HBM]...  0.99 us
    pallas_call x1, Pallas kernels, shards(): kernel_call(project_kernel, 'project', 8, [VMEM] * 4, [(share, out_weight...  0.81 us
  transfers between devices with their start and end apart: 10, of which 4 were waited for; matrix products, arithmetic and copies ran while one was open for 0% of the time, Pallas kernels for 7%

profile of v33, /device:TPU:0, one launch (start us, length us, event | category | flops | bytes accessed | tf_op | source)
XLA Modules:
  0.0 20.2 jit_solution(13633467204228820436)
XLA Ops:
  0.0 1.0 %pack.1 = (bf16[256,128]{1,0:T(8,128)(2,1)S(1)}, bf16[256,256]{1,0:T(8,128)(2,1)S(1)}, bf16[192,256]{1,0:T(8,128)(2,1)S(1)}, bf16[192,256]{1,0:T(8,128)(2,1)S(1)}, bf16[64,256]{1,0:T(8,128)(2,1)S(1)}) custom-call(bf16[256,128]{1,0:T(8,128)(2,1)} %queries.1, bf16[256,128]{1,0:T(8,128)(2,1)} %keys.1, bf16[256,128]{1,0:T(8,128)(2,1)} %values.1), custom_call_target="tpu_custom_call" | custom-call | bytes 1048576 | tf_op jit(solution)/shard_map/pack/pallas_call | solution.py:319
  1.0 3.0 %collective-permute-start.3 = (bf16[64,256]{1,0:T(8,128)(2,1)S(1)}, bf16[64,256]{1,0:T(8,128)(2,1)S(1)}, u32[]{:S(2)}, u32[]{:S(2)}) collective-permute-start(bf16[64,256]{1,0:T(8,128)(2,1)S(1)} %get-tuple-element.29.quarter), channel_id=1, source_target_pairs={{0,4},{4,0},{8,12},{12,8},{16,20},{20,16},{24,28},{28,24},{1,5},{5... | collective-permute-start | bytes 98312 | tf_op jit(solution)/shard_map/ppermute | solution.py:317
  4.0 0.1 collective-permute-start.2
  4.1 2.0 %collective-permute-start = (bf16[192,256]{1,0:T(8,128)(2,1)S(1)}, bf16[192,256]{1,0:T(8,128)(2,1)S(1)}, u32[]{:S(2)}, u32[]{:S(2)}) collective-permute-start(bf16[192,256]{1,0:T(8,128)(2,1)S(1)} %get-tuple-element.27), channel_id=1, source_target_pairs={{0,4},{4,0},{8,12},{12,8},{16,20},{20,16},{24,28},{28,24},{1,5},{5... | collective-permute-start | bytes 294920 | tf_op jit(solution)/shard_map/ppermute | solution.py:317
  6.1 0.0 collective-permute-start.1
  6.1 0.0 collective-permute-done.3.theirs
  6.2 2.0 %collective-permute-start.4 = (bf16[64,256]{1,0:T(8,128)(2,1)S(1)}, bf16[64,256]{1,0:T(8,128)(2,1)S(1)}, u32[]{:S(2)}, u32[]{:S(2)}) collective-permute-start(bf16[64,256]{1,0:T(8,128)(2,1)S(1)} %get-tuple-element.33), channel_id=1, source_target_pairs={{0,8},{4,12},{8,16},{12,20},{16,24},{20,28},{24,0},{28,4},{1,9},{5... | collective-permute-start | bytes 98312 | tf_op jit(solution)/shard_map/ppermute | solution.py:362
  8.2 2.8 %collective-permute-start.5 = (bf16[64,256]{1,0:T(8,128)(2,1)S(1)}, bf16[64,256]{1,0:T(8,128)(2,1)S(1)}, u32[]{:S(2)}, u32[]{:S(2)}) collective-permute-start(bf16[64,256]{1,0:T(8,128)(2,1)S(1)} %get-tuple-element.34), channel_id=1, source_target_pairs={{0,16},{4,20},{8,24},{12,28},{16,0},{20,4},{24,8},{28,12},{1,17},{... | collective-permute-start | bytes 98312 | tf_op jit(solution)/shard_map/ppermute | solution.py:317
  11.0 0.0 collective-permute-done.2.rest_0_
  11.0 1.2 %collective-permute-start.6 = (bf16[64,256]{1,0:T(8,128)(2,1)S(1)}, bf16[64,256]{1,0:T(8,128)(2,1)S(1)}, u32[]{:S(2)}, u32[]{:S(2)}) collective-permute-start(bf16[64,256]{1,0:T(8,128)(2,1)S(1)} %get-tuple-element.37), channel_id=1, source_target_pairs={{8,0},{12,4},{16,8},{20,12},{24,16},{28,20},{0,24},{4,28},{9,1},{1... | collective-permute-start | bytes 98312 | tf_op jit(solution)/shard_map/ppermute | solution.py:363
  12.1 0.0 collective-permute-done.inner
  12.1 0.0 collective-permute-done.1.outer
  12.2 0.4 %near.1 = (f32[2,256,512]{2,1,0:T(8,128)S(1)}, bf16[2,512,128]{2,1,0:T(8,128)(2,1)S(1)}, bf16[128,256]{1,0:T(8,128)(2,1)S(1)}) custom-call(bf16[256,128]{1,0:T(8,128)(2,1)S(1)} %get-tuple-element.25.queries, bf16[256,256]{1,0:T(8,128)(2,1)S(1)} %get-tuple-element.26.own, bf16[192,256]{1,0:T(8,128)(2,1)S(1)} %collective-permute-done.inner, ...), custom_call_target="tpu_custom_call" | custom-call | flops 67108864 | bytes 1048576 | tf_op jit(solution)/shard_map/near/pallas_call | solution.py:368
  12.5 1.1 %collective-permute-done.4.rest_0_ = bf16[64,256]{1,0:T(8,128)(2,1)S(1)} collective-permute-done((bf16[64,256]{1,0:T(8,128)(2,1)S(1)}, bf16[64,256]{1,0:T(8,128)(2,1)S(1)}, u32[]{:S(2)}, u32[]{:S(2)}) %collective-permute-start.4) | collective-permute-done | bytes 32800 | tf_op jit(solution)/shard_map/ppermute | solution.py:362
  13.6 0.0 collective-permute-done.5.rest_1_
  13.6 0.2 %mid.1 = (f32[2,256,256]{2,1,0:T(8,128)S(1)}, bf16[256,128]{1,0:T(8,128)(2,1)S(1)}) custom-call(bf16[256,128]{1,0:T(8,128)(2,1)S(1)} %get-tuple-element.25.queries, bf16[128,256]{1,0:T(8,128)(2,1)S(1)} %get-tuple-element.32.shared, bf16[64,256]{1,0:T(8,128)(2,1)S(1)} %collective-permute-done.4.rest_0_, bf16[64,256]{1,0:T(8,128)(2,1)S(1)} %collective-permute-done.5.rest_1_), custom_call_target="tpu_custom_call" | custom-call | flops 1000000000 | bytes 1048576 | tf_op jit(solution)/shard_map/mid/pallas_call | solution.py:382
  13.9 1.0 %collective-permute-done.6.rest_0_ = bf16[64,256]{1,0:T(8,128)(2,1)S(1)} collective-permute-done((bf16[64,256]{1,0:T(8,128)(2,1)S(1)}, bf16[64,256]{1,0:T(8,128)(2,1)S(1)}, u32[]{:S(2)}, u32[]{:S(2)}) %collective-permute-start.6) | collective-permute-done | bytes 32800 | tf_op jit(solution)/shard_map/ppermute | solution.py:363
  14.9 0.5 %leaves.1 = (bf16[80,128]{1,0:T(8,128)(2,1)S(1)}, bf16[80,128]{1,0:T(8,128)(2,1)S(1)}, bf16[64,128]{1,0:T(8,128)(2,1)S(1)}, bf16[64,128]{1,0:T(8,128)(2,1)S(1)}, f32[8,64]{1,0:T(8,128)S(1)}) custom-call(bf16[256,128]{1,0:T(8,128)(2,1)S(1)} %get-tuple-element.25.queries, f32[2,256,512]{2,1,0:T(8,128)S(1)} %get-tuple-element.30.near_scores, ...), custom_call_target="tpu_custom_call" | custom-call | flops 109051904 | bytes 1048576 | tf_op jit(solution)/shard_map/leaves/pallas_call | solution.py:394
  15.4 0.1 collective-permute-start.8
  15.5 1.6 %collective-permute-start.9 = (bf16[80,128]{1,0:T(8,128)(2,1)S(1)}, bf16[80,128]{1,0:T(8,128)(2,1)S(1)}, u32[]{:S(2)}, u32[]{:S(2)}) collective-permute-start(bf16[80,128]{1,0:T(8,128)(2,1)S(1)} %get-tuple-element.44), channel_id=1, source_target_pairs={{0,2},{1,3},{2,0},{3,1},{4,6},{5,7},{6,4},{7,5},{8,10},{9,11},{10,... | collective-permute-start | bytes 61448 | tf_op jit(solution)/shard_map/ppermute | solution.py:317
  17.1 0.0 copy-start
  17.1 0.5 %stays.1 = (bf16[64,128]{1,0:T(8,128)(2,1)S(1)}, bf16[64,128]{1,0:T(8,128)(2,1)S(1)}) custom-call(bf16[256,128]{1,0:T(8,128)(2,1)S(1)} %get-tuple-element.25.queries, f32[2,256,512]{2,1,0:T(8,128)S(1)} %get-tuple-element.30.near_scores, bf16[2,512,128]{2,1,0:T(8,128)(2,1)S(1)} %get-tuple-element.31.near_values, ...), custom_call_target="tpu_custom_call" | custom-call | flops 109051904 | bytes 1048576 | tf_op jit(solution)/shard_map/stays/pallas_call | solution.py:409
  17.6 0.3 %collective-permute-start.7 = (bf16[64,128]{1,0:T(8,128)(2,1)S(1)}, bf16[64,128]{1,0:T(8,128)(2,1)S(1)}, u32[]{:S(2)}, u32[]{:S(2)}) collective-permute-start(bf16[64,128]{1,0:T(8,128)(2,1)S(1)} %get-tuple-element.42), channel_id=1, source_target_pairs={{0,1},{1,0},{2,3},{3,2},{4,5},{5,4},{6,7},{7,6},{8,9},{9,8},{10,11... | collective-permute-start | bytes 49160 | tf_op jit(solution)/shard_map/ppermute | solution.py:317
  18.0 0.9 %collective-permute-done.7.other = bf16[64,128]{1,0:T(8,128)(2,1)S(1)} collective-permute-done((bf16[64,128]{1,0:T(8,128)(2,1)S(1)}, bf16[64,128]{1,0:T(8,128)(2,1)S(1)}, u32[]{:S(2)}, u32[]{:S(2)}) %collective-permute-start.7) | collective-permute-done | bytes 16416 | tf_op jit(solution)/shard_map/ppermute | solution.py:317
  18.9 0.0 copy-done
  18.9 0.2 begin.1.partial
  19.0 0.0 collective-permute-done.8.other
  19.1 0.3 %collective-permute-done.9.same = bf16[80,128]{1,0:T(8,128)(2,1)S(1)} collective-permute-done((bf16[80,128]{1,0:T(8,128)(2,1)S(1)}, bf16[80,128]{1,0:T(8,128)(2,1)S(1)}, u32[]{:S(2)}, u32[]{:S(2)}) %collective-permute-start.9) | collective-permute-done | bytes 20512 | tf_op jit(solution)/shard_map/ppermute | solution.py:317
  19.3 0.8 %project.1 = bf16[64,512]{1,0:T(8,128)(2,1)} custom-call(f32[64,512]{1,0:T(8,128)S(1)} %begin.1.partial, bf16[80,128]{1,0:T(8,128)(2,1)S(1)} %collective-permute-done.8.other, bf16[80,128]{1,0:T(8,128)(2,1)S(1)} %collective-permute-done.9.same, bf16[512,512]{1,0:T(8,128)(2,1)S(1)} %copy-done), custom_call_target="tpu_custom_call" | custom-call | bytes 1048576 | tf_op jit(solution)/shard_map/project/pallas_call | solution.py:422
  (1 shorter events, 0.0 us)
Async XLA Ops:
  1.0 5.1 %collective-permute-start.3 = (bf16[64,256]{1,0:T(8,128)(2,1)S(1)}, bf16[64,256]{1,0:T(8,128)(2,1)S(1)}, u32[]{:S(2)}, u32[]{:S(2)}) collective-permute-start(bf16[64,256]{1,0:T(8,128)(2,1)S(1)} %get-tuple-element.29.quarter), channel_id=1, source_target_pairs={{0,4},{4,0},{8,12},{12,8},{16,20},{20,16},{24,28},{28,24},{1,5},{5... | collective-permute-start | bytes 98312 | tf_op jit(solution)/shard_map/ppermute | solution.py:317
  4.0 7.0 %collective-permute-start.2 = (bf16[64,256]{1,0:T(8,128)(2,1)S(1)}, bf16[64,256]{1,0:T(8,128)(2,1)S(1)}, u32[]{:S(2)}, u32[]{:S(2)}) collective-permute-start(bf16[64,256]{1,0:T(8,128)(2,1)S(1)} %get-tuple-element.29.quarter), channel_id=1, source_target_pairs={{4,12},{8,0},{12,20},{16,8},{20,28},{24,16},{0,4},{28,24},{5,13},{... | collective-permute-start | bytes 98312 | tf_op jit(solution)/shard_map/ppermute | solution.py:361
  4.1 8.1 %collective-permute-start = (bf16[192,256]{1,0:T(8,128)(2,1)S(1)}, bf16[192,256]{1,0:T(8,128)(2,1)S(1)}, u32[]{:S(2)}, u32[]{:S(2)}) collective-permute-start(bf16[192,256]{1,0:T(8,128)(2,1)S(1)} %get-tuple-element.27), channel_id=1, source_target_pairs={{0,4},{4,0},{8,12},{12,8},{16,20},{20,16},{24,28},{28,24},{1,5},{5... | collective-permute-start | bytes 294920 | tf_op jit(solution)/shard_map/ppermute | solution.py:317
  6.1 6.0 %collective-permute-start.1 = (bf16[192,256]{1,0:T(8,128)(2,1)S(1)}, bf16[192,256]{1,0:T(8,128)(2,1)S(1)}, u32[]{:S(2)}, u32[]{:S(2)}) collective-permute-start(bf16[192,256]{1,0:T(8,128)(2,1)S(1)} %get-tuple-element.28), channel_id=1, source_target_pairs={{0,1},{1,0},{2,3},{3,2},{4,8},{5,9},{6,10},{7,11},{8,4},{9,5},{10,... | collective-permute-start | bytes 294920 | tf_op jit(solution)/shard_map/ppermute | solution.py:336
  6.2 7.5 %collective-permute-start.4 = (bf16[64,256]{1,0:T(8,128)(2,1)S(1)}, bf16[64,256]{1,0:T(8,128)(2,1)S(1)}, u32[]{:S(2)}, u32[]{:S(2)}) collective-permute-start(bf16[64,256]{1,0:T(8,128)(2,1)S(1)} %get-tuple-element.33), channel_id=1, source_target_pairs={{0,8},{4,12},{8,16},{12,20},{16,24},{20,28},{24,0},{28,4},{1,9},{5... | collective-permute-start | bytes 98312 | tf_op jit(solution)/shard_map/ppermute | solution.py:362
  8.2 5.4 %collective-permute-start.5 = (bf16[64,256]{1,0:T(8,128)(2,1)S(1)}, bf16[64,256]{1,0:T(8,128)(2,1)S(1)}, u32[]{:S(2)}, u32[]{:S(2)}) collective-permute-start(bf16[64,256]{1,0:T(8,128)(2,1)S(1)} %get-tuple-element.34), channel_id=1, source_target_pairs={{0,16},{4,20},{8,24},{12,28},{16,0},{20,4},{24,8},{28,12},{1,17},{... | collective-permute-start | bytes 98312 | tf_op jit(solution)/shard_map/ppermute | solution.py:317
  11.0 3.9 %collective-permute-start.6 = (bf16[64,256]{1,0:T(8,128)(2,1)S(1)}, bf16[64,256]{1,0:T(8,128)(2,1)S(1)}, u32[]{:S(2)}, u32[]{:S(2)}) collective-permute-start(bf16[64,256]{1,0:T(8,128)(2,1)S(1)} %get-tuple-element.37), channel_id=1, source_target_pairs={{8,0},{12,4},{16,8},{20,12},{24,16},{28,20},{0,24},{4,28},{9,1},{1... | collective-permute-start | bytes 98312 | tf_op jit(solution)/shard_map/ppermute | solution.py:363
  15.4 3.6 %collective-permute-start.8 = (bf16[80,128]{1,0:T(8,128)(2,1)S(1)}, bf16[80,128]{1,0:T(8,128)(2,1)S(1)}, u32[]{:S(2)}, u32[]{:S(2)}) collective-permute-start(bf16[80,128]{1,0:T(8,128)(2,1)S(1)} %get-tuple-element.43), channel_id=1, source_target_pairs={{0,3},{1,2},{2,1},{3,0},{4,7},{5,6},{6,5},{7,4},{8,11},{9,10},{10,... | collective-permute-start | bytes 61448 | tf_op jit(solution)/shard_map/ppermute | solution.py:317
  15.5 3.8 %collective-permute-start.9 = (bf16[80,128]{1,0:T(8,128)(2,1)S(1)}, bf16[80,128]{1,0:T(8,128)(2,1)S(1)}, u32[]{:S(2)}, u32[]{:S(2)}) collective-permute-start(bf16[80,128]{1,0:T(8,128)(2,1)S(1)} %get-tuple-element.44), channel_id=1, source_target_pairs={{0,2},{1,3},{2,0},{3,1},{4,6},{5,7},{6,4},{7,5},{8,10},{9,11},{10,... | collective-permute-start | bytes 61448 | tf_op jit(solution)/shard_map/ppermute | solution.py:317
  17.1 1.8 %copy-start = (bf16[512,512]{1,0:T(8,128)(2,1)S(1)}, bf16[512,512]{1,0:T(8,128)(2,1)}, u32[]{:S(2)}) copy-start(bf16[512,512]{1,0:T(8,128)(2,1)} %weight.3) | copy-start | bytes 1572868
  17.6 1.2 %collective-permute-start.7 = (bf16[64,128]{1,0:T(8,128)(2,1)S(1)}, bf16[64,128]{1,0:T(8,128)(2,1)S(1)}, u32[]{:S(2)}, u32[]{:S(2)}) collective-permute-start(bf16[64,128]{1,0:T(8,128)(2,1)S(1)} %get-tuple-element.42), channel_id=1, source_target_pairs={{0,1},{1,0},{2,3},{3,2},{4,5},{5,4},{6,7},{7,6},{8,9},{9,8},{10,11... | collective-permute-start | bytes 49160 | tf_op jit(solution)/shard_map/ppermute | solution.py:317

commit v34 on v31

--- a/solution.py
+++ b/solution.py
@@ -228,8 +228,9 @@
         numer = numer + jnp.dot(
             weights.astype(jnp.bfloat16), part_values, preferred_element_type=jnp.float32
         )
-    mean = numer / total
-    attended = jnp.where(first_head, mean[:LEAF], mean[LEAF:]).astype(jnp.bfloat16)
+    own_numer = jnp.where(first_head, numer[:LEAF], numer[LEAF:])
+    own_total = jnp.where(first_head, total[:LEAF], total[LEAF:])
+    attended = (own_numer / own_total).astype(jnp.bfloat16)
     second = (lax.axis_index("head") & 1) == 1
     same[:HALF] = jnp.where(second, attended[HALF:], attended[:HALF])
     other[:HALF] = jnp.where(second, attended[:HALF], attended[HALF:])

time: 20.3 us -> 20.3 us (level)
  no operation moved by 1% of the time
where the time goes in v34:
time: 20.3 us; the launch traced here: 20.1 us
  starting transfers between devices  13 us (64%)
  Pallas kernels  3.7 us (18%)
  waiting for transfers between devices  3.39 us (17%)
    ppermute x6, starting transfers between devices, swap(): lax.ppermute(array, axis, [(i, i ^ bit) for i in range(lax.axis_size(axis...  9.96 us
    ppermute x1, starting transfers between devices, shards(): early = (lax.ppermute(upward, 'seq', shift), swap(eighth, 4))  1.85 us
    ppermute x6, waiting for transfers between devices, swap(): lax.ppermute(array, axis, [(i, i ^ bit) for i in range(lax.axis_size(axis...  1.22 us
    ppermute x1, waiting for transfers between devices, shards(): early = (lax.ppermute(upward, 'seq', shift), swap(eighth, 4))  1.19 us
    ppermute x1, starting transfers between devices, shards(): lax.ppermute(downward, 'seq', [(target, source) for source, target in shi...  1.11 us
    pallas_call x1, Pallas kernels, shards(): kernel_call(functools.partial(pack_kernel, not paired), 'pack', 16, [HBM]...  0.98 us
    ppermute x1, waiting for transfers between devices, shards(): lax.ppermute(downward, 'seq', [(target, source) for source, target in shi...  0.97 us
    pallas_call x1, Pallas kernels, shards(): kernel_call(project_kernel, 'project', 8, [VMEM] * 4, [(share, out_weight...  0.81 us
  transfers between devices with their start and end apart: 10, of which 4 were waited for; matrix products, arithmetic and copies ran while one was open for 0% of the time, Pallas kernels for 7%

profile of v34, /device:TPU:0, one launch (start us, length us, event | category | flops | bytes accessed | tf_op | source)
XLA Modules:
  0.0 20.1 jit_solution(12417558991313291854)
XLA Ops:
  0.0 1.0 %pack.1 = (bf16[256,128]{1,0:T(8,128)(2,1)S(1)}, bf16[256,256]{1,0:T(8,128)(2,1)S(1)}, bf16[128,256]{1,0:T(8,128)(2,1)S(1)}, bf16[64,256]{1,0:T(8,128)(2,1)S(1)}) custom-call(bf16[256,128]{1,0:T(8,128)(2,1)} %queries.1, bf16[256,128]{1,0:T(8,128)(2,1)} %keys.1, bf16[256,128]{1,0:T(8,128)(2,1)} %values.1), custom_call_target="tpu_custom_call" | custom-call | bytes 1048576 | tf_op jit(solution)/shard_map/pack/pallas_call | solution.py:320
  1.0 3.0 %collective-permute-start.3 = (bf16[64,256]{1,0:T(8,128)(2,1)S(1)}, bf16[64,256]{1,0:T(8,128)(2,1)S(1)}, u32[]{:S(2)}, u32[]{:S(2)}) collective-permute-start(bf16[64,256]{1,0:T(8,128)(2,1)S(1)} %get-tuple-element.31.quarter), channel_id=1, source_target_pairs={{0,4},{4,0},{8,12},{12,8},{16,20},{20,16},{24,28},{28,24},{1,5},{5... | collective-permute-start | bytes 98312 | tf_op jit(solution)/shard_map/ppermute | solution.py:318
  4.0 0.1 collective-permute-start.2
  4.1 2.1 %collective-permute-start = (bf16[192,256]{1,0:T(8,128)(2,1)S(1)}, bf16[192,256]{1,0:T(8,128)(2,1)S(1)}, u32[]{:S(2)}, u32[]{:S(2)}) collective-permute-start(bf16[192,256]{1,0:T(8,128)(2,1)S(1)} %get-tuple-element.29), channel_id=1, source_target_pairs={{0,4},{4,0},{8,12},{12,8},{16,20},{20,16},{24,28},{28,24},{1,5},{5... | collective-permute-start | bytes 294920 | tf_op jit(solution)/shard_map/ppermute | solution.py:318
  6.2 0.0 collective-permute-start.1
  6.2 0.0 collective-permute-done.3.theirs
  6.2 1.9 %collective-permute-start.4 = (bf16[64,256]{1,0:T(8,128)(2,1)S(1)}, bf16[64,256]{1,0:T(8,128)(2,1)S(1)}, u32[]{:S(2)}, u32[]{:S(2)}) collective-permute-start(bf16[64,256]{1,0:T(8,128)(2,1)S(1)} %get-tuple-element.35), channel_id=1, source_target_pairs={{0,8},{4,12},{8,16},{12,20},{16,24},{20,28},{24,0},{28,4},{1,9},{5... | collective-permute-start | bytes 98312 | tf_op jit(solution)/shard_map/ppermute | solution.py:365
  8.1 2.9 %collective-permute-start.5 = (bf16[64,256]{1,0:T(8,128)(2,1)S(1)}, bf16[64,256]{1,0:T(8,128)(2,1)S(1)}, u32[]{:S(2)}, u32[]{:S(2)}) collective-permute-start(bf16[64,256]{1,0:T(8,128)(2,1)S(1)} %get-tuple-element.36), channel_id=1, source_target_pairs={{0,16},{4,20},{8,24},{12,28},{16,0},{20,4},{24,8},{28,12},{1,17},{... | collective-permute-start | bytes 98312 | tf_op jit(solution)/shard_map/ppermute | solution.py:318
  11.0 0.0 collective-permute-done.2.rest_0_
  11.0 1.1 %collective-permute-start.6 = (bf16[64,256]{1,0:T(8,128)(2,1)S(1)}, bf16[64,256]{1,0:T(8,128)(2,1)S(1)}, u32[]{:S(2)}, u32[]{:S(2)}) collective-permute-start(bf16[64,256]{1,0:T(8,128)(2,1)S(1)} %get-tuple-element.39), channel_id=1, source_target_pairs={{8,0},{12,4},{16,8},{20,12},{24,16},{28,20},{0,24},{4,28},{9,1},{1... | collective-permute-start | bytes 98312 | tf_op jit(solution)/shard_map/ppermute | solution.py:366
  12.1 0.0 collective-permute-done.inner
  12.1 0.0 collective-permute-done.1.outer
  12.1 0.4 %near.1 = (f32[2,256,512]{2,1,0:T(8,128)S(1)}, bf16[2,512,128]{2,1,0:T(8,128)(2,1)S(1)}, bf16[128,256]{1,0:T(8,128)(2,1)S(1)}) custom-call(bf16[256,128]{1,0:T(8,128)(2,1)S(1)} %get-tuple-element.26.queries, bf16[256,256]{1,0:T(8,128)(2,1)S(1)} %get-tuple-element.27.own, bf16[192,256]{1,0:T(8,128)(2,1)S(1)} %collective-permute-done.inner, ...), custom_call_target="tpu_custom_call" | custom-call | flops 67108864 | bytes 1048576 | tf_op jit(solution)/shard_map/near/pallas_call | solution.py:371
  12.5 1.2 %collective-permute-done.4.rest_0_ = bf16[64,256]{1,0:T(8,128)(2,1)S(1)} collective-permute-done((bf16[64,256]{1,0:T(8,128)(2,1)S(1)}, bf16[64,256]{1,0:T(8,128)(2,1)S(1)}, u32[]{:S(2)}, u32[]{:S(2)}) %collective-permute-start.4) | collective-permute-done | bytes 32800 | tf_op jit(solution)/shard_map/ppermute | solution.py:365
  13.7 0.0 collective-permute-done.5.rest_1_
  13.7 0.2 %mid.1 = (f32[2,256,256]{2,1,0:T(8,128)S(1)}, bf16[256,128]{1,0:T(8,128)(2,1)S(1)}) custom-call(bf16[256,128]{1,0:T(8,128)(2,1)S(1)} %get-tuple-element.26.queries, bf16[128,256]{1,0:T(8,128)(2,1)S(1)} %get-tuple-element.34.shared, bf16[64,256]{1,0:T(8,128)(2,1)S(1)} %collective-permute-done.4.rest_0_, bf16[64,256]{1,0:T(8,128)(2,1)S(1)} %collective-permute-done.5.rest_1_), custom_call_target="tpu_custom_call" | custom-call | flops 1000000000 | bytes 1048576 | tf_op jit(solution)/shard_map/mid/pallas_call | solution.py:385
  13.9 1.0 %collective-permute-done.6.rest_0_ = bf16[64,256]{1,0:T(8,128)(2,1)S(1)} collective-permute-done((bf16[64,256]{1,0:T(8,128)(2,1)S(1)}, bf16[64,256]{1,0:T(8,128)(2,1)S(1)}, u32[]{:S(2)}, u32[]{:S(2)}) %collective-permute-start.6) | collective-permute-done | bytes 32800 | tf_op jit(solution)/shard_map/ppermute | solution.py:366
  14.9 0.5 %leaves.1 = (bf16[80,128]{1,0:T(8,128)(2,1)S(1)}, bf16[80,128]{1,0:T(8,128)(2,1)S(1)}, bf16[64,128]{1,0:T(8,128)(2,1)S(1)}, bf16[64,128]{1,0:T(8,128)(2,1)S(1)}, f32[8,64]{1,0:T(8,128)S(1)}) custom-call(bf16[256,128]{1,0:T(8,128)(2,1)S(1)} %get-tuple-element.26.queries, f32[2,256,512]{2,1,0:T(8,128)S(1)} %get-tuple-element.32.near_scores, ...), custom_call_target="tpu_custom_call" | custom-call | flops 109051904 | bytes 1048576 | tf_op jit(solution)/shard_map/leaves/pallas_call | solution.py:397
  15.4 0.1 collective-permute-start.8
  15.5 1.6 %collective-permute-start.9 = (bf16[80,128]{1,0:T(8,128)(2,1)S(1)}, bf16[80,128]{1,0:T(8,128)(2,1)S(1)}, u32[]{:S(2)}, u32[]{:S(2)}) collective-permute-start(bf16[80,128]{1,0:T(8,128)(2,1)S(1)} %get-tuple-element.46), channel_id=1, source_target_pairs={{0,2},{1,3},{2,0},{3,1},{4,6},{5,7},{6,4},{7,5},{8,10},{9,11},{10,... | collective-permute-start | bytes 61448 | tf_op jit(solution)/shard_map/ppermute | solution.py:318
  17.1 0.0 copy-start
  17.1 0.5 %stays.1 = (bf16[64,128]{1,0:T(8,128)(2,1)S(1)}, bf16[64,128]{1,0:T(8,128)(2,1)S(1)}) custom-call(bf16[256,128]{1,0:T(8,128)(2,1)S(1)} %get-tuple-element.26.queries, f32[2,256,512]{2,1,0:T(8,128)S(1)} %get-tuple-element.32.near_scores, bf16[2,512,128]{2,1,0:T(8,128)(2,1)S(1)} %get-tuple-element.33.near_values, ...), custom_call_target="tpu_custom_call" | custom-call | flops 109051904 | bytes 1048576 | tf_op jit(solution)/shard_map/stays/pallas_call | solution.py:412
  17.6 0.3 %collective-permute-start.7 = (bf16[64,128]{1,0:T(8,128)(2,1)S(1)}, bf16[64,128]{1,0:T(8,128)(2,1)S(1)}, u32[]{:S(2)}, u32[]{:S(2)}) collective-permute-start(bf16[64,128]{1,0:T(8,128)(2,1)S(1)} %get-tuple-element.44), channel_id=1, source_target_pairs={{0,1},{1,0},{2,3},{3,2},{4,5},{5,4},{6,7},{7,6},{8,9},{9,8},{10,11... | collective-permute-start | bytes 49160 | tf_op jit(solution)/shard_map/ppermute | solution.py:318
  17.9 0.9 %collective-permute-done.7.other = bf16[64,128]{1,0:T(8,128)(2,1)S(1)} collective-permute-done((bf16[64,128]{1,0:T(8,128)(2,1)S(1)}, bf16[64,128]{1,0:T(8,128)(2,1)S(1)}, u32[]{:S(2)}, u32[]{:S(2)}) %collective-permute-start.7) | collective-permute-done | bytes 16416 | tf_op jit(solution)/shard_map/ppermute | solution.py:318
  18.9 0.0 copy-done
  18.9 0.2 begin.1.partial
  19.0 0.0 collective-permute-done.8.other
  19.0 0.3 %collective-permute-done.9.same = bf16[80,128]{1,0:T(8,128)(2,1)S(1)} collective-permute-done((bf16[80,128]{1,0:T(8,128)(2,1)S(1)}, bf16[80,128]{1,0:T(8,128)(2,1)S(1)}, u32[]{:S(2)}, u32[]{:S(2)}) %collective-permute-start.9) | collective-permute-done | bytes 20512 | tf_op jit(solution)/shard_map/ppermute | solution.py:318
  19.3 0.8 %project.1 = bf16[64,512]{1,0:T(8,128)(2,1)} custom-call(f32[64,512]{1,0:T(8,128)S(1)} %begin.1.partial, bf16[80,128]{1,0:T(8,128)(2,1)S(1)} %collective-permute-done.8.other, bf16[80,128]{1,0:T(8,128)(2,1)S(1)} %collective-permute-done.9.same, bf16[512,512]{1,0:T(8,128)(2,1)S(1)} %copy-done), custom_call_target="tpu_custom_call" | custom-call | bytes 1048576 | tf_op jit(solution)/shard_map/project/pallas_call | solution.py:425
  (2 shorter events, 0.1 us)
Async XLA Ops:
  1.0 5.2 %collective-permute-start.3 = (bf16[64,256]{1,0:T(8,128)(2,1)S(1)}, bf16[64,256]{1,0:T(8,128)(2,1)S(1)}, u32[]{:S(2)}, u32[]{:S(2)}) collective-permute-start(bf16[64,256]{1,0:T(8,128)(2,1)S(1)} %get-tuple-element.31.quarter), channel_id=1, source_target_pairs={{0,4},{4,0},{8,12},{12,8},{16,20},{20,16},{24,28},{28,24},{1,5},{5... | collective-permute-start | bytes 98312 | tf_op jit(solution)/shard_map/ppermute | solution.py:318
  4.0 7.0 %collective-permute-start.2 = (bf16[64,256]{1,0:T(8,128)(2,1)S(1)}, bf16[64,256]{1,0:T(8,128)(2,1)S(1)}, u32[]{:S(2)}, u32[]{:S(2)}) collective-permute-start(bf16[64,256]{1,0:T(8,128)(2,1)S(1)} %get-tuple-element.31.quarter), channel_id=1, source_target_pairs={{4,12},{8,0},{12,20},{16,8},{20,28},{24,16},{0,4},{28,24},{5,13},{... | collective-permute-start | bytes 98312 | tf_op jit(solution)/shard_map/ppermute | solution.py:364
  4.1 8.0 %collective-permute-start = (bf16[192,256]{1,0:T(8,128)(2,1)S(1)}, bf16[192,256]{1,0:T(8,128)(2,1)S(1)}, u32[]{:S(2)}, u32[]{:S(2)}) collective-permute-start(bf16[192,256]{1,0:T(8,128)(2,1)S(1)} %get-tuple-element.29), channel_id=1, source_target_pairs={{0,4},{4,0},{8,12},{12,8},{16,20},{20,16},{24,28},{28,24},{1,5},{5... | collective-permute-start | bytes 294920 | tf_op jit(solution)/shard_map/ppermute | solution.py:318
  6.2 5.9 %collective-permute-start.1 = (bf16[192,256]{1,0:T(8,128)(2,1)S(1)}, bf16[192,256]{1,0:T(8,128)(2,1)S(1)}, u32[]{:S(2)}, u32[]{:S(2)}) collective-permute-start(bf16[192,256]{1,0:T(8,128)(2,1)S(1)} %get-tuple-element.30), channel_id=1, source_target_pairs={{0,1},{1,0},{2,3},{3,2},{4,8},{5,9},{6,10},{7,11},{8,4},{9,5},{10,... | collective-permute-start | bytes 294920 | tf_op jit(solution)/shard_map/ppermute | solution.py:339
  6.2 7.4 %collective-permute-start.4 = (bf16[64,256]{1,0:T(8,128)(2,1)S(1)}, bf16[64,256]{1,0:T(8,128)(2,1)S(1)}, u32[]{:S(2)}, u32[]{:S(2)}) collective-permute-start(bf16[64,256]{1,0:T(8,128)(2,1)S(1)} %get-tuple-element.35), channel_id=1, source_target_pairs={{0,8},{4,12},{8,16},{12,20},{16,24},{20,28},{24,0},{28,4},{1,9},{5... | collective-permute-start | bytes 98312 | tf_op jit(solution)/shard_map/ppermute | solution.py:365
  8.1 5.6 %collective-permute-start.5 = (bf16[64,256]{1,0:T(8,128)(2,1)S(1)}, bf16[64,256]{1,0:T(8,128)(2,1)S(1)}, u32[]{:S(2)}, u32[]{:S(2)}) collective-permute-start(bf16[64,256]{1,0:T(8,128)(2,1)S(1)} %get-tuple-element.36), channel_id=1, source_target_pairs={{0,16},{4,20},{8,24},{12,28},{16,0},{20,4},{24,8},{28,12},{1,17},{... | collective-permute-start | bytes 98312 | tf_op jit(solution)/shard_map/ppermute | solution.py:318
  11.0 3.9 %collective-permute-start.6 = (bf16[64,256]{1,0:T(8,128)(2,1)S(1)}, bf16[64,256]{1,0:T(8,128)(2,1)S(1)}, u32[]{:S(2)}, u32[]{:S(2)}) collective-permute-start(bf16[64,256]{1,0:T(8,128)(2,1)S(1)} %get-tuple-element.39), channel_id=1, source_target_pairs={{8,0},{12,4},{16,8},{20,12},{24,16},{28,20},{0,24},{4,28},{9,1},{1... | collective-permute-start | bytes 98312 | tf_op jit(solution)/shard_map/ppermute | solution.py:366
  15.4 3.6 %collective-permute-start.8 = (bf16[80,128]{1,0:T(8,128)(2,1)S(1)}, bf16[80,128]{1,0:T(8,128)(2,1)S(1)}, u32[]{:S(2)}, u32[]{:S(2)}) collective-permute-start(bf16[80,128]{1,0:T(8,128)(2,1)S(1)} %get-tuple-element.45), channel_id=1, source_target_pairs={{0,3},{1,2},{2,1},{3,0},{4,7},{5,6},{6,5},{7,4},{8,11},{9,10},{10,... | collective-permute-start | bytes 61448 | tf_op jit(solution)/shard_map/ppermute | solution.py:318
  15.5 3.8 %collective-permute-start.9 = (bf16[80,128]{1,0:T(8,128)(2,1)S(1)}, bf16[80,128]{1,0:T(8,128)(2,1)S(1)}, u32[]{:S(2)}, u32[]{:S(2)}) collective-permute-start(bf16[80,128]{1,0:T(8,128)(2,1)S(1)} %get-tuple-element.46), channel_id=1, source_target_pairs={{0,2},{1,3},{2,0},{3,1},{4,6},{5,7},{6,4},{7,5},{8,10},{9,11},{10,... | collective-permute-start | bytes 61448 | tf_op jit(solution)/shard_map/ppermute | solution.py:318
  17.1 1.8 %copy-start = (bf16[512,512]{1,0:T(8,128)(2,1)S(1)}, bf16[512,512]{1,0:T(8,128)(2,1)}, u32[]{:S(2)}) copy-start(bf16[512,512]{1,0:T(8,128)(2,1)} %weight.3) | copy-start | bytes 1572868
  17.6 1.2 %collective-permute-start.7 = (bf16[64,128]{1,0:T(8,128)(2,1)S(1)}, bf16[64,128]{1,0:T(8,128)(2,1)S(1)}, u32[]{:S(2)}, u32[]{:S(2)}) collective-permute-start(bf16[64,128]{1,0:T(8,128)(2,1)S(1)} %get-tuple-element.44), channel_id=1, source_target_pairs={{0,1},{1,0},{2,3},{3,2},{4,5},{5,4},{6,7},{7,6},{8,9},{9,8},{10,11... | collective-permute-start | bytes 49160 | tf_op jit(solution)/shard_map/ppermute | solution.py:318
